TPU v7x, 32 devices: a whole 2x2x4 slice. The times are simulated.
32 devices in a mesh: ex: 4 (over z), row: 4 (over y, x), col: 2 (over core).
Axes of the slice: x: 2, y: 2, z: 4, core: 2. Of those that a mesh axis runs over, the one named last changes fastest.
Arguments:
- x_in: bfloat16 [4096, 768], P(('ex', 'row')), may hold values from -6 to 6
- gain_attn: float32 [768], replicated, may hold values from 0.25 to 1.75
- w_qkv: float32 [3, 768, 768], P(None, ('ex', 'row'), 'col'), may hold values from -0.21875 to 0.21875
- rel_bias: float32 [32, 12], P(None, 'col'), may hold values from -4 to 4
- w_out: float32 [768, 768], P('col', ('ex', 'row')), may hold values from -1.75 to 1.75
- gain_ffn: float32 [768], replicated, may hold values from 0.25 to 1.75
- w_router: float32 [768, 16], P(('ex', 'row')), may hold values from -0.109375 to 0.109375
- w_up: float32 [16, 768, 3072], P(('ex', 'row'), None, 'col'), may hold values from -0.21875 to 0.21875
- w_down: float32 [16, 3072, 768], P(('ex', 'row'), 'col'), may hold values from -2.5 to 2.5
- seg_ids: int32 [16, 256], P(('ex', 'row')), may hold values from 0 to 3, never falling along the last dimension, each value on 1 to 128 neighbouring positions
- expert_ids: int32 [4096], P(('ex', 'row')), may hold values from 0 to 15, as said below
- slot_ids: int32 [4096], P(('ex', 'row')), may hold values from 0 to 19, as said below
- drop_flags: int32 [4096], P(('ex', 'row')), may hold values from 0 to 1, as said below
- d_out: bfloat16 [4096, 768], P(('ex', 'row'), 'col'), may hold values from -6 to 6
Outputs:
- layer_out: bfloat16 [4096, 768], P(('ex', 'row'), 'col')
- grad_x: bfloat16 [4096, 768], P(('ex', 'row'))
- grad_gain_attn: float32 [768], replicated
- grad_w_qkv: float32 [3, 768, 768], P(None, ('ex', 'row'), 'col')
- grad_rel_bias: float32 [32, 12], P(None, 'col')
- grad_w_out: float32 [768, 768], P('col', ('ex', 'row'))
- grad_gain_ffn: float32 [768], replicated
- grad_w_router: float32 [768, 16], P(('ex', 'row'))
- grad_w_up: float32 [16, 768, 3072], P(('ex', 'row'), None, 'col')
- grad_w_down: float32 [16, 3072, 768], P(('ex', 'row'), 'col')
Inputs may be any that keep to these rules, and one draw needn't show every extreme that they name: `expert_ids`: within the 256 tokens of one sequence, the kept tokens that chose one expert hold slots 0, 1, 2, ... in token order. In every draw one expert receives 20 kept tokens from every sequence. `slot_ids`: A kept token's slot is the number of earlier tokens of its sequence that chose its expert. `drop_flags`: A token is dropped exactly when 20 earlier tokens of its sequence chose its expert. `seg_ids`: document numbers never fall along a sequence; each of the 4 documents of a sequence has a token.
All inputs are finite; a program needn't handle non-finite values.
Results may differ from a plain program's by a relative error of at most 0.022.
Values may be sent and summed in bfloat16 or wider, within the bound.
No kernel may reach another device: no remote copies, remote signals or barrier semaphores. Data moves between devices by JAX's collectives and lax.ppermute only.
A program may use at most 128 MiB of HBM per device.

v0:
```python
import math

import jax
import jax.numpy as jnp
from jax import lax
from jax.sharding import PartitionSpec as P

HEAD = 64
BUCKETS = 32

norm_eps = 1e-06
bucket_edges = (12, 16, 23, 32, 46, 64, 91)
highest = lax.Precision.HIGHEST
bf16 = jnp.bfloat16
f32 = jnp.float32


def bucket_of(offset):
    distance = jnp.abs(offset)
    far_part = jnp.zeros(distance.shape, jnp.int32)
    for edge_at in bucket_edges:
        far_part = far_part + (distance >= edge_at).astype(jnp.int32)
    inside = jnp.where(distance < 8, distance, far_part + jnp.int32(8))
    upper = jnp.where(offset > 0, jnp.int32(BUCKETS // 2), jnp.int32(0))
    return inside + upper


def rms_scale(values):
    return lax.rsqrt(jnp.mean(values * values, axis=-1, keepdims=True) + norm_eps)


def gelu_slope(values):
    cdf_vals = 0.5 * (1.0 + lax.erf(values * (1.0 / math.sqrt(2.0))))
    pdf_vals = jnp.exp(-0.5 * values * values) * (1.0 / math.sqrt(2.0 * math.pi))
    return cdf_vals + values * pdf_vals


def spread_offsets(per_offset, q_rows, seq_len):
    span_len = seq_len + q_rows - 1
    tiled_rows = jnp.tile(per_offset, (1, q_rows))
    tiled_rows = jnp.pad(tiled_rows, ((0, 0), (0, q_rows)))
    shaped = tiled_rows.reshape(per_offset.shape[0], q_rows, span_len + 1)[:, :, :seq_len]
    return shaped[:, ::-1, :]


def diagonal_sums(block_vals, q_rows, seq_len):
    span_len = seq_len + q_rows - 1
    heads_here = block_vals.shape[0]
    flipped = block_vals[:, ::-1, :]
    padded = jnp.pad(flipped, ((0, 0), (0, 0), (0, q_rows)))
    flat_vals = padded.reshape(heads_here, q_rows * (span_len + 1))[:, : q_rows * span_len]
    return jnp.sum(flat_vals.reshape(heads_here, q_rows, span_len), axis=1)


def dot(a, b, ca, cb):
    return lax.dot_general(a, b, (((ca,), (cb,)), ((), ())), preferred_element_type=f32)


def swap_cores(values):
    return lax.ppermute(values, "col", [(0, 1), (1, 0)])


def make_per_device(mesh):
    n_ex, n_row = mesh.shape["ex"], mesh.shape["row"]
    groups = n_ex * n_row

    def gather_groups(shard):
        rows, width = shard.shape
        part = lax.all_gather(shard, "ex", axis=0)
        part = jnp.broadcast_to(part[None], (n_row, n_ex, rows, width))
        part = lax.all_to_all(part, "row", split_axis=0, concat_axis=0, tiled=True)
        return part.transpose(1, 0, 2, 3).reshape(groups * rows, width)

    def scatter_groups(terms):
        _, rows, width = terms.shape
        part = terms.reshape(n_ex, n_row, rows, width).transpose(1, 0, 2, 3)
        part = lax.all_to_all(part, "row", split_axis=0, concat_axis=0, tiled=True)
        part = jnp.sum(part.astype(f32), axis=0).astype(bf16)
        part = lax.all_to_all(part, "ex", split_axis=0, concat_axis=0, tiled=True)
        return jnp.sum(part.astype(f32), axis=0)

    def per_device(
        x_in,
        gain_attn,
        w_qkv,
        rel_bias,
        w_out,
        gain_ffn,
        w_router,
        w_up,
        w_down,
        seg_ids,
        expert_ids,
        slot_ids,
        drop_flags,
        d_out,
    ):
        seq_len, width = x_in.shape
        heads_here = rel_bias.shape[1]
        inner = w_qkv.shape[2]
        own_rows = w_qkv.shape[1]
        experts = w_router.shape[1]
        capacity = 5 * seq_len // (4 * experts)
        slots = -(-capacity // 8) * 8
        slot_total = experts * slots
        half = d_out.shape[1]
        col_at = lax.axis_index("col")
        expert_at = lax.axis_index("ex") * n_row + lax.axis_index("row")

        packed = jnp.concatenate(
            [
                w_qkv.astype(bf16).transpose(1, 0, 2).reshape(own_rows, 3 * inner),
                w_out.astype(bf16).T,
                w_router.astype(bf16),
            ],
            axis=1,
        )
        full = gather_groups(packed)
        qkv_w = full[:, : 3 * inner]
        out_wt = full[:, 3 * inner : 4 * inner]
        router_w = full[:, 4 * inner :]

        x_float = x_in.astype(f32)
        scale_one = rms_scale(x_float)
        normed_one = x_float * scale_one
        h_one = (normed_one * gain_attn).astype(bf16)
        qkv = dot(h_one, qkv_w, 1, 0).astype(bf16)
        split = lambda v: v.reshape(seq_len, heads_here, HEAD)
        queries, keys, values = (split(qkv[:, i * inner : (i + 1) * inner]) for i in range(3))
        doc_ids = seg_ids[0]
        offsets = jnp.arange(2 * seq_len - 1, dtype=jnp.int32) - (seq_len - 1)
        offset_hot = (
            bucket_of(offsets)[:, None] == jnp.arange(BUCKETS, dtype=jnp.int32)[None, :]
        ).astype(f32)
        per_offset = jnp.einsum("bh,ob->ho", rel_bias, offset_hot, precision=highest)
        same_doc = (doc_ids[:, None] == doc_ids[None, :])[None]
        scores = jnp.einsum("qhe,khe->hqk", queries, keys, preferred_element_type=f32) * 0.125
        scores = scores + spread_offsets(per_offset, seq_len, seq_len)
        scores = jnp.where(same_doc, scores, -1e30)
        peak = jnp.max(scores, axis=-1, keepdims=True)
        expo = jnp.exp(scores - peak)
        probs = expo / jnp.sum(expo, axis=-1, keepdims=True)
        probs_b = probs.astype(bf16)
        context = (
            jnp.einsum("hqk,khe->qhe", probs_b, values, preferred_element_type=f32)
            .reshape(seq_len, inner)
            .astype(bf16)
        )
        attn_part = dot(context, out_wt, 1, 1).astype(bf16)
        attn_out = attn_part.astype(f32) + swap_cores(attn_part).astype(f32)
        x_one = x_float + attn_out
        scale_two = rms_scale(x_one)
        normed_two = x_one * scale_two
        h_two = (normed_two * gain_ffn).astype(bf16)

        slot_of = jnp.where(drop_flags == 1, slot_total, expert_ids * slots + slot_ids)
        place = (slot_of[:, None] == jnp.arange(slot_total, dtype=jnp.int32)[None, :]).astype(bf16)
        mine = lambda v: jnp.where(col_at == 0, v[:, :half], v[:, half:])
        other = lambda v: jnp.where(col_at == 0, v[:, half:], v[:, :half])
        send = dot(place, jnp.concatenate([mine(h_two), d_out], axis=1), 0, 0).astype(bf16)
        got = lax.all_to_all(
            send.reshape(experts, slots, 2 * half), ("ex", "row"), 0, 0, tiled=True
        ).reshape(slot_total, 2 * half)
        both = lax.all_gather(got, "col", axis=0)
        rows = jnp.concatenate([both[0, :, :half], both[1, :, :half]], axis=1)
        g_rows = jnp.concatenate([both[0, :, half:], both[1, :, half:]], axis=1)

        up_w = w_up[0].astype(bf16)
        down_w = w_down[0].astype(bf16)
        router_probs = jax.nn.softmax(dot(rows, router_w, 1, 0), axis=-1)
        chosen = (jnp.arange(experts, dtype=jnp.int32) == expert_at).astype(f32)[None, :]
        gate = jnp.sum(router_probs * chosen, axis=-1, keepdims=True)
        d_y = (g_rows.astype(f32) * gate).astype(bf16)
        pre_act = dot(rows, up_w, 1, 0)
        act_b = jax.nn.gelu(pre_act, approximate=False).astype(bf16)
        y_part = dot(act_b, down_w, 1, 0)
        gate_part = jnp.sum(g_rows.astype(f32) * y_part, axis=-1, keepdims=True)
        d_pre = (dot(d_y, down_w, 1, 1) * gelu_slope(pre_act)).astype(bf16)
        d_in_part = dot(d_pre, up_w, 1, 1)
        crossing = jnp.concatenate([other(y_part), other(d_in_part)], axis=1).astype(bf16)
        crossed = swap_cores(crossing).astype(f32)
        d_gate = gate_part + swap_cores(gate_part)
        d_logits = (d_gate * gate * (chosen - router_probs)).astype(bf16)
        d_router_in = dot(d_logits, router_w, 1, 1)
        y_gated = gate * (mine(y_part) + crossed[:, :half])
        d_in = mine(d_in_part) + crossed[:, half:] + mine(d_router_in)
        back = jnp.concatenate([y_gated, d_in], axis=1).astype(bf16)
        home = lax.all_to_all(
            back.reshape(experts, slots, 2 * half), ("ex", "row"), 0, 0, tiled=True
        ).reshape(slot_total, 2 * half)
        grad_down = dot(act_b, d_y, 0, 0)
        grad_up = dot(rows, d_pre, 0, 0)
        grad_router = dot(rows, d_logits, 0, 0)

        home_tok = dot(place, home, 1, 0)
        layer_out = (mine(x_one) + home_tok[:, :half]).astype(bf16)
        cross_back = jnp.concatenate([home_tok[:, half:].astype(bf16), d_out], axis=1)
        both_back = lax.all_gather(cross_back, "col", axis=0).astype(f32)
        d_h_two = jnp.concatenate([both_back[0, :, :half], both_back[1, :, :half]], axis=1)
        g_full = jnp.concatenate([both_back[0, :, half:], both_back[1, :, half:]], axis=1)

        grad_gain_ffn = jnp.sum(d_h_two * normed_two, axis=0)
        d_norm_two = d_h_two * gain_ffn
        d_x_one = g_full + scale_two * (
            d_norm_two - normed_two * jnp.mean(d_norm_two * normed_two, axis=-1, keepdims=True)
        )
        d_attn_b = d_x_one.astype(bf16)
        grad_out_t = dot(d_attn_b, context, 0, 0)
        d_context = split(dot(d_attn_b, out_wt, 1, 0).astype(bf16))
        d_probs = jnp.einsum("qhe,khe->hqk", d_context, values, preferred_element_type=f32)
        row_delta = jnp.sum(probs * d_probs, axis=-1, keepdims=True)
        d_scores = (probs * (d_probs - row_delta)).astype(bf16)
        d_vals = jnp.einsum("hqk,qhe->khe", probs_b, d_context, preferred_element_type=f32)
        d_keys = jnp.einsum("hqk,qhe->khe", d_scores, queries, preferred_element_type=f32) * 0.125
        d_quer = jnp.einsum("hqk,khe->qhe", d_scores, keys, preferred_element_type=f32) * 0.125
        d_qkv = jnp.concatenate(
            [v.reshape(seq_len, inner) for v in (d_quer, d_keys, d_vals)], axis=1
        ).astype(bf16)
        grad_offset = diagonal_sums(d_scores.astype(f32), seq_len, seq_len)
        grad_rel = jnp.einsum("ho,ob->bh", grad_offset, offset_hot, precision=highest)
        grad_qkv = dot(h_one, d_qkv, 0, 0)
        d_h_one_part = dot(d_qkv, qkv_w, 1, 1).astype(bf16)
        d_h_one = d_h_one_part.astype(f32) + swap_cores(d_h_one_part).astype(f32)
        grad_gain_attn = jnp.sum(d_h_one * normed_one, axis=0)
        d_norm_one = d_h_one * gain_attn
        grad_x = d_x_one + scale_one * (
            d_norm_one - normed_one * jnp.mean(d_norm_one * normed_one, axis=-1, keepdims=True)
        )

        terms = jnp.concatenate([grad_qkv, grad_out_t, grad_router], axis=1).astype(bf16)
        sums = scatter_groups(terms.reshape(groups, own_rows, 4 * inner + experts))
        small = jnp.concatenate([grad_gain_attn, grad_gain_ffn, grad_rel.reshape(-1)])[None]
        small = jnp.broadcast_to(small, (groups, small.shape[1]))
        small = jnp.sum(lax.all_to_all(small, ("ex", "row"), 0, 0, tiled=True), axis=0)
        return (
            layer_out,
            grad_x.astype(bf16),
            small[:width],
            sums[:, : 3 * inner].reshape(own_rows, 3, inner).transpose(1, 0, 2),
            small[2 * width :].reshape(BUCKETS, heads_here),
            sums[:, 3 * inner : 4 * inner].T,
            small[width : 2 * width],
            sums[:, 4 * inner :],
            grad_up[None],
            grad_down[None],
        )

    return per_device


def solution(mesh):
    return jax.shard_map(
        make_per_device(mesh),
        mesh=mesh,
        in_specs=(
            P(("ex", "row"), None),
            P(),
            P(None, ("ex", "row"), "col"),
            P(None, "col"),
            P("col", ("ex", "row")),
            P(),
            P(("ex", "row"), None),
            P(("ex", "row"), None, "col"),
            P(("ex", "row"), "col", None),
            P(("ex", "row"), None),
            P(("ex", "row")),
            P(("ex", "row")),
            P(("ex", "row")),
            P(("ex", "row"), "col"),
        ),
        out_specs=(
            P(("ex", "row"), "col"),
            P(("ex", "row"), None),
            P(),
            P(None, ("ex", "row"), "col"),
            P(None, "col"),
            P("col", ("ex", "row")),
            P(),
            P(("ex", "row"), None),
            P(("ex", "row"), None, "col"),
            P(("ex", "row"), "col", None),
        ),
        check_vma=False,
    )
```

profile of v0, /device:TPU:0, one launch (start us, length us, event | category | flops | bytes accessed | tf_op | source)
XLA Modules:
  0.0 260.9 jit_solution(18286317781432440149)
XLA Ops:
  9.9 19.4 %all-gather = bf16[192,1552]{1,0:T(8,128)(2,1)S(1)} all-gather(bf16[48,1552]{1,0:T(8,128)(2,1)S(1)} %pad_maximum_fusion.11), channel_id=2, replica_groups=mesh['ex'=4,'row'=4,'col'=2] {'ex'}, dimensions={0}, use_global_device_ids=true | all-gather | bytes 744960 | tf_op jit(solution)/shard_map/all_gather | solution.py:69
  30.9 3.7 %all-to-all-start = ((bf16[4,4,48,1552]{3,2,1,0:T(8,128)(2,1)}), bf16[4,4,48,1552]{3,2,1,0:T(8,128)(2,1)S(1)}, u32[]{:S(2)}, u32[]{:S(2)}) async-start(bf16[4,4,48,1552]{3,2,1,0:T(8,128)(2,1)} %broadcast_in_dim.32), calls=%async_computation | async-start | bytes 5111808 | tf_op jit(solution)/shard_map/all_to_all | solution.py:71
  35.0 2.1 tile.4
  37.1 6.6 %tile.10 = f32[6,130816]{1,0:T(8,128)} reshape(f32[6,256,511]{2,1,0:T(8,128)} %tile.4) | data formatting | bytes 6279168 | tf_op jit(solution)/shard_map/tile | solution.py:40
  43.7 2.5 pad.8
  49.3 3.0 %copy.181 = f32[6,256,256]{1,2,0:T(8,128)} copy(f32[6,256,256]{2,1,0:T(8,128)} %slice.161) | data formatting | bytes 3145728
  52.3 13.5 %rev.6 = f32[6,256,256]{1,2,0:T(8,128)} reverse(f32[6,256,256]{1,2,0:T(8,128)} %copy.181), dimensions={1} | reverse | bytes 3145728 | tf_op jit(solution)/shard_map/rev | solution.py:43
  76.7 24.2 %all_to_all.31 = bf16[16,24,768]{2,1,0:T(8,128)(2,1)} all-to-all(bf16[16,24,768]{2,1,0:T(8,128)(2,1)S(1)} %bitcast.141), channel_id=1, replica_groups=mesh['ex'=4,'row'=4,'col'=2] {'ex','row'}, dimensions={0} | all-to-all | bytes 1179648 | tf_op jit(solution)/shard_map/all_to_all | solution.py:161
  100.9 6.7 %all-gather.4.cloned.1.call-done = bf16[2,384,768]{2,1,0:T(8,128)(2,1)} async-done(((bf16[1,384,768]{2,1,0:T(8,128)(2,1)}), bf16[2,384,768]{2,1,0:T(8,128)(2,1)}) %all-gather.4.cloned.1.call-update) | async-done | bytes 1179664 | tf_op jit(solution)/shard_map/all_gather | solution.py:164
  109.2 2.4 fusion.99
  111.6 7.6 %fusion.4 = (bf16[384,1536]{1,0:T(8,128)(2,1)S(1)}, f32[384,1536]{1,0:T(8,128)S(1)}) fusion(f32[1,768,1536]{2,1,0:T(8,128)} %param.21, bf16[384,384]{1,0:T(8,128)(2,1)S(1)} %get-tuple-element.96, bf16[384,384]{1,0:T(8,128)(2,1)S(1)} %get-tuple-element.97), kind=kOutput, calls=%fused_computation.14 | convolution fusion | flops 946667520 | bytes 8847360 | tf_op jit(solution)/shard_map/dot_general | solution.py:56
  119.4 2.3 fusion.1
  128.9 6.8 %all-to-all-start.2 = ((bf16[16,24,768]{2,1,0:T(8,128)(2,1)}), bf16[16,24,768]{2,1,0:T(8,128)(2,1)S(1)}, u32[]{:S(2)}, u32[]{:S(2)}) async-start(bf16[16,24,768]{2,1,0:T(8,128)(2,1)} %pad_maximum_fusion.4), calls=%async_computation.2 | async-start | bytes 1179648 | tf_op jit(solution)/shard_map/all_to_all | solution.py:188
  136.8 15.4 %all-to-all-done.2 = bf16[16,24,768]{2,1,0:T(8,128)(2,1)S(1)} async-done(((bf16[16,24,768]{2,1,0:T(8,128)(2,1)}), bf16[16,24,768]{2,1,0:T(8,128)(2,1)S(1)}, u32[]{:S(2)}, u32[]{:S(2)}) %all-to-all-start.2) | async-done | bytes 589856 | tf_op jit(solution)/shard_map/all_to_all | solution.py:188
  152.8 2.4 all-gather.1
  158.8 3.2 %convolution_convert_fusion.5 = bf16[6,64,256]{2,1,0:T(8,128)(2,1)} fusion(bf16[256,6,64]{0,2,1:T(8,128)(2,1)S(1)} %bitcast.149, f32[6,256]{1,0:T(8,128)S(1)} %get-tuple-element.103, f32[6,256,256]{1,2,0:T(8,128)} %copy-done.2), kind=kOutput, calls=%fused_computation.73 | convolution fusion | flops 51611392 | bytes 1972224 | tf_op jit(solution)/shard_map/hqk,qhe->khe/dot_general | solution.py:213
  162.0 1.9 multiply_reduce_fusion
  166.9 1.9 copy.165
  170.3 2.0 convolution_convert_fusion
  174.0 4.8 %all-to-all-start.4 = ((bf16[4,4,48,1552]{3,2,1,0:T(8,128)(2,1)}), bf16[4,4,48,1552]{3,2,1,0:T(8,128)(2,1)}, u32[]{:S(2)}, u32[]{:S(2)}) async-start(bf16[4,4,48,1552]{3,2,1,0:T(8,128)(2,1)} %maximum_bitcast_fusion), calls=%async_computation.4 | async-start | bytes 5111808 | tf_op jit(solution)/shard_map/all_to_all | solution.py:77
  178.8 4.7 %convolution_bitcast_fusion = f32[1,1536,768]{2,1,0:T(8,128)} fusion(bf16[384,1536]{1,0:T(8,128)(2,1)S(1)} %get-tuple-element.107, f32[384]{0:T(512)S(1)} %multiply_reduce_fusion.4, bf16[384,384]{1,0:T(8,128)(2,1)} %copy-done.12, bf16[384,384]{1,0:T(8,128)(2,1)} %copy-done.11), kind=kOutput, calls=%fused_computation.1 | convolution fusion | flops 907739136 | bytes 6489600 | tf_op jit(solution)/shard_map/dot_general | solution.py:56
  183.5 8.7 %rev.7 = f32[6,256,256]{1,2,0:T(8,128)} reverse(bf16[6,256,256]{1,2,0:T(8,128)(2,1)S(1)} %multiply_convert_fusion), dimensions={1} | reverse | bytes 2359296 | tf_op jit(solution)/shard_map/rev | solution.py:49
  192.2 2.6 fusion.28
  200.4 2.3 slice.186
  202.6 6.4 %reshape.221 = f32[6,256,511]{2,1,0:T(8,128)} reshape(f32[6,130816]{1,0:T(8,128)} %slice.186) | data formatting | bytes 6279168 | tf_op jit(solution)/shard_map/reshape | solution.py:52
  209.1 2.3 reduce_sum.149
  216.7 5.2 %all-to-all-start.3 = ((f32[16,1,1728]{2,1,0:T(1,128)}), f32[16,1,1728]{2,1,0:T(1,128)S(1)}, u32[]{:S(2)}, u32[]{:S(2)}) async-start(f32[16,1,1728]{2,1,0:T(1,128)} %broadcast_in_dim.38), calls=%async_computation.3 | async-start | bytes 229376 | tf_op jit(solution)/shard_map/all_to_all | solution.py:234
  221.9 4.7 %convolution_bitcast_fusion.1 = f32[1,768,1536]{2,1,0:T(8,128)} fusion(bf16[384,1536]{1,0:T(8,128)(2,1)S(1)} %copy-done.10, bf16[384,384]{1,0:T(8,128)(2,1)} %copy-done.20, bf16[384,384]{1,0:T(8,128)(2,1)} %copy-done.21), kind=kOutput, calls=%fused_computation.2 | convolution fusion | flops 907149312 | bytes 6488064 | tf_op jit(solution)/shard_map/dot_general | solution.py:56
  226.6 3.2 %reduce_sum.151 = bf16[4,48,1552]{2,1,0:T(8,128)(2,1)} reduce(bf16[4,4,48,1552]{3,2,1,0:T(8,128)(2,1)} %all-to-all-done.4, bf16[]{:T(256)} %constant.125.clone.1), dimensions={0}, to_apply=%region_15.16 | reduce | flops 893952 | bytes 2979842 | tf_op jit(solution)/shard_map/reduce_sum | solution.py:78
  229.8 5.0 %all-to-all-start.5 = ((bf16[4,48,1552]{2,1,0:T(8,128)(2,1)}), bf16[4,48,1552]{2,1,0:T(8,128)(2,1)S(1)}, u32[]{:S(2)}, u32[]{:S(2)}) async-start(bf16[4,48,1552]{2,1,0:T(8,128)(2,1)} %reduce_sum.151), calls=%async_computation.5 | async-start | bytes 1277952 | tf_op jit(solution)/shard_map/all_to_all | solution.py:79
  235.5 2.2 fusion.48
  239.1 12.7 %all-to-all-done.5 = bf16[4,48,1552]{2,1,0:T(8,128)(2,1)S(1)} async-done(((bf16[4,48,1552]{2,1,0:T(8,128)(2,1)}), bf16[4,48,1552]{2,1,0:T(8,128)(2,1)S(1)}, u32[]{:S(2)}, u32[]{:S(2)}) %all-to-all-start.5) | async-done | bytes 596000 | tf_op jit(solution)/shard_map/all_to_all | solution.py:79
  (190 shorter events, 53.9 us)
Async XLA Ops:
  7.2 27.5 %copy-start = (f32[32,6]{0,1:T(8,128)S(1)}, f32[32,6]{0,1:T(8,128)}, u32[]{:S(2)}) copy-start(f32[32,6]{0,1:T(8,128)} %param.17) | copy-start | bytes 2308
  30.9 35.1 %all-to-all-start = ((bf16[4,4,48,1552]{3,2,1,0:T(8,128)(2,1)}), bf16[4,4,48,1552]{3,2,1,0:T(8,128)(2,1)S(1)}, u32[]{:S(2)}, u32[]{:S(2)}) async-start(bf16[4,4,48,1552]{3,2,1,0:T(8,128)(2,1)} %broadcast_in_dim.32), calls=%async_computation | async-start | bytes 5111808 | tf_op jit(solution)/shard_map/all_to_all | solution.py:71
  34.7 73.0 %all-gather.4.cloned.1.call-start = ((), (), s32[]{:S(2)}) async-start(), calls=%async_computation.6 | async-start | bytes 1769472 | tf_op jit(solution)/shard_map/all_gather | solution.py:164
  34.7 9.0 %copy-start.37 = (s32[511]{0:T(512)}, s32[511]{0:T(512)S(1)}, u32[]{:S(2)}) copy-start(s32[511]{0:T(512)S(1)} %fusion.81) | copy-start | bytes 6136
  52.3 13.5 %copy-start.5 = (bf16[256,768]{1,0:T(8,128)(2,1)S(1)}, bf16[256,768]{1,0:T(8,128)(2,1)}, u32[]{:S(2)}) copy-start(bf16[256,768]{1,0:T(8,128)(2,1)} %param.14) | copy-start | bytes 1179652
  52.3 13.7 %copy-start.36 = (s32[1,256]{1,0:T(1,128)S(1)}, s32[1,256]{1,0:T(1,128)}, u32[]{:S(2)}) copy-start(s32[1,256]{1,0:T(1,128)} %param.23) | copy-start | bytes 3076
  74.0 1.8 collective-permute-start
  107.7 11.7 %slice-start.2 = ((s8[4718592]{0:T(1024)(128)(4,1)}), s8[4194304]{0:T(1024)(128)(4,1)S(1)}, s32[]{:S(2)}) async-start(s8[4718592]{0:T(1024)(128)(4,1)} %bitcast.124), calls=%async_computation.9 | async-start | bytes 8388608
  107.7 14.0 %slice-start = ((s8[4718592]{0:T(1024)(128)(4,1)}), s8[4194304]{0:T(1024)(128)(4,1)S(1)}, s32[]{:S(2)}) async-start(s8[4718592]{0:T(1024)(128)(4,1)} %bitcast.122), calls=%async_computation.7 | async-start | bytes 8388608
  109.2 13.7 %copy-start.11 = (bf16[384,384]{1,0:T(8,128)(2,1)}, bf16[384,384]{1,0:T(8,128)(2,1)S(1)}, u32[]{:S(2)}) copy-start(bf16[384,384]{1,0:T(8,128)(2,1)S(1)} %get-tuple-element.94) | copy-start | bytes 884740
  109.2 13.7 %copy-start.12 = (bf16[384,384]{1,0:T(8,128)(2,1)}, bf16[384,384]{1,0:T(8,128)(2,1)S(1)}, u32[]{:S(2)}) copy-start(bf16[384,384]{1,0:T(8,128)(2,1)S(1)} %get-tuple-element.95) | copy-start | bytes 884740
  109.2 26.4 %copy-start.20 = (bf16[384,384]{1,0:T(8,128)(2,1)}, bf16[384,384]{1,0:T(8,128)(2,1)S(1)}, u32[]{:S(2)}) copy-start(bf16[384,384]{1,0:T(8,128)(2,1)S(1)} %get-tuple-element.96) | copy-start | bytes 884740
  109.2 26.4 %copy-start.21 = (bf16[384,384]{1,0:T(8,128)(2,1)}, bf16[384,384]{1,0:T(8,128)(2,1)S(1)}, u32[]{:S(2)}) copy-start(bf16[384,384]{1,0:T(8,128)(2,1)S(1)} %get-tuple-element.97) | copy-start | bytes 884740
  111.6 7.8 %slice-start.3 = ((s8[4718592]{0:T(1024)(128)(4,1)}), s8[524288]{0:T(1024)(128)(4,1)S(1)}, s32[]{:S(2)}) async-start(s8[4718592]{0:T(1024)(128)(4,1)} %bitcast.124), calls=%async_computation.10 | async-start | bytes 1048576
  111.6 10.1 %slice-start.1 = ((s8[4718592]{0:T(1024)(128)(4,1)}), s8[524288]{0:T(1024)(128)(4,1)S(1)}, s32[]{:S(2)}) async-start(s8[4718592]{0:T(1024)(128)(4,1)} %bitcast.122), calls=%async_computation.8 | async-start | bytes 1048576
  124.2 3.4 %collective-permute-start.1 = (bf16[384,768]{1,0:T(8,128)(2,1)S(1)}, bf16[384,768]{1,0:T(8,128)(2,1)S(1)}, u32[]{:S(2)}, u32[]{:S(2)}) collective-permute-start(bf16[384,768]{1,0:T(8,128)(2,1)S(1)} %pad_maximum_fusion.3), channel_id=1, source_target_pairs={{0,1},{1,0},{2,3},{3,2},{4,5},{5,4},{6,7},{7,6},{8,9},{9,8},{10,11... | collective-permute-start | bytes 1769480 | tf_op jit(solution)/shard_map/ppermute | solution.py:60
  124.4 1.8 collective-permute-start.2
  128.0 24.3 %copy-start.35 = (s32[256]{0:T(256)S(1)}, s32[256]{0:T(256)}, u32[]{:S(2)}) copy-start(s32[256]{0:T(256)} %copy-done.34) | copy-start | bytes 3076
  128.9 23.4 %all-to-all-start.2 = ((bf16[16,24,768]{2,1,0:T(8,128)(2,1)}), bf16[16,24,768]{2,1,0:T(8,128)(2,1)S(1)}, u32[]{:S(2)}, u32[]{:S(2)}) async-start(bf16[16,24,768]{2,1,0:T(8,128)(2,1)} %pad_maximum_fusion.4), calls=%async_computation.2 | async-start | bytes 1179648 | tf_op jit(solution)/shard_map/all_to_all | solution.py:188
  164.9 5.4 %copy-start.29 = (f32[768]{0:T(1024)S(1)}, f32[768]{0:T(1024)}, u32[]{:S(2)}) copy-start(f32[768]{0:T(1024)} %param.15) | copy-start | bytes 9220
  164.9 5.4 %copy-start.32 = (f32[256]{0:T(256)S(1)}, f32[256]{0:T(256)}, u32[]{:S(2)}) copy-start(f32[256]{0:T(256)} %copy-done.31) | copy-start | bytes 3076
  174.0 42.0 %all-to-all-start.4 = ((bf16[4,4,48,1552]{3,2,1,0:T(8,128)(2,1)}), bf16[4,4,48,1552]{3,2,1,0:T(8,128)(2,1)}, u32[]{:S(2)}, u32[]{:S(2)}) async-start(bf16[4,4,48,1552]{3,2,1,0:T(8,128)(2,1)} %maximum_bitcast_fusion), calls=%async_computation.4 | async-start | bytes 5111808 | tf_op jit(solution)/shard_map/all_to_all | solution.py:77
  194.8 19.1 %copy-start.19 = (bf16[256,768]{1,0:T(8,128)(2,1)}, bf16[256,768]{1,0:T(8,128)(2,1)S(1)}, u32[]{:S(2)}) copy-start(bf16[256,768]{1,0:T(8,128)(2,1)S(1)} %fusion.28) | copy-start | bytes 1179652
  194.8 19.1 %collective-permute-start.3 = (bf16[256,768]{1,0:T(8,128)(2,1)S(1)}, bf16[256,768]{1,0:T(8,128)(2,1)}, u32[]{:S(2)}, u32[]{:S(2)}) collective-permute-start(bf16[256,768]{1,0:T(8,128)(2,1)S(1)} %fusion.28), channel_id=1, source_target_pairs={{0,1},{1,0},{2,3},{3,2},{4,5},{5,4},{6,7},{7,6},{8,9},{9,8},{10,11... | collective-permute-start | bytes 1179656 | tf_op jit(solution)/shard_map/ppermute | solution.py:60
  209.1 4.9 %copy-start.7 = (bf16[256,768]{1,0:T(8,128)(2,1)S(1)}, bf16[256,768]{1,0:T(8,128)(2,1)}, u32[]{:S(2)}) copy-start(bf16[256,768]{1,0:T(8,128)(2,1)} %param.14) | copy-start | bytes 1179652
  209.1 12.8 %copy-start.10 = (bf16[384,1536]{1,0:T(8,128)(2,1)S(1)}, bf16[384,1536]{1,0:T(8,128)(2,1)}, u32[]{:S(2)}) copy-start(bf16[384,1536]{1,0:T(8,128)(2,1)} %copy-done.9) | copy-start | bytes 3538948
  216.7 13.1 %all-to-all-start.3 = ((f32[16,1,1728]{2,1,0:T(1,128)}), f32[16,1,1728]{2,1,0:T(1,128)S(1)}, u32[]{:S(2)}, u32[]{:S(2)}) async-start(f32[16,1,1728]{2,1,0:T(1,128)} %broadcast_in_dim.38), calls=%async_computation.3 | async-start | bytes 229376 | tf_op jit(solution)/shard_map/all_to_all | solution.py:234
  226.5 8.2 %copy-start.14 = (f32[256,768]{1,0:T(8,128)S(1)}, f32[256,768]{1,0:T(8,128)}, u32[]{:S(2)}) copy-start(f32[256,768]{1,0:T(8,128)} %copy-done.13) | copy-start | bytes 2359300
  226.5 8.9 %copy-start.30 = (f32[768]{0:T(1024)S(1)}, f32[768]{0:T(1024)}, u32[]{:S(2)}) copy-start(f32[768]{0:T(1024)} %param.15) | copy-start | bytes 9220
  226.5 8.9 %copy-start.33 = (f32[256]{0:T(256)S(1)}, f32[256]{0:T(256)}, u32[]{:S(2)}) copy-start(f32[256]{0:T(256)} %copy-done.31) | copy-start | bytes 3076
  229.8 22.0 %all-to-all-start.5 = ((bf16[4,48,1552]{2,1,0:T(8,128)(2,1)}), bf16[4,48,1552]{2,1,0:T(8,128)(2,1)S(1)}, u32[]{:S(2)}, u32[]{:S(2)}) async-start(bf16[4,48,1552]{2,1,0:T(8,128)(2,1)} %reduce_sum.151), calls=%async_computation.5 | async-start | bytes 1277952 | tf_op jit(solution)/shard_map/all_to_all | solution.py:79
  235.5 18.5 %copy-start.1 = (f32[32,6]{0,1:T(8,128)S(1)}, f32[32,6]{0,1:T(8,128)}, u32[]{:S(2)}) copy-start(f32[32,6]{0,1:T(8,128)} %param.17) | copy-start | bytes 2308
  (23 other events, 56.5 us)
Sparse Core Ops, SparseCore 0:
  101.0 6.5 all-gather.3
where the time goes:
time: 263 us; the launch traced here: 261 us
  local copies, waits for them, and re-layouts  67 us (25%)
  matrix products  47.7 us (18%)
  blocking collectives  46 us (17%)
  waiting for transfers between devices  38 us (14%)
  starting transfers between devices  26.2 us (10%)
  other arithmetic  21.1 us (8%)
  between operations  14.9 us (6%)
    dot_general x17, matrix products, dot(): lax.dot_general(a, b, (((ca,), (cb,)), ((), ())), preferred_element_type=...  36.2 us
    all_to_all x1, blocking collectives, per_device(): lax.all_to_all(send.reshape(experts, slots, 2 * half), ('ex', 'row'), 0,...  24.2 us
    all_gather x1, blocking collectives, gather_groups(): part = lax.all_gather(shard, 'ex', axis=0)  19.4 us
    all_to_all x1, waiting for transfers between devices, per_device(): lax.all_to_all(back.reshape(experts, slots, 2 * half), ('ex', 'row'), 0,...  15.4 us
    unnamed x98, local copies, waits for them, and re-layouts  13.6 us
    rev x1, local copies, waits for them, and re-layouts, spread_offsets(): return shaped[:, ::-1, :]  13.5 us
    all_to_all x1, waiting for transfers between devices, scatter_groups(): part = lax.all_to_all(part, 'ex', split_axis=0, concat_axis=0, tiled=True)  12.7 us
    rev x1, local copies, waits for them, and re-layouts, diagonal_sums(): flipped = block_vals[:, ::-1, :]  8.67 us
  transfers between devices with their start and end apart: 10, of which 5 were waited for; matrix products, arithmetic and copies ran while one was open for 32% of the time, Pallas kernels for 0%

commit v1 on v0

v1 whole, which is shorter than its diff:
```python
import functools
import math

import jax
import jax.numpy as jnp
from jax import lax
from jax.experimental import pallas as pl
from jax.experimental.pallas import tpu as pltpu
from jax.sharding import PartitionSpec as P

HEAD = 64
BUCKETS = 32

norm_eps = 1e-06
bucket_edges = (12, 16, 23, 32, 46, 64, 91)
highest = lax.Precision.HIGHEST
bf16 = jnp.bfloat16
f32 = jnp.float32

GATHER_ORDER = tuple(((k, m),) for m in range(4) for k in range(4))
SCATTER_ORDER = (
    ((0, 0), (1, 0), (2, 0), (3, 0)),
    ((0, 1), (1, 1)),
    ((2, 1), (3, 1)),
    ((0, 2), (1, 2)),
    ((2, 2), (3, 2)),
    ((0, 3), (1, 3)),
    ((2, 3), (3, 3)),
)


def bucket_of(offset):
    distance = jnp.abs(offset)
    far_part = jnp.zeros(distance.shape, jnp.int32)
    for edge_at in bucket_edges:
        far_part = far_part + (distance >= edge_at).astype(jnp.int32)
    inside = jnp.where(distance < 8, distance, far_part + jnp.int32(8))
    upper = jnp.where(offset > 0, jnp.int32(BUCKETS // 2), jnp.int32(0))
    return inside + upper


def rms_scale(values):
    return lax.rsqrt(jnp.mean(values * values, axis=-1, keepdims=True) + norm_eps)


def dot(a, b, ca, cb):
    return lax.dot_general(a, b, (((ca,), (cb,)), ((), ())), preferred_element_type=f32)


def swap_cores(values):
    return lax.ppermute(values, "col", [(0, 1), (1, 0)])


def shape(dims, dtype):
    return jax.ShapeDtypeStruct(tuple(dims), dtype)


def vmem_call(kernel, out_shape, flops, *args, scalars=(), scratch=(), limit=12):
    nbytes = sum(math.prod(v.shape) * v.dtype.itemsize for v in (*args, *out_shape))
    spec = pl.BlockSpec(memory_space=pltpu.VMEM)
    limit = limit if nbytes < 16 * 2**20 else 48
    return pl.pallas_call(
        kernel,
        out_shape=out_shape,
        in_specs=[pl.BlockSpec(memory_space=pltpu.SMEM)] * len(scalars) + [spec] * len(args),
        out_specs=[spec] * len(out_shape),
        scratch_shapes=scratch,
        compiler_params=pltpu.CompilerParams(vmem_limit_bytes=limit * 2**20),
        cost_estimate=pl.CostEstimate(flops=flops, bytes_accessed=nbytes, transcendentals=0),
    )(*scalars, *args)


def block_rows(at_ref, order, count):
    if order is None:
        return [pl.ds(0, count)]
    ex_at, row_at = at_ref[0], at_ref[1]
    return [
        pl.ds(pl.multiple_of(((ex_at ^ k) * 4 + (row_at ^ m)) * count, 16), count)
        for part in order
        for k, m in part
    ]


def take_blocks(at_ref, order, full_ref, block_refs):
    rows = iter(block_rows(at_ref, order, block_refs[0].shape[1]))
    for block_ref in block_refs:
        for i in range(block_ref.shape[0]):
            block_ref[i] = full_ref[next(rows), :]


def eye(size):
    dims = (size, size)
    same = lax.broadcasted_iota(jnp.int32, dims, 0) == lax.broadcasted_iota(jnp.int32, dims, 1)
    return same.astype(bf16)


def pack_weights(qkv_ref, out_ref, router_ref, packed_ref):
    inner, experts = qkv_ref.shape[2], router_ref.shape[1]
    for part in range(3):
        packed_ref[:, part * inner : (part + 1) * inner] = qkv_ref[part].astype(bf16)
    turned = dot(out_ref[...].astype(bf16), eye(inner), 0, 0)
    packed_ref[:, 3 * inner : 4 * inner] = turned.astype(bf16)
    packed_ref[:, 4 * inner :] = jnp.zeros((packed_ref.shape[0], packed_ref.shape[1] - 4 * inner), bf16)
    packed_ref[:, 4 * inner : 4 * inner + experts] = router_ref[...].astype(bf16)


def attend_forward(order, at_ref, x_ref, gain_ref, offset_ref, seg_ref, *refs):
    *block_refs, part_ref, h_ref, qkv_ref, probs_ref, ctx_ref, w_ref, out_w_ref, router_ref = refs
    seq_len = x_ref.shape[0]
    heads, inner = probs_ref.shape[0], ctx_ref.shape[1]
    for rows, block_ref in zip(block_rows(at_ref, order, block_refs[0].shape[0]), block_refs):
        w_ref[rows, :] = block_ref[:, : 3 * inner]
        out_w_ref[rows, :] = block_ref[:, 3 * inner : 4 * inner]
        router_ref[rows, :] = block_ref[:, 4 * inner :]
    x_float = x_ref[...].astype(f32)
    h_one = (x_float * rms_scale(x_float) * gain_ref[...]).astype(bf16)
    h_ref[...] = h_one
    documents = lax.broadcasted_iota(jnp.int32, (8, seq_len), 0) == seg_ref[...]
    same_doc = dot(documents.astype(bf16), documents.astype(bf16), 0, 0) > 0.5
    qkv_ref[...] = dot(h_one, w_ref[...], 1, 0).astype(bf16)
    span = offset_ref.shape[1]
    for at in range(heads):
        take = lambda part: qkv_ref[:, part * inner + at * HEAD : part * inner + (at + 1) * HEAD]
        spread = jnp.broadcast_to(offset_ref[at : at + 1, :], (seq_len, span))
        bias = pltpu.roll(spread, span - seq_len + 1, 1, stride=1, stride_axis=0)[:, :seq_len]
        scores = jnp.where(same_doc, dot(take(0), take(1), 1, 1) * 0.125 + bias, -1e30)
        expo = jnp.exp(scores - jnp.max(scores, axis=1, keepdims=True))
        probs = expo / jnp.sum(expo, axis=1, keepdims=True)
        probs_ref[at] = probs
        ctx = dot(probs.astype(bf16), take(2), 1, 0)
        ctx_ref[:, at * HEAD : (at + 1) * HEAD] = ctx.astype(bf16)
    part_ref[...] = dot(ctx_ref[...], out_w_ref[...], 1, 1).astype(bf16)


def dispatch(at_ref, x_ref, part_ref, peer_ref, gain_ref, slot_ref, g_ref, send_ref):
    half = g_ref.shape[1]
    x_one = x_ref[...].astype(f32) + (part_ref[...].astype(f32) + peer_ref[...].astype(f32))
    h_two = (x_one * rms_scale(x_one) * gain_ref[...]).astype(bf16)
    mine = jnp.where(at_ref[2] == 0, h_two[:, :half], h_two[:, half:])
    dims = (send_ref.shape[0], x_ref.shape[0])
    place = (lax.broadcasted_iota(jnp.int32, dims, 0) == slot_ref[...]).astype(bf16)
    send_ref[:, :half] = dot(place, mine, 1, 0).astype(bf16)
    send_ref[:, half:] = dot(place, g_ref[...], 1, 0).astype(bf16)


def run_expert(
    experts, row_size, at_ref, got_ref, peer_ref, router_ref, up_ref, down_ref,
    cross_ref, mine_ref, probs_ref, gate_part_ref, rows_ref, d_y_ref, act_ref, d_pre_ref, d_in_ref,
):
    half = got_ref.shape[1] // 2
    hidden = up_ref.shape[1]
    first_core = at_ref[2] == 0
    for at, refs in ((0, (got_ref, peer_ref)), (1, (peer_ref, got_ref))):
        pick = lambda lo: jnp.where(first_core, refs[0][:, lo : lo + half], refs[1][:, lo : lo + half])
        rows_ref[:, at * half : (at + 1) * half] = pick(0)
        d_y_ref[:, at * half : (at + 1) * half] = pick(half)
    rows, g_rows = rows_ref[...], d_y_ref[...].astype(f32)
    logits = dot(rows, router_ref[...], 1, 0)[:, :experts]
    expo = jnp.exp(logits - jnp.max(logits, axis=1, keepdims=True))
    probs = expo / jnp.sum(expo, axis=1, keepdims=True)
    probs_ref[...] = probs
    expert_at = at_ref[0] * row_size + at_ref[1]
    chosen = lax.broadcasted_iota(jnp.int32, probs.shape, 1) == expert_at
    gate = jnp.sum(jnp.where(chosen, probs, 0.0), axis=1, keepdims=True)
    d_y_ref[...] = (g_rows * gate).astype(bf16)
    step = 512 if hidden % 512 == 0 else hidden
    y_part = None
    for lo in range(0, hidden, step):
        cols = pl.ds(lo, step)
        pre_act = dot(rows_ref[...], up_ref[:, cols], 1, 0)
        cdf = 0.5 * (1.0 + lax.erf(pre_act * (1.0 / math.sqrt(2.0))))
        pdf = jnp.exp(-0.5 * pre_act * pre_act) * (1.0 / math.sqrt(2.0 * math.pi))
        act = (pre_act * cdf).astype(bf16)
        act_ref[:, cols] = act
        y_more = dot(act, down_ref[cols, :], 1, 0)
        d_pre = (dot(d_y_ref[...], down_ref[cols, :], 1, 1) * (cdf + pre_act * pdf)).astype(bf16)
        d_pre_ref[:, cols] = d_pre
        d_more = dot(d_pre, up_ref[:, cols], 1, 1)
        if lo == 0:
            y_part = y_more
            d_in_ref[...] = d_more
        else:
            y_part = y_part + y_more
            d_in_ref[...] += d_more
    gate_part_ref[...] = jnp.sum(g_rows * y_part, axis=1, keepdims=True)
    d_in = d_in_ref[...]
    mine_ref[:, :half] = jnp.where(first_core, y_part[:, :half], y_part[:, half:])
    mine_ref[:, half:] = jnp.where(first_core, d_in[:, :half], d_in[:, half:])
    cross_ref[:, :half] = jnp.where(first_core, y_part[:, half:], y_part[:, :half]).astype(bf16)
    cross_ref[:, half:] = jnp.where(first_core, d_in[:, half:], d_in[:, :half]).astype(bf16)


def settle(
    row_size, at_ref, mine_ref, crossed_ref, probs_ref, gate_part_ref, gate_peer_ref, router_ref,
    back_ref, d_logits_ref,
):
    half = mine_ref.shape[1] // 2
    probs = probs_ref[...]
    expert_at = at_ref[0] * row_size + at_ref[1]
    chosen = (lax.broadcasted_iota(jnp.int32, probs.shape, 1) == expert_at).astype(f32)
    gate = jnp.sum(probs * chosen, axis=1, keepdims=True)
    d_gate = gate_part_ref[...] + gate_peer_ref[...]
    d_logits = (d_gate * gate * (chosen - probs)).astype(bf16)
    d_logits_ref[...] = d_logits
    router_w = router_ref[...][:, : probs.shape[1]]
    router_mine = jnp.where(at_ref[2] == 0, router_w[:half], router_w[half:])
    back_ref[:, :half] = (gate * (mine_ref[:, :half] + crossed_ref[:, :half].astype(f32))).astype(bf16)
    d_in = mine_ref[:, half:] + crossed_ref[:, half:].astype(f32)
    back_ref[:, half:] = (d_in + dot(d_logits, router_mine, 1, 1)).astype(bf16)


def come_home(
    order, at_ref, home_ref, peer_ref, slot_ref, x_ref, part_ref, part_peer_ref, g_ref, g_peer_ref,
    gain_ref, out_w_ref, ctx_ref, router_ref, layer_ref, d_x_ref, gain_grad_ref, d_ctx_ref, *refs,
):
    *block_refs, grads_ref = refs
    half = g_ref.shape[1]
    inner = ctx_ref.shape[1]
    first_core = at_ref[2] == 0
    both = lambda a, b: jnp.concatenate(
        [jnp.where(first_core, a, b), jnp.where(first_core, b, a)], axis=1
    )
    dims = (home_ref.shape[0], x_ref.shape[0])
    place = (lax.broadcasted_iota(jnp.int32, dims, 0) == slot_ref[...]).astype(bf16)
    d_h = both(dot(place, home_ref[:, half:], 0, 0), dot(place, peer_ref[...], 0, 0))
    x_one = x_ref[...].astype(f32) + (part_ref[...].astype(f32) + part_peer_ref[...].astype(f32))
    g_full = both(g_ref[...], g_peer_ref[...]).astype(f32)
    scale = rms_scale(x_one)
    normed = x_one * scale
    gain_grad_ref[...] = jnp.sum(d_h * normed, axis=0, keepdims=True)
    d_norm = d_h * gain_ref[...]
    d_x = g_full + scale * (d_norm - normed * jnp.mean(d_norm * normed, axis=-1, keepdims=True))
    d_x_ref[...] = d_x
    d_x_b = d_x.astype(bf16)
    d_ctx_ref[...] = dot(d_x_b, out_w_ref[...], 1, 0).astype(bf16)
    grads_ref[:, :inner] = dot(d_x_b, ctx_ref[...], 0, 0).astype(bf16)
    grads_ref[:, inner:] = router_ref[...].astype(bf16)
    take_blocks(at_ref, order, grads_ref, block_refs)
    y_home = dot(place, home_ref[:, :half], 0, 0)
    x_mine = jnp.where(first_core, x_one[:, :half], x_one[:, half:])
    layer_ref[...] = (x_mine + y_home).astype(bf16)


def attend_backward(order, at_ref, d_ctx_ref, qkv_ref, probs_ref, h_ref, w_ref, d_h_ref, grad_offset_ref, *refs):
    *block_refs, d_qkv_ref, grads_ref = refs
    heads, seq_len, _ = probs_ref.shape
    inner = d_ctx_ref.shape[1]
    span = grad_offset_ref.shape[1]
    flip = (
        lax.broadcasted_iota(jnp.int32, (seq_len, seq_len), 0)
        + lax.broadcasted_iota(jnp.int32, (seq_len, seq_len), 1)
        == seq_len - 1
    ).astype(bf16)
    for at in range(heads):
        cols = lambda part: pl.ds(part * inner + at * HEAD, HEAD)
        d_ctx = d_ctx_ref[:, at * HEAD : (at + 1) * HEAD]
        probs = probs_ref[at]
        d_probs = dot(d_ctx, qkv_ref[:, cols(2)], 1, 1)
        row_delta = jnp.sum(probs * d_probs, axis=1, keepdims=True)
        d_scores = (probs * (d_probs - row_delta)).astype(bf16)
        d_qkv_ref[:, cols(0)] = (dot(d_scores, qkv_ref[:, cols(1)], 1, 0) * 0.125).astype(bf16)
        d_qkv_ref[:, cols(1)] = (dot(d_scores, qkv_ref[:, cols(0)], 0, 0) * 0.125).astype(bf16)
        d_qkv_ref[:, cols(2)] = dot(probs.astype(bf16), d_ctx, 0, 0).astype(bf16)
        turned = jnp.concatenate(
            [dot(flip, d_scores, 1, 0), jnp.zeros((seq_len, span - seq_len), f32)], axis=1
        )
        lined = pltpu.roll(turned, 0, 1, stride=1, stride_axis=0)
        grad_offset_ref[at : at + 1, :] = jnp.sum(lined, axis=0, keepdims=True)
    grads_ref[...] = dot(h_ref[...], d_qkv_ref[...], 0, 0).astype(bf16)
    take_blocks(at_ref, order, grads_ref, block_refs)
    d_h_ref[...] = dot(d_qkv_ref[...], w_ref[...], 1, 1).astype(bf16)


def experts_pad(experts):
    return -(-experts // 128) * 128


def make_per_device(mesh):
    n_ex, n_row = mesh.shape["ex"], mesh.shape["row"]
    groups = n_ex * n_row

    def hop(values, axis, step):
        return lax.ppermute(values, axis, [(i, i ^ step) for i in range(mesh.shape[axis])])

    def whole_cube(rows):
        return n_ex == 4 and n_row == 4 and rows % 16 == 0

    def gather_blocks(shard):
        rows, width = shard.shape
        if whole_cube(rows):
            line = [shard] + [hop(shard, "ex", k) for k in (1, 2, 3)]
            xs = [hop(part, "row", 1) for part in line]
            ys = [hop(part, "row", 2) for part in line]
            diagonal = [
                hop(ys[k], "row", 1) if k % 2 else hop(xs[k], "row", 2) for k in range(4)
            ]
            return [*line, *xs, *ys, *diagonal]
        part = lax.all_gather(shard, "ex", axis=0)
        part = jnp.broadcast_to(part[None], (n_row, n_ex, rows, width))
        part = lax.all_to_all(part, "row", split_axis=0, concat_axis=0, tiled=True)
        return [part.transpose(1, 0, 2, 3).reshape(groups * rows, width)]

    def block_shapes(rows, width):
        if whole_cube(rows):
            return [shape((len(part), rows, width), bf16) for part in SCATTER_ORDER]
        return [shape((1, groups * rows, width), bf16)]

    def scatter_blocks(parts, rows):
        if whole_cube(rows):
            here, x_low, x_high, y_low, y_high, d_low, d_high = parts
            from_x, from_y = hop(d_low, "row", 1), hop(d_high, "row", 2)
            x_first, y_first = hop(x_low, "row", 1), hop(y_high, "row", 2)
            x_last = hop(x_high + from_y, "row", 1)
            y_last = hop(y_low + from_x, "row", 2)
            low = here[:2].astype(f32) + x_first.astype(f32) + y_last.astype(f32)
            high = here[2:].astype(f32) + y_first.astype(f32) + x_last.astype(f32)
            return (
                low[0]
                + hop(low[1].astype(bf16), "ex", 1).astype(f32)
                + hop(high[0].astype(bf16), "ex", 2).astype(f32)
                + hop(high[1].astype(bf16), "ex", 3).astype(f32)
            )
        part = parts[0].reshape(n_ex, n_row, rows, -1).transpose(1, 0, 2, 3)
        part = lax.all_to_all(part, "row", split_axis=0, concat_axis=0, tiled=True)
        part = jnp.sum(part.astype(f32), axis=0).astype(bf16)
        part = lax.all_to_all(part, "ex", split_axis=0, concat_axis=0, tiled=True)
        return jnp.sum(part.astype(f32), axis=0)

    def sum_groups(values):
        for axis in ("row", "ex"):
            step = 1
            while step < mesh.shape[axis]:
                values = values + hop(values, axis, step)
                step *= 2
        return values

    def per_device(
        x_in,
        gain_attn,
        w_qkv,
        rel_bias,
        w_out,
        gain_ffn,
        w_router,
        w_up,
        w_down,
        seg_ids,
        expert_ids,
        slot_ids,
        drop_flags,
        d_out,
    ):
        seq_len, width = x_in.shape
        heads_here = rel_bias.shape[1]
        inner = w_qkv.shape[2]
        own_rows = w_qkv.shape[1]
        experts = w_router.shape[1]
        wide = inner + experts_pad(experts)
        capacity = 5 * seq_len // (4 * experts)
        slots = -(-capacity // 8) * 8
        slot_total = experts * slots
        half = d_out.shape[1]
        hidden = w_up.shape[2]
        device_at = jnp.stack([lax.axis_index(axis).astype(jnp.int32) for axis in ("ex", "row", "col")])
        device_at, w_qkv = lax.optimization_barrier((device_at, w_qkv))
        gather_order = GATHER_ORDER if whole_cube(own_rows) else None
        scatter_order = SCATTER_ORDER if whole_cube(own_rows) else None

        (packed,) = vmem_call(
            pack_weights,
            (shape((own_rows, 3 * inner + wide), bf16),),
            0,
            w_qkv,
            w_out,
            w_router,
        )
        blocks = gather_blocks(packed)
        up_w = w_up[0].astype(bf16)
        down_w = w_down[0].astype(bf16)
        *blocks, up_w, down_w = lax.optimization_barrier((*blocks, up_w, down_w))
        g_peer = swap_cores(d_out)

        span = 2 * seq_len
        offsets = jnp.arange(span, dtype=jnp.int32) - (seq_len - 1)
        offset_hot = (
            bucket_of(offsets)[:, None] == jnp.arange(BUCKETS, dtype=jnp.int32)[None, :]
        ).astype(f32)
        per_offset = jnp.einsum("bh,ob->ho", rel_bias, offset_hot, precision=highest)
        square = seq_len * seq_len * heads_here * HEAD
        attn_part, h_one, qkv, probs, context, qkv_w, out_w, router_w = vmem_call(
            functools.partial(attend_forward, gather_order),
            (
                shape((seq_len, width), bf16),
                shape((seq_len, width), bf16),
                shape((seq_len, 3 * inner), bf16),
                shape((heads_here, seq_len, seq_len), f32),
                shape((seq_len, inner), bf16),
                shape((width, 3 * inner), bf16),
                shape((width, inner), bf16),
                shape((width, wide - inner), bf16),
            ),
            8 * seq_len * width * inner + 4 * square,
            x_in,
            gain_attn[None],
            per_offset,
            seg_ids,
            *blocks,
            scalars=(device_at,),
        )
        attn_peer = swap_cores(attn_part)
        slot_of = jnp.where(drop_flags == 1, slot_total, expert_ids * slots + slot_ids)[None]
        (send,) = vmem_call(
            dispatch,
            (shape((slot_total, width), bf16),),
            2 * seq_len * slot_total * width,
            x_in,
            attn_part,
            attn_peer,
            gain_ffn[None],
            slot_of,
            d_out,
            scalars=(device_at,),
        )
        got = lax.all_to_all(
            send.reshape(experts, slots, width), ("ex", "row"), 0, 0, tiled=True
        ).reshape(slot_total, width)
        crossing, mine, router_probs, gate_part, rows, d_y, act_b, d_pre = vmem_call(
            functools.partial(run_expert, experts, n_row),
            (
                shape((slot_total, width), bf16),
                shape((slot_total, width), f32),
                shape((slot_total, experts), f32),
                shape((slot_total, 1), f32),
                shape((slot_total, width), bf16),
                shape((slot_total, width), bf16),
                shape((slot_total, hidden), bf16),
                shape((slot_total, hidden), bf16),
            ),
            8 * slot_total * width * hidden,
            got,
            swap_cores(got),
            router_w,
            up_w,
            down_w,
            scalars=(device_at,),
            scratch=(pltpu.VMEM((slot_total, width), f32),),
        )
        back, d_logits = vmem_call(
            functools.partial(settle, n_row),
            (shape((slot_total, width), bf16), shape((slot_total, experts), bf16)),
            2 * slot_total * half * experts,
            mine,
            swap_cores(crossing),
            router_probs,
            gate_part,
            swap_cores(gate_part),
            router_w,
            scalars=(device_at,),
        )
        home = lax.all_to_all(
            back.reshape(experts, slots, width), ("ex", "row"), 0, 0, tiled=True
        ).reshape(slot_total, width)
        grad_down = dot(act_b, d_y, 0, 0)
        grad_up = dot(rows, d_pre, 0, 0)
        grad_router = jnp.pad(dot(rows, d_logits, 0, 0), ((0, 0), (0, wide - inner - experts)))
        home, grad_down, grad_up = lax.optimization_barrier((home, grad_down, grad_up))

        layer_out, d_x_one, grad_gain_ffn, d_context, *out_terms = vmem_call(
            functools.partial(come_home, scatter_order),
            (
                shape((seq_len, half), bf16),
                shape((seq_len, width), f32),
                shape((1, width), f32),
                shape((seq_len, inner), bf16),
                *block_shapes(own_rows, wide),
            ),
            2 * seq_len * (slot_total * 3 * half + 2 * width * inner),
            home,
            swap_cores(home[:, half:]),
            slot_of,
            x_in,
            attn_part,
            attn_peer,
            d_out,
            g_peer,
            gain_ffn[None],
            out_w,
            context,
            grad_router,
            scalars=(device_at,),
            scratch=(pltpu.VMEM((width, wide), bf16),),
        )
        out_sums = scatter_blocks(out_terms, own_rows)
        d_h_part, grad_offset, *qkv_terms = vmem_call(
            functools.partial(attend_backward, scatter_order),
            (
                shape((seq_len, width), bf16),
                shape((heads_here, span), f32),
                *block_shapes(own_rows, 3 * inner),
            ),
            12 * seq_len * width * inner + 10 * square,
            d_context,
            qkv,
            probs,
            h_one,
            qkv_w,
            scalars=(device_at,),
            scratch=(
                pltpu.VMEM((seq_len, 3 * inner), bf16),
                pltpu.VMEM((width, 3 * inner), bf16),
            ),
        )
        qkv_sums = scatter_blocks(qkv_terms, own_rows)
        grad_rel = jnp.einsum("ho,ob->bh", grad_offset, offset_hot, precision=highest)
        d_h_one = d_h_part.astype(f32) + swap_cores(d_h_part).astype(f32)
        x_float = x_in.astype(f32)
        scale_one = rms_scale(x_float)
        normed_one = x_float * scale_one
        grad_gain_attn = jnp.sum(d_h_one * normed_one, axis=0)
        d_norm_one = d_h_one * gain_attn
        grad_x = d_x_one + scale_one * (
            d_norm_one - normed_one * jnp.mean(d_norm_one * normed_one, axis=-1, keepdims=True)
        )
        small = sum_groups(
            jnp.concatenate([grad_gain_attn, grad_gain_ffn[0], grad_rel.reshape(-1)])
        )
        return (
            layer_out,
            grad_x.astype(bf16),
            small[:width],
            qkv_sums.reshape(own_rows, 3, inner).transpose(1, 0, 2),
            small[2 * width :].reshape(BUCKETS, heads_here),
            out_sums[:, :inner].T,
            small[width : 2 * width],
            out_sums[:, inner : inner + experts],
            grad_up[None],
            grad_down[None],
        )

    return per_device


def solution(mesh):
    return jax.shard_map(
        make_per_device(mesh),
        mesh=mesh,
        in_specs=(
            P(("ex", "row"), None),
            P(),
            P(None, ("ex", "row"), "col"),
            P(None, "col"),
            P("col", ("ex", "row")),
            P(),
            P(("ex", "row"), None),
            P(("ex", "row"), None, "col"),
            P(("ex", "row"), "col", None),
            P(("ex", "row"), None),
            P(("ex", "row")),
            P(("ex", "row")),
            P(("ex", "row")),
            P(("ex", "row"), "col"),
        ),
        out_specs=(
            P(("ex", "row"), "col"),
            P(("ex", "row"), None),
            P(),
            P(None, ("ex", "row"), "col"),
            P(None, "col"),
            P("col", ("ex", "row")),
            P(),
            P(("ex", "row"), None),
            P(("ex", "row"), None, "col"),
            P(("ex", "row"), "col", None),
        ),
        check_vma=False,
    )
```

time: 263 us -> 174 us (0.66)
  local copies, waits for them, and re-layouts: 67 us -> 13.6 us
  matrix products: 47.7 us -> 10.5 us
  blocking collectives: 46 us -> 21.6 us
  starting transfers between devices: 26.2 us -> 48.1 us
  Pallas kernels: 0 us -> 20.4 us
  between operations: 14.9 us -> 1.28 us
  other arithmetic: 21.1 us -> 12.6 us
  waiting for transfers between devices: 38 us -> 45.2 us
    ppermute x0 -> x37, starting transfers between devices: none -> 43.5 us  [hop(): lax.ppermute(values, axis, [(i, i ^ step) for i in range(mesh.shape[axis])])]
    ppermute x0 -> x37, waiting for transfers between devices: none -> 32.9 us  [hop(): lax.ppermute(values, axis, [(i, i ^ step) for i in range(mesh.shape[axis])])]
    dot_general x17 -> x3, matrix products: 36.2 us -> 9.81 us  [dot(): lax.dot_general(a, b, (((ca,), (cb,)), ((), ())), preferred_element_type=...]
    rev x2 -> x0, local copies, waits for them, and re-layouts: 22.1 us -> none  [the longest x1 13.5 us: spread_offsets(): return shaped[:, ::-1, :]]
    all_gather x2 -> x0, blocking collectives: 21.8 us -> none  [the longest x1 19.4 us: gather_groups(): part = lax.all_gather(shard, 'ex', axis=0)]
    all_to_all x5 -> x1, starting transfers between devices: 25.4 us -> 3.76 us  [per_device(): lax.all_to_all(back.reshape(experts, slots, width), ('ex', 'row'), 0, 0,...]
    all_to_all x5 -> x1, waiting for transfers between devices: 28.1 us -> 6.9 us  [per_device(): lax.all_to_all(back.reshape(experts, slots, width), ('ex', 'row'), 0, 0,...]
    pallas_call x0 -> x7, Pallas kernels: none -> 20.4 us  [vmem_call(): pl.pallas_call(kernel, out_shape=out_shape, in_specs=[pl.BlockSpec(memory...]
  transfers between devices with their start and end apart: 10 -> 45, of which waited for: 5 -> 17; matrix products, arithmetic and copies ran while one was open for 32% -> 14% of each run, Pallas kernels for 0% -> 3%
where the time goes in v1:
time: 174 us; the launch traced here: 173 us
  starting transfers between devices  48.1 us (28%)
  waiting for transfers between devices  45.2 us (26%)
  blocking collectives  21.6 us (12%)
  Pallas kernels  20.4 us (12%)
  local copies, waits for them, and re-layouts  13.6 us (8%)
  other arithmetic  12.6 us (7%)
  matrix products  10.5 us (6%)
    ppermute x37, starting transfers between devices, hop(): lax.ppermute(values, axis, [(i, i ^ step) for i in range(mesh.shape[axis])])  43.5 us
    ppermute x37, waiting for transfers between devices, hop(): lax.ppermute(values, axis, [(i, i ^ step) for i in range(mesh.shape[axis])])  32.9 us
    all_to_all x1, blocking collectives, per_device(): lax.all_to_all(send.reshape(experts, slots, width), ('ex', 'row'), 0, 0,...  21.6 us
    pallas_call x7, Pallas kernels, vmem_call(): pl.pallas_call(kernel, out_shape=out_shape, in_specs=[pl.BlockSpec(memory...  20.4 us
    unnamed x89, local copies, waits for them, and re-layouts  11.9 us
    dot_general x3, matrix products, dot(): lax.dot_general(a, b, (((ca,), (cb,)), ((), ())), preferred_element_type=...  9.81 us
    all_to_all x1, waiting for transfers between devices, per_device(): lax.all_to_all(back.reshape(experts, slots, width), ('ex', 'row'), 0, 0,...  6.9 us
    ppermute x7, waiting for transfers between devices, swap_cores(): return lax.ppermute(values, 'col', [(0, 1), (1, 0)])  5.43 us
  transfers between devices with their start and end apart: 45, of which 17 were waited for; matrix products, arithmetic and copies ran while one was open for 14% of the time, Pallas kernels for 3%

profile of v1, /device:TPU:0, one launch (start us, length us, event | category | flops | bytes accessed | tf_op | source)
XLA Modules:
  0.0 173.3 jit_solution(7017287100675005833)
XLA Ops:
  3.7 3.1 %collective-permute-start = (bf16[48,1664]{1,0:T(8,128)(2,1)S(1)}, bf16[48,1664]{1,0:T(8,128)(2,1)S(1)}, u32[]{:S(2)}, u32[]{:S(2)}) collective-permute-start(bf16[48,1664]{1,0:T(8,128)(2,1)S(1)} %shard_map.213.refs_0_), channel_id=1, source_target_pairs={{0,8},{8,0},{16,24},{24,16},{1,9},{9,1},{17,25},{25,17},{2,10},{10... | collective-permute-start | bytes 479240 | tf_op jit(solution)/shard_map/ppermute | solution.py:283
  6.8 2.6 %collective-permute-start.1 = (bf16[48,1664]{1,0:T(8,128)(2,1)S(1)}, bf16[48,1664]{1,0:T(8,128)(2,1)S(1)}, u32[]{:S(2)}, u32[]{:S(2)}) collective-permute-start(bf16[48,1664]{1,0:T(8,128)(2,1)S(1)} %shard_map.213.refs_0_), channel_id=1, source_target_pairs={{0,16},{8,24},{16,0},{24,8},{1,17},{9,25},{17,1},{25,9},{2,18},{10... | collective-permute-start | bytes 479240 | tf_op jit(solution)/shard_map/ppermute | solution.py:283
  9.4 1.7 collective-permute-start.3
  11.1 1.5 collective-permute-start.7
  12.6 2.6 %convert_bitcast_fusion.down_ref = bf16[1536,768]{1,0:T(8,128)(2,1)S(1)} fusion(f32[1,1536,768]{2,1,0:T(8,128)} %param.22), kind=kLoop, calls=%fused_computation | loop fusion | flops 1179648 | bytes 7077888 | tf_op jit(solution)/shard_map/convert_element_type | solution.py:379
  15.8 5.8 %collective-permute-done.1.refs_2_ = bf16[48,1664]{1,0:T(8,128)(2,1)S(1)} collective-permute-done((bf16[48,1664]{1,0:T(8,128)(2,1)S(1)}, bf16[48,1664]{1,0:T(8,128)(2,1)S(1)}, u32[]{:S(2)}, u32[]{:S(2)}) %collective-permute-start.1) | collective-permute-done | bytes 159776 | tf_op jit(solution)/shard_map/ppermute | solution.py:283
  23.1 1.5 collective-permute-start.10
  27.6 5.6 %collective-permute-done.5.refs_6_ = bf16[48,1664]{1,0:T(8,128)(2,1)S(1)} collective-permute-done((bf16[48,1664]{1,0:T(8,128)(2,1)S(1)}, bf16[48,1664]{1,0:T(8,128)(2,1)S(1)}, u32[]{:S(2)}, u32[]{:S(2)}) %collective-permute-start.5) | collective-permute-done | bytes 159776 | tf_op jit(solution)/shard_map/ppermute | solution.py:283
  34.2 2.0 %collective-permute-start.13 = (bf16[48,1664]{1,0:T(8,128)(2,1)S(1)}, bf16[48,1664]{1,0:T(8,128)(2,1)S(1)}, u32[]{:S(2)}, u32[]{:S(2)}) collective-permute-start(bf16[48,1664]{1,0:T(8,128)(2,1)S(1)} %collective-permute-done.5.refs_6_), channel_id=1, source_target_pairs={{0,4},{2,6},{4,0},{6,2},{1,5},{3,7},{5,1},{7,3},{8,12},{10,14},{12... | collective-permute-start | bytes 479240 | tf_op jit(solution)/shard_map/ppermute | solution.py:283
  38.5 1.7 collective-permute-done.13.refs_14_
  41.5 4.5 %shard_map.214 = (bf16[256,768]{1,0:T(8,128)(2,1)S(1)}, bf16[256,768]{1,0:T(8,128)(2,1)S(1)}, bf16[256,1152]{1,0:T(8,128)(2,1)S(1)}, f32[6,256,256]{2,1,0:T(8,12...) custom-call(s32[3]{0:T(128)S(1)} %pad_add_fusion.at_ref, ...), custom_call_target="tpu_custom_call" | custom-call | flops 704643072 | bytes 8667136 | tf_op jit(solution)/shard_map/pallas_call | solution.py:62
  47.9 1.6 collective-permute-done.15.peer_ref.part_peer_ref
  50.7 21.6 %all_to_all.10 = bf16[16,24,768]{2,1,0:T(8,128)(2,1)S(1)} all-to-all(bf16[16,24,768]{2,1,0:T(8,128)(2,1)S(1)} %bitcast.57), channel_id=1, replica_groups=mesh['ex'=4,'row'=4,'col'=2] {'ex','row'}, dimensions={0} | all-to-all | bytes 1179648 | tf_op jit(solution)/shard_map/all_to_all | solution.py:424
  72.3 2.0 %collective-permute-done.16.peer_ref = bf16[384,768]{1,0:T(8,128)(2,1)S(1)} collective-permute-done((bf16[384,768]{1,0:T(8,128)(2,1)S(1)}, bf16[384,768]{1,0:T(8,128)(2,1)S(1)}, u32[]{:S(2)}, u32[]{:S(2)}) %collective-permute-start.16) | collective-permute-done | bytes 589856 | tf_op jit(solution)/shard_map/ppermute | solution.py:51
  74.3 5.4 %shard_map.216 = (bf16[384,768]{1,0:T(8,128)(2,1)S(1)}, f32[384,768]{1,0:T(8,128)S(1)}, f32[384,16]{1,0:T(8,128)S(1)}, f32[384,1]{1,0:T(8,128)S(1)}, bf16[384,76...) custom-call(s32[3]{0:T(128)S(1)} %pad_add_fusion.at_ref, ...), custom_call_target="tpu_custom_call" | custom-call | flops 3623878656 | bytes 11429376 | tf_op jit(solution)/shard_map/pallas_call | solution.py:62
  81.2 1.8 %collective-permute-done.18.gate_peer_ref = f32[384,1]{1,0:T(8,128)S(1)} collective-permute-done((f32[384,1]{1,0:T(8,128)S(1)}, f32[384,1]{1,0:T(8,128)S(1)}, u32[]{:S(2)}, u32[]{:S(2)}) %collective-permute-start.18) | collective-permute-done | bytes 1568 | tf_op jit(solution)/shard_map/ppermute | solution.py:51
  85.5 3.8 %all-to-all-start.1 = ((bf16[16,24,768]{2,1,0:T(8,128)(2,1)}), bf16[16,24,768]{2,1,0:T(8,128)(2,1)S(1)}, u32[]{:S(2)}, u32[]{:S(2)}) async-start(bf16[16,24,768]{2,1,0:T(8,128)(2,1)} %bitcast.58), calls=%async_computation.1 | async-start | bytes 1179648 | tf_op jit(solution)/shard_map/all_to_all | solution.py:460
  90.2 4.9 %fusion.36 = f32[768,1536]{1,0:T(8,128)} fusion(bf16[384,768]{1,0:T(8,128)(2,1)S(1)} %get-tuple-element.100, bf16[384,1536]{1,0:T(8,128)(2,1)} %copy-done.6), kind=kOutput, calls=%fused_computation.62 | convolution fusion | flops 905969664 | bytes 6488064 | tf_op jit(solution)/shard_map/dot_general | solution.py:47
  95.1 3.6 %fusion.35 = f32[1536,768]{1,0:T(8,128)} fusion(bf16[384,1536]{1,0:T(8,128)(2,1)S(1)} %get-tuple-element.98, bf16[384,768]{1,0:T(8,128)(2,1)S(1)} %copy-done.14), kind=kOutput, calls=%fused_computation.61 | convolution fusion | flops 905969664 | bytes 6488064 | tf_op jit(solution)/shard_map/dot_general | solution.py:47
  98.7 6.9 %all-to-all-done.1 = bf16[16,24,768]{2,1,0:T(8,128)(2,1)S(1)} async-done(((bf16[16,24,768]{2,1,0:T(8,128)(2,1)}), bf16[16,24,768]{2,1,0:T(8,128)(2,1)S(1)}, u32[]{:S(2)}, u32[]{:S(2)}) %all-to-all-start.1) | async-done | bytes 589856 | tf_op jit(solution)/shard_map/all_to_all | solution.py:460
  108.5 3.4 %shard_map.218 = (bf16[256,384]{1,0:T(8,128)(2,1)}, f32[256,768]{1,0:T(8,128)S(1)}, f32[1,768]{1,0:T(1,128)S(1)}, bf16[256,384]{1,0:T(8,128)(2,1)S(1)}, bf16[4,4...) custom-call(s32[3]{0:T(128)S(1)} %pad_add_fusion.at_ref, ...), custom_call_target="tpu_custom_call" | custom-call | flops 528482304 | bytes 5610496 | tf_op jit(solution)/shard_map/pallas_call | solution.py:62
  114.6 1.5 collective-permute-start.35
  116.8 4.8 %shard_map.219 = (bf16[256,768]{1,0:T(8,128)(2,1)S(1)}, f32[6,512]{1,0:T(8,128)S(1)}, bf16[4,48,1152]{2,1,0:T(8,128)(2,1)S(1)}, bf16[2,48,1152]{2,1,0:T(8,128)(2...) custom-call(s32[3]{0:T(128)S(1)} %pad_add_fusion.at_ref, ...), custom_call_target="tpu_custom_call" | custom-call | flops 1157627904 | bytes 6696960 | tf_op jit(solution)/shard_map/pallas_call | solution.py:62
  125.0 1.5 collective-permute-start.41
  129.6 3.4 %collective-permute-done.41 = bf16[2,48,512]{2,1,0:T(8,128)(2,1)S(1)} collective-permute-done((bf16[2,48,512]{2,1,0:T(8,128)(2,1)}, bf16[2,48,512]{2,1,0:T(8,128)(2,1)S(1)}, u32[]{:S(2)}, u32[]{:S(2)}) %collective-permute-start.41) | collective-permute-done | bytes 98336 | tf_op jit(solution)/shard_map/ppermute | solution.py:283
  136.0 1.8 %add.183 = bf16[2,48,1152]{2,1,0:T(8,128)(2,1)} add(bf16[2,48,1152]{2,1,0:T(8,128)(2,1)} %copy-done.23, bf16[2,48,1152]{2,1,0:T(8,128)(2,1)} %collective-permute-done.27) | non-fusion elementwise | flops 110592 | bytes 663552 | tf_op jit(solution)/shard_map/add | solution.py:314
  137.8 2.9 %collective-permute-start.43 = (bf16[48,512]{1,0:T(8,128)(2,1)S(1)}, bf16[48,512]{1,0:T(8,128)(2,1)S(1)}, u32[]{:S(2)}, u32[]{:S(2)}) collective-permute-start(bf16[48,512]{1,0:T(8,128)(2,1)S(1)} %get-tuple-element.161), channel_id=1, source_target_pairs={{0,24},{8,16},{16,8},{24,0},{1,25},{9,17},{17,9},{25,1},{2,26},{10... | collective-permute-start | bytes 147464 | tf_op jit(solution)/shard_map/ppermute | solution.py:283
  145.9 4.0 %collective-permute-done.22 = f32[1728]{0:T(1024)S(1)} collective-permute-done((f32[1728]{0:T(1024)S(1)}, f32[1728]{0:T(1024)S(1)}, u32[]{:S(2)}, u32[]{:S(2)}) %collective-permute-start.22) | collective-permute-done | bytes 6944 | tf_op jit(solution)/shard_map/ppermute | solution.py:283
  154.3 2.9 %collective-permute-done.24 = f32[1728]{0:T(1024)S(1)} collective-permute-done((f32[1728]{0:T(1024)S(1)}, f32[1728]{0:T(1024)S(1)}, u32[]{:S(2)}, u32[]{:S(2)}) %collective-permute-start.24) | collective-permute-done | bytes 6944 | tf_op jit(solution)/shard_map/ppermute | solution.py:283
  158.5 2.1 %fusion.7 = bf16[256,768]{1,0:T(8,128)(2,1)} fusion(f32[256,768]{1,0:T(8,128)S(1)} %copy-done.10, bf16[256,768]{1,0:T(8,128)(2,1)S(1)} %copy-done.1, bf16[256,768]{1,0:T(8,128)(2,1)} %copy-done.30, bf16[256,768]{1,0:T(8,128)(2,1)S(1)} %get-tuple-element.113, f32[256]{0:T(256)S(1)} %broadcast_multiply_fusion, f32[768]{0:T(1024)S(1)} %copy-done.34, ...), kind=kLoop, calls=%fused_computation.12 | loop fusion | flops 2162688 | bytes 2364416 | tf_op jit(solution)/shard_map/convert_element_type | solution.py:529
  164.6 1.9 %collective-permute-start.34 = (bf16[48,1152]{1,0:T(8,128)(2,1)S(1)}, bf16[48,1152]{1,0:T(8,128)(2,1)S(1)}, u32[]{:S(2)}, u32[]{:S(2)}) collective-permute-start(bf16[48,1152]{1,0:T(8,128)(2,1)S(1)} %get-tuple-element.157), channel_id=1, source_target_pairs={{0,24},{8,16},{16,8},{24,0},{1,25},{9,17},{17,9},{25,1},{2,26},{10... | collective-permute-start | bytes 331784 | tf_op jit(solution)/shard_map/ppermute | solution.py:283
  168.4 2.9 %collective-permute-done.33 = bf16[48,1152]{1,0:T(8,128)(2,1)S(1)} collective-permute-done((bf16[48,1152]{1,0:T(8,128)(2,1)S(1)}, bf16[48,1152]{1,0:T(8,128)(2,1)S(1)}, u32[]{:S(2)}, u32[]{:S(2)}) %collective-permute-start.33) | collective-permute-done | bytes 110624 | tf_op jit(solution)/shard_map/ppermute | solution.py:283
  (199 shorter events, 54.9 us)
Async XLA Ops:
  3.7 11.5 %collective-permute-start = (bf16[48,1664]{1,0:T(8,128)(2,1)S(1)}, bf16[48,1664]{1,0:T(8,128)(2,1)S(1)}, u32[]{:S(2)}, u32[]{:S(2)}) collective-permute-start(bf16[48,1664]{1,0:T(8,128)(2,1)S(1)} %shard_map.213.refs_0_), channel_id=1, source_target_pairs={{0,8},{8,0},{16,24},{24,16},{1,9},{9,1},{17,25},{25,17},{2,10},{10... | collective-permute-start | bytes 479240 | tf_op jit(solution)/shard_map/ppermute | solution.py:283
  6.8 14.8 %collective-permute-start.1 = (bf16[48,1664]{1,0:T(8,128)(2,1)S(1)}, bf16[48,1664]{1,0:T(8,128)(2,1)S(1)}, u32[]{:S(2)}, u32[]{:S(2)}) collective-permute-start(bf16[48,1664]{1,0:T(8,128)(2,1)S(1)} %shard_map.213.refs_0_), channel_id=1, source_target_pairs={{0,16},{8,24},{16,0},{24,8},{1,17},{9,25},{17,1},{25,9},{2,18},{10... | collective-permute-start | bytes 479240 | tf_op jit(solution)/shard_map/ppermute | solution.py:283
  9.4 13.7 %collective-permute-start.2 = (bf16[48,1664]{1,0:T(8,128)(2,1)S(1)}, bf16[48,1664]{1,0:T(8,128)(2,1)S(1)}, u32[]{:S(2)}, u32[]{:S(2)}) collective-permute-start(bf16[48,1664]{1,0:T(8,128)(2,1)S(1)} %shard_map.213.refs_0_), channel_id=1, source_target_pairs={{0,24},{8,16},{16,8},{24,0},{1,25},{9,17},{17,9},{25,1},{2,26},{10... | collective-permute-start | bytes 479240 | tf_op jit(solution)/shard_map/ppermute | solution.py:283
  9.4 15.2 %collective-permute-start.3 = (bf16[48,1664]{1,0:T(8,128)(2,1)S(1)}, bf16[48,1664]{1,0:T(8,128)(2,1)S(1)}, u32[]{:S(2)}, u32[]{:S(2)}) collective-permute-start(bf16[48,1664]{1,0:T(8,128)(2,1)S(1)} %shard_map.213.refs_0_), channel_id=1, source_target_pairs={{0,2},{2,0},{4,6},{6,4},{1,3},{3,1},{5,7},{7,5},{8,10},{10,8},{12,... | collective-permute-start | bytes 479240 | tf_op jit(solution)/shard_map/ppermute | solution.py:283
  11.1 14.0 %collective-permute-start.7 = (bf16[48,1664]{1,0:T(8,128)(2,1)S(1)}, bf16[48,1664]{1,0:T(8,128)(2,1)S(1)}, u32[]{:S(2)}, u32[]{:S(2)}) collective-permute-start(bf16[48,1664]{1,0:T(8,128)(2,1)S(1)} %shard_map.213.refs_0_), channel_id=1, source_target_pairs={{0,4},{2,6},{4,0},{6,2},{1,5},{3,7},{5,1},{7,3},{8,12},{10,14},{12... | collective-permute-start | bytes 479240 | tf_op jit(solution)/shard_map/ppermute | solution.py:283
  15.2 11.8 %collective-permute-start.8 = (bf16[48,1664]{1,0:T(8,128)(2,1)S(1)}, bf16[48,1664]{1,0:T(8,128)(2,1)S(1)}, u32[]{:S(2)}, u32[]{:S(2)}) collective-permute-start(bf16[48,1664]{1,0:T(8,128)(2,1)S(1)} %collective-permute-done.refs_1_), channel_id=1, source_target_pairs={{0,4},{2,6},{4,0},{6,2},{1,5},{3,7},{5,1},{7,3},{8,12},{10,14},{12... | collective-permute-start | bytes 479240 | tf_op jit(solution)/shard_map/ppermute | solution.py:283
  21.6 12.6 %collective-permute-start.4 = (bf16[48,1664]{1,0:T(8,128)(2,1)S(1)}, bf16[48,1664]{1,0:T(8,128)(2,1)S(1)}, u32[]{:S(2)}, u32[]{:S(2)}) collective-permute-start(bf16[48,1664]{1,0:T(8,128)(2,1)S(1)} %collective-permute-done.refs_1_), channel_id=1, source_target_pairs={{0,2},{2,0},{4,6},{6,4},{1,3},{3,1},{5,7},{7,5},{8,10},{10,8},{12,... | collective-permute-start | bytes 479240 | tf_op jit(solution)/shard_map/ppermute | solution.py:283
  23.1 10.1 %collective-permute-start.10 = (bf16[48,1664]{1,0:T(8,128)(2,1)S(1)}, bf16[48,1664]{1,0:T(8,128)(2,1)S(1)}, u32[]{:S(2)}, u32[]{:S(2)}) collective-permute-start(bf16[48,1664]{1,0:T(8,128)(2,1)S(1)} %collective-permute-done.2.refs_3_), channel_id=1, source_target_pairs={{0,4},{2,6},{4,0},{6,2},{1,5},{3,7},{5,1},{7,3},{8,12},{10,14},{12... | collective-permute-start | bytes 479240 | tf_op jit(solution)/shard_map/ppermute | solution.py:283
  24.6 11.6 %collective-permute-start.6 = (bf16[48,1664]{1,0:T(8,128)(2,1)S(1)}, bf16[48,1664]{1,0:T(8,128)(2,1)S(1)}, u32[]{:S(2)}, u32[]{:S(2)}) collective-permute-start(bf16[48,1664]{1,0:T(8,128)(2,1)S(1)} %collective-permute-done.2.refs_3_), channel_id=1, source_target_pairs={{0,2},{2,0},{4,6},{6,4},{1,3},{3,1},{5,7},{7,5},{8,10},{10,8},{12,... | collective-permute-start | bytes 479240 | tf_op jit(solution)/shard_map/ppermute | solution.py:283
  25.1 8.0 %collective-permute-start.5 = (bf16[48,1664]{1,0:T(8,128)(2,1)S(1)}, bf16[48,1664]{1,0:T(8,128)(2,1)S(1)}, u32[]{:S(2)}, u32[]{:S(2)}) collective-permute-start(bf16[48,1664]{1,0:T(8,128)(2,1)S(1)} %collective-permute-done.1.refs_2_), channel_id=1, source_target_pairs={{0,2},{2,0},{4,6},{6,4},{1,3},{3,1},{5,7},{7,5},{8,10},{10,8},{12,... | collective-permute-start | bytes 479240 | tf_op jit(solution)/shard_map/ppermute | solution.py:283
  27.0 10.5 %collective-permute-start.9 = (bf16[48,1664]{1,0:T(8,128)(2,1)S(1)}, bf16[48,1664]{1,0:T(8,128)(2,1)S(1)}, u32[]{:S(2)}, u32[]{:S(2)}) collective-permute-start(bf16[48,1664]{1,0:T(8,128)(2,1)S(1)} %collective-permute-done.1.refs_2_), channel_id=1, source_target_pairs={{0,4},{2,6},{4,0},{6,2},{1,5},{3,7},{5,1},{7,3},{8,12},{10,14},{12... | collective-permute-start | bytes 479240 | tf_op jit(solution)/shard_map/ppermute | solution.py:283
  34.2 6.0 %collective-permute-start.13 = (bf16[48,1664]{1,0:T(8,128)(2,1)S(1)}, bf16[48,1664]{1,0:T(8,128)(2,1)S(1)}, u32[]{:S(2)}, u32[]{:S(2)}) collective-permute-start(bf16[48,1664]{1,0:T(8,128)(2,1)S(1)} %collective-permute-done.5.refs_6_), channel_id=1, source_target_pairs={{0,4},{2,6},{4,0},{6,2},{1,5},{3,7},{5,1},{7,3},{8,12},{10,14},{12... | collective-permute-start | bytes 479240 | tf_op jit(solution)/shard_map/ppermute | solution.py:283
  85.5 20.1 %all-to-all-start.1 = ((bf16[16,24,768]{2,1,0:T(8,128)(2,1)}), bf16[16,24,768]{2,1,0:T(8,128)(2,1)S(1)}, u32[]{:S(2)}, u32[]{:S(2)}) async-start(bf16[16,24,768]{2,1,0:T(8,128)(2,1)} %bitcast.58), calls=%async_computation.1 | async-start | bytes 1179648 | tf_op jit(solution)/shard_map/all_to_all | solution.py:460
  89.2 19.2 %collective-permute-start.20 = (bf16[256,384]{1,0:T(8,128)(2,1)}, bf16[256,384]{1,0:T(8,128)(2,1)}, u32[]{:S(2)}, u32[]{:S(2)}) collective-permute-start(bf16[256,384]{1,0:T(8,128)(2,1)} %g_ref.3), channel_id=1, source_target_pairs={{0,1},{1,0},{2,3},{3,2},{4,5},{5,4},{6,7},{7,6},{8,9},{9,8},{10,11... | collective-permute-start | bytes 589832 | tf_op jit(solution)/shard_map/ppermute | solution.py:51
  112.7 10.1 %collective-permute-start.36 = (bf16[2,48,512]{2,1,0:T(8,128)(2,1)S(1)}, bf16[2,48,512]{2,1,0:T(8,128)(2,1)S(1)}, u32[]{:S(2)}, u32[]{:S(2)}) collective-permute-start(bf16[2,48,512]{2,1,0:T(8,128)(2,1)S(1)} %get-tuple-element.126), channel_id=1, source_target_pairs={{0,2},{2,0},{4,6},{6,4},{1,3},{3,1},{5,7},{7,5},{8,10},{10,8},{12,... | collective-permute-start | bytes 294920 | tf_op jit(solution)/shard_map/ppermute | solution.py:283
  113.3 11.0 %collective-permute-start.40 = (bf16[2,48,512]{2,1,0:T(8,128)(2,1)S(1)}, bf16[2,48,512]{2,1,0:T(8,128)(2,1)S(1)}, u32[]{:S(2)}, u32[]{:S(2)}) collective-permute-start(bf16[2,48,512]{2,1,0:T(8,128)(2,1)S(1)} %get-tuple-element.129), channel_id=1, source_target_pairs={{0,4},{2,6},{4,0},{6,2},{1,5},{3,7},{5,1},{7,3},{8,12},{10,14},{12... | collective-permute-start | bytes 294920 | tf_op jit(solution)/shard_map/ppermute | solution.py:283
  114.6 12.4 %collective-permute-start.35 = (bf16[2,48,512]{2,1,0:T(8,128)(2,1)}, bf16[2,48,512]{2,1,0:T(8,128)(2,1)S(1)}, u32[]{:S(2)}, u32[]{:S(2)}) collective-permute-start(bf16[2,48,512]{2,1,0:T(8,128)(2,1)} %get-tuple-element.124), channel_id=1, source_target_pairs={{0,2},{2,0},{4,6},{6,4},{1,3},{3,1},{5,7},{7,5},{8,10},{10,8},{12,... | collective-permute-start | bytes 294920 | tf_op jit(solution)/shard_map/ppermute | solution.py:283
  116.1 11.6 %collective-permute-start.39 = (bf16[2,48,512]{2,1,0:T(8,128)(2,1)}, bf16[2,48,512]{2,1,0:T(8,128)(2,1)S(1)}, u32[]{:S(2)}, u32[]{:S(2)}) collective-permute-start(bf16[2,48,512]{2,1,0:T(8,128)(2,1)} %get-tuple-element.127), channel_id=1, source_target_pairs={{0,4},{2,6},{4,0},{6,2},{1,5},{3,7},{5,1},{7,3},{8,12},{10,14},{12... | collective-permute-start | bytes 294920 | tf_op jit(solution)/shard_map/ppermute | solution.py:283
  122.3 12.5 %collective-permute-start.27 = (bf16[2,48,1152]{2,1,0:T(8,128)(2,1)}, bf16[2,48,1152]{2,1,0:T(8,128)(2,1)}, u32[]{:S(2)}, u32[]{:S(2)}) collective-permute-start(bf16[2,48,1152]{2,1,0:T(8,128)(2,1)} %get-tuple-element.119), channel_id=1, source_target_pairs={{0,2},{2,0},{4,6},{6,4},{1,3},{3,1},{5,7},{7,5},{8,10},{10,8},{12,... | collective-permute-start | bytes 663560 | tf_op jit(solution)/shard_map/ppermute | solution.py:283
  122.9 5.4 %collective-permute-start.37 = (bf16[2,48,512]{2,1,0:T(8,128)(2,1)S(1)}, bf16[2,48,512]{2,1,0:T(8,128)(2,1)S(1)}, u32[]{:S(2)}, u32[]{:S(2)}) collective-permute-start(bf16[2,48,512]{2,1,0:T(8,128)(2,1)S(1)} %add.192), channel_id=1, source_target_pairs={{0,4},{2,6},{4,0},{6,2},{1,5},{3,7},{5,1},{7,3},{8,12},{10,14},{12... | collective-permute-start | bytes 294920 | tf_op jit(solution)/shard_map/ppermute | solution.py:283
  125.0 8.0 %collective-permute-start.41 = (bf16[2,48,512]{2,1,0:T(8,128)(2,1)}, bf16[2,48,512]{2,1,0:T(8,128)(2,1)S(1)}, u32[]{:S(2)}, u32[]{:S(2)}) collective-permute-start(bf16[2,48,512]{2,1,0:T(8,128)(2,1)} %add.196), channel_id=1, source_target_pairs={{0,2},{2,0},{4,6},{6,4},{1,3},{3,1},{5,7},{7,5},{8,10},{10,8},{12,... | collective-permute-start | bytes 294920 | tf_op jit(solution)/shard_map/ppermute | solution.py:283
  127.0 10.8 %collective-permute-start.31 = (bf16[2,48,1152]{2,1,0:T(8,128)(2,1)S(1)}, bf16[2,48,1152]{2,1,0:T(8,128)(2,1)S(1)}, u32[]{:S(2)}, u32[]{:S(2)}) collective-permute-start(bf16[2,48,1152]{2,1,0:T(8,128)(2,1)S(1)} %get-tuple-element.122), channel_id=1, source_target_pairs={{0,4},{2,6},{4,0},{6,2},{1,5},{3,7},{5,1},{7,3},{8,12},{10,14},{12... | collective-permute-start | bytes 663560 | tf_op jit(solution)/shard_map/ppermute | solution.py:283
  127.7 34.0 %collective-permute-start.26 = (bf16[2,48,1152]{2,1,0:T(8,128)(2,1)S(1)}, bf16[2,48,1152]{2,1,0:T(8,128)(2,1)}, u32[]{:S(2)}, u32[]{:S(2)}) collective-permute-start(bf16[2,48,1152]{2,1,0:T(8,128)(2,1)S(1)} %get-tuple-element.117), channel_id=1, source_target_pairs={{0,2},{2,0},{4,6},{6,4},{1,3},{3,1},{5,7},{7,5},{8,10},{10,8},{12,... | collective-permute-start | bytes 663560 | tf_op jit(solution)/shard_map/ppermute | solution.py:283
  128.3 33.5 %collective-permute-start.30 = (bf16[2,48,1152]{2,1,0:T(8,128)(2,1)S(1)}, bf16[2,48,1152]{2,1,0:T(8,128)(2,1)}, u32[]{:S(2)}, u32[]{:S(2)}) collective-permute-start(bf16[2,48,1152]{2,1,0:T(8,128)(2,1)S(1)} %get-tuple-element.120), channel_id=1, source_target_pairs={{0,4},{2,6},{4,0},{6,2},{1,5},{3,7},{5,1},{7,3},{8,12},{10,14},{12... | collective-permute-start | bytes 663560 | tf_op jit(solution)/shard_map/ppermute | solution.py:283
  133.0 7.8 %collective-permute-start.21 = (bf16[256,768]{1,0:T(8,128)(2,1)S(1)}, bf16[256,768]{1,0:T(8,128)(2,1)S(1)}, u32[]{:S(2)}, u32[]{:S(2)}) collective-permute-start(bf16[256,768]{1,0:T(8,128)(2,1)S(1)} %get-tuple-element.113), channel_id=1, source_target_pairs={{0,1},{1,0},{2,3},{3,2},{4,5},{5,4},{6,7},{7,6},{8,9},{9,8},{10,11... | collective-permute-start | bytes 1179656 | tf_op jit(solution)/shard_map/ppermute | solution.py:51
  134.8 7.2 %collective-permute-start.42 = (bf16[48,512]{1,0:T(8,128)(2,1)S(1)}, bf16[48,512]{1,0:T(8,128)(2,1)S(1)}, u32[]{:S(2)}, u32[]{:S(2)}) collective-permute-start(bf16[48,512]{1,0:T(8,128)(2,1)S(1)} %get-tuple-element.160), channel_id=1, source_target_pairs={{0,16},{8,24},{16,0},{24,8},{1,17},{9,25},{17,1},{25,9},{2,18},{10... | collective-permute-start | bytes 147464 | tf_op jit(solution)/shard_map/ppermute | solution.py:283
  137.8 6.0 %collective-permute-start.43 = (bf16[48,512]{1,0:T(8,128)(2,1)S(1)}, bf16[48,512]{1,0:T(8,128)(2,1)S(1)}, u32[]{:S(2)}, u32[]{:S(2)}) collective-permute-start(bf16[48,512]{1,0:T(8,128)(2,1)S(1)} %get-tuple-element.161), channel_id=1, source_target_pairs={{0,24},{8,16},{16,8},{24,0},{1,25},{9,17},{17,9},{25,1},{2,26},{10... | collective-permute-start | bytes 147464 | tf_op jit(solution)/shard_map/ppermute | solution.py:283
  142.0 19.8 %collective-permute-start.28 = (bf16[2,48,1152]{2,1,0:T(8,128)(2,1)}, bf16[2,48,1152]{2,1,0:T(8,128)(2,1)S(1)}, u32[]{:S(2)}, u32[]{:S(2)}) collective-permute-start(bf16[2,48,1152]{2,1,0:T(8,128)(2,1)} %add.183), channel_id=1, source_target_pairs={{0,4},{2,6},{4,0},{6,2},{1,5},{3,7},{5,1},{7,3},{8,12},{10,14},{12... | collective-permute-start | bytes 663560 | tf_op jit(solution)/shard_map/ppermute | solution.py:283
  143.8 18.0 %collective-permute-start.32 = (bf16[2,48,1152]{2,1,0:T(8,128)(2,1)S(1)}, bf16[2,48,1152]{2,1,0:T(8,128)(2,1)}, u32[]{:S(2)}, u32[]{:S(2)}) collective-permute-start(bf16[2,48,1152]{2,1,0:T(8,128)(2,1)S(1)} %add.187), channel_id=1, source_target_pairs={{0,2},{2,0},{4,6},{6,4},{1,3},{3,1},{5,7},{7,5},{8,10},{10,8},{12,... | collective-permute-start | bytes 663560 | tf_op jit(solution)/shard_map/ppermute | solution.py:283
  163.2 8.2 %collective-permute-start.33 = (bf16[48,1152]{1,0:T(8,128)(2,1)S(1)}, bf16[48,1152]{1,0:T(8,128)(2,1)S(1)}, u32[]{:S(2)}, u32[]{:S(2)}) collective-permute-start(bf16[48,1152]{1,0:T(8,128)(2,1)S(1)} %get-tuple-element.156), channel_id=1, source_target_pairs={{0,16},{8,24},{16,0},{24,8},{1,17},{9,25},{17,1},{25,9},{2,18},{10... | collective-permute-start | bytes 331784 | tf_op jit(solution)/shard_map/ppermute | solution.py:283
  164.6 6.8 %collective-permute-start.34 = (bf16[48,1152]{1,0:T(8,128)(2,1)S(1)}, bf16[48,1152]{1,0:T(8,128)(2,1)S(1)}, u32[]{:S(2)}, u32[]{:S(2)}) collective-permute-start(bf16[48,1152]{1,0:T(8,128)(2,1)S(1)} %get-tuple-element.157), channel_id=1, source_target_pairs={{0,24},{8,16},{16,8},{24,0},{1,25},{9,17},{17,9},{25,1},{2,26},{10... | collective-permute-start | bytes 331784 | tf_op jit(solution)/shard_map/ppermute | solution.py:283
  166.5 6.0 %collective-permute-start.29 = (bf16[48,1152]{1,0:T(8,128)(2,1)S(1)}, bf16[48,1152]{1,0:T(8,128)(2,1)S(1)}, u32[]{:S(2)}, u32[]{:S(2)}) collective-permute-start(bf16[48,1152]{1,0:T(8,128)(2,1)S(1)} %fusion.19), channel_id=1, source_target_pairs={{0,8},{8,0},{16,24},{24,16},{1,9},{9,1},{17,25},{25,17},{2,10},{10... | collective-permute-start | bytes 331784 | tf_op jit(solution)/shard_map/ppermute | solution.py:283
  (55 other events, 593.5 us)

commit v2 on v1

--- a/solution.py
+++ b/solution.py
@@ -18,16 +18,6 @@
 f32 = jnp.float32
 
 GATHER_ORDER = tuple(((k, m),) for m in range(4) for k in range(4))
-SCATTER_ORDER = (
-    ((0, 0), (1, 0), (2, 0), (3, 0)),
-    ((0, 1), (1, 1)),
-    ((2, 1), (3, 1)),
-    ((0, 2), (1, 2)),
-    ((2, 2), (3, 2)),
-    ((0, 3), (1, 3)),
-    ((2, 3), (3, 3)),
-)
-
 
 def bucket_of(offset):
     distance = jnp.abs(offset)
@@ -81,31 +71,32 @@
     ]
 
 
-def take_blocks(at_ref, order, full_ref, block_refs):
-    rows = iter(block_rows(at_ref, order, block_refs[0].shape[1]))
-    for block_ref in block_refs:
-        for i in range(block_ref.shape[0]):
-            block_ref[i] = full_ref[next(rows), :]
-
-
 def eye(size):
     dims = (size, size)
     same = lax.broadcasted_iota(jnp.int32, dims, 0) == lax.broadcasted_iota(jnp.int32, dims, 1)
     return same.astype(bf16)
 
 
-def pack_weights(qkv_ref, out_ref, router_ref, packed_ref):
-    inner, experts = qkv_ref.shape[2], router_ref.shape[1]
+def pack_weights(qkv_ref, out_turned_ref, router_turned_ref, packed_ref):
+    inner, experts = qkv_ref.shape[2], router_turned_ref.shape[0]
     for part in range(3):
         packed_ref[:, part * inner : (part + 1) * inner] = qkv_ref[part].astype(bf16)
-    turned = dot(out_ref[...].astype(bf16), eye(inner), 0, 0)
-    packed_ref[:, 3 * inner : 4 * inner] = turned.astype(bf16)
+    packed_ref[:, 3 * inner : 4 * inner] = out_turned_ref[...].astype(bf16)
     packed_ref[:, 4 * inner :] = jnp.zeros((packed_ref.shape[0], packed_ref.shape[1] - 4 * inner), bf16)
-    packed_ref[:, 4 * inner : 4 * inner + experts] = router_ref[...].astype(bf16)
+    router = dot(router_turned_ref[...].astype(bf16), eye(experts), 0, 0)
+    packed_ref[:, 4 * inner : 4 * inner + experts] = router.astype(bf16)
+
+
+def turn_normed(at_ref, x_ref, gain_ref, turned_ref, mine_ref):
+    x_float = x_ref[...].astype(f32)
+    h_one = (x_float * rms_scale(x_float) * gain_ref[...]).astype(bf16)
+    turned_ref[...] = dot(h_one, eye(h_one.shape[0]), 0, 0).astype(bf16)
+    half = mine_ref.shape[0]
+    mine_ref[...] = jnp.where(at_ref[2] == 0, turned_ref[:half, :], turned_ref[half:, :])
 
 
 def attend_forward(order, at_ref, x_ref, gain_ref, offset_ref, seg_ref, *refs):
-    *block_refs, part_ref, h_ref, qkv_ref, probs_ref, ctx_ref, w_ref, out_w_ref, router_ref = refs
+    *block_refs, part_ref, qkv_ref, probs_ref, ctx_ref, w_ref, out_w_ref, router_ref = refs
     seq_len = x_ref.shape[0]
     heads, inner = probs_ref.shape[0], ctx_ref.shape[1]
     for rows, block_ref in zip(block_rows(at_ref, order, block_refs[0].shape[0]), block_refs):
@@ -114,7 +105,6 @@
         router_ref[rows, :] = block_ref[:, 4 * inner :]
     x_float = x_ref[...].astype(f32)
     h_one = (x_float * rms_scale(x_float) * gain_ref[...]).astype(bf16)
-    h_ref[...] = h_one
     documents = lax.broadcasted_iota(jnp.int32, (8, seq_len), 0) == seg_ref[...]
     same_doc = dot(documents.astype(bf16), documents.astype(bf16), 0, 0) > 0.5
     qkv_ref[...] = dot(h_one, w_ref[...], 1, 0).astype(bf16)
@@ -191,8 +181,8 @@
 
 
 def settle(
-    row_size, at_ref, mine_ref, crossed_ref, probs_ref, gate_part_ref, gate_peer_ref, router_ref,
-    back_ref, d_logits_ref,
+    row_size, at_ref, mine_ref, crossed_ref, probs_ref, gate_part_ref, gate_peer_ref, router_ref, rows_ref,
+    back_ref, grad_router_ref,
 ):
     half = mine_ref.shape[1] // 2
     probs = probs_ref[...]
@@ -201,21 +191,20 @@
     gate = jnp.sum(probs * chosen, axis=1, keepdims=True)
     d_gate = gate_part_ref[...] + gate_peer_ref[...]
     d_logits = (d_gate * gate * (chosen - probs)).astype(bf16)
-    d_logits_ref[...] = d_logits
     router_w = router_ref[...][:, : probs.shape[1]]
     router_mine = jnp.where(at_ref[2] == 0, router_w[:half], router_w[half:])
     back_ref[:, :half] = (gate * (mine_ref[:, :half] + crossed_ref[:, :half].astype(f32))).astype(bf16)
     d_in = mine_ref[:, half:] + crossed_ref[:, half:].astype(f32)
     back_ref[:, half:] = (d_in + dot(d_logits, router_mine, 1, 1)).astype(bf16)
+    grad_router_ref[...] = dot(d_logits, rows_ref[...], 0, 0)
 
 
 def come_home(
-    order, at_ref, home_ref, peer_ref, slot_ref, x_ref, part_ref, part_peer_ref, g_ref, g_peer_ref,
-    gain_ref, out_w_ref, ctx_ref, router_ref, layer_ref, d_x_ref, gain_grad_ref, d_ctx_ref, *refs,
+    cube, at_ref, home_ref, peer_ref, slot_ref, x_ref, part_ref, part_peer_ref, g_ref, g_peer_ref,
+    gain_ref, out_w_ref, ctx_ref, layer_ref, d_x_ref, gain_grad_ref, d_ctx_ref, *refs,
 ):
-    *block_refs, grads_ref = refs
+    *piece_refs, grads_ref = refs
     half = g_ref.shape[1]
-    inner = ctx_ref.shape[1]
     first_core = at_ref[2] == 0
     both = lambda a, b: jnp.concatenate(
         [jnp.where(first_core, a, b), jnp.where(first_core, b, a)], axis=1
@@ -233,16 +222,22 @@
     d_x_ref[...] = d_x
     d_x_b = d_x.astype(bf16)
     d_ctx_ref[...] = dot(d_x_b, out_w_ref[...], 1, 0).astype(bf16)
-    grads_ref[:, :inner] = dot(d_x_b, ctx_ref[...], 0, 0).astype(bf16)
-    grads_ref[:, inner:] = router_ref[...].astype(bf16)
-    take_blocks(at_ref, order, grads_ref, block_refs)
+    grads_ref[...] = dot(d_x_b, ctx_ref[...], 0, 0).astype(bf16)
+    rows = grads_ref.shape[0] // 16
+    for m, piece_ref in enumerate(piece_refs):
+        if not cube:
+            piece_ref[...] = grads_ref[...]
+            continue
+        for k in range(4):
+            start = pl.multiple_of(((at_ref[0] ^ k) * 4 + (at_ref[1] ^ m)) * rows, 16)
+            piece_ref[k * rows : (k + 1) * rows, :] = grads_ref[pl.ds(start, rows), :]
     y_home = dot(place, home_ref[:, :half], 0, 0)
     x_mine = jnp.where(first_core, x_one[:, :half], x_one[:, half:])
     layer_ref[...] = (x_mine + y_home).astype(bf16)
 
 
-def attend_backward(order, at_ref, d_ctx_ref, qkv_ref, probs_ref, h_ref, w_ref, d_h_ref, grad_offset_ref, *refs):
-    *block_refs, d_qkv_ref, grads_ref = refs
+def attend_backward(cube, at_ref, d_ctx_ref, qkv_ref, probs_ref, w_ref, d_h_ref, grad_offset_ref, *refs):
+    *piece_refs, turned_ref = refs
     heads, seq_len, _ = probs_ref.shape
     inner = d_ctx_ref.shape[1]
     span = grad_offset_ref.shape[1]
@@ -251,6 +246,7 @@
         + lax.broadcasted_iota(jnp.int32, (seq_len, seq_len), 1)
         == seq_len - 1
     ).astype(bf16)
+    grad_offset_ref[...] = jnp.zeros(grad_offset_ref.shape, f32)
     for at in range(heads):
         cols = lambda part: pl.ds(part * inner + at * HEAD, HEAD)
         d_ctx = d_ctx_ref[:, at * HEAD : (at + 1) * HEAD]
@@ -258,17 +254,142 @@
         d_probs = dot(d_ctx, qkv_ref[:, cols(2)], 1, 1)
         row_delta = jnp.sum(probs * d_probs, axis=1, keepdims=True)
         d_scores = (probs * (d_probs - row_delta)).astype(bf16)
-        d_qkv_ref[:, cols(0)] = (dot(d_scores, qkv_ref[:, cols(1)], 1, 0) * 0.125).astype(bf16)
-        d_qkv_ref[:, cols(1)] = (dot(d_scores, qkv_ref[:, cols(0)], 0, 0) * 0.125).astype(bf16)
-        d_qkv_ref[:, cols(2)] = dot(probs.astype(bf16), d_ctx, 0, 0).astype(bf16)
-        turned = jnp.concatenate(
+        turned_ref[cols(0), :] = (dot(qkv_ref[:, cols(1)], d_scores, 0, 1) * 0.125).astype(bf16)
+        turned_ref[cols(1), :] = (dot(qkv_ref[:, cols(0)], d_scores, 0, 0) * 0.125).astype(bf16)
+        turned_ref[cols(2), :] = dot(d_ctx, probs.astype(bf16), 0, 0).astype(bf16)
+        flipped = jnp.concatenate(
             [dot(flip, d_scores, 1, 0), jnp.zeros((seq_len, span - seq_len), f32)], axis=1
         )
-        lined = pltpu.roll(turned, 0, 1, stride=1, stride_axis=0)
+        lined = pltpu.roll(flipped, 0, 1, stride=1, stride_axis=0)
         grad_offset_ref[at : at + 1, :] = jnp.sum(lined, axis=0, keepdims=True)
-    grads_ref[...] = dot(h_ref[...], d_qkv_ref[...], 0, 0).astype(bf16)
-    take_blocks(at_ref, order, grads_ref, block_refs)
-    d_h_ref[...] = dot(d_qkv_ref[...], w_ref[...], 1, 1).astype(bf16)
+    size = piece_refs[0].shape[0]
+    for m, piece_ref in enumerate(piece_refs):
+        start = pl.multiple_of((at_ref[1] ^ m) * size, 16) if cube else 0
+        piece_ref[...] = turned_ref[pl.ds(start, size), :]
+    d_h_ref[...] = dot(turned_ref[...], w_ref[...], 0, 1).astype(bf16)
+
+
+def qkv_terms(at_ref, turned_ref, small_ref, router_ref, *refs):
+    mine_ref, peer_ref, piece_refs, block_refs, grads_ref = refs[0], refs[1], refs[2:6], refs[6:10], refs[10]
+    half = mine_ref.shape[0] // 3
+    from_mine = from_peer = 0.0
+    for m in range(1, 4):
+        rows = slice((m - 1) * half, m * half)
+        from_mine = from_mine + dot(mine_ref[rows, :], piece_refs[m][...], 1, 1)
+        from_peer = from_peer + dot(peer_ref[rows, :], piece_refs[m][...], 1, 1)
+    own = dot(turned_ref[...], piece_refs[0][...], 1, 1)
+    first_core = at_ref[2] == 0
+    grads_ref[:half, :] = (own[:half] + jnp.where(first_core, from_mine, from_peer)).astype(bf16)
+    grads_ref[half:, :] = (own[half:] + jnp.where(first_core, from_peer, from_mine)).astype(bf16)
+    rows, size = block_refs[0].shape[0] - 8, grads_ref.shape[1]
+    width = small_ref.shape[1]
+    part = width // 4
+    for k, block_ref in enumerate(block_refs):
+        block_ref[rows:, :width] = small_ref[...].astype(bf16)
+        router = jnp.zeros((router_ref.shape[0], part), f32)
+        for z in range(4):
+            router = jnp.where((at_ref[0] ^ k) == z, router_ref[:, z * part : (z + 1) * part], router)
+        for i in range(2):
+            low = width + i * part
+            block_ref[rows:, low : low + part] = router[i * 8 : (i + 1) * 8].astype(bf16)
+        for m in range(4):
+            start = ((at_ref[0] ^ k) * 4 + (at_ref[1] ^ m)) * rows
+            block_ref[:rows, m * size : (m + 1) * size] = grads_ref[pl.ds(pl.multiple_of(start, 16), rows), :]
+
+
+def pair_sum(refs):
+    a, b, c, d = (ref[...].astype(f32) for ref in refs)
+    return (a + b) + (c + d)
+
+
+def join_line(at_ref, *refs):
+    total = pair_sum(refs[:4])
+    rows = refs[4].shape[0]
+    size = total.shape[1] // 4
+    width = size * 8 // 3
+    part = width // 16
+    extra = total[rows:]
+    for m, piece_ref in enumerate(refs[4:]):
+        piece_ref[...] = jnp.zeros(piece_ref.shape, bf16)
+        piece_ref[:, :size] = total[:rows, m * size : (m + 1) * size].astype(bf16)
+        for i in range(2):
+            for j in range(width // 128):
+                line = extra[6 + i : 7 + i, j * 128 : (j + 1) * 128]
+                piece_ref[i * 8 + j : i * 8 + j + 1, 384:] = line.astype(bf16)
+            router = jnp.zeros((8, part), f32)
+            for row in range(4):
+                low = width + i * 4 * part + row * part
+                router = jnp.where((at_ref[1] ^ m) == row, extra[:, low : low + part], router)
+            piece_ref[32 + i * 8 : 40 + i * 8, 384 : 384 + part] = router.astype(bf16)
+        piece_ref[16:24, 384:] = extra[:, :128].astype(bf16)
+
+
+def join_plane(at_ref, *refs):
+    piece_refs, (out_ref, gain_one_ref, gain_two_ref, rel_ref, router_ref, line_ref) = refs[:4], refs[4:]
+    size = line_ref.shape[1] // 4
+    for quarter in range(4):
+        piece = 0.0
+        for m, piece_ref in enumerate(piece_refs):
+            piece = jnp.where((at_ref[1] ^ m) == quarter, piece_ref[:, :size].astype(f32), piece)
+        line_ref[:, quarter * size : (quarter + 1) * size] = piece
+    inner = out_ref.shape[2]
+    for part in range(3):
+        out_ref[part] = line_ref[:, part * inner : (part + 1) * inner]
+    extra = pair_sum([ref.at[:, 384:] for ref in piece_refs])
+    for i, gain_ref in enumerate((gain_one_ref, gain_two_ref)):
+        for j in range(gain_ref.shape[1] // 128):
+            gain_ref[:, j * 128 : (j + 1) * 128] = extra[i * 8 + j : i * 8 + j + 1]
+    rel_ref[...] = extra[16 : 16 + rel_ref.shape[0], : rel_ref.shape[1]]
+    router_ref[...] = extra[32 : 32 + router_ref.shape[0], : router_ref.shape[1]]
+
+
+def join_blocks(*refs):
+    total = pair_sum(refs[:4])
+    rows = total.shape[0] // 4
+    for k, block_ref in enumerate(refs[4:]):
+        block_ref[...] = total[k * rows : (k + 1) * rows].astype(bf16)
+
+
+def finish(
+    d_h_ref, peer_ref, x_ref, d_x_ref, gain_ref, gain_grad_ref, grad_offset_ref, hot_ref, grad_x_ref, small_ref,
+):
+    d_h = d_h_ref[...].astype(f32) + peer_ref[...].astype(f32)
+    x_float = x_ref[...].astype(f32)
+    scale = rms_scale(x_float)
+    normed = x_float * scale
+    d_norm = d_h * gain_ref[...]
+    grad_x = d_x_ref[...] + scale * (
+        d_norm - normed * jnp.mean(d_norm * normed, axis=-1, keepdims=True)
+    )
+    grad_x_ref[...] = grad_x.astype(bf16)
+    heads, buckets = grad_offset_ref.shape[0] - 2, hot_ref.shape[1]
+    small_ref[...] = jnp.zeros(small_ref.shape, f32)
+    grad_rel = lax.dot_general(
+        grad_offset_ref[...], hot_ref[...], (((1,), (0,)), ((), ())), precision=highest, preferred_element_type=f32
+    )
+    small_ref[:, :buckets] = grad_rel
+    small_ref[heads : heads + 1, :] = jnp.sum(d_h * normed, axis=0, keepdims=True)
+    small_ref[heads + 1 : heads + 2, :] = gain_grad_ref[...]
+
+
+def expert_grads(rows_ref, d_y_ref, act_ref, d_pre_ref, down_ref, up_ref, held_ref, sems):
+    (hidden, width), steps = down_ref.shape, 3
+    copies = []
+    chunk = 0
+    for left_ref, right_ref, out_ref in ((act_ref, d_y_ref, down_ref), (rows_ref, d_pre_ref, up_ref)):
+        count = out_ref.shape[0] // steps
+        for at in range(steps):
+            rows = pl.ds(at * count, count)
+            slot = chunk % 3
+            if chunk >= 3:
+                copies[chunk - 3].wait()
+            held = held_ref.at[slot, pl.ds(0, count), pl.ds(0, out_ref.shape[1])]
+            held[...] = dot(left_ref[:, rows], right_ref[...], 0, 0)
+            copies.append(pltpu.make_async_copy(held, out_ref.at[rows, :], sems.at[chunk]))
+            copies[-1].start()
+            chunk += 1
+    for copy in copies[-3:]:
+        copy.wait()
 
 
 def experts_pad(experts):
@@ -283,7 +404,7 @@
         return lax.ppermute(values, axis, [(i, i ^ step) for i in range(mesh.shape[axis])])
 
     def whole_cube(rows):
-        return n_ex == 4 and n_row == 4 and rows % 16 == 0
+        return n_ex == 4 and n_row == 4 and rows == 48
 
     def gather_blocks(shard):
         rows, width = shard.shape
@@ -300,31 +421,18 @@
         part = lax.all_to_all(part, "row", split_axis=0, concat_axis=0, tiled=True)
         return [part.transpose(1, 0, 2, 3).reshape(groups * rows, width)]
 
-    def block_shapes(rows, width):
-        if whole_cube(rows):
-            return [shape((len(part), rows, width), bf16) for part in SCATTER_ORDER]
-        return [shape((1, groups * rows, width), bf16)]
-
-    def scatter_blocks(parts, rows):
-        if whole_cube(rows):
-            here, x_low, x_high, y_low, y_high, d_low, d_high = parts
-            from_x, from_y = hop(d_low, "row", 1), hop(d_high, "row", 2)
-            x_first, y_first = hop(x_low, "row", 1), hop(y_high, "row", 2)
-            x_last = hop(x_high + from_y, "row", 1)
-            y_last = hop(y_low + from_x, "row", 2)
-            low = here[:2].astype(f32) + x_first.astype(f32) + y_last.astype(f32)
-            high = here[2:].astype(f32) + y_first.astype(f32) + x_last.astype(f32)
-            return (
-                low[0]
-                + hop(low[1].astype(bf16), "ex", 1).astype(f32)
-                + hop(high[0].astype(bf16), "ex", 2).astype(f32)
-                + hop(high[1].astype(bf16), "ex", 3).astype(f32)
-            )
-        part = parts[0].reshape(n_ex, n_row, rows, -1).transpose(1, 0, 2, 3)
+    def scatter_groups(grads, rows):
+        part = grads.astype(bf16).reshape(n_ex, n_row, rows, -1).transpose(1, 0, 2, 3)
         part = lax.all_to_all(part, "row", split_axis=0, concat_axis=0, tiled=True)
         part = jnp.sum(part.astype(f32), axis=0).astype(bf16)
         part = lax.all_to_all(part, "ex", split_axis=0, concat_axis=0, tiled=True)
         return jnp.sum(part.astype(f32), axis=0)
+
+    def plane_hops(parts):
+        return [hop(part, "row", m + 1) for m, part in enumerate(parts)]
+
+    def line_hops(parts):
+        return [hop(part, "ex", k + 1) for k, part in enumerate(parts)]
 
     def sum_groups(values):
         for axis in ("row", "ex"):
@@ -363,21 +471,31 @@
         hidden = w_up.shape[2]
         device_at = jnp.stack([lax.axis_index(axis).astype(jnp.int32) for axis in ("ex", "row", "col")])
         device_at, w_qkv = lax.optimization_barrier((device_at, w_qkv))
-        gather_order = GATHER_ORDER if whole_cube(own_rows) else None
-        scatter_order = SCATTER_ORDER if whole_cube(own_rows) else None
+        cube = whole_cube(own_rows)
+        gather_order = GATHER_ORDER if cube else None
 
         (packed,) = vmem_call(
             pack_weights,
             (shape((own_rows, 3 * inner + wide), bf16),),
             0,
             w_qkv,
-            w_out,
-            w_router,
+            w_out.T,
+            w_router.T,
         )
         blocks = gather_blocks(packed)
+        normed_turned, normed_mine = vmem_call(
+            turn_normed,
+            (shape((width, seq_len), bf16), shape((half, seq_len), bf16)),
+            0,
+            x_in,
+            gain_attn[None],
+            scalars=(device_at,),
+        )
         up_w = w_up[0].astype(bf16)
         down_w = w_down[0].astype(bf16)
-        *blocks, up_w, down_w = lax.optimization_barrier((*blocks, up_w, down_w))
+        *blocks, up_w, down_w, normed_mine, normed_turned = lax.optimization_barrier(
+            (*blocks, up_w, down_w, normed_mine, normed_turned)
+        )
         g_peer = swap_cores(d_out)
 
         span = 2 * seq_len
@@ -387,10 +505,9 @@
         ).astype(f32)
         per_offset = jnp.einsum("bh,ob->ho", rel_bias, offset_hot, precision=highest)
         square = seq_len * seq_len * heads_here * HEAD
-        attn_part, h_one, qkv, probs, context, qkv_w, out_w, router_w = vmem_call(
+        attn_part, qkv, probs, context, qkv_w, out_w, router_w = vmem_call(
             functools.partial(attend_forward, gather_order),
             (
-                shape((seq_len, width), bf16),
                 shape((seq_len, width), bf16),
                 shape((seq_len, 3 * inner), bf16),
                 shape((heads_here, seq_len, seq_len), f32),
@@ -424,6 +541,9 @@
         got = lax.all_to_all(
             send.reshape(experts, slots, width), ("ex", "row"), 0, 0, tiled=True
         ).reshape(slot_total, width)
+        if cube:
+            later_normed, got = lax.optimization_barrier((normed_mine, got))
+            normed_hops = plane_hops([later_normed] * 2)
         crossing, mine, router_probs, gate_part, rows, d_y, act_b, d_pre = vmem_call(
             functools.partial(run_expert, experts, n_row),
             (
@@ -445,9 +565,13 @@
             scalars=(device_at,),
             scratch=(pltpu.VMEM((slot_total, width), f32),),
         )
-        back, d_logits = vmem_call(
+        if cube:
+            crossing, gate_part, *normed_hops = lax.optimization_barrier((crossing, gate_part, *normed_hops))
+            from_x, from_y = normed_hops
+            normed_hops += [hop(from_x[: half // 2], "row", 2), hop(from_y[half // 2 :], "row", 1)]
+        back, grad_router = vmem_call(
             functools.partial(settle, n_row),
-            (shape((slot_total, width), bf16), shape((slot_total, experts), bf16)),
+            (shape((slot_total, width), bf16), shape((experts, width), f32)),
             2 * slot_total * half * experts,
             mine,
             swap_cores(crossing),
@@ -455,24 +579,40 @@
             gate_part,
             swap_cores(gate_part),
             router_w,
+            rows,
             scalars=(device_at,),
         )
+        if cube:
+            back, *normed_hops = lax.optimization_barrier((back, *normed_hops))
         home = lax.all_to_all(
             back.reshape(experts, slots, width), ("ex", "row"), 0, 0, tiled=True
         ).reshape(slot_total, width)
-        grad_down = dot(act_b, d_y, 0, 0)
-        grad_up = dot(rows, d_pre, 0, 0)
-        grad_router = jnp.pad(dot(rows, d_logits, 0, 0), ((0, 0), (0, wide - inner - experts)))
-        home, grad_down, grad_up = lax.optimization_barrier((home, grad_down, grad_up))
-
-        layer_out, d_x_one, grad_gain_ffn, d_context, *out_terms = vmem_call(
-            functools.partial(come_home, scatter_order),
+        def grads_of_expert(rows, d_y, act_b, d_pre):
+            return pl.pallas_call(
+                expert_grads,
+                out_shape=(shape((hidden, width), f32), shape((width, hidden), f32)),
+                in_specs=[pl.BlockSpec(memory_space=pltpu.VMEM)] * 4,
+                out_specs=[pl.BlockSpec(memory_space=pltpu.HBM)] * 2,
+                scratch_shapes=[
+                    pltpu.VMEM((3, max(hidden, width) // 3, max(hidden, width)), f32),
+                    pltpu.SemaphoreType.DMA((6,)),
+                ],
+                compiler_params=pltpu.CompilerParams(vmem_limit_bytes=24 * 2**20),
+                cost_estimate=pl.CostEstimate(
+                    flops=4 * slot_total * width * hidden, bytes_accessed=12 * width * hidden, transcendentals=0
+                ),
+            )(rows, d_y, act_b, d_pre)
+
+        quarter = (width // 4, 3 * inner // 4) if cube else (width, 3 * inner)
+        pieces = 4 if cube else 1
+        layer_out, d_x_one, grad_gain_ffn, d_context, *out_pieces = vmem_call(
+            functools.partial(come_home, cube),
             (
                 shape((seq_len, half), bf16),
                 shape((seq_len, width), f32),
                 shape((1, width), f32),
                 shape((seq_len, inner), bf16),
-                *block_shapes(own_rows, wide),
+                *[shape((quarter[0], inner), bf16)] * pieces,
             ),
             2 * seq_len * (slot_total * 3 * half + 2 * width * inner),
             home,
@@ -486,53 +626,115 @@
             gain_ffn[None],
             out_w,
             context,
-            grad_router,
             scalars=(device_at,),
-            scratch=(pltpu.VMEM((width, wide), bf16),),
-        )
-        out_sums = scatter_blocks(out_terms, own_rows)
-        d_h_part, grad_offset, *qkv_terms = vmem_call(
-            functools.partial(attend_backward, scatter_order),
+            scratch=(pltpu.VMEM((width, inner), bf16),),
+        )
+        d_h_part, grad_offset, *d_qkv_turned = vmem_call(
+            functools.partial(attend_backward, cube),
             (
                 shape((seq_len, width), bf16),
-                shape((heads_here, span), f32),
-                *block_shapes(own_rows, 3 * inner),
+                shape((heads_here + 2, span), f32),
+                *[shape((quarter[1], seq_len), bf16)] * pieces,
             ),
-            12 * seq_len * width * inner + 10 * square,
+            6 * seq_len * width * inner + 10 * square,
             d_context,
             qkv,
             probs,
-            h_one,
             qkv_w,
             scalars=(device_at,),
-            scratch=(
-                pltpu.VMEM((seq_len, 3 * inner), bf16),
-                pltpu.VMEM((width, 3 * inner), bf16),
-            ),
-        )
-        qkv_sums = scatter_blocks(qkv_terms, own_rows)
-        grad_rel = jnp.einsum("ho,ob->bh", grad_offset, offset_hot, precision=highest)
-        d_h_one = d_h_part.astype(f32) + swap_cores(d_h_part).astype(f32)
-        x_float = x_in.astype(f32)
-        scale_one = rms_scale(x_float)
-        normed_one = x_float * scale_one
-        grad_gain_attn = jnp.sum(d_h_one * normed_one, axis=0)
-        d_norm_one = d_h_one * gain_attn
-        grad_x = d_x_one + scale_one * (
-            d_norm_one - normed_one * jnp.mean(d_norm_one * normed_one, axis=-1, keepdims=True)
-        )
-        small = sum_groups(
-            jnp.concatenate([grad_gain_attn, grad_gain_ffn[0], grad_rel.reshape(-1)])
-        )
+            scratch=(pltpu.VMEM((3 * inner, seq_len), bf16),),
+        )
+        grad_x, small = vmem_call(
+            finish,
+            (shape((seq_len, width), bf16), shape((heads_here + 2, width), f32)),
+            0,
+            d_h_part,
+            swap_cores(d_h_part),
+            x_in,
+            d_x_one,
+            gain_attn[None],
+            grad_gain_ffn,
+            grad_offset,
+            offset_hot,
+        )
+        if cube:
+            *normed_hops, _ = lax.optimization_barrier((*normed_hops, d_h_part))
+            normed_near = jnp.concatenate(normed_hops, axis=0)
+            normed_peer = swap_cores(normed_near)
+            terms = vmem_call(
+                qkv_terms,
+                [shape((own_rows + 8, 3 * inner), bf16)] * 4,
+                6 * seq_len * width * inner,
+                normed_turned,
+                small,
+                grad_router,
+                normed_near,
+                normed_peer,
+                d_qkv_turned[0],
+                *plane_hops(d_qkv_turned[1:]),
+                scalars=(device_at,),
+                scratch=(pltpu.VMEM((width, quarter[1]), bf16),),
+            )
+            line = line_hops(terms[1:])
+            first_line = line[0]
+            rows, d_y, act_b, d_pre, _ = lax.optimization_barrier((rows, d_y, act_b, d_pre, terms[0]))
+            grad_down, grad_up = grads_of_expert(rows, d_y, act_b, d_pre)
+            *line, grad_down, grad_up = lax.optimization_barrier((*line, grad_down, grad_up))
+            split = vmem_call(
+                join_line,
+                [shape((own_rows, 512), bf16)] * 4,
+                0,
+                terms[0],
+                *line,
+                scalars=(device_at,),
+            )
+            last = plane_hops(split[1:])
+            grad_qkv, gain_one, gain_two, grad_rel, grad_router = vmem_call(
+                join_plane,
+                (
+                    shape((3, own_rows, inner), f32),
+                    shape((1, width), f32),
+                    shape((1, width), f32),
+                    shape((heads_here, BUCKETS), f32),
+                    shape((experts, own_rows), f32),
+                ),
+                0,
+                split[0],
+                *last,
+                scalars=(device_at,),
+                scratch=(pltpu.VMEM((own_rows, 3 * inner), f32),),
+            )
+            *out_pieces, _ = lax.optimization_barrier((*out_pieces, first_line))
+            out_hops = plane_hops(out_pieces[1:])
+            out_blocks = vmem_call(
+                join_blocks,
+                [shape((own_rows, inner), bf16)] * 4,
+                0,
+                out_pieces[0],
+                *out_hops,
+            )
+            *out_blocks, _ = lax.optimization_barrier((*out_blocks, last[0]))
+            out_blocks = (out_blocks[0], *line_hops(out_blocks[1:]))
+            grad_out = sum(part.astype(f32) for part in out_blocks)
+        else:
+            grad_down, grad_up = grads_of_expert(rows, d_y, act_b, d_pre)
+            grad_qkv = scatter_groups(dot(normed_turned, d_qkv_turned[0], 1, 1), own_rows)
+            grad_qkv = grad_qkv.reshape(own_rows, 3, inner).transpose(1, 0, 2)
+            grad_out = scatter_groups(out_pieces[0], own_rows)
+            small = sum_groups(jnp.concatenate([small, grad_router]))
+            gain_one, gain_two = small[heads_here], small[heads_here + 1]
+            grad_rel = small[:heads_here, :BUCKETS]
+            own_at = (device_at[0] * n_row + device_at[1]) * own_rows
+            grad_router = lax.dynamic_slice(small, (heads_here + 2, own_at), (experts, own_rows))
         return (
             layer_out,
-            grad_x.astype(bf16),
-            small[:width],
-            qkv_sums.reshape(own_rows, 3, inner).transpose(1, 0, 2),
-            small[2 * width :].reshape(BUCKETS, heads_here),
-            out_sums[:, :inner].T,
-            small[width : 2 * width],
-            out_sums[:, inner : inner + experts],
+            grad_x,
+            gain_one.reshape(width),
+            grad_qkv,
+            grad_rel.T,
+            grad_out.T,
+            gain_two.reshape(width),
+            grad_router.T,
             grad_up[None],
             grad_down[None],
         )

time: 174 us -> 154 us (0.89)
  blocking collectives: 21.6 us -> 43.1 us
  waiting for transfers between devices: 45.2 us -> 28.3 us
  local copies, waits for them, and re-layouts: 13.6 us -> 2.68 us
  matrix products: 10.5 us -> 0.31 us
  Pallas kernels: 20.4 us -> 30 us
  other arithmetic: 12.6 us -> 4.94 us
  starting transfers between devices: 48.1 us -> 43.1 us
    all_to_all x0 -> x1, blocking collectives: none -> 21.5 us  [per_device(): lax.all_to_all(back.reshape(experts, slots, width), ('ex', 'row'), 0, 0,...]
    dot_general x4 -> x0, matrix products: 10.2 us -> none  [the longest x3 9.81 us: dot(): lax.dot_general(a, b, (((ca,), (cb,)), ((), ())), preferred_element_type=...]
    ppermute x37 -> x34, waiting for transfers between devices: 32.9 us -> 23 us  [hop(): lax.ppermute(values, axis, [(i, i ^ step) for i in range(mesh.shape[axis])])]
    unnamed x89 -> x29, local copies, waits for them, and re-layouts: 11.9 us -> 2.62 us
    all_to_all x1 -> x0, waiting for transfers between devices: 6.9 us -> none  [per_device(): lax.all_to_all(back.reshape(experts, slots, width), ('ex', 'row'), 0, 0,...]
    pallas_call x0 -> x1, Pallas kernels: none -> 4.99 us  [grads_of_expert(): pl.pallas_call(expert_grads, out_shape=(shape((hidden, width), f32), shap...]
    pallas_call x7 -> x13, Pallas kernels: 20.4 us -> 25 us  [vmem_call(): pl.pallas_call(kernel, out_shape=out_shape, in_specs=[pl.BlockSpec(memory...]
    all_to_all x1 -> x0, starting transfers between devices: 3.76 us -> none  [per_device(): lax.all_to_all(back.reshape(experts, slots, width), ('ex', 'row'), 0, 0,...]
  transfers between devices with their start and end apart: 45 -> 42, of which waited for: 17 -> 17; matrix products, arithmetic and copies ran while one was open for 14% -> 3% of each run, Pallas kernels for 3% -> 10%
where the time goes in v2:
time: 154 us; the launch traced here: 153 us
  starting transfers between devices  43.1 us (28%)
  blocking collectives  43.1 us (28%)
  Pallas kernels  30 us (19%)
  waiting for transfers between devices  28.3 us (18%)
  other arithmetic  4.94 us (3%)
  local copies, waits for them, and re-layouts  2.68 us (2%)
    ppermute x34, starting transfers between devices, hop(): lax.ppermute(values, axis, [(i, i ^ step) for i in range(mesh.shape[axis])])  41.9 us
    pallas_call x13, Pallas kernels, vmem_call(): pl.pallas_call(kernel, out_shape=out_shape, in_specs=[pl.BlockSpec(memory...  25 us
    ppermute x34, waiting for transfers between devices, hop(): lax.ppermute(values, axis, [(i, i ^ step) for i in range(mesh.shape[axis])])  23 us
    all_to_all x1, blocking collectives, per_device(): lax.all_to_all(send.reshape(experts, slots, width), ('ex', 'row'), 0, 0,...  21.6 us
    all_to_all x1, blocking collectives, per_device(): lax.all_to_all(back.reshape(experts, slots, width), ('ex', 'row'), 0, 0,...  21.5 us
    ppermute x8, waiting for transfers between devices, swap_cores(): return lax.ppermute(values, 'col', [(0, 1), (1, 0)])  5.28 us
    pallas_call x1, Pallas kernels, grads_of_expert(): pl.pallas_call(expert_grads, out_shape=(shape((hidden, width), f32), shap...  4.99 us
  transfers between devices with their start and end apart: 42, of which 17 were waited for; matrix products, arithmetic and copies ran while one was open for 3% of the time, Pallas kernels for 10%

profile of v2, /device:TPU:0, one launch (start us, length us, event | category | flops | bytes accessed | tf_op | source)
XLA Modules:
  0.0 153.3 jit_solution(8418839279504169203)
XLA Ops:
  3.4 3.1 %collective-permute-start = (bf16[48,1664]{1,0:T(8,128)(2,1)S(1)}, bf16[48,1664]{1,0:T(8,128)(2,1)S(1)}, u32[]{:S(2)}, u32[]{:S(2)}) collective-permute-start(bf16[48,1664]{1,0:T(8,128)(2,1)S(1)} %shard_map.213.refs_0_), channel_id=1, source_target_pairs={{0,8},{8,0},{16,24},{24,16},{1,9},{9,1},{17,25},{25,17},{2,10},{10... | collective-permute-start | bytes 479240 | tf_op jit(solution)/shard_map/ppermute | solution.py:404
  6.5 2.6 %collective-permute-start.1 = (bf16[48,1664]{1,0:T(8,128)(2,1)S(1)}, bf16[48,1664]{1,0:T(8,128)(2,1)S(1)}, u32[]{:S(2)}, u32[]{:S(2)}) collective-permute-start(bf16[48,1664]{1,0:T(8,128)(2,1)S(1)} %shard_map.213.refs_0_), channel_id=1, source_target_pairs={{0,16},{8,24},{16,0},{24,8},{1,17},{9,25},{17,1},{25,9},{2,18},{10... | collective-permute-start | bytes 479240 | tf_op jit(solution)/shard_map/ppermute | solution.py:404
  9.1 1.7 %collective-permute-start.3 = (bf16[48,1664]{1,0:T(8,128)(2,1)S(1)}, bf16[48,1664]{1,0:T(8,128)(2,1)S(1)}, u32[]{:S(2)}, u32[]{:S(2)}) collective-permute-start(bf16[48,1664]{1,0:T(8,128)(2,1)S(1)} %shard_map.213.refs_0_), channel_id=1, source_target_pairs={{0,2},{2,0},{4,6},{6,4},{1,3},{3,1},{5,7},{7,5},{8,10},{10,8},{12,... | collective-permute-start | bytes 479240 | tf_op jit(solution)/shard_map/ppermute | solution.py:404
  10.8 1.5 collective-permute-start.7
  12.3 2.6 %convert_bitcast_fusion.down_ref = bf16[1536,768]{1,0:T(8,128)(2,1)S(1)} fusion(f32[1,1536,768]{2,1,0:T(8,128)} %param.22), kind=kLoop, calls=%fused_computation | loop fusion | flops 1179648 | bytes 7077888 | tf_op jit(solution)/shard_map/convert_element_type | solution.py:495
  15.5 5.8 %collective-permute-done.1.refs_2_ = bf16[48,1664]{1,0:T(8,128)(2,1)S(1)} collective-permute-done((bf16[48,1664]{1,0:T(8,128)(2,1)S(1)}, bf16[48,1664]{1,0:T(8,128)(2,1)S(1)}, u32[]{:S(2)}, u32[]{:S(2)}) %collective-permute-start.1) | collective-permute-done | bytes 159776 | tf_op jit(solution)/shard_map/ppermute | solution.py:404
  21.3 1.5 collective-permute-start.4
  22.8 1.5 collective-permute-start.10
  24.9 1.5 collective-permute-start.5
  28.3 4.6 %collective-permute-done.5.refs_6_ = bf16[48,1664]{1,0:T(8,128)(2,1)S(1)} collective-permute-done((bf16[48,1664]{1,0:T(8,128)(2,1)S(1)}, bf16[48,1664]{1,0:T(8,128)(2,1)S(1)}, u32[]{:S(2)}, u32[]{:S(2)}) %collective-permute-start.5) | collective-permute-done | bytes 159776 | tf_op jit(solution)/shard_map/ppermute | solution.py:404
  33.9 2.0 %collective-permute-start.13 = (bf16[48,1664]{1,0:T(8,128)(2,1)S(1)}, bf16[48,1664]{1,0:T(8,128)(2,1)S(1)}, u32[]{:S(2)}, u32[]{:S(2)}) collective-permute-start(bf16[48,1664]{1,0:T(8,128)(2,1)S(1)} %collective-permute-done.5.refs_6_), channel_id=1, source_target_pairs={{0,4},{2,6},{4,0},{6,2},{1,5},{3,7},{5,1},{7,3},{8,12},{10,14},{12... | collective-permute-start | bytes 479240 | tf_op jit(solution)/shard_map/ppermute | solution.py:404
  38.2 1.7 %collective-permute-done.13.refs_14_ = bf16[48,1664]{1,0:T(8,128)(2,1)S(1)} collective-permute-done((bf16[48,1664]{1,0:T(8,128)(2,1)S(1)}, bf16[48,1664]{1,0:T(8,128)(2,1)S(1)}, u32[]{:S(2)}, u32[]{:S(2)}) %collective-permute-start.13) | collective-permute-done | bytes 159776 | tf_op jit(solution)/shard_map/ppermute | solution.py:404
  41.2 4.5 %shard_map.215 = (bf16[256,768]{1,0:T(8,128)(2,1)S(1)}, bf16[256,1152]{1,0:T(8,128)(2,1)S(1)}, f32[6,256,256]{2,1,0:T(8,128)S(1)}, bf16[256,384]{1,0:T(8,128)(2,...) custom-call(s32[3]{0:T(128)S(1)} %pad_add_fusion.at_ref, ...), custom_call_target="tpu_custom_call" | custom-call | flops 704643072 | bytes 8273920 | tf_op jit(solution)/shard_map/pallas_call | solution.py:52
  45.9 1.6 %collective-permute-done.15.peer_ref.part_peer_ref = bf16[256,768]{1,0:T(8,128)(2,1)S(1)} collective-permute-done((bf16[256,768]{1,0:T(8,128)(2,1)S(1)}, bf16[256,768]{1,0:T(8,128)(2,1)S(1)}, u32[]{:S(2)}, u32[]{:S(2)}) %collective-permute-start.15) | collective-permute-done | bytes 393248 | tf_op jit(solution)/shard_map/ppermute | solution.py:41
  48.7 21.6 %all_to_all.10 = bf16[16,24,768]{2,1,0:T(8,128)(2,1)S(1)} all-to-all(bf16[16,24,768]{2,1,0:T(8,128)(2,1)S(1)} %bitcast.25), channel_id=1, replica_groups=mesh['ex'=4,'row'=4,'col'=2] {'ex','row'}, dimensions={0} | all-to-all | bytes 1179648 | tf_op jit(solution)/shard_map/all_to_all | solution.py:541
  72.3 5.4 %shard_map.217 = (bf16[384,768]{1,0:T(8,128)(2,1)S(1)}, f32[384,768]{1,0:T(8,128)S(1)}, f32[384,16]{1,0:T(8,128)S(1)}, f32[384,1]{1,0:T(8,128)S(1)}, bf16[384,76...) custom-call(s32[3]{0:T(128)S(1)} %pad_add_fusion.at_ref, ...), custom_call_target="tpu_custom_call" | custom-call | flops 3623878656 | bytes 11429376 | tf_op jit(solution)/shard_map/pallas_call | solution.py:52
  78.6 1.5 collective-permute-start.22
  80.2 1.4 collective-permute-done.20.gate_peer_ref
  83.6 21.5 %all_to_all.11 = bf16[16,24,768]{2,1,0:T(8,128)(2,1)S(1)} all-to-all(bf16[16,24,768]{2,1,0:T(8,128)(2,1)S(1)} %bitcast.28), channel_id=1, replica_groups=mesh['ex'=4,'row'=4,'col'=2] {'ex','row'}, dimensions={0} | all-to-all | bytes 1179648 | tf_op jit(solution)/shard_map/all_to_all | solution.py:587
  107.0 2.7 %shard_map.219 = (bf16[256,384]{1,0:T(8,128)(2,1)}, f32[256,768]{1,0:T(8,128)S(1)}, f32[1,768]{1,0:T(1,128)S(1)}, bf16[256,384]{1,0:T(8,128)(2,1)S(1)}, bf16[192...) custom-call(s32[3]{0:T(128)S(1)} %pad_add_fusion.at_ref, ...), custom_call_target="tpu_custom_call" | custom-call | flops 528482304 | bytes 5020672 | tf_op jit(solution)/shard_map/pallas_call | solution.py:52
  109.7 3.7 %shard_map.220 = (bf16[256,768]{1,0:T(8,128)(2,1)S(1)}, f32[8,512]{1,0:T(8,128)S(1)}, bf16[288,256]{1,0:T(8,128)(2,1)S(1)}, bf16[288,256]{1,0:T(8,128)(2,1)S(1)}...) custom-call(s32[3]{0:T(128)S(1)} %pad_add_fusion.at_ref, bf16[256,384]{1,0:T(8,128)(2,1)S(1)} %get-tuple-element.159.d_ctx_ref, ...), custom_call_target="tpu_custom_call" | custom-call | flops 704643072 | bytes 5128192 | tf_op jit(solution)/shard_map/pallas_call | solution.py:52
  115.3 2.3 %collective-permute-start.29 = (bf16[288,256]{1,0:T(8,128)(2,1)S(1)}, bf16[288,256]{1,0:T(8,128)(2,1)S(1)}, u32[]{:S(2)}, u32[]{:S(2)}) collective-permute-start(bf16[288,256]{1,0:T(8,128)(2,1)S(1)} %get-tuple-element.182), channel_id=1, source_target_pairs={{0,6},{2,4},{4,2},{6,0},{1,7},{3,5},{5,3},{7,1},{8,14},{10,12},{12... | collective-permute-start | bytes 442376 | tf_op jit(solution)/shard_map/ppermute | solution.py:404
  119.1 1.8 %collective-permute-done.27.refs_3_ = bf16[288,256]{1,0:T(8,128)(2,1)S(1)} collective-permute-done((bf16[288,256]{1,0:T(8,128)(2,1)S(1)}, bf16[288,256]{1,0:T(8,128)(2,1)S(1)}, u32[]{:S(2)}, u32[]{:S(2)}) %collective-permute-start.27) | collective-permute-done | bytes 147488 | tf_op jit(solution)/shard_map/ppermute | solution.py:404
  120.8 2.6 %collective-permute-done.28.refs_4_ = bf16[288,256]{1,0:T(8,128)(2,1)S(1)} collective-permute-done((bf16[288,256]{1,0:T(8,128)(2,1)S(1)}, bf16[288,256]{1,0:T(8,128)(2,1)S(1)}, u32[]{:S(2)}, u32[]{:S(2)}) %collective-permute-start.28) | collective-permute-done | bytes 147488 | tf_op jit(solution)/shard_map/ppermute | solution.py:404
  123.5 1.7 %shard_map.222 = (bf16[56,1152]{1,0:T(8,128)(2,1)S(1)}, bf16[56,1152]{1,0:T(8,128)(2,1)S(1)}, bf16[56,1152]{1,0:T(8,128)(2,1)S(1)}, bf16[56,1152]{1,0:T(8,128)(2,1)S(1)}) custom-call(s32[3]{0:T(128)S(1)} %pad_add_fusion.at_ref, bf16[768,256]{1,0:T(8,128)(2,1)S(1)} %get-tuple-element.168.turned_ref, f32[8,768]{1,0:T(8,128)S(1)} %get-tuple-element.169.small_ref, ...), custom_call_target="tpu_custom_call" | custom-call | flops 452984832 | bytes 2752512 | tf_op jit(solution)/shard_map/pallas_call | solution.py:52
  125.9 1.5 collective-permute-start.31
  127.4 2.3 %collective-permute-start.32 = (bf16[56,1152]{1,0:T(8,128)(2,1)S(1)}, bf16[56,1152]{1,0:T(8,128)(2,1)S(1)}, u32[]{:S(2)}, u32[]{:S(2)}) collective-permute-start(bf16[56,1152]{1,0:T(8,128)(2,1)S(1)} %get-tuple-element.186), channel_id=1, source_target_pairs={{0,24},{8,16},{16,8},{24,0},{1,25},{9,17},{17,9},{25,1},{2,26},{10... | collective-permute-start | bytes 387080 | tf_op jit(solution)/shard_map/ppermute | solution.py:404
  129.7 1.7 %collective-permute-done.30.refs_1_ = bf16[56,1152]{1,0:T(8,128)(2,1)S(1)} collective-permute-done((bf16[56,1152]{1,0:T(8,128)(2,1)S(1)}, bf16[56,1152]{1,0:T(8,128)(2,1)S(1)}, u32[]{:S(2)}, u32[]{:S(2)}) %collective-permute-start.30) | collective-permute-done | bytes 129056 | tf_op jit(solution)/shard_map/ppermute | solution.py:404
  131.3 1.4 collective-permute-start.36
  134.8 5.0 %shard_map.223 = (f32[1536,768]{1,0:T(8,128)}, f32[768,1536]{1,0:T(8,128)}) custom-call(bf16[384,768]{1,0:T(8,128)(2,1)S(1)} %get-tuple-element.190.rows_ref, bf16[384,768]{1,0:T(8,128)(2,1)S(1)} %get-tuple-element.191.d_y_ref, bf16[384,1536]{1,0:T(8,128)(2,1)S(1)} %get-tuple-element.192.act_ref, bf16[384,1536]{1,0:T(8,128)(2,1)S(1)} %get-tuple-element.193.d_pre_ref), custom_call_target="tpu_custom_call" | custom-call | flops 1811939328 | bytes 14155776 | tf_op jit(solution)/shard_map/pallas_call | solution.py:591
  140.7 1.5 collective-permute-start.33
  146.9 2.3 %collective-permute-start.41 = (bf16[48,384]{1,0:T(8,128)(2,1)S(1)}, bf16[48,384]{1,0:T(8,128)(2,1)S(1)}, u32[]{:S(2)}, u32[]{:S(2)}) collective-permute-start(bf16[48,384]{1,0:T(8,128)(2,1)S(1)} %get-tuple-element.221), channel_id=1, source_target_pairs={{0,24},{8,16},{16,8},{24,0},{1,25},{9,17},{17,9},{25,1},{2,26},{10... | collective-permute-start | bytes 110600 | tf_op jit(solution)/shard_map/ppermute | solution.py:404
  (113 shorter events, 34.2 us)
Async XLA Ops:
  3.4 11.5 %collective-permute-start = (bf16[48,1664]{1,0:T(8,128)(2,1)S(1)}, bf16[48,1664]{1,0:T(8,128)(2,1)S(1)}, u32[]{:S(2)}, u32[]{:S(2)}) collective-permute-start(bf16[48,1664]{1,0:T(8,128)(2,1)S(1)} %shard_map.213.refs_0_), channel_id=1, source_target_pairs={{0,8},{8,0},{16,24},{24,16},{1,9},{9,1},{17,25},{25,17},{2,10},{10... | collective-permute-start | bytes 479240 | tf_op jit(solution)/shard_map/ppermute | solution.py:404
  6.5 14.8 %collective-permute-start.1 = (bf16[48,1664]{1,0:T(8,128)(2,1)S(1)}, bf16[48,1664]{1,0:T(8,128)(2,1)S(1)}, u32[]{:S(2)}, u32[]{:S(2)}) collective-permute-start(bf16[48,1664]{1,0:T(8,128)(2,1)S(1)} %shard_map.213.refs_0_), channel_id=1, source_target_pairs={{0,16},{8,24},{16,0},{24,8},{1,17},{9,25},{17,1},{25,9},{2,18},{10... | collective-permute-start | bytes 479240 | tf_op jit(solution)/shard_map/ppermute | solution.py:404
  9.1 13.7 %collective-permute-start.2 = (bf16[48,1664]{1,0:T(8,128)(2,1)S(1)}, bf16[48,1664]{1,0:T(8,128)(2,1)S(1)}, u32[]{:S(2)}, u32[]{:S(2)}) collective-permute-start(bf16[48,1664]{1,0:T(8,128)(2,1)S(1)} %shard_map.213.refs_0_), channel_id=1, source_target_pairs={{0,24},{8,16},{16,8},{24,0},{1,25},{9,17},{17,9},{25,1},{2,26},{10... | collective-permute-start | bytes 479240 | tf_op jit(solution)/shard_map/ppermute | solution.py:404
  9.1 15.2 %collective-permute-start.3 = (bf16[48,1664]{1,0:T(8,128)(2,1)S(1)}, bf16[48,1664]{1,0:T(8,128)(2,1)S(1)}, u32[]{:S(2)}, u32[]{:S(2)}) collective-permute-start(bf16[48,1664]{1,0:T(8,128)(2,1)S(1)} %shard_map.213.refs_0_), channel_id=1, source_target_pairs={{0,2},{2,0},{4,6},{6,4},{1,3},{3,1},{5,7},{7,5},{8,10},{10,8},{12,... | collective-permute-start | bytes 479240 | tf_op jit(solution)/shard_map/ppermute | solution.py:404
  10.8 14.0 %collective-permute-start.7 = (bf16[48,1664]{1,0:T(8,128)(2,1)S(1)}, bf16[48,1664]{1,0:T(8,128)(2,1)S(1)}, u32[]{:S(2)}, u32[]{:S(2)}) collective-permute-start(bf16[48,1664]{1,0:T(8,128)(2,1)S(1)} %shard_map.213.refs_0_), channel_id=1, source_target_pairs={{0,4},{2,6},{4,0},{6,2},{1,5},{3,7},{5,1},{7,3},{8,12},{10,14},{12... | collective-permute-start | bytes 479240 | tf_op jit(solution)/shard_map/ppermute | solution.py:404
  15.0 12.8 %collective-permute-start.8 = (bf16[48,1664]{1,0:T(8,128)(2,1)S(1)}, bf16[48,1664]{1,0:T(8,128)(2,1)S(1)}, u32[]{:S(2)}, u32[]{:S(2)}) collective-permute-start(bf16[48,1664]{1,0:T(8,128)(2,1)S(1)} %collective-permute-done.refs_1_), channel_id=1, source_target_pairs={{0,4},{2,6},{4,0},{6,2},{1,5},{3,7},{5,1},{7,3},{8,12},{10,14},{12... | collective-permute-start | bytes 479240 | tf_op jit(solution)/shard_map/ppermute | solution.py:404
  21.3 12.6 %collective-permute-start.4 = (bf16[48,1664]{1,0:T(8,128)(2,1)S(1)}, bf16[48,1664]{1,0:T(8,128)(2,1)S(1)}, u32[]{:S(2)}, u32[]{:S(2)}) collective-permute-start(bf16[48,1664]{1,0:T(8,128)(2,1)S(1)} %collective-permute-done.refs_1_), channel_id=1, source_target_pairs={{0,2},{2,0},{4,6},{6,4},{1,3},{3,1},{5,7},{7,5},{8,10},{10,8},{12,... | collective-permute-start | bytes 479240 | tf_op jit(solution)/shard_map/ppermute | solution.py:404
  22.8 10.1 %collective-permute-start.10 = (bf16[48,1664]{1,0:T(8,128)(2,1)S(1)}, bf16[48,1664]{1,0:T(8,128)(2,1)S(1)}, u32[]{:S(2)}, u32[]{:S(2)}) collective-permute-start(bf16[48,1664]{1,0:T(8,128)(2,1)S(1)} %collective-permute-done.2.refs_3_), channel_id=1, source_target_pairs={{0,4},{2,6},{4,0},{6,2},{1,5},{3,7},{5,1},{7,3},{8,12},{10,14},{12... | collective-permute-start | bytes 479240 | tf_op jit(solution)/shard_map/ppermute | solution.py:404
  24.3 11.6 %collective-permute-start.6 = (bf16[48,1664]{1,0:T(8,128)(2,1)S(1)}, bf16[48,1664]{1,0:T(8,128)(2,1)S(1)}, u32[]{:S(2)}, u32[]{:S(2)}) collective-permute-start(bf16[48,1664]{1,0:T(8,128)(2,1)S(1)} %collective-permute-done.2.refs_3_), channel_id=1, source_target_pairs={{0,2},{2,0},{4,6},{6,4},{1,3},{3,1},{5,7},{7,5},{8,10},{10,8},{12,... | collective-permute-start | bytes 479240 | tf_op jit(solution)/shard_map/ppermute | solution.py:404
  24.9 8.0 %collective-permute-start.5 = (bf16[48,1664]{1,0:T(8,128)(2,1)S(1)}, bf16[48,1664]{1,0:T(8,128)(2,1)S(1)}, u32[]{:S(2)}, u32[]{:S(2)}) collective-permute-start(bf16[48,1664]{1,0:T(8,128)(2,1)S(1)} %collective-permute-done.1.refs_2_), channel_id=1, source_target_pairs={{0,2},{2,0},{4,6},{6,4},{1,3},{3,1},{5,7},{7,5},{8,10},{10,8},{12,... | collective-permute-start | bytes 479240 | tf_op jit(solution)/shard_map/ppermute | solution.py:404
  27.8 9.5 %collective-permute-start.9 = (bf16[48,1664]{1,0:T(8,128)(2,1)S(1)}, bf16[48,1664]{1,0:T(8,128)(2,1)S(1)}, u32[]{:S(2)}, u32[]{:S(2)}) collective-permute-start(bf16[48,1664]{1,0:T(8,128)(2,1)S(1)} %collective-permute-done.1.refs_2_), channel_id=1, source_target_pairs={{0,4},{2,6},{4,0},{6,2},{1,5},{3,7},{5,1},{7,3},{8,12},{10,14},{12... | collective-permute-start | bytes 479240 | tf_op jit(solution)/shard_map/ppermute | solution.py:404
  32.9 5.3 %collective-permute-start.11 = (bf16[48,1664]{1,0:T(8,128)(2,1)S(1)}, bf16[48,1664]{1,0:T(8,128)(2,1)S(1)}, u32[]{:S(2)}, u32[]{:S(2)}) collective-permute-start(bf16[48,1664]{1,0:T(8,128)(2,1)S(1)} %collective-permute-done.3.refs_4_), channel_id=1, source_target_pairs={{0,4},{2,6},{4,0},{6,2},{1,5},{3,7},{5,1},{7,3},{8,12},{10,14},{12... | collective-permute-start | bytes 479240 | tf_op jit(solution)/shard_map/ppermute | solution.py:404
  32.9 5.3 %collective-permute-start.12 = (bf16[48,1664]{1,0:T(8,128)(2,1)S(1)}, bf16[48,1664]{1,0:T(8,128)(2,1)S(1)}, u32[]{:S(2)}, u32[]{:S(2)}) collective-permute-start(bf16[48,1664]{1,0:T(8,128)(2,1)S(1)} %collective-permute-done.8.refs_9_), channel_id=1, source_target_pairs={{0,2},{2,0},{4,6},{6,4},{1,3},{3,1},{5,7},{7,5},{8,10},{10,8},{12,... | collective-permute-start | bytes 479240 | tf_op jit(solution)/shard_map/ppermute | solution.py:404
  33.9 6.0 %collective-permute-start.13 = (bf16[48,1664]{1,0:T(8,128)(2,1)S(1)}, bf16[48,1664]{1,0:T(8,128)(2,1)S(1)}, u32[]{:S(2)}, u32[]{:S(2)}) collective-permute-start(bf16[48,1664]{1,0:T(8,128)(2,1)S(1)} %collective-permute-done.5.refs_6_), channel_id=1, source_target_pairs={{0,4},{2,6},{4,0},{6,2},{1,5},{3,7},{5,1},{7,3},{8,12},{10,14},{12... | collective-permute-start | bytes 479240 | tf_op jit(solution)/shard_map/ppermute | solution.py:404
  36.0 5.3 %collective-permute-start.14 = (bf16[48,1664]{1,0:T(8,128)(2,1)S(1)}, bf16[48,1664]{1,0:T(8,128)(2,1)S(1)}, u32[]{:S(2)}, u32[]{:S(2)}) collective-permute-start(bf16[48,1664]{1,0:T(8,128)(2,1)S(1)} %collective-permute-done.10.refs_11_), channel_id=1, source_target_pairs={{0,2},{2,0},{4,6},{6,4},{1,3},{3,1},{5,7},{7,5},{8,10},{10,8},{12,... | collective-permute-start | bytes 479240 | tf_op jit(solution)/shard_map/ppermute | solution.py:404
  70.3 7.4 %collective-permute-start.17 = (bf16[384,256]{1,0:T(8,128)(2,1)S(1)}, bf16[384,256]{1,0:T(8,128)(2,1)S(1)}, u32[]{:S(2)}, u32[]{:S(2)}) collective-permute-start(bf16[384,256]{1,0:T(8,128)(2,1)S(1)} %get-tuple-element.147), channel_id=1, source_target_pairs={{0,2},{2,0},{4,6},{6,4},{1,3},{3,1},{5,7},{7,5},{8,10},{10,8},{12,... | collective-permute-start | bytes 589832 | tf_op jit(solution)/shard_map/ppermute | solution.py:404
  70.9 7.0 %collective-permute-start.18 = (bf16[384,256]{1,0:T(8,128)(2,1)S(1)}, bf16[384,256]{1,0:T(8,128)(2,1)S(1)}, u32[]{:S(2)}, u32[]{:S(2)}) collective-permute-start(bf16[384,256]{1,0:T(8,128)(2,1)S(1)} %get-tuple-element.147), channel_id=1, source_target_pairs={{0,4},{2,6},{4,0},{6,2},{1,5},{3,7},{5,1},{7,3},{8,12},{10,14},{12... | collective-permute-start | bytes 589832 | tf_op jit(solution)/shard_map/ppermute | solution.py:404
  113.6 9.9 %collective-permute-start.26 = (bf16[1152,256]{1,0:T(8,128)(2,1)S(1)}, bf16[1152,256]{1,0:T(8,128)(2,1)S(1)}, u32[]{:S(2)}, u32[]{:S(2)}) collective-permute-start(bf16[1152,256]{1,0:T(8,128)(2,1)S(1)} %constant_dynamic-update-slice_fusion.refs_0_), channel_id=1, source_target_pairs={{0,1},{1,0},{2,3},{3,2},{4,5},{5,4},{6,7},{7,6},{8,9},{9,8},{10,11... | collective-permute-start | bytes 1769480 | tf_op jit(solution)/shard_map/ppermute | solution.py:41
  114.1 6.7 %collective-permute-start.27 = (bf16[288,256]{1,0:T(8,128)(2,1)S(1)}, bf16[288,256]{1,0:T(8,128)(2,1)S(1)}, u32[]{:S(2)}, u32[]{:S(2)}) collective-permute-start(bf16[288,256]{1,0:T(8,128)(2,1)S(1)} %get-tuple-element.180), channel_id=1, source_target_pairs={{0,2},{2,0},{4,6},{6,4},{1,3},{3,1},{5,7},{7,5},{8,10},{10,8},{12,... | collective-permute-start | bytes 442376 | tf_op jit(solution)/shard_map/ppermute | solution.py:404
  114.7 8.8 %collective-permute-start.28 = (bf16[288,256]{1,0:T(8,128)(2,1)S(1)}, bf16[288,256]{1,0:T(8,128)(2,1)S(1)}, u32[]{:S(2)}, u32[]{:S(2)}) collective-permute-start(bf16[288,256]{1,0:T(8,128)(2,1)S(1)} %get-tuple-element.181), channel_id=1, source_target_pairs={{0,4},{2,6},{4,0},{6,2},{1,5},{3,7},{5,1},{7,3},{8,12},{10,14},{12... | collective-permute-start | bytes 442376 | tf_op jit(solution)/shard_map/ppermute | solution.py:404
  115.3 8.2 %collective-permute-start.29 = (bf16[288,256]{1,0:T(8,128)(2,1)S(1)}, bf16[288,256]{1,0:T(8,128)(2,1)S(1)}, u32[]{:S(2)}, u32[]{:S(2)}) collective-permute-start(bf16[288,256]{1,0:T(8,128)(2,1)S(1)} %get-tuple-element.182), channel_id=1, source_target_pairs={{0,6},{2,4},{4,2},{6,0},{1,7},{3,5},{5,3},{7,1},{8,14},{10,12},{12... | collective-permute-start | bytes 442376 | tf_op jit(solution)/shard_map/ppermute | solution.py:404
  125.2 6.1 %collective-permute-start.30 = (bf16[56,1152]{1,0:T(8,128)(2,1)S(1)}, bf16[56,1152]{1,0:T(8,128)(2,1)S(1)}, u32[]{:S(2)}, u32[]{:S(2)}) collective-permute-start(bf16[56,1152]{1,0:T(8,128)(2,1)S(1)} %get-tuple-element.184), channel_id=1, source_target_pairs={{0,8},{8,0},{16,24},{24,16},{1,9},{9,1},{17,25},{25,17},{2,10},{10... | collective-permute-start | bytes 387080 | tf_op jit(solution)/shard_map/ppermute | solution.py:404
  125.9 13.9 %collective-permute-start.31 = (bf16[56,1152]{1,0:T(8,128)(2,1)S(1)}, bf16[56,1152]{1,0:T(8,128)(2,1)S(1)}, u32[]{:S(2)}, u32[]{:S(2)}) collective-permute-start(bf16[56,1152]{1,0:T(8,128)(2,1)S(1)} %get-tuple-element.185), channel_id=1, source_target_pairs={{0,16},{8,24},{16,0},{24,8},{1,17},{9,25},{17,1},{25,9},{2,18},{10... | collective-permute-start | bytes 387080 | tf_op jit(solution)/shard_map/ppermute | solution.py:404
  127.4 12.4 %collective-permute-start.32 = (bf16[56,1152]{1,0:T(8,128)(2,1)S(1)}, bf16[56,1152]{1,0:T(8,128)(2,1)S(1)}, u32[]{:S(2)}, u32[]{:S(2)}) collective-permute-start(bf16[56,1152]{1,0:T(8,128)(2,1)S(1)} %get-tuple-element.186), channel_id=1, source_target_pairs={{0,24},{8,16},{16,8},{24,0},{1,25},{9,17},{17,9},{25,1},{2,26},{10... | collective-permute-start | bytes 387080 | tf_op jit(solution)/shard_map/ppermute | solution.py:404
  131.3 11.5 %collective-permute-start.36 = (bf16[192,384]{1,0:T(8,128)(2,1)S(1)}, bf16[192,384]{1,0:T(8,128)(2,1)S(1)}, u32[]{:S(2)}, u32[]{:S(2)}) collective-permute-start(bf16[192,384]{1,0:T(8,128)(2,1)S(1)} %get-tuple-element.211), channel_id=1, source_target_pairs={{0,2},{2,0},{4,6},{6,4},{1,3},{3,1},{5,7},{7,5},{8,10},{10,8},{12,... | collective-permute-start | bytes 442376 | tf_op jit(solution)/shard_map/ppermute | solution.py:404
  132.8 11.5 %collective-permute-start.37 = (bf16[192,384]{1,0:T(8,128)(2,1)S(1)}, bf16[192,384]{1,0:T(8,128)(2,1)S(1)}, u32[]{:S(2)}, u32[]{:S(2)}) collective-permute-start(bf16[192,384]{1,0:T(8,128)(2,1)S(1)} %get-tuple-element.212), channel_id=1, source_target_pairs={{0,4},{2,6},{4,0},{6,2},{1,5},{3,7},{5,1},{7,3},{8,12},{10,14},{12... | collective-permute-start | bytes 442376 | tf_op jit(solution)/shard_map/ppermute | solution.py:404
  133.4 10.8 %collective-permute-start.38 = (bf16[192,384]{1,0:T(8,128)(2,1)S(1)}, bf16[192,384]{1,0:T(8,128)(2,1)S(1)}, u32[]{:S(2)}, u32[]{:S(2)}) collective-permute-start(bf16[192,384]{1,0:T(8,128)(2,1)S(1)} %get-tuple-element.213), channel_id=1, source_target_pairs={{0,6},{2,4},{4,2},{6,0},{1,7},{3,5},{5,3},{7,1},{8,14},{10,12},{12... | collective-permute-start | bytes 442376 | tf_op jit(solution)/shard_map/ppermute | solution.py:404
  142.2 7.0 %collective-permute-start.34 = (bf16[48,512]{1,0:T(8,128)(2,1)S(1)}, bf16[48,512]{1,0:T(8,128)(2,1)S(1)}, u32[]{:S(2)}, u32[]{:S(2)}) collective-permute-start(bf16[48,512]{1,0:T(8,128)(2,1)S(1)} %get-tuple-element.201), channel_id=1, source_target_pairs={{0,4},{2,6},{4,0},{6,2},{1,5},{3,7},{5,1},{7,3},{8,12},{10,14},{12... | collective-permute-start | bytes 147464 | tf_op jit(solution)/shard_map/ppermute | solution.py:404
  142.8 6.4 %collective-permute-start.35 = (bf16[48,512]{1,0:T(8,128)(2,1)S(1)}, bf16[48,512]{1,0:T(8,128)(2,1)S(1)}, u32[]{:S(2)}, u32[]{:S(2)}) collective-permute-start(bf16[48,512]{1,0:T(8,128)(2,1)S(1)} %get-tuple-element.202), channel_id=1, source_target_pairs={{0,6},{2,4},{4,2},{6,0},{1,7},{3,5},{5,3},{7,1},{8,14},{10,12},{12... | collective-permute-start | bytes 147464 | tf_op jit(solution)/shard_map/ppermute | solution.py:404
  144.8 7.0 %collective-permute-start.39 = (bf16[48,384]{1,0:T(8,128)(2,1)S(1)}, bf16[48,384]{1,0:T(8,128)(2,1)S(1)}, u32[]{:S(2)}, u32[]{:S(2)}) collective-permute-start(bf16[48,384]{1,0:T(8,128)(2,1)S(1)} %get-tuple-element.219), channel_id=1, source_target_pairs={{0,8},{8,0},{16,24},{24,16},{1,9},{9,1},{17,25},{25,17},{2,10},{10... | collective-permute-start | bytes 110600 | tf_op jit(solution)/shard_map/ppermute | solution.py:404
  145.8 6.0 %collective-permute-start.40 = (bf16[48,384]{1,0:T(8,128)(2,1)S(1)}, bf16[48,384]{1,0:T(8,128)(2,1)S(1)}, u32[]{:S(2)}, u32[]{:S(2)}) collective-permute-start(bf16[48,384]{1,0:T(8,128)(2,1)S(1)} %get-tuple-element.220), channel_id=1, source_target_pairs={{0,16},{8,24},{16,0},{24,8},{1,17},{9,25},{17,1},{25,9},{2,18},{10... | collective-permute-start | bytes 110600 | tf_op jit(solution)/shard_map/ppermute | solution.py:404
  146.9 5.8 %collective-permute-start.41 = (bf16[48,384]{1,0:T(8,128)(2,1)S(1)}, bf16[48,384]{1,0:T(8,128)(2,1)S(1)}, u32[]{:S(2)}, u32[]{:S(2)}) collective-permute-start(bf16[48,384]{1,0:T(8,128)(2,1)S(1)} %get-tuple-element.221), channel_id=1, source_target_pairs={{0,24},{8,16},{16,8},{24,0},{1,25},{9,17},{17,9},{25,1},{2,26},{10... | collective-permute-start | bytes 110600 | tf_op jit(solution)/shard_map/ppermute | solution.py:404
  (23 other events, 240.4 us)

commit v3 on v2

--- a/solution.py
+++ b/solution.py
@@ -122,22 +122,67 @@
     part_ref[...] = dot(ctx_ref[...], out_w_ref[...], 1, 1).astype(bf16)
 
 
+def spare_rows(experts, chunk):
+    dims = (experts * 24, experts * 4)
+    row, column = lax.broadcasted_iota(jnp.int32, dims, 0), lax.broadcasted_iota(jnp.int32, dims, 1)
+    expert = lax.shift_right_logical(row * 2731, 16)
+    inside = row - expert * 24
+    wanted = expert * 4 + (inside - chunk * 4)
+    return ((column == wanted) & (inside >= chunk * 4) & (inside < chunk * 4 + 4)).astype(bf16)
+
+
+def pack_slots(values, packed_ref):
+    if len(packed_ref.shape) == 2:
+        packed_ref[...] = values.astype(bf16)
+        return
+    experts, chunks = packed_ref.shape[0], values.shape[1] // 128
+    values = values.astype(bf16)
+    spare = 0.0
+    for c in range(chunks):
+        chunk = values[:, c * 128 : (c + 1) * 128]
+        for e in range(experts):
+            packed_ref[e, c * 16 : (c + 1) * 16, :] = chunk[e * 16 : (e + 1) * 16]
+        spare = spare + dot(spare_rows(experts, c), chunk[experts * 16 :], 1, 0)
+    for e in range(experts):
+        packed_ref[e, chunks * 16 :, :] = spare[e * 24 : (e + 1) * 24].astype(bf16)
+
+
+def unpack_slots(packed_ref, low, target_ref, spare_ref):
+    experts, chunks = packed_ref.shape[0], target_ref.shape[1] // 128
+    first = (packed_ref.shape[1] - 24) // 16 * 16
+    for e in range(experts):
+        spare_ref[e * 24 : (e + 1) * 24, :] = packed_ref[e, first:, :].astype(f32)
+    spare = spare_ref[...].astype(bf16)
+    for c in range(chunks):
+        lanes = slice(c * 128, (c + 1) * 128)
+        for e in range(experts):
+            rows = slice((low + c) * 16, (low + c + 1) * 16)
+            target_ref[e * 16 : (e + 1) * 16, lanes] = packed_ref[e, rows, :]
+        target_ref[experts * 16 :, lanes] = dot(spare_rows(experts, low + c), spare, 0, 0).astype(bf16)
+
+
 def dispatch(at_ref, x_ref, part_ref, peer_ref, gain_ref, slot_ref, g_ref, send_ref):
     half = g_ref.shape[1]
     x_one = x_ref[...].astype(f32) + (part_ref[...].astype(f32) + peer_ref[...].astype(f32))
     h_two = (x_one * rms_scale(x_one) * gain_ref[...]).astype(bf16)
     mine = jnp.where(at_ref[2] == 0, h_two[:, :half], h_two[:, half:])
-    dims = (send_ref.shape[0], x_ref.shape[0])
+    slots = send_ref.shape[0] * (1 if len(send_ref.shape) == 2 else 20)
+    dims = (slots, x_ref.shape[0])
     place = (lax.broadcasted_iota(jnp.int32, dims, 0) == slot_ref[...]).astype(bf16)
-    send_ref[:, :half] = dot(place, mine, 1, 0).astype(bf16)
-    send_ref[:, half:] = dot(place, g_ref[...], 1, 0).astype(bf16)
+    sent = jnp.concatenate([dot(place, mine, 1, 0), dot(place, g_ref[...], 1, 0)], axis=1)
+    pack_slots(sent, send_ref)
 
 
 def run_expert(
     experts, row_size, at_ref, got_ref, peer_ref, router_ref, up_ref, down_ref,
     cross_ref, mine_ref, probs_ref, gate_part_ref, rows_ref, d_y_ref, act_ref, d_pre_ref, d_in_ref,
+    got_rows_ref, peer_rows_ref, spare_ref,
 ):
-    half = got_ref.shape[1] // 2
+    half = rows_ref.shape[1] // 2
+    if len(got_ref.shape) == 3:
+        unpack_slots(got_ref, 0, got_rows_ref, spare_ref)
+        unpack_slots(peer_ref, 0, peer_rows_ref, spare_ref)
+        got_ref, peer_ref = got_rows_ref, peer_rows_ref
     hidden = up_ref.shape[1]
     first_core = at_ref[2] == 0
     for at, refs in ((0, (got_ref, peer_ref)), (1, (peer_ref, got_ref))):
@@ -193,25 +238,35 @@
     d_logits = (d_gate * gate * (chosen - probs)).astype(bf16)
     router_w = router_ref[...][:, : probs.shape[1]]
     router_mine = jnp.where(at_ref[2] == 0, router_w[:half], router_w[half:])
-    back_ref[:, :half] = (gate * (mine_ref[:, :half] + crossed_ref[:, :half].astype(f32))).astype(bf16)
-    d_in = mine_ref[:, half:] + crossed_ref[:, half:].astype(f32)
-    back_ref[:, half:] = (d_in + dot(d_logits, router_mine, 1, 1)).astype(bf16)
+    y_gated = gate * (mine_ref[:, :half] + crossed_ref[:, :half].astype(f32))
+    d_in = mine_ref[:, half:] + crossed_ref[:, half:].astype(f32) + dot(d_logits, router_mine, 1, 1)
+    pack_slots(jnp.concatenate([y_gated, d_in], axis=1), back_ref)
     grad_router_ref[...] = dot(d_logits, rows_ref[...], 0, 0)
 
 
+def arrive(at_ref, home_ref, slot_ref, x_ref, part_ref, peer_ref, layer_ref, d_h_ref, rows_ref, spare_ref):
+    half = layer_ref.shape[1]
+    if len(home_ref.shape) == 3:
+        unpack_slots(home_ref, 0, rows_ref, spare_ref)
+        home_ref = rows_ref
+    dims = (home_ref.shape[0], x_ref.shape[0])
+    place = (lax.broadcasted_iota(jnp.int32, dims, 0) == slot_ref[...]).astype(bf16)
+    d_h_ref[...] = dot(place, home_ref[:, half:], 0, 0).astype(bf16)
+    y_home = dot(place, home_ref[:, :half], 0, 0)
+    mine = lambda ref: jnp.where(at_ref[2] == 0, ref[:, :half], ref[:, half:]).astype(f32)
+    layer_ref[...] = (mine(x_ref) + (mine(part_ref) + mine(peer_ref)) + y_home).astype(bf16)
+
+
 def come_home(
-    cube, at_ref, home_ref, peer_ref, slot_ref, x_ref, part_ref, part_peer_ref, g_ref, g_peer_ref,
-    gain_ref, out_w_ref, ctx_ref, layer_ref, d_x_ref, gain_grad_ref, d_ctx_ref, *refs,
+    cube, at_ref, mine_ref, peer_ref, x_ref, part_ref, part_peer_ref, g_ref, g_peer_ref,
+    gain_ref, out_w_ref, ctx_ref, d_x_ref, gain_grad_ref, d_ctx_ref, *refs,
 ):
     *piece_refs, grads_ref = refs
-    half = g_ref.shape[1]
     first_core = at_ref[2] == 0
     both = lambda a, b: jnp.concatenate(
         [jnp.where(first_core, a, b), jnp.where(first_core, b, a)], axis=1
     )
-    dims = (home_ref.shape[0], x_ref.shape[0])
-    place = (lax.broadcasted_iota(jnp.int32, dims, 0) == slot_ref[...]).astype(bf16)
-    d_h = both(dot(place, home_ref[:, half:], 0, 0), dot(place, peer_ref[...], 0, 0))
+    d_h = both(mine_ref[...], peer_ref[...]).astype(f32)
     x_one = x_ref[...].astype(f32) + (part_ref[...].astype(f32) + part_peer_ref[...].astype(f32))
     g_full = both(g_ref[...], g_peer_ref[...]).astype(f32)
     scale = rms_scale(x_one)
@@ -231,9 +286,6 @@
         for k in range(4):
             start = pl.multiple_of(((at_ref[0] ^ k) * 4 + (at_ref[1] ^ m)) * rows, 16)
             piece_ref[k * rows : (k + 1) * rows, :] = grads_ref[pl.ds(start, rows), :]
-    y_home = dot(place, home_ref[:, :half], 0, 0)
-    x_mine = jnp.where(first_core, x_one[:, :half], x_one[:, half:])
-    layer_ref[...] = (x_mine + y_home).astype(bf16)
 
 
 def attend_backward(cube, at_ref, d_ctx_ref, qkv_ref, probs_ref, w_ref, d_h_ref, grad_offset_ref, *refs):
@@ -464,14 +516,22 @@
         own_rows = w_qkv.shape[1]
         experts = w_router.shape[1]
         wide = inner + experts_pad(experts)
-        capacity = 5 * seq_len // (4 * experts)
-        slots = -(-capacity // 8) * 8
-        slot_total = experts * slots
         half = d_out.shape[1]
         hidden = w_up.shape[2]
         device_at = jnp.stack([lax.axis_index(axis).astype(jnp.int32) for axis in ("ex", "row", "col")])
         device_at, w_qkv = lax.optimization_barrier((device_at, w_qkv))
         cube = whole_cube(own_rows)
+        capacity = 5 * seq_len // (4 * experts)
+        tight = cube and experts == 16 and capacity == 20 and width == 768
+        slots = capacity if tight else -(-capacity // 8) * 8
+        slot_total = experts * slots
+        packed_slots = (experts, slots * width // 128, 128) if tight else (slot_total, width)
+        exchange = packed_slots if tight else (experts, slots, width)
+        slot_scratch = (
+            pltpu.VMEM((slot_total, width), bf16),
+            pltpu.VMEM((slot_total, width), bf16),
+            pltpu.VMEM((experts * 24, 128), f32),
+        )
         gather_order = GATHER_ORDER if cube else None
 
         (packed,) = vmem_call(
@@ -525,10 +585,14 @@
             scalars=(device_at,),
         )
         attn_peer = swap_cores(attn_part)
-        slot_of = jnp.where(drop_flags == 1, slot_total, expert_ids * slots + slot_ids)[None]
+        slot_of = expert_ids * slots + slot_ids
+        if tight:
+            spare_of = experts * 16 + expert_ids * 4 + slot_ids - 16
+            slot_of = jnp.where(slot_ids < 16, expert_ids * 16 + slot_ids, spare_of)
+        slot_of = jnp.where(drop_flags == 1, slot_total, slot_of)[None]
         (send,) = vmem_call(
             dispatch,
-            (shape((slot_total, width), bf16),),
+            (shape(packed_slots, bf16),),
             2 * seq_len * slot_total * width,
             x_in,
             attn_part,
@@ -538,9 +602,7 @@
             d_out,
             scalars=(device_at,),
         )
-        got = lax.all_to_all(
-            send.reshape(experts, slots, width), ("ex", "row"), 0, 0, tiled=True
-        ).reshape(slot_total, width)
+        got = lax.all_to_all(send.reshape(exchange), ("ex", "row"), 0, 0, tiled=True).reshape(packed_slots)
         if cube:
             later_normed, got = lax.optimization_barrier((normed_mine, got))
             normed_hops = plane_hops([later_normed] * 2)
@@ -563,15 +625,17 @@
             up_w,
             down_w,
             scalars=(device_at,),
-            scratch=(pltpu.VMEM((slot_total, width), f32),),
+            scratch=(pltpu.VMEM((slot_total, width), f32), *slot_scratch),
         )
         if cube:
-            crossing, gate_part, *normed_hops = lax.optimization_barrier((crossing, gate_part, *normed_hops))
+            crossing, gate_part, g_peer, *normed_hops = lax.optimization_barrier(
+                (crossing, gate_part, g_peer, *normed_hops)
+            )
             from_x, from_y = normed_hops
             normed_hops += [hop(from_x[: half // 2], "row", 2), hop(from_y[half // 2 :], "row", 1)]
         back, grad_router = vmem_call(
             functools.partial(settle, n_row),
-            (shape((slot_total, width), bf16), shape((experts, width), f32)),
+            (shape(packed_slots, bf16), shape((experts, width), f32)),
             2 * slot_total * half * experts,
             mine,
             swap_cores(crossing),
@@ -584,9 +648,19 @@
         )
         if cube:
             back, *normed_hops = lax.optimization_barrier((back, *normed_hops))
-        home = lax.all_to_all(
-            back.reshape(experts, slots, width), ("ex", "row"), 0, 0, tiled=True
-        ).reshape(slot_total, width)
+        home = lax.all_to_all(back.reshape(exchange), ("ex", "row"), 0, 0, tiled=True).reshape(packed_slots)
+        layer_out, d_h_mine = vmem_call(
+            arrive,
+            (shape((seq_len, half), bf16), shape((seq_len, half), bf16)),
+            2 * seq_len * slot_total * width,
+            home,
+            slot_of,
+            x_in,
+            attn_part,
+            attn_peer,
+            scalars=(device_at,),
+            scratch=slot_scratch[1:],
+        )
         def grads_of_expert(rows, d_y, act_b, d_pre):
             return pl.pallas_call(
                 expert_grads,
@@ -605,19 +679,17 @@
 
         quarter = (width // 4, 3 * inner // 4) if cube else (width, 3 * inner)
         pieces = 4 if cube else 1
-        layer_out, d_x_one, grad_gain_ffn, d_context, *out_pieces = vmem_call(
+        d_x_one, grad_gain_ffn, d_context, *out_pieces = vmem_call(
             functools.partial(come_home, cube),
             (
-                shape((seq_len, half), bf16),
                 shape((seq_len, width), f32),
                 shape((1, width), f32),
                 shape((seq_len, inner), bf16),
                 *[shape((quarter[0], inner), bf16)] * pieces,
             ),
-            2 * seq_len * (slot_total * 3 * half + 2 * width * inner),
-            home,
-            swap_cores(home[:, half:]),
-            slot_of,
+            4 * seq_len * width * inner,
+            d_h_mine,
+            swap_cores(d_h_mine),
             x_in,
             attn_part,
             attn_peer,

time: 154 us -> 150 us (0.974)
  blocking collectives: 43.1 us -> 37.2 us
  Pallas kernels: 30 us -> 31.8 us
    all_to_all x2, blocking collectives: 43.1 us -> 37.2 us  [the longest x1 18.6 us: per_device(): lax.all_to_all(send.reshape(exchange), ('ex', 'row'), 0, 0, tiled=True)]
    pallas_call x13 -> x14, Pallas kernels: 25 us -> 26.8 us  [vmem_call(): pl.pallas_call(kernel, out_shape=out_shape, in_specs=[pl.BlockSpec(memory...]
  transfers between devices with their start and end apart: 42 -> 42, of which waited for: 17 -> 16; matrix products, arithmetic and copies ran while one was open for 3% -> 3% of each run, Pallas kernels for 10% -> 11%
where the time goes in v3:
time: 150 us
  starting transfers between devices  43.7 us (29%)
  blocking collectives  37.2 us (25%)
  Pallas kernels  31.8 us (21%)
  waiting for transfers between devices  27.9 us (19%)
  other arithmetic  4.94 us (3%)
  local copies, waits for them, and re-layouts  2.65 us (2%)
    ppermute x34, starting transfers between devices, hop(): lax.ppermute(values, axis, [(i, i ^ step) for i in range(mesh.shape[axis])])  42.5 us
    pallas_call x14, Pallas kernels, vmem_call(): pl.pallas_call(kernel, out_shape=out_shape, in_specs=[pl.BlockSpec(memory...  26.8 us
    ppermute x34, waiting for transfers between devices, hop(): lax.ppermute(values, axis, [(i, i ^ step) for i in range(mesh.shape[axis])])  23.5 us
    all_to_all x1, blocking collectives, per_device(): lax.all_to_all(send.reshape(exchange), ('ex', 'row'), 0, 0, tiled=True)  18.6 us
    all_to_all x1, blocking collectives, per_device(): lax.all_to_all(back.reshape(exchange), ('ex', 'row'), 0, 0, tiled=True)  18.6 us
    pallas_call x1, Pallas kernels, grads_of_expert(): pl.pallas_call(expert_grads, out_shape=(shape((hidden, width), f32), shap...  5 us
    ppermute x8, waiting for transfers between devices, swap_cores(): return lax.ppermute(values, 'col', [(0, 1), (1, 0)])  4.49 us
  transfers between devices with their start and end apart: 42, of which 16 were waited for; matrix products, arithmetic and copies ran while one was open for 3% of the time, Pallas kernels for 11%

profile of v3, /device:TPU:0, one launch (start us, length us, event | category | flops | bytes accessed | tf_op | source)
XLA Modules:
  0.0 149.6 jit_solution(4179608176135059887)
XLA Ops:
  3.4 3.0 %collective-permute-start = (bf16[48,1664]{1,0:T(8,128)(2,1)S(1)}, bf16[48,1664]{1,0:T(8,128)(2,1)S(1)}, u32[]{:S(2)}, u32[]{:S(2)}) collective-permute-start(bf16[48,1664]{1,0:T(8,128)(2,1)S(1)} %shard_map.213.refs_0_), channel_id=1, source_target_pairs={{0,8},{8,0},{16,24},{24,16},{1,9},{9,1},{17,25},{25,17},{2,10},{10... | collective-permute-start | bytes 479240 | tf_op jit(solution)/shard_map/ppermute | solution.py:456
  6.5 2.6 %collective-permute-start.1 = (bf16[48,1664]{1,0:T(8,128)(2,1)S(1)}, bf16[48,1664]{1,0:T(8,128)(2,1)S(1)}, u32[]{:S(2)}, u32[]{:S(2)}) collective-permute-start(bf16[48,1664]{1,0:T(8,128)(2,1)S(1)} %shard_map.213.refs_0_), channel_id=1, source_target_pairs={{0,16},{8,24},{16,0},{24,8},{1,17},{9,25},{17,1},{25,9},{2,18},{10... | collective-permute-start | bytes 479240 | tf_op jit(solution)/shard_map/ppermute | solution.py:456
  9.1 1.7 %collective-permute-start.3 = (bf16[48,1664]{1,0:T(8,128)(2,1)S(1)}, bf16[48,1664]{1,0:T(8,128)(2,1)S(1)}, u32[]{:S(2)}, u32[]{:S(2)}) collective-permute-start(bf16[48,1664]{1,0:T(8,128)(2,1)S(1)} %shard_map.213.refs_0_), channel_id=1, source_target_pairs={{0,2},{2,0},{4,6},{6,4},{1,3},{3,1},{5,7},{7,5},{8,10},{10,8},{12,... | collective-permute-start | bytes 479240 | tf_op jit(solution)/shard_map/ppermute | solution.py:456
  10.8 1.5 %collective-permute-start.7 = (bf16[48,1664]{1,0:T(8,128)(2,1)S(1)}, bf16[48,1664]{1,0:T(8,128)(2,1)S(1)}, u32[]{:S(2)}, u32[]{:S(2)}) collective-permute-start(bf16[48,1664]{1,0:T(8,128)(2,1)S(1)} %shard_map.213.refs_0_), channel_id=1, source_target_pairs={{0,4},{2,6},{4,0},{6,2},{1,5},{3,7},{5,1},{7,3},{8,12},{10,14},{12... | collective-permute-start | bytes 479240 | tf_op jit(solution)/shard_map/ppermute | solution.py:456
  12.3 2.6 %convert_bitcast_fusion.down_ref = bf16[1536,768]{1,0:T(8,128)(2,1)S(1)} fusion(f32[1,1536,768]{2,1,0:T(8,128)} %param.22), kind=kLoop, calls=%fused_computation | loop fusion | flops 1179648 | bytes 7077888 | tf_op jit(solution)/shard_map/convert_element_type | solution.py:555
  15.5 5.7 %collective-permute-done.1.refs_2_ = bf16[48,1664]{1,0:T(8,128)(2,1)S(1)} collective-permute-done((bf16[48,1664]{1,0:T(8,128)(2,1)S(1)}, bf16[48,1664]{1,0:T(8,128)(2,1)S(1)}, u32[]{:S(2)}, u32[]{:S(2)}) %collective-permute-start.1) | collective-permute-done | bytes 159776 | tf_op jit(solution)/shard_map/ppermute | solution.py:456
  21.2 1.5 collective-permute-start.4
  22.7 1.5 %collective-permute-start.10 = (bf16[48,1664]{1,0:T(8,128)(2,1)S(1)}, bf16[48,1664]{1,0:T(8,128)(2,1)S(1)}, u32[]{:S(2)}, u32[]{:S(2)}) collective-permute-start(bf16[48,1664]{1,0:T(8,128)(2,1)S(1)} %collective-permute-done.2.refs_3_), channel_id=1, source_target_pairs={{0,4},{2,6},{4,0},{6,2},{1,5},{3,7},{5,1},{7,3},{8,12},{10,14},{12... | collective-permute-start | bytes 479240 | tf_op jit(solution)/shard_map/ppermute | solution.py:456
  24.8 1.5 collective-permute-start.5
  28.2 4.6 %collective-permute-done.5.refs_6_ = bf16[48,1664]{1,0:T(8,128)(2,1)S(1)} collective-permute-done((bf16[48,1664]{1,0:T(8,128)(2,1)S(1)}, bf16[48,1664]{1,0:T(8,128)(2,1)S(1)}, u32[]{:S(2)}, u32[]{:S(2)}) %collective-permute-start.5) | collective-permute-done | bytes 159776 | tf_op jit(solution)/shard_map/ppermute | solution.py:456
  33.9 2.0 %collective-permute-start.13 = (bf16[48,1664]{1,0:T(8,128)(2,1)S(1)}, bf16[48,1664]{1,0:T(8,128)(2,1)S(1)}, u32[]{:S(2)}, u32[]{:S(2)}) collective-permute-start(bf16[48,1664]{1,0:T(8,128)(2,1)S(1)} %collective-permute-done.5.refs_6_), channel_id=1, source_target_pairs={{0,4},{2,6},{4,0},{6,2},{1,5},{3,7},{5,1},{7,3},{8,12},{10,14},{12... | collective-permute-start | bytes 479240 | tf_op jit(solution)/shard_map/ppermute | solution.py:456
  38.1 1.7 %collective-permute-done.13.refs_14_ = bf16[48,1664]{1,0:T(8,128)(2,1)S(1)} collective-permute-done((bf16[48,1664]{1,0:T(8,128)(2,1)S(1)}, bf16[48,1664]{1,0:T(8,128)(2,1)S(1)}, u32[]{:S(2)}, u32[]{:S(2)}) %collective-permute-start.13) | collective-permute-done | bytes 159776 | tf_op jit(solution)/shard_map/ppermute | solution.py:456
  41.2 4.5 %shard_map.215 = (bf16[256,768]{1,0:T(8,128)(2,1)S(1)}, bf16[256,1152]{1,0:T(8,128)(2,1)S(1)}, f32[6,256,256]{2,1,0:T(8,128)S(1)}, bf16[256,384]{1,0:T(8,128)(2,...) custom-call(s32[3]{0:T(128)S(1)} %pad_add_fusion.at_ref, ...), custom_call_target="tpu_custom_call" | custom-call | flops 704643072 | bytes 8273920 | tf_op jit(solution)/shard_map/pallas_call | solution.py:52
  45.9 1.6 %collective-permute-done.15.peer_ref.part_peer_ref = bf16[256,768]{1,0:T(8,128)(2,1)S(1)} collective-permute-done((bf16[256,768]{1,0:T(8,128)(2,1)S(1)}, bf16[256,768]{1,0:T(8,128)(2,1)S(1)}, u32[]{:S(2)}, u32[]{:S(2)}) %collective-permute-start.15) | collective-permute-done | bytes 393248 | tf_op jit(solution)/shard_map/ppermute | solution.py:41
  49.0 18.6 %all_to_all.10.got_ref = bf16[16,120,128]{2,1,0:T(8,128)(2,1)S(1)} all-to-all(bf16[16,120,128]{2,1,0:T(8,128)(2,1)S(1)} %shard_map.216), channel_id=1, replica_groups=mesh['ex'=4,'row'=4,'col'=2] {'ex','row'}, dimensions={0} | all-to-all | bytes 983040 | tf_op jit(solution)/shard_map/all_to_all | solution.py:605
  69.6 5.4 %shard_map.217 = (bf16[320,768]{1,0:T(8,128)(2,1)S(1)}, f32[320,768]{1,0:T(8,128)S(1)}, f32[320,16]{1,0:T(8,128)S(1)}, f32[320,1]{1,0:T(8,128)S(1)}, bf16[320,76...) custom-call(s32[3]{0:T(128)S(1)} %pad_add_fusion.at_ref, ...), custom_call_target="tpu_custom_call" | custom-call | flops 3019898880 | bytes 10343680 | tf_op jit(solution)/shard_map/pallas_call | solution.py:52
  76.3 1.5 %collective-permute-start.23 = (bf16[192,256]{1,0:T(8,128)(2,1)S(1)}, bf16[192,256]{1,0:T(8,128)(2,1)S(1)}, u32[]{:S(2)}, u32[]{:S(2)}) collective-permute-start(bf16[192,256]{1,0:T(8,128)(2,1)S(1)} %slice.7), channel_id=1, source_target_pairs={{0,2},{2,0},{4,6},{6,4},{1,3},{3,1},{5,7},{7,5},{8,10},{10,8},{12,... | collective-permute-start | bytes 294920 | tf_op jit(solution)/shard_map/ppermute | solution.py:456
  81.3 18.6 %all_to_all.11.home_ref = bf16[16,120,128]{2,1,0:T(8,128)(2,1)S(1)} all-to-all(bf16[16,120,128]{2,1,0:T(8,128)(2,1)S(1)} %get-tuple-element.157), channel_id=1, replica_groups=mesh['ex'=4,'row'=4,'col'=2] {'ex','row'}, dimensions={0} | all-to-all | bytes 983040 | tf_op jit(solution)/shard_map/all_to_all | solution.py:651
  99.9 2.1 %shard_map.219 = (bf16[256,384]{1,0:T(8,128)(2,1)}, bf16[256,384]{1,0:T(8,128)(2,1)S(1)}) custom-call(s32[3]{0:T(128)S(1)} %pad_add_fusion.at_ref, bf16[16,120,128]{2,1,0:T(8,128)(2,1)S(1)} %all_to_all.11.home_ref, s32[1,256]{1,0:T(1,128)S(1)} %bitcast.21, bf16[256,768]{1,0:T(8,128)(2,1)S(1)} %copy-done.1, bf16[256,768]{1,0:T(8,128)(2,1)S(1)} %get-tuple-element.141.part_ref, ...), custom_call_target="tpu_custom_call" | custom-call | flops 125829120 | bytes 2065408 | tf_op jit(solution)/shard_map/pallas_call | solution.py:52
  103.5 1.7 %shard_map.220 = (f32[256,768]{1,0:T(8,128)S(1)}, f32[1,768]{1,0:T(1,128)S(1)}, bf16[256,384]{1,0:T(8,128)(2,1)S(1)}, bf16[192,384]{1,0:T(8,128)(2,1)S(1)}, bf16...) custom-call(s32[3]{0:T(128)S(1)} %pad_add_fusion.at_ref, ...), custom_call_target="tpu_custom_call" | custom-call | flops 301989888 | bytes 4331520 | tf_op jit(solution)/shard_map/pallas_call | solution.py:52
  105.2 3.7 %shard_map.221 = (bf16[256,768]{1,0:T(8,128)(2,1)S(1)}, f32[8,512]{1,0:T(8,128)S(1)}, bf16[288,256]{1,0:T(8,128)(2,1)S(1)}, bf16[288,256]{1,0:T(8,128)(2,1)S(1)}...) custom-call(s32[3]{0:T(128)S(1)} %pad_add_fusion.at_ref, bf16[256,384]{1,0:T(8,128)(2,1)S(1)} %get-tuple-element.163.d_ctx_ref, ...), custom_call_target="tpu_custom_call" | custom-call | flops 704643072 | bytes 5128192 | tf_op jit(solution)/shard_map/pallas_call | solution.py:52
  111.1 2.0 %collective-permute-start.29 = (bf16[288,256]{1,0:T(8,128)(2,1)S(1)}, bf16[288,256]{1,0:T(8,128)(2,1)S(1)}, u32[]{:S(2)}, u32[]{:S(2)}) collective-permute-start(bf16[288,256]{1,0:T(8,128)(2,1)S(1)} %get-tuple-element.186), channel_id=1, source_target_pairs={{0,6},{2,4},{4,2},{6,0},{1,7},{3,5},{5,3},{7,1},{8,14},{10,12},{12... | collective-permute-start | bytes 442376 | tf_op jit(solution)/shard_map/ppermute | solution.py:456
  114.6 1.7 %collective-permute-done.27.refs_3_ = bf16[288,256]{1,0:T(8,128)(2,1)S(1)} collective-permute-done((bf16[288,256]{1,0:T(8,128)(2,1)S(1)}, bf16[288,256]{1,0:T(8,128)(2,1)S(1)}, u32[]{:S(2)}, u32[]{:S(2)}) %collective-permute-start.27) | collective-permute-done | bytes 147488 | tf_op jit(solution)/shard_map/ppermute | solution.py:456
  116.5 2.5 %collective-permute-done.29.refs_5_ = bf16[288,256]{1,0:T(8,128)(2,1)S(1)} collective-permute-done((bf16[288,256]{1,0:T(8,128)(2,1)S(1)}, bf16[288,256]{1,0:T(8,128)(2,1)S(1)}, u32[]{:S(2)}, u32[]{:S(2)}) %collective-permute-start.29) | collective-permute-done | bytes 147488 | tf_op jit(solution)/shard_map/ppermute | solution.py:456
  119.0 1.7 %shard_map.223 = (bf16[56,1152]{1,0:T(8,128)(2,1)S(1)}, bf16[56,1152]{1,0:T(8,128)(2,1)S(1)}, bf16[56,1152]{1,0:T(8,128)(2,1)S(1)}, bf16[56,1152]{1,0:T(8,128)(2,1)S(1)}) custom-call(s32[3]{0:T(128)S(1)} %pad_add_fusion.at_ref, bf16[768,256]{1,0:T(8,128)(2,1)S(1)} %get-tuple-element.172.turned_ref, f32[8,768]{1,0:T(8,128)S(1)} %get-tuple-element.173.small_ref, ...), custom_call_target="tpu_custom_call" | custom-call | flops 452984832 | bytes 2752512 | tf_op jit(solution)/shard_map/pallas_call | solution.py:52
  123.4 1.8 %collective-permute-start.32 = (bf16[56,1152]{1,0:T(8,128)(2,1)S(1)}, bf16[56,1152]{1,0:T(8,128)(2,1)S(1)}, u32[]{:S(2)}, u32[]{:S(2)}) collective-permute-start(bf16[56,1152]{1,0:T(8,128)(2,1)S(1)} %get-tuple-element.190), channel_id=1, source_target_pairs={{0,24},{8,16},{16,8},{24,0},{1,25},{9,17},{17,9},{25,1},{2,26},{10... | collective-permute-start | bytes 387080 | tf_op jit(solution)/shard_map/ppermute | solution.py:456
  125.2 1.6 %collective-permute-done.30.refs_1_ = bf16[56,1152]{1,0:T(8,128)(2,1)S(1)} collective-permute-done((bf16[56,1152]{1,0:T(8,128)(2,1)S(1)}, bf16[56,1152]{1,0:T(8,128)(2,1)S(1)}, u32[]{:S(2)}, u32[]{:S(2)}) %collective-permute-start.30) | collective-permute-done | bytes 129056 | tf_op jit(solution)/shard_map/ppermute | solution.py:456
  126.8 1.9 %collective-permute-start.36 = (bf16[192,384]{1,0:T(8,128)(2,1)S(1)}, bf16[192,384]{1,0:T(8,128)(2,1)S(1)}, u32[]{:S(2)}, u32[]{:S(2)}) collective-permute-start(bf16[192,384]{1,0:T(8,128)(2,1)S(1)} %get-tuple-element.215), channel_id=1, source_target_pairs={{0,2},{2,0},{4,6},{6,4},{1,3},{3,1},{5,7},{7,5},{8,10},{10,8},{12,... | collective-permute-start | bytes 442376 | tf_op jit(solution)/shard_map/ppermute | solution.py:456
  130.3 5.0 %shard_map.224 = (f32[1536,768]{1,0:T(8,128)}, f32[768,1536]{1,0:T(8,128)}) custom-call(bf16[320,768]{1,0:T(8,128)(2,1)S(1)} %get-tuple-element.194.rows_ref, bf16[320,768]{1,0:T(8,128)(2,1)S(1)} %get-tuple-element.195.d_y_ref, bf16[320,1536]{1,0:T(8,128)(2,1)S(1)} %get-tuple-element.196.act_ref, bf16[320,1536]{1,0:T(8,128)(2,1)S(1)} %get-tuple-element.197.d_pre_ref), custom_call_target="tpu_custom_call" | custom-call | flops 1509949440 | bytes 14155776 | tf_op jit(solution)/shard_map/pallas_call | solution.py:665
  136.2 1.9 %collective-permute-start.33 = (bf16[48,512]{1,0:T(8,128)(2,1)S(1)}, bf16[48,512]{1,0:T(8,128)(2,1)S(1)}, u32[]{:S(2)}, u32[]{:S(2)}) collective-permute-start(bf16[48,512]{1,0:T(8,128)(2,1)S(1)} %get-tuple-element.204), channel_id=1, source_target_pairs={{0,2},{2,0},{4,6},{6,4},{1,3},{3,1},{5,7},{7,5},{8,10},{10,8},{12,... | collective-permute-start | bytes 147464 | tf_op jit(solution)/shard_map/ppermute | solution.py:456
  140.3 1.6 %collective-permute-start.39 = (bf16[48,384]{1,0:T(8,128)(2,1)S(1)}, bf16[48,384]{1,0:T(8,128)(2,1)S(1)}, u32[]{:S(2)}, u32[]{:S(2)}) collective-permute-start(bf16[48,384]{1,0:T(8,128)(2,1)S(1)} %get-tuple-element.223), channel_id=1, source_target_pairs={{0,8},{8,0},{16,24},{24,16},{1,9},{9,1},{17,25},{25,17},{2,10},{10... | collective-permute-start | bytes 110600 | tf_op jit(solution)/shard_map/ppermute | solution.py:456
  147.3 1.7 %collective-permute-done.41 = bf16[48,384]{1,0:T(8,128)(2,1)S(1)} collective-permute-done((bf16[48,384]{1,0:T(8,128)(2,1)S(1)}, bf16[48,384]{1,0:T(8,128)(2,1)S(1)}, u32[]{:S(2)}, u32[]{:S(2)}) %collective-permute-start.41) | collective-permute-done | bytes 36896 | tf_op jit(solution)/shard_map/ppermute | solution.py:456
  (113 shorter events, 37.3 us)
Async XLA Ops:
  3.4 11.5 %collective-permute-start = (bf16[48,1664]{1,0:T(8,128)(2,1)S(1)}, bf16[48,1664]{1,0:T(8,128)(2,1)S(1)}, u32[]{:S(2)}, u32[]{:S(2)}) collective-permute-start(bf16[48,1664]{1,0:T(8,128)(2,1)S(1)} %shard_map.213.refs_0_), channel_id=1, source_target_pairs={{0,8},{8,0},{16,24},{24,16},{1,9},{9,1},{17,25},{25,17},{2,10},{10... | collective-permute-start | bytes 479240 | tf_op jit(solution)/shard_map/ppermute | solution.py:456
  6.5 14.8 %collective-permute-start.1 = (bf16[48,1664]{1,0:T(8,128)(2,1)S(1)}, bf16[48,1664]{1,0:T(8,128)(2,1)S(1)}, u32[]{:S(2)}, u32[]{:S(2)}) collective-permute-start(bf16[48,1664]{1,0:T(8,128)(2,1)S(1)} %shard_map.213.refs_0_), channel_id=1, source_target_pairs={{0,16},{8,24},{16,0},{24,8},{1,17},{9,25},{17,1},{25,9},{2,18},{10... | collective-permute-start | bytes 479240 | tf_op jit(solution)/shard_map/ppermute | solution.py:456
  9.1 13.7 %collective-permute-start.2 = (bf16[48,1664]{1,0:T(8,128)(2,1)S(1)}, bf16[48,1664]{1,0:T(8,128)(2,1)S(1)}, u32[]{:S(2)}, u32[]{:S(2)}) collective-permute-start(bf16[48,1664]{1,0:T(8,128)(2,1)S(1)} %shard_map.213.refs_0_), channel_id=1, source_target_pairs={{0,24},{8,16},{16,8},{24,0},{1,25},{9,17},{17,9},{25,1},{2,26},{10... | collective-permute-start | bytes 479240 | tf_op jit(solution)/shard_map/ppermute | solution.py:456
  9.1 15.2 %collective-permute-start.3 = (bf16[48,1664]{1,0:T(8,128)(2,1)S(1)}, bf16[48,1664]{1,0:T(8,128)(2,1)S(1)}, u32[]{:S(2)}, u32[]{:S(2)}) collective-permute-start(bf16[48,1664]{1,0:T(8,128)(2,1)S(1)} %shard_map.213.refs_0_), channel_id=1, source_target_pairs={{0,2},{2,0},{4,6},{6,4},{1,3},{3,1},{5,7},{7,5},{8,10},{10,8},{12,... | collective-permute-start | bytes 479240 | tf_op jit(solution)/shard_map/ppermute | solution.py:456
  10.8 14.0 %collective-permute-start.7 = (bf16[48,1664]{1,0:T(8,128)(2,1)S(1)}, bf16[48,1664]{1,0:T(8,128)(2,1)S(1)}, u32[]{:S(2)}, u32[]{:S(2)}) collective-permute-start(bf16[48,1664]{1,0:T(8,128)(2,1)S(1)} %shard_map.213.refs_0_), channel_id=1, source_target_pairs={{0,4},{2,6},{4,0},{6,2},{1,5},{3,7},{5,1},{7,3},{8,12},{10,14},{12... | collective-permute-start | bytes 479240 | tf_op jit(solution)/shard_map/ppermute | solution.py:456
  15.0 12.7 %collective-permute-start.8 = (bf16[48,1664]{1,0:T(8,128)(2,1)S(1)}, bf16[48,1664]{1,0:T(8,128)(2,1)S(1)}, u32[]{:S(2)}, u32[]{:S(2)}) collective-permute-start(bf16[48,1664]{1,0:T(8,128)(2,1)S(1)} %collective-permute-done.refs_1_), channel_id=1, source_target_pairs={{0,4},{2,6},{4,0},{6,2},{1,5},{3,7},{5,1},{7,3},{8,12},{10,14},{12... | collective-permute-start | bytes 479240 | tf_op jit(solution)/shard_map/ppermute | solution.py:456
  21.2 12.6 %collective-permute-start.4 = (bf16[48,1664]{1,0:T(8,128)(2,1)S(1)}, bf16[48,1664]{1,0:T(8,128)(2,1)S(1)}, u32[]{:S(2)}, u32[]{:S(2)}) collective-permute-start(bf16[48,1664]{1,0:T(8,128)(2,1)S(1)} %collective-permute-done.refs_1_), channel_id=1, source_target_pairs={{0,2},{2,0},{4,6},{6,4},{1,3},{3,1},{5,7},{7,5},{8,10},{10,8},{12,... | collective-permute-start | bytes 479240 | tf_op jit(solution)/shard_map/ppermute | solution.py:456
  22.7 10.1 %collective-permute-start.10 = (bf16[48,1664]{1,0:T(8,128)(2,1)S(1)}, bf16[48,1664]{1,0:T(8,128)(2,1)S(1)}, u32[]{:S(2)}, u32[]{:S(2)}) collective-permute-start(bf16[48,1664]{1,0:T(8,128)(2,1)S(1)} %collective-permute-done.2.refs_3_), channel_id=1, source_target_pairs={{0,4},{2,6},{4,0},{6,2},{1,5},{3,7},{5,1},{7,3},{8,12},{10,14},{12... | collective-permute-start | bytes 479240 | tf_op jit(solution)/shard_map/ppermute | solution.py:456
  24.3 11.6 %collective-permute-start.6 = (bf16[48,1664]{1,0:T(8,128)(2,1)S(1)}, bf16[48,1664]{1,0:T(8,128)(2,1)S(1)}, u32[]{:S(2)}, u32[]{:S(2)}) collective-permute-start(bf16[48,1664]{1,0:T(8,128)(2,1)S(1)} %collective-permute-done.2.refs_3_), channel_id=1, source_target_pairs={{0,2},{2,0},{4,6},{6,4},{1,3},{3,1},{5,7},{7,5},{8,10},{10,8},{12,... | collective-permute-start | bytes 479240 | tf_op jit(solution)/shard_map/ppermute | solution.py:456
  24.8 8.0 %collective-permute-start.5 = (bf16[48,1664]{1,0:T(8,128)(2,1)S(1)}, bf16[48,1664]{1,0:T(8,128)(2,1)S(1)}, u32[]{:S(2)}, u32[]{:S(2)}) collective-permute-start(bf16[48,1664]{1,0:T(8,128)(2,1)S(1)} %collective-permute-done.1.refs_2_), channel_id=1, source_target_pairs={{0,2},{2,0},{4,6},{6,4},{1,3},{3,1},{5,7},{7,5},{8,10},{10,8},{12,... | collective-permute-start | bytes 479240 | tf_op jit(solution)/shard_map/ppermute | solution.py:456
  27.6 9.6 %collective-permute-start.9 = (bf16[48,1664]{1,0:T(8,128)(2,1)S(1)}, bf16[48,1664]{1,0:T(8,128)(2,1)S(1)}, u32[]{:S(2)}, u32[]{:S(2)}) collective-permute-start(bf16[48,1664]{1,0:T(8,128)(2,1)S(1)} %collective-permute-done.1.refs_2_), channel_id=1, source_target_pairs={{0,4},{2,6},{4,0},{6,2},{1,5},{3,7},{5,1},{7,3},{8,12},{10,14},{12... | collective-permute-start | bytes 479240 | tf_op jit(solution)/shard_map/ppermute | solution.py:456
  32.8 5.3 %collective-permute-start.12 = (bf16[48,1664]{1,0:T(8,128)(2,1)S(1)}, bf16[48,1664]{1,0:T(8,128)(2,1)S(1)}, u32[]{:S(2)}, u32[]{:S(2)}) collective-permute-start(bf16[48,1664]{1,0:T(8,128)(2,1)S(1)} %collective-permute-done.8.refs_9_), channel_id=1, source_target_pairs={{0,2},{2,0},{4,6},{6,4},{1,3},{3,1},{5,7},{7,5},{8,10},{10,8},{12,... | collective-permute-start | bytes 479240 | tf_op jit(solution)/shard_map/ppermute | solution.py:456
  33.9 6.0 %collective-permute-start.13 = (bf16[48,1664]{1,0:T(8,128)(2,1)S(1)}, bf16[48,1664]{1,0:T(8,128)(2,1)S(1)}, u32[]{:S(2)}, u32[]{:S(2)}) collective-permute-start(bf16[48,1664]{1,0:T(8,128)(2,1)S(1)} %collective-permute-done.5.refs_6_), channel_id=1, source_target_pairs={{0,4},{2,6},{4,0},{6,2},{1,5},{3,7},{5,1},{7,3},{8,12},{10,14},{12... | collective-permute-start | bytes 479240 | tf_op jit(solution)/shard_map/ppermute | solution.py:456
  67.6 7.4 %collective-permute-start.17 = (bf16[256,384]{1,0:T(8,128)(2,1)S(1)}, bf16[256,384]{1,0:T(8,128)(2,1)S(1)}, u32[]{:S(2)}, u32[]{:S(2)}) collective-permute-start(bf16[256,384]{1,0:T(8,128)(2,1)S(1)} %copy-done.2), channel_id=1, source_target_pairs={{0,1},{1,0},{2,3},{3,2},{4,5},{5,4},{6,7},{7,6},{8,9},{9,8},{10,11... | collective-permute-start | bytes 589832 | tf_op jit(solution)/shard_map/ppermute | solution.py:41
  68.1 6.9 %collective-permute-start.18 = (bf16[384,256]{1,0:T(8,128)(2,1)S(1)}, bf16[384,256]{1,0:T(8,128)(2,1)S(1)}, u32[]{:S(2)}, u32[]{:S(2)}) collective-permute-start(bf16[384,256]{1,0:T(8,128)(2,1)S(1)} %get-tuple-element.149), channel_id=1, source_target_pairs={{0,2},{2,0},{4,6},{6,4},{1,3},{3,1},{5,7},{7,5},{8,10},{10,8},{12,... | collective-permute-start | bytes 589832 | tf_op jit(solution)/shard_map/ppermute | solution.py:456
  68.7 6.5 %collective-permute-start.19 = (bf16[384,256]{1,0:T(8,128)(2,1)S(1)}, bf16[384,256]{1,0:T(8,128)(2,1)S(1)}, u32[]{:S(2)}, u32[]{:S(2)}) collective-permute-start(bf16[384,256]{1,0:T(8,128)(2,1)S(1)} %get-tuple-element.149), channel_id=1, source_target_pairs={{0,4},{2,6},{4,0},{6,2},{1,5},{3,7},{5,1},{7,3},{8,12},{10,14},{12... | collective-permute-start | bytes 589832 | tf_op jit(solution)/shard_map/ppermute | solution.py:456
  75.2 5.4 %collective-permute-start.22 = (bf16[192,256]{1,0:T(8,128)(2,1)S(1)}, bf16[192,256]{1,0:T(8,128)(2,1)S(1)}, u32[]{:S(2)}, u32[]{:S(2)}) collective-permute-start(bf16[192,256]{1,0:T(8,128)(2,1)S(1)} %slice.6), channel_id=1, source_target_pairs={{0,4},{2,6},{4,0},{6,2},{1,5},{3,7},{5,1},{7,3},{8,12},{10,14},{12... | collective-permute-start | bytes 294920 | tf_op jit(solution)/shard_map/ppermute | solution.py:456
  109.0 10.0 %collective-permute-start.26 = (bf16[1152,256]{1,0:T(8,128)(2,1)S(1)}, bf16[1152,256]{1,0:T(8,128)(2,1)S(1)}, u32[]{:S(2)}, u32[]{:S(2)}) collective-permute-start(bf16[1152,256]{1,0:T(8,128)(2,1)S(1)} %constant_dynamic-update-slice_fusion.refs_0_), channel_id=1, source_target_pairs={{0,1},{1,0},{2,3},{3,2},{4,5},{5,4},{6,7},{7,6},{8,9},{9,8},{10,11... | collective-permute-start | bytes 1769480 | tf_op jit(solution)/shard_map/ppermute | solution.py:41
  109.6 6.7 %collective-permute-start.27 = (bf16[288,256]{1,0:T(8,128)(2,1)S(1)}, bf16[288,256]{1,0:T(8,128)(2,1)S(1)}, u32[]{:S(2)}, u32[]{:S(2)}) collective-permute-start(bf16[288,256]{1,0:T(8,128)(2,1)S(1)} %get-tuple-element.184), channel_id=1, source_target_pairs={{0,2},{2,0},{4,6},{6,4},{1,3},{3,1},{5,7},{7,5},{8,10},{10,8},{12,... | collective-permute-start | bytes 442376 | tf_op jit(solution)/shard_map/ppermute | solution.py:456
  110.2 6.4 %collective-permute-start.28 = (bf16[288,256]{1,0:T(8,128)(2,1)S(1)}, bf16[288,256]{1,0:T(8,128)(2,1)S(1)}, u32[]{:S(2)}, u32[]{:S(2)}) collective-permute-start(bf16[288,256]{1,0:T(8,128)(2,1)S(1)} %get-tuple-element.185), channel_id=1, source_target_pairs={{0,4},{2,6},{4,0},{6,2},{1,5},{3,7},{5,1},{7,3},{8,12},{10,14},{12... | collective-permute-start | bytes 442376 | tf_op jit(solution)/shard_map/ppermute | solution.py:456
  111.1 7.9 %collective-permute-start.29 = (bf16[288,256]{1,0:T(8,128)(2,1)S(1)}, bf16[288,256]{1,0:T(8,128)(2,1)S(1)}, u32[]{:S(2)}, u32[]{:S(2)}) collective-permute-start(bf16[288,256]{1,0:T(8,128)(2,1)S(1)} %get-tuple-element.186), channel_id=1, source_target_pairs={{0,6},{2,4},{4,2},{6,0},{1,7},{3,5},{5,3},{7,1},{8,14},{10,12},{12... | collective-permute-start | bytes 442376 | tf_op jit(solution)/shard_map/ppermute | solution.py:456
  120.7 6.1 %collective-permute-start.30 = (bf16[56,1152]{1,0:T(8,128)(2,1)S(1)}, bf16[56,1152]{1,0:T(8,128)(2,1)S(1)}, u32[]{:S(2)}, u32[]{:S(2)}) collective-permute-start(bf16[56,1152]{1,0:T(8,128)(2,1)S(1)} %get-tuple-element.188), channel_id=1, source_target_pairs={{0,8},{8,0},{16,24},{24,16},{1,9},{9,1},{17,25},{25,17},{2,10},{10... | collective-permute-start | bytes 387080 | tf_op jit(solution)/shard_map/ppermute | solution.py:456
  122.0 13.3 %collective-permute-start.31 = (bf16[56,1152]{1,0:T(8,128)(2,1)S(1)}, bf16[56,1152]{1,0:T(8,128)(2,1)S(1)}, u32[]{:S(2)}, u32[]{:S(2)}) collective-permute-start(bf16[56,1152]{1,0:T(8,128)(2,1)S(1)} %get-tuple-element.189), channel_id=1, source_target_pairs={{0,16},{8,24},{16,0},{24,8},{1,17},{9,25},{17,1},{25,9},{2,18},{10... | collective-permute-start | bytes 387080 | tf_op jit(solution)/shard_map/ppermute | solution.py:456
  123.4 11.9 %collective-permute-start.32 = (bf16[56,1152]{1,0:T(8,128)(2,1)S(1)}, bf16[56,1152]{1,0:T(8,128)(2,1)S(1)}, u32[]{:S(2)}, u32[]{:S(2)}) collective-permute-start(bf16[56,1152]{1,0:T(8,128)(2,1)S(1)} %get-tuple-element.190), channel_id=1, source_target_pairs={{0,24},{8,16},{16,8},{24,0},{1,25},{9,17},{17,9},{25,1},{2,26},{10... | collective-permute-start | bytes 387080 | tf_op jit(solution)/shard_map/ppermute | solution.py:456
  126.8 11.7 %collective-permute-start.36 = (bf16[192,384]{1,0:T(8,128)(2,1)S(1)}, bf16[192,384]{1,0:T(8,128)(2,1)S(1)}, u32[]{:S(2)}, u32[]{:S(2)}) collective-permute-start(bf16[192,384]{1,0:T(8,128)(2,1)S(1)} %get-tuple-element.215), channel_id=1, source_target_pairs={{0,2},{2,0},{4,6},{6,4},{1,3},{3,1},{5,7},{7,5},{8,10},{10,8},{12,... | collective-permute-start | bytes 442376 | tf_op jit(solution)/shard_map/ppermute | solution.py:456
  128.7 11.0 %collective-permute-start.37 = (bf16[192,384]{1,0:T(8,128)(2,1)S(1)}, bf16[192,384]{1,0:T(8,128)(2,1)S(1)}, u32[]{:S(2)}, u32[]{:S(2)}) collective-permute-start(bf16[192,384]{1,0:T(8,128)(2,1)S(1)} %get-tuple-element.216), channel_id=1, source_target_pairs={{0,4},{2,6},{4,0},{6,2},{1,5},{3,7},{5,1},{7,3},{8,12},{10,14},{12... | collective-permute-start | bytes 442376 | tf_op jit(solution)/shard_map/ppermute | solution.py:456
  129.2 10.6 %collective-permute-start.38 = (bf16[192,384]{1,0:T(8,128)(2,1)S(1)}, bf16[192,384]{1,0:T(8,128)(2,1)S(1)}, u32[]{:S(2)}, u32[]{:S(2)}) collective-permute-start(bf16[192,384]{1,0:T(8,128)(2,1)S(1)} %get-tuple-element.217), channel_id=1, source_target_pairs={{0,6},{2,4},{4,2},{6,0},{1,7},{3,5},{5,3},{7,1},{8,14},{10,12},{12... | collective-permute-start | bytes 442376 | tf_op jit(solution)/shard_map/ppermute | solution.py:456
  138.1 6.6 %collective-permute-start.34 = (bf16[48,512]{1,0:T(8,128)(2,1)S(1)}, bf16[48,512]{1,0:T(8,128)(2,1)S(1)}, u32[]{:S(2)}, u32[]{:S(2)}) collective-permute-start(bf16[48,512]{1,0:T(8,128)(2,1)S(1)} %get-tuple-element.205), channel_id=1, source_target_pairs={{0,4},{2,6},{4,0},{6,2},{1,5},{3,7},{5,1},{7,3},{8,12},{10,14},{12... | collective-permute-start | bytes 147464 | tf_op jit(solution)/shard_map/ppermute | solution.py:456
  138.6 6.1 %collective-permute-start.35 = (bf16[48,512]{1,0:T(8,128)(2,1)S(1)}, bf16[48,512]{1,0:T(8,128)(2,1)S(1)}, u32[]{:S(2)}, u32[]{:S(2)}) collective-permute-start(bf16[48,512]{1,0:T(8,128)(2,1)S(1)} %get-tuple-element.206), channel_id=1, source_target_pairs={{0,6},{2,4},{4,2},{6,0},{1,7},{3,5},{5,3},{7,1},{8,14},{10,12},{12... | collective-permute-start | bytes 147464 | tf_op jit(solution)/shard_map/ppermute | solution.py:456
  140.3 7.0 %collective-permute-start.39 = (bf16[48,384]{1,0:T(8,128)(2,1)S(1)}, bf16[48,384]{1,0:T(8,128)(2,1)S(1)}, u32[]{:S(2)}, u32[]{:S(2)}) collective-permute-start(bf16[48,384]{1,0:T(8,128)(2,1)S(1)} %get-tuple-element.223), channel_id=1, source_target_pairs={{0,8},{8,0},{16,24},{24,16},{1,9},{9,1},{17,25},{25,17},{2,10},{10... | collective-permute-start | bytes 110600 | tf_op jit(solution)/shard_map/ppermute | solution.py:456
  141.9 5.4 %collective-permute-start.40 = (bf16[48,384]{1,0:T(8,128)(2,1)S(1)}, bf16[48,384]{1,0:T(8,128)(2,1)S(1)}, u32[]{:S(2)}, u32[]{:S(2)}) collective-permute-start(bf16[48,384]{1,0:T(8,128)(2,1)S(1)} %get-tuple-element.224), channel_id=1, source_target_pairs={{0,16},{8,24},{16,0},{24,8},{1,17},{9,25},{17,1},{25,9},{2,18},{10... | collective-permute-start | bytes 110600 | tf_op jit(solution)/shard_map/ppermute | solution.py:456
  143.2 5.8 %collective-permute-start.41 = (bf16[48,384]{1,0:T(8,128)(2,1)S(1)}, bf16[48,384]{1,0:T(8,128)(2,1)S(1)}, u32[]{:S(2)}, u32[]{:S(2)}) collective-permute-start(bf16[48,384]{1,0:T(8,128)(2,1)S(1)} %get-tuple-element.225), channel_id=1, source_target_pairs={{0,24},{8,16},{16,8},{24,0},{1,25},{9,17},{17,9},{25,1},{2,26},{10... | collective-permute-start | bytes 110600 | tf_op jit(solution)/shard_map/ppermute | solution.py:456
  (23 other events, 302.1 us)

commit v4 on v3

--- a/solution.py
+++ b/solution.py
@@ -87,16 +87,8 @@
     packed_ref[:, 4 * inner : 4 * inner + experts] = router.astype(bf16)
 
 
-def turn_normed(at_ref, x_ref, gain_ref, turned_ref, mine_ref):
-    x_float = x_ref[...].astype(f32)
-    h_one = (x_float * rms_scale(x_float) * gain_ref[...]).astype(bf16)
-    turned_ref[...] = dot(h_one, eye(h_one.shape[0]), 0, 0).astype(bf16)
-    half = mine_ref.shape[0]
-    mine_ref[...] = jnp.where(at_ref[2] == 0, turned_ref[:half, :], turned_ref[half:, :])
-
-
 def attend_forward(order, at_ref, x_ref, gain_ref, offset_ref, seg_ref, *refs):
-    *block_refs, part_ref, qkv_ref, probs_ref, ctx_ref, w_ref, out_w_ref, router_ref = refs
+    *block_refs, part_ref, qkv_ref, probs_ref, ctx_ref, w_ref, out_w_ref, router_ref, turned_ref, half_ref = refs
     seq_len = x_ref.shape[0]
     heads, inner = probs_ref.shape[0], ctx_ref.shape[1]
     for rows, block_ref in zip(block_rows(at_ref, order, block_refs[0].shape[0]), block_refs):
@@ -104,7 +96,10 @@
         out_w_ref[rows, :] = block_ref[:, 3 * inner : 4 * inner]
         router_ref[rows, :] = block_ref[:, 4 * inner :]
     x_float = x_ref[...].astype(f32)
-    h_one = (x_float * rms_scale(x_float) * gain_ref[...]).astype(bf16)
+    h_one = (x_float * rms_scale(x_float) * gain_ref[...].reshape(1, -1)).astype(bf16)
+    turned_ref[...] = dot(h_one, eye(seq_len), 0, 0).astype(bf16)
+    half = half_ref.shape[0]
+    half_ref[...] = jnp.where(at_ref[2] == 0, turned_ref[:half, :], turned_ref[half:, :])
     documents = lax.broadcasted_iota(jnp.int32, (8, seq_len), 0) == seg_ref[...]
     same_doc = dot(documents.astype(bf16), documents.astype(bf16), 0, 0) > 0.5
     qkv_ref[...] = dot(h_one, w_ref[...], 1, 0).astype(bf16)
@@ -164,7 +159,7 @@
 def dispatch(at_ref, x_ref, part_ref, peer_ref, gain_ref, slot_ref, g_ref, send_ref):
     half = g_ref.shape[1]
     x_one = x_ref[...].astype(f32) + (part_ref[...].astype(f32) + peer_ref[...].astype(f32))
-    h_two = (x_one * rms_scale(x_one) * gain_ref[...]).astype(bf16)
+    h_two = (x_one * rms_scale(x_one) * gain_ref[...].reshape(1, -1)).astype(bf16)
     mine = jnp.where(at_ref[2] == 0, h_two[:, :half], h_two[:, half:])
     slots = send_ref.shape[0] * (1 if len(send_ref.shape) == 2 else 20)
     dims = (slots, x_ref.shape[0])
@@ -217,16 +212,22 @@
         else:
             y_part = y_part + y_more
             d_in_ref[...] += d_more
-    gate_part_ref[...] = jnp.sum(g_rows * y_part, axis=1, keepdims=True)
+    gate_part = jnp.sum(g_rows * y_part, axis=1, keepdims=True)
+    high = gate_part.astype(bf16)
+    low = (gate_part - high.astype(f32)).astype(bf16)
+    gate_part_ref[...] = high.astype(f32) + low.astype(f32)
+    lane = lax.broadcasted_iota(jnp.int32, (rows.shape[0], 128), 1)
+    beside = jnp.where(lane == 0, high.astype(f32), jnp.where(lane == 1, low.astype(f32), 0.0))
+    cross_ref[:, 2 * half :] = beside.astype(bf16)
     d_in = d_in_ref[...]
     mine_ref[:, :half] = jnp.where(first_core, y_part[:, :half], y_part[:, half:])
     mine_ref[:, half:] = jnp.where(first_core, d_in[:, :half], d_in[:, half:])
     cross_ref[:, :half] = jnp.where(first_core, y_part[:, half:], y_part[:, :half]).astype(bf16)
-    cross_ref[:, half:] = jnp.where(first_core, d_in[:, half:], d_in[:, :half]).astype(bf16)
+    cross_ref[:, half : 2 * half] = jnp.where(first_core, d_in[:, half:], d_in[:, :half]).astype(bf16)
 
 
 def settle(
-    row_size, at_ref, mine_ref, crossed_ref, probs_ref, gate_part_ref, gate_peer_ref, router_ref, rows_ref,
+    row_size, at_ref, mine_ref, crossed_ref, probs_ref, gate_part_ref, router_ref, rows_ref,
     back_ref, grad_router_ref,
 ):
     half = mine_ref.shape[1] // 2
@@ -234,12 +235,13 @@
     expert_at = at_ref[0] * row_size + at_ref[1]
     chosen = (lax.broadcasted_iota(jnp.int32, probs.shape, 1) == expert_at).astype(f32)
     gate = jnp.sum(probs * chosen, axis=1, keepdims=True)
-    d_gate = gate_part_ref[...] + gate_peer_ref[...]
+    beside = crossed_ref[:, 2 * half :].astype(f32)
+    d_gate = gate_part_ref[...] + (beside[:, 0:1] + beside[:, 1:2])
     d_logits = (d_gate * gate * (chosen - probs)).astype(bf16)
     router_w = router_ref[...][:, : probs.shape[1]]
     router_mine = jnp.where(at_ref[2] == 0, router_w[:half], router_w[half:])
     y_gated = gate * (mine_ref[:, :half] + crossed_ref[:, :half].astype(f32))
-    d_in = mine_ref[:, half:] + crossed_ref[:, half:].astype(f32) + dot(d_logits, router_mine, 1, 1)
+    d_in = mine_ref[:, half:] + crossed_ref[:, half : 2 * half].astype(f32) + dot(d_logits, router_mine, 1, 1)
     pack_slots(jnp.concatenate([y_gated, d_in], axis=1), back_ref)
     grad_router_ref[...] = dot(d_logits, rows_ref[...], 0, 0)
 
@@ -272,7 +274,7 @@
     scale = rms_scale(x_one)
     normed = x_one * scale
     gain_grad_ref[...] = jnp.sum(d_h * normed, axis=0, keepdims=True)
-    d_norm = d_h * gain_ref[...]
+    d_norm = d_h * gain_ref[...].reshape(1, -1)
     d_x = g_full + scale * (d_norm - normed * jnp.mean(d_norm * normed, axis=-1, keepdims=True))
     d_x_ref[...] = d_x
     d_x_b = d_x.astype(bf16)
@@ -389,8 +391,8 @@
         out_ref[part] = line_ref[:, part * inner : (part + 1) * inner]
     extra = pair_sum([ref.at[:, 384:] for ref in piece_refs])
     for i, gain_ref in enumerate((gain_one_ref, gain_two_ref)):
-        for j in range(gain_ref.shape[1] // 128):
-            gain_ref[:, j * 128 : (j + 1) * 128] = extra[i * 8 + j : i * 8 + j + 1]
+        for j in range(gain_ref.shape[0] // 128):
+            gain_ref[pl.ds(j * 128, 128)] = extra[i * 8 + j]
     rel_ref[...] = extra[16 : 16 + rel_ref.shape[0], : rel_ref.shape[1]]
     router_ref[...] = extra[32 : 32 + router_ref.shape[0], : router_ref.shape[1]]
 
@@ -409,7 +411,7 @@
     x_float = x_ref[...].astype(f32)
     scale = rms_scale(x_float)
     normed = x_float * scale
-    d_norm = d_h * gain_ref[...]
+    d_norm = d_h * gain_ref[...].reshape(1, -1)
     grad_x = d_x_ref[...] + scale * (
         d_norm - normed * jnp.mean(d_norm * normed, axis=-1, keepdims=True)
     )
@@ -458,20 +460,25 @@
     def whole_cube(rows):
         return n_ex == 4 and n_row == 4 and rows == 48
 
-    def gather_blocks(shard):
+    def gather_blocks(shard, meanwhile):
         rows, width = shard.shape
         if whole_cube(rows):
-            line = [shard] + [hop(shard, "ex", k) for k in (1, 2, 3)]
-            xs = [hop(part, "row", 1) for part in line]
-            ys = [hop(part, "row", 2) for part in line]
-            diagonal = [
-                hop(ys[k], "row", 1) if k % 2 else hop(xs[k], "row", 2) for k in range(4)
-            ]
-            return [*line, *xs, *ys, *diagonal]
+            near, far, farther = (hop(shard, "ex", k) for k in (1, 2, 3))
+            x_own, y_own = hop(shard, "row", 1), hop(shard, "row", 2)
+            near, x_own, y_own = lax.optimization_barrier((near, x_own, y_own))
+            xs, ys = [x_own, hop(near, "row", 1)], [y_own, hop(near, "row", 2)]
+            diagonal = [hop(x_own, "row", 2)]
+            beside = meanwhile(near)
+            far, farther, diagonal[0], *beside = lax.optimization_barrier((far, farther, diagonal[0], *beside))
+            for part in (far, farther):
+                xs.append(hop(part, "row", 1))
+                ys.append(hop(part, "row", 2))
+            diagonal += [hop(ys[1], "row", 1), hop(xs[2], "row", 2), hop(ys[3], "row", 1)]
+            return [shard, near, far, farther, *xs, *ys, *diagonal], beside
         part = lax.all_gather(shard, "ex", axis=0)
         part = jnp.broadcast_to(part[None], (n_row, n_ex, rows, width))
         part = lax.all_to_all(part, "row", split_axis=0, concat_axis=0, tiled=True)
-        return [part.transpose(1, 0, 2, 3).reshape(groups * rows, width)]
+        return [part.transpose(1, 0, 2, 3).reshape(groups * rows, width)], meanwhile(shard)
 
     def scatter_groups(grads, rows):
         part = grads.astype(bf16).reshape(n_ex, n_row, rows, -1).transpose(1, 0, 2, 3)
@@ -542,20 +549,12 @@
             w_out.T,
             w_router.T,
         )
-        blocks = gather_blocks(packed)
-        normed_turned, normed_mine = vmem_call(
-            turn_normed,
-            (shape((width, seq_len), bf16), shape((half, seq_len), bf16)),
-            0,
-            x_in,
-            gain_attn[None],
-            scalars=(device_at,),
-        )
-        up_w = w_up[0].astype(bf16)
-        down_w = w_down[0].astype(bf16)
-        *blocks, up_w, down_w, normed_mine, normed_turned = lax.optimization_barrier(
-            (*blocks, up_w, down_w, normed_mine, normed_turned)
-        )
+
+        def round_weights(after):
+            late_up, late_down, _ = lax.optimization_barrier((w_up[0], w_down[0], after))
+            return [late_up.astype(bf16), late_down.astype(bf16)]
+
+        blocks, (up_w, down_w) = gather_blocks(packed, round_weights)
         g_peer = swap_cores(d_out)
 
         span = 2 * seq_len
@@ -565,7 +564,7 @@
         ).astype(f32)
         per_offset = jnp.einsum("bh,ob->ho", rel_bias, offset_hot, precision=highest)
         square = seq_len * seq_len * heads_here * HEAD
-        attn_part, qkv, probs, context, qkv_w, out_w, router_w = vmem_call(
+        attn_part, qkv, probs, context, qkv_w, out_w, router_w, normed_turned, normed_mine = vmem_call(
             functools.partial(attend_forward, gather_order),
             (
                 shape((seq_len, width), bf16),
@@ -575,10 +574,12 @@
                 shape((width, 3 * inner), bf16),
                 shape((width, inner), bf16),
                 shape((width, wide - inner), bf16),
+                shape((width, seq_len), bf16),
+                shape((half, seq_len), bf16),
             ),
             8 * seq_len * width * inner + 4 * square,
             x_in,
-            gain_attn[None],
+            gain_attn,
             per_offset,
             seg_ids,
             *blocks,
@@ -597,7 +598,7 @@
             x_in,
             attn_part,
             attn_peer,
-            gain_ffn[None],
+            gain_ffn,
             slot_of,
             d_out,
             scalars=(device_at,),
@@ -609,7 +610,7 @@
         crossing, mine, router_probs, gate_part, rows, d_y, act_b, d_pre = vmem_call(
             functools.partial(run_expert, experts, n_row),
             (
-                shape((slot_total, width), bf16),
+                shape((slot_total, width + 128), bf16),
                 shape((slot_total, width), f32),
                 shape((slot_total, experts), f32),
                 shape((slot_total, 1), f32),
@@ -628,11 +629,7 @@
             scratch=(pltpu.VMEM((slot_total, width), f32), *slot_scratch),
         )
         if cube:
-            crossing, gate_part, g_peer, *normed_hops = lax.optimization_barrier(
-                (crossing, gate_part, g_peer, *normed_hops)
-            )
-            from_x, from_y = normed_hops
-            normed_hops += [hop(from_x[: half // 2], "row", 2), hop(from_y[half // 2 :], "row", 1)]
+            crossing, g_peer, *normed_hops = lax.optimization_barrier((crossing, g_peer, *normed_hops))
         back, grad_router = vmem_call(
             functools.partial(settle, n_row),
             (shape(packed_slots, bf16), shape((experts, width), f32)),
@@ -641,13 +638,10 @@
             swap_cores(crossing),
             router_probs,
             gate_part,
-            swap_cores(gate_part),
             router_w,
             rows,
             scalars=(device_at,),
         )
-        if cube:
-            back, *normed_hops = lax.optimization_barrier((back, *normed_hops))
         home = lax.all_to_all(back.reshape(exchange), ("ex", "row"), 0, 0, tiled=True).reshape(packed_slots)
         layer_out, d_h_mine = vmem_call(
             arrive,
@@ -679,6 +673,9 @@
 
         quarter = (width // 4, 3 * inner // 4) if cube else (width, 3 * inner)
         pieces = 4 if cube else 1
+        if cube:
+            d_h_mine, from_x, from_y = lax.optimization_barrier((d_h_mine, *normed_hops))
+            normed_hops += [hop(from_x[: half // 2], "row", 2), hop(from_y[half // 2 :], "row", 1)]
         d_x_one, grad_gain_ffn, d_context, *out_pieces = vmem_call(
             functools.partial(come_home, cube),
             (
@@ -695,7 +692,7 @@
             attn_peer,
             d_out,
             g_peer,
-            gain_ffn[None],
+            gain_ffn,
             out_w,
             context,
             scalars=(device_at,),
@@ -724,7 +721,7 @@
             swap_cores(d_h_part),
             x_in,
             d_x_one,
-            gain_attn[None],
+            gain_attn,
             grad_gain_ffn,
             grad_offset,
             offset_hot,
@@ -765,8 +762,8 @@
                 join_plane,
                 (
                     shape((3, own_rows, inner), f32),
-                    shape((1, width), f32),
-                    shape((1, width), f32),
+                    shape((width,), f32),
+                    shape((width,), f32),
                     shape((heads_here, BUCKETS), f32),
                     shape((experts, own_rows), f32),
                 ),
@@ -801,11 +798,11 @@
         return (
             layer_out,
             grad_x,
-            gain_one.reshape(width),
+            gain_one,
             grad_qkv,
             grad_rel.T,
             grad_out.T,
-            gain_two.reshape(width),
+            gain_two,
             grad_router.T,
             grad_up[None],
             grad_down[None],

time: 150 us -> 147 us (0.980)
  blocking collectives: 37.2 us -> 40.5 us
  waiting for transfers between devices: 27.9 us -> 26 us
  starting transfers between devices: 43.7 us -> 42 us
    all_to_all x1, blocking collectives: 18.6 us -> 21.2 us  [per_device(): lax.all_to_all(send.reshape(exchange), ('ex', 'row'), 0, 0, tiled=True)]
    ppermute x34, starting transfers between devices: 42.5 us -> 40.9 us  [hop(): lax.ppermute(values, axis, [(i, i ^ step) for i in range(mesh.shape[axis])])]
    pallas_call x14 -> x13, Pallas kernels: 26.8 us -> 25.9 us  [vmem_call(): pl.pallas_call(kernel, out_shape=out_shape, in_specs=[pl.BlockSpec(memory...]
    ppermute x8 -> x7, waiting for transfers between devices: 4.49 us -> 3.66 us  [swap_cores(): return lax.ppermute(values, 'col', [(0, 1), (1, 0)])]
  transfers between devices with their start and end apart: 42 -> 41, of which waited for: 16 -> 16; matrix products, arithmetic and copies ran while one was open for 3% -> 2% of each run, Pallas kernels for 11% -> 13%
where the time goes in v4:
time: 147 us
  starting transfers between devices  42 us (29%)
  blocking collectives  40.5 us (28%)
  Pallas kernels  30.9 us (21%)
  waiting for transfers between devices  26 us (18%)
  other arithmetic  3.73 us (3%)
  local copies, waits for them, and re-layouts  2.64 us (2%)
    ppermute x34, starting transfers between devices, hop(): lax.ppermute(values, axis, [(i, i ^ step) for i in range(mesh.shape[axis])])  40.9 us
    pallas_call x13, Pallas kernels, vmem_call(): pl.pallas_call(kernel, out_shape=out_shape, in_specs=[pl.BlockSpec(memory...  25.9 us
    ppermute x34, waiting for transfers between devices, hop(): lax.ppermute(values, axis, [(i, i ^ step) for i in range(mesh.shape[axis])])  22.3 us
    all_to_all x1, blocking collectives, per_device(): lax.all_to_all(send.reshape(exchange), ('ex', 'row'), 0, 0, tiled=True)  21.2 us
    all_to_all x1, blocking collectives, per_device(): lax.all_to_all(back.reshape(exchange), ('ex', 'row'), 0, 0, tiled=True)  19.3 us
    pallas_call x1, Pallas kernels, grads_of_expert(): pl.pallas_call(expert_grads, out_shape=(shape((hidden, width), f32), shap...  5 us
    ppermute x7, waiting for transfers between devices, swap_cores(): return lax.ppermute(values, 'col', [(0, 1), (1, 0)])  3.66 us
  transfers between devices with their start and end apart: 41, of which 16 were waited for; matrix products, arithmetic and copies ran while one was open for 2% of the time, Pallas kernels for 13%

profile of v4, /device:TPU:0, one launch (start us, length us, event | category | flops | bytes accessed | tf_op | source)
XLA Modules:
  0.0 147.0 jit_solution(12284737096511885839)
XLA Ops:
  3.4 3.0 %collective-permute-start = (bf16[48,1664]{1,0:T(8,128)(2,1)S(1)}, bf16[48,1664]{1,0:T(8,128)(2,1)S(1)}, u32[]{:S(2)}, u32[]{:S(2)}) collective-permute-start(bf16[48,1664]{1,0:T(8,128)(2,1)S(1)} %shard_map.213.refs_0_), channel_id=1, source_target_pairs={{0,8},{8,0},{16,24},{24,16},{1,9},{9,1},{17,25},{25,17},{2,10},{10... | collective-permute-start | bytes 479240 | tf_op jit(solution)/shard_map/ppermute | solution.py:458
  6.5 1.5 %collective-permute-start.1 = (bf16[48,1664]{1,0:T(8,128)(2,1)S(1)}, bf16[48,1664]{1,0:T(8,128)(2,1)S(1)}, u32[]{:S(2)}, u32[]{:S(2)}) collective-permute-start(bf16[48,1664]{1,0:T(8,128)(2,1)S(1)} %shard_map.213.refs_0_), channel_id=1, source_target_pairs={{0,2},{2,0},{4,6},{6,4},{1,3},{3,1},{5,7},{7,5},{8,10},{10,8},{12,... | collective-permute-start | bytes 479240 | tf_op jit(solution)/shard_map/ppermute | solution.py:458
  8.0 1.5 %collective-permute-start.2 = (bf16[48,1664]{1,0:T(8,128)(2,1)S(1)}, bf16[48,1664]{1,0:T(8,128)(2,1)S(1)}, u32[]{:S(2)}, u32[]{:S(2)}) collective-permute-start(bf16[48,1664]{1,0:T(8,128)(2,1)S(1)} %shard_map.213.refs_0_), channel_id=1, source_target_pairs={{0,4},{2,6},{4,0},{6,2},{1,5},{3,7},{5,1},{7,3},{8,12},{10,14},{12... | collective-permute-start | bytes 479240 | tf_op jit(solution)/shard_map/ppermute | solution.py:458
  9.5 2.6 %collective-permute-start.3 = (bf16[48,1664]{1,0:T(8,128)(2,1)S(1)}, bf16[48,1664]{1,0:T(8,128)(2,1)S(1)}, u32[]{:S(2)}, u32[]{:S(2)}) collective-permute-start(bf16[48,1664]{1,0:T(8,128)(2,1)S(1)} %shard_map.213.refs_0_), channel_id=1, source_target_pairs={{0,16},{8,24},{16,0},{24,8},{1,17},{9,25},{17,1},{25,9},{2,18},{10... | collective-permute-start | bytes 479240 | tf_op jit(solution)/shard_map/ppermute | solution.py:458
  13.2 1.5 %collective-permute-start.5 = (bf16[48,1664]{1,0:T(8,128)(2,1)S(1)}, bf16[48,1664]{1,0:T(8,128)(2,1)S(1)}, u32[]{:S(2)}, u32[]{:S(2)}) collective-permute-start(bf16[48,1664]{1,0:T(8,128)(2,1)S(1)} %collective-permute-done.1.refs_4_), channel_id=1, source_target_pairs={{0,4},{2,6},{4,0},{6,2},{1,5},{3,7},{5,1},{7,3},{8,12},{10,14},{12... | collective-permute-start | bytes 479240 | tf_op jit(solution)/shard_map/ppermute | solution.py:458
  15.8 2.6 %convert_element_type.91.up_ref = bf16[768,1536]{1,0:T(8,128)(2,1)S(1)} convert(f32[768,1536]{1,0:T(8,128)} %bitcast.21) | non-fusion elementwise | flops 1179648 | bytes 7077888 | tf_op jit(solution)/shard_map/convert_element_type | solution.py:555
  18.8 4.4 %collective-permute-done.3.refs_2_ = bf16[48,1664]{1,0:T(8,128)(2,1)S(1)} collective-permute-done((bf16[48,1664]{1,0:T(8,128)(2,1)S(1)}, bf16[48,1664]{1,0:T(8,128)(2,1)S(1)}, u32[]{:S(2)}, u32[]{:S(2)}) %collective-permute-start.3) | collective-permute-done | bytes 159776 | tf_op jit(solution)/shard_map/ppermute | solution.py:458
  28.3 2.0 %collective-permute-done.7.refs_6_ = bf16[48,1664]{1,0:T(8,128)(2,1)S(1)} collective-permute-done((bf16[48,1664]{1,0:T(8,128)(2,1)S(1)}, bf16[48,1664]{1,0:T(8,128)(2,1)S(1)}, u32[]{:S(2)}, u32[]{:S(2)}) %collective-permute-start.7) | collective-permute-done | bytes 159776 | tf_op jit(solution)/shard_map/ppermute | solution.py:458
  33.7 2.2 %collective-permute-done.12.refs_13_ = bf16[48,1664]{1,0:T(8,128)(2,1)S(1)} collective-permute-done((bf16[48,1664]{1,0:T(8,128)(2,1)S(1)}, bf16[48,1664]{1,0:T(8,128)(2,1)S(1)}, u32[]{:S(2)}, u32[]{:S(2)}) %collective-permute-start.12) | collective-permute-done | bytes 159776 | tf_op jit(solution)/shard_map/ppermute | solution.py:458
  35.9 1.7 %collective-permute-done.14.refs_15_ = bf16[48,1664]{1,0:T(8,128)(2,1)S(1)} collective-permute-done((bf16[48,1664]{1,0:T(8,128)(2,1)S(1)}, bf16[48,1664]{1,0:T(8,128)(2,1)S(1)}, u32[]{:S(2)}, u32[]{:S(2)}) %collective-permute-start.14) | collective-permute-done | bytes 159776 | tf_op jit(solution)/shard_map/ppermute | solution.py:458
  37.6 4.5 %shard_map.214 = (bf16[256,768]{1,0:T(8,128)(2,1)S(1)}, bf16[256,1152]{1,0:T(8,128)(2,1)S(1)}, f32[6,256,256]{2,1,0:T(8,128)S(1)}, bf16[256,384]{1,0:T(8,128)(2,...) custom-call(s32[3]{0:T(128)S(1)} %pad_add_fusion.at_ref, ...), custom_call_target="tpu_custom_call" | custom-call | flops 704643072 | bytes 8863744 | tf_op jit(solution)/shard_map/pallas_call | solution.py:52
  42.2 1.7 %collective-permute-done.15.peer_ref.part_peer_ref = bf16[256,768]{1,0:T(8,128)(2,1)S(1)} collective-permute-done((bf16[256,768]{1,0:T(8,128)(2,1)S(1)}, bf16[256,768]{1,0:T(8,128)(2,1)S(1)}, u32[]{:S(2)}, u32[]{:S(2)}) %collective-permute-start.15) | collective-permute-done | bytes 393248 | tf_op jit(solution)/shard_map/ppermute | solution.py:41
  45.3 21.2 %all_to_all.10.got_ref = bf16[16,120,128]{2,1,0:T(8,128)(2,1)S(1)} all-to-all(bf16[16,120,128]{2,1,0:T(8,128)(2,1)S(1)} %shard_map.215), channel_id=1, replica_groups=mesh['ex'=4,'row'=4,'col'=2] {'ex','row'}, dimensions={0} | all-to-all | bytes 983040 | tf_op jit(solution)/shard_map/all_to_all | solution.py:606
  68.5 5.3 %shard_map.216 = (bf16[320,896]{1,0:T(8,128)(2,1)S(1)}, f32[320,768]{1,0:T(8,128)S(1)}, f32[320,16]{1,0:T(8,128)S(1)}, f32[320,1]{1,0:T(8,128)S(1)}, bf16[320,76...) custom-call(s32[3]{0:T(128)S(1)} %pad_add_fusion.at_ref, ...), custom_call_target="tpu_custom_call" | custom-call | flops 3019898880 | bytes 10425600 | tf_op jit(solution)/shard_map/pallas_call | solution.py:52
  74.1 2.0 %collective-permute-done.20.crossed_ref = bf16[320,896]{1,0:T(8,128)(2,1)S(1)} collective-permute-done((bf16[320,896]{1,0:T(8,128)(2,1)S(1)}, bf16[320,896]{1,0:T(8,128)(2,1)S(1)}, u32[]{:S(2)}, u32[]{:S(2)}) %collective-permute-start.20) | collective-permute-done | bytes 573472 | tf_op jit(solution)/shard_map/ppermute | solution.py:41
  76.1 1.5 %shard_map.217 = (bf16[16,120,128]{2,1,0:T(8,128)(2,1)S(1)}, f32[16,768]{1,0:T(8,128)S(1)}) custom-call(s32[3]{0:T(128)S(1)} %pad_add_fusion.at_ref, f32[320,768]{1,0:T(8,128)S(1)} %get-tuple-element.123.mine_ref, bf16[320,896]{1,0:T(8,128)(2,1)S(1)} %collective-permute-done.20.crossed_ref, f32[320,16]{1,0:T(8,128)S(1)} %get-tuple-element.127.probs_ref, ...), custom_call_target="tpu_custom_call" | custom-call | flops 3932160 | bytes 2807040 | tf_op jit(solution)/shard_map/pallas_call | solution.py:52
  77.6 19.3 %all_to_all.11.home_ref = bf16[16,120,128]{2,1,0:T(8,128)(2,1)S(1)} all-to-all(bf16[16,120,128]{2,1,0:T(8,128)(2,1)S(1)} %get-tuple-element.130), channel_id=1, replica_groups=mesh['ex'=4,'row'=4,'col'=2] {'ex','row'}, dimensions={0} | all-to-all | bytes 983040 | tf_op jit(solution)/shard_map/all_to_all | solution.py:645
  96.9 2.1 %shard_map.218 = (bf16[256,384]{1,0:T(8,128)(2,1)}, bf16[256,384]{1,0:T(8,128)(2,1)S(1)}) custom-call(s32[3]{0:T(128)S(1)} %pad_add_fusion.at_ref, bf16[16,120,128]{2,1,0:T(8,128)(2,1)S(1)} %all_to_all.11.home_ref, s32[1,256]{1,0:T(1,128)S(1)} %bitcast.19, bf16[256,768]{1,0:T(8,128)(2,1)S(1)} %copy-done.1, bf16[256,768]{1,0:T(8,128)(2,1)S(1)} %get-tuple-element.118.part_ref, ...), custom_call_target="tpu_custom_call" | custom-call | flops 125829120 | bytes 2065408 | tf_op jit(solution)/shard_map/pallas_call | solution.py:52
  100.7 1.7 %shard_map.219 = (f32[256,768]{1,0:T(8,128)S(1)}, f32[1,768]{1,0:T(1,128)S(1)}, bf16[256,384]{1,0:T(8,128)(2,1)S(1)}, bf16[192,384]{1,0:T(8,128)(2,1)S(1)}, bf16...) custom-call(s32[3]{0:T(128)S(1)} %pad_add_fusion.at_ref, ...), custom_call_target="tpu_custom_call" | custom-call | flops 301989888 | bytes 4331520 | tf_op jit(solution)/shard_map/pallas_call | solution.py:52
  102.4 3.8 %shard_map.220 = (bf16[256,768]{1,0:T(8,128)(2,1)S(1)}, f32[8,512]{1,0:T(8,128)S(1)}, bf16[288,256]{1,0:T(8,128)(2,1)S(1)}, bf16[288,256]{1,0:T(8,128)(2,1)S(1)}...) custom-call(s32[3]{0:T(128)S(1)} %pad_add_fusion.at_ref, bf16[256,384]{1,0:T(8,128)(2,1)S(1)} %get-tuple-element.139.d_ctx_ref, ...), custom_call_target="tpu_custom_call" | custom-call | flops 704643072 | bytes 5128192 | tf_op jit(solution)/shard_map/pallas_call | solution.py:52
  106.8 1.5 collective-permute-start.26
  111.8 1.6 %collective-permute-done.26.refs_3_ = bf16[288,256]{1,0:T(8,128)(2,1)S(1)} collective-permute-done((bf16[288,256]{1,0:T(8,128)(2,1)S(1)}, bf16[288,256]{1,0:T(8,128)(2,1)S(1)}, u32[]{:S(2)}, u32[]{:S(2)}) %collective-permute-start.26) | collective-permute-done | bytes 147488 | tf_op jit(solution)/shard_map/ppermute | solution.py:458
  113.4 3.6 %collective-permute-done.27.refs_4_ = bf16[288,256]{1,0:T(8,128)(2,1)S(1)} collective-permute-done((bf16[288,256]{1,0:T(8,128)(2,1)S(1)}, bf16[288,256]{1,0:T(8,128)(2,1)S(1)}, u32[]{:S(2)}, u32[]{:S(2)}) %collective-permute-start.27) | collective-permute-done | bytes 147488 | tf_op jit(solution)/shard_map/ppermute | solution.py:458
  117.0 1.7 %shard_map.222 = (bf16[56,1152]{1,0:T(8,128)(2,1)S(1)}, bf16[56,1152]{1,0:T(8,128)(2,1)S(1)}, bf16[56,1152]{1,0:T(8,128)(2,1)S(1)}, bf16[56,1152]{1,0:T(8,128)(2,1)S(1)}) custom-call(s32[3]{0:T(128)S(1)} %pad_add_fusion.at_ref, bf16[768,256]{1,0:T(8,128)(2,1)S(1)} %get-tuple-element.148.turned_ref, f32[8,768]{1,0:T(8,128)S(1)} %get-tuple-element.149.small_ref, ...), custom_call_target="tpu_custom_call" | custom-call | flops 452984832 | bytes 2752512 | tf_op jit(solution)/shard_map/pallas_call | solution.py:52
  120.0 1.5 collective-permute-start.30
  121.5 1.7 %collective-permute-start.31 = (bf16[56,1152]{1,0:T(8,128)(2,1)S(1)}, bf16[56,1152]{1,0:T(8,128)(2,1)S(1)}, u32[]{:S(2)}, u32[]{:S(2)}) collective-permute-start(bf16[56,1152]{1,0:T(8,128)(2,1)S(1)} %get-tuple-element.164), channel_id=1, source_target_pairs={{0,24},{8,16},{16,8},{24,0},{1,25},{9,17},{17,9},{25,1},{2,26},{10... | collective-permute-start | bytes 387080 | tf_op jit(solution)/shard_map/ppermute | solution.py:458
  123.2 1.5 %collective-permute-done.29.refs_1_ = bf16[56,1152]{1,0:T(8,128)(2,1)S(1)} collective-permute-done((bf16[56,1152]{1,0:T(8,128)(2,1)S(1)}, bf16[56,1152]{1,0:T(8,128)(2,1)S(1)}, u32[]{:S(2)}, u32[]{:S(2)}) %collective-permute-start.29) | collective-permute-done | bytes 129056 | tf_op jit(solution)/shard_map/ppermute | solution.py:458
  126.5 1.7 %collective-permute-start.37 = (bf16[192,384]{1,0:T(8,128)(2,1)S(1)}, bf16[192,384]{1,0:T(8,128)(2,1)S(1)}, u32[]{:S(2)}, u32[]{:S(2)}) collective-permute-start(bf16[192,384]{1,0:T(8,128)(2,1)S(1)} %get-tuple-element.191), channel_id=1, source_target_pairs={{0,6},{2,4},{4,2},{6,0},{1,7},{3,5},{5,3},{7,1},{8,14},{10,12},{12... | collective-permute-start | bytes 442376 | tf_op jit(solution)/shard_map/ppermute | solution.py:458
  128.2 5.0 %shard_map.223 = (f32[1536,768]{1,0:T(8,128)}, f32[768,1536]{1,0:T(8,128)}) custom-call(bf16[320,768]{1,0:T(8,128)(2,1)S(1)} %get-tuple-element.168.rows_ref, bf16[320,768]{1,0:T(8,128)(2,1)S(1)} %get-tuple-element.169.d_y_ref, bf16[320,1536]{1,0:T(8,128)(2,1)S(1)} %get-tuple-element.170.act_ref, bf16[320,1536]{1,0:T(8,128)(2,1)S(1)} %get-tuple-element.171.d_pre_ref), custom_call_target="tpu_custom_call" | custom-call | flops 1509949440 | bytes 14155776 | tf_op jit(solution)/shard_map/pallas_call | solution.py:659
  136.0 1.7 %collective-permute-start.34 = (bf16[48,512]{1,0:T(8,128)(2,1)S(1)}, bf16[48,512]{1,0:T(8,128)(2,1)S(1)}, u32[]{:S(2)}, u32[]{:S(2)}) collective-permute-start(bf16[48,512]{1,0:T(8,128)(2,1)S(1)} %get-tuple-element.180), channel_id=1, source_target_pairs={{0,6},{2,4},{4,2},{6,0},{1,7},{3,5},{5,3},{7,1},{8,14},{10,12},{12... | collective-permute-start | bytes 147464 | tf_op jit(solution)/shard_map/ppermute | solution.py:458
  138.2 1.7 %collective-permute-start.38 = (bf16[48,384]{1,0:T(8,128)(2,1)S(1)}, bf16[48,384]{1,0:T(8,128)(2,1)S(1)}, u32[]{:S(2)}, u32[]{:S(2)}) collective-permute-start(bf16[48,384]{1,0:T(8,128)(2,1)S(1)} %get-tuple-element.197), channel_id=1, source_target_pairs={{0,8},{8,0},{16,24},{24,16},{1,9},{9,1},{17,25},{25,17},{2,10},{10... | collective-permute-start | bytes 110600 | tf_op jit(solution)/shard_map/ppermute | solution.py:458
  140.6 2.0 %collective-permute-start.40 = (bf16[48,384]{1,0:T(8,128)(2,1)S(1)}, bf16[48,384]{1,0:T(8,128)(2,1)S(1)}, u32[]{:S(2)}, u32[]{:S(2)}) collective-permute-start(bf16[48,384]{1,0:T(8,128)(2,1)S(1)} %get-tuple-element.199), channel_id=1, source_target_pairs={{0,24},{8,16},{16,8},{24,0},{1,25},{9,17},{17,9},{25,1},{2,26},{10... | collective-permute-start | bytes 110600 | tf_op jit(solution)/shard_map/ppermute | solution.py:458
  (106 shorter events, 34.7 us)
Async XLA Ops:
  3.4 8.9 %collective-permute-start = (bf16[48,1664]{1,0:T(8,128)(2,1)S(1)}, bf16[48,1664]{1,0:T(8,128)(2,1)S(1)}, u32[]{:S(2)}, u32[]{:S(2)}) collective-permute-start(bf16[48,1664]{1,0:T(8,128)(2,1)S(1)} %shard_map.213.refs_0_), channel_id=1, source_target_pairs={{0,8},{8,0},{16,24},{24,16},{1,9},{9,1},{17,25},{25,17},{2,10},{10... | collective-permute-start | bytes 479240 | tf_op jit(solution)/shard_map/ppermute | solution.py:458
  6.5 5.8 %collective-permute-start.1 = (bf16[48,1664]{1,0:T(8,128)(2,1)S(1)}, bf16[48,1664]{1,0:T(8,128)(2,1)S(1)}, u32[]{:S(2)}, u32[]{:S(2)}) collective-permute-start(bf16[48,1664]{1,0:T(8,128)(2,1)S(1)} %shard_map.213.refs_0_), channel_id=1, source_target_pairs={{0,2},{2,0},{4,6},{6,4},{1,3},{3,1},{5,7},{7,5},{8,10},{10,8},{12,... | collective-permute-start | bytes 479240 | tf_op jit(solution)/shard_map/ppermute | solution.py:458
  9.5 13.7 %collective-permute-start.3 = (bf16[48,1664]{1,0:T(8,128)(2,1)S(1)}, bf16[48,1664]{1,0:T(8,128)(2,1)S(1)}, u32[]{:S(2)}, u32[]{:S(2)}) collective-permute-start(bf16[48,1664]{1,0:T(8,128)(2,1)S(1)} %shard_map.213.refs_0_), channel_id=1, source_target_pairs={{0,16},{8,24},{16,0},{24,8},{1,17},{9,25},{17,1},{25,9},{2,18},{10... | collective-permute-start | bytes 479240 | tf_op jit(solution)/shard_map/ppermute | solution.py:458
  12.1 11.1 %collective-permute-start.4 = (bf16[48,1664]{1,0:T(8,128)(2,1)S(1)}, bf16[48,1664]{1,0:T(8,128)(2,1)S(1)}, u32[]{:S(2)}, u32[]{:S(2)}) collective-permute-start(bf16[48,1664]{1,0:T(8,128)(2,1)S(1)} %shard_map.213.refs_0_), channel_id=1, source_target_pairs={{0,24},{8,16},{16,8},{24,0},{1,25},{9,17},{17,9},{25,1},{2,26},{10... | collective-permute-start | bytes 479240 | tf_op jit(solution)/shard_map/ppermute | solution.py:458
  13.2 10.0 %collective-permute-start.5 = (bf16[48,1664]{1,0:T(8,128)(2,1)S(1)}, bf16[48,1664]{1,0:T(8,128)(2,1)S(1)}, u32[]{:S(2)}, u32[]{:S(2)}) collective-permute-start(bf16[48,1664]{1,0:T(8,128)(2,1)S(1)} %collective-permute-done.1.refs_4_), channel_id=1, source_target_pairs={{0,4},{2,6},{4,0},{6,2},{1,5},{3,7},{5,1},{7,3},{8,12},{10,14},{12... | collective-permute-start | bytes 479240 | tf_op jit(solution)/shard_map/ppermute | solution.py:458
  14.8 11.5 %collective-permute-start.9 = (bf16[48,1664]{1,0:T(8,128)(2,1)S(1)}, bf16[48,1664]{1,0:T(8,128)(2,1)S(1)}, u32[]{:S(2)}, u32[]{:S(2)}) collective-permute-start(bf16[48,1664]{1,0:T(8,128)(2,1)S(1)} %collective-permute-done.refs_1_), channel_id=1, source_target_pairs={{0,4},{2,6},{4,0},{6,2},{1,5},{3,7},{5,1},{7,3},{8,12},{10,14},{12... | collective-permute-start | bytes 479240 | tf_op jit(solution)/shard_map/ppermute | solution.py:458
  15.3 12.1 %collective-permute-start.6 = (bf16[48,1664]{1,0:T(8,128)(2,1)S(1)}, bf16[48,1664]{1,0:T(8,128)(2,1)S(1)}, u32[]{:S(2)}, u32[]{:S(2)}) collective-permute-start(bf16[48,1664]{1,0:T(8,128)(2,1)S(1)} %collective-permute-done.refs_1_), channel_id=1, source_target_pairs={{0,2},{2,0},{4,6},{6,4},{1,3},{3,1},{5,7},{7,5},{8,10},{10,8},{12,... | collective-permute-start | bytes 479240 | tf_op jit(solution)/shard_map/ppermute | solution.py:458
  23.2 7.0 %collective-permute-start.7 = (bf16[48,1664]{1,0:T(8,128)(2,1)S(1)}, bf16[48,1664]{1,0:T(8,128)(2,1)S(1)}, u32[]{:S(2)}, u32[]{:S(2)}) collective-permute-start(bf16[48,1664]{1,0:T(8,128)(2,1)S(1)} %collective-permute-done.3.refs_2_), channel_id=1, source_target_pairs={{0,2},{2,0},{4,6},{6,4},{1,3},{3,1},{5,7},{7,5},{8,10},{10,8},{12,... | collective-permute-start | bytes 479240 | tf_op jit(solution)/shard_map/ppermute | solution.py:458
  24.1 7.0 %collective-permute-start.11 = (bf16[48,1664]{1,0:T(8,128)(2,1)S(1)}, bf16[48,1664]{1,0:T(8,128)(2,1)S(1)}, u32[]{:S(2)}, u32[]{:S(2)}) collective-permute-start(bf16[48,1664]{1,0:T(8,128)(2,1)S(1)} %collective-permute-done.4.refs_3_), channel_id=1, source_target_pairs={{0,4},{2,6},{4,0},{6,2},{1,5},{3,7},{5,1},{7,3},{8,12},{10,14},{12... | collective-permute-start | bytes 479240 | tf_op jit(solution)/shard_map/ppermute | solution.py:458
  25.1 7.8 %collective-permute-start.10 = (bf16[48,1664]{1,0:T(8,128)(2,1)S(1)}, bf16[48,1664]{1,0:T(8,128)(2,1)S(1)}, u32[]{:S(2)}, u32[]{:S(2)}) collective-permute-start(bf16[48,1664]{1,0:T(8,128)(2,1)S(1)} %collective-permute-done.3.refs_2_), channel_id=1, source_target_pairs={{0,4},{2,6},{4,0},{6,2},{1,5},{3,7},{5,1},{7,3},{8,12},{10,14},{12... | collective-permute-start | bytes 479240 | tf_op jit(solution)/shard_map/ppermute | solution.py:458
  26.2 7.4 %collective-permute-start.8 = (bf16[48,1664]{1,0:T(8,128)(2,1)S(1)}, bf16[48,1664]{1,0:T(8,128)(2,1)S(1)}, u32[]{:S(2)}, u32[]{:S(2)}) collective-permute-start(bf16[48,1664]{1,0:T(8,128)(2,1)S(1)} %collective-permute-done.4.refs_3_), channel_id=1, source_target_pairs={{0,2},{2,0},{4,6},{6,4},{1,3},{3,1},{5,7},{7,5},{8,10},{10,8},{12,... | collective-permute-start | bytes 479240 | tf_op jit(solution)/shard_map/ppermute | solution.py:458
  27.3 8.6 %collective-permute-start.12 = (bf16[48,1664]{1,0:T(8,128)(2,1)S(1)}, bf16[48,1664]{1,0:T(8,128)(2,1)S(1)}, u32[]{:S(2)}, u32[]{:S(2)}) collective-permute-start(bf16[48,1664]{1,0:T(8,128)(2,1)S(1)} %collective-permute-done.9.refs_9_), channel_id=1, source_target_pairs={{0,2},{2,0},{4,6},{6,4},{1,3},{3,1},{5,7},{7,5},{8,10},{10,8},{12,... | collective-permute-start | bytes 479240 | tf_op jit(solution)/shard_map/ppermute | solution.py:458
  31.2 6.4 %collective-permute-start.14 = (bf16[48,1664]{1,0:T(8,128)(2,1)S(1)}, bf16[48,1664]{1,0:T(8,128)(2,1)S(1)}, u32[]{:S(2)}, u32[]{:S(2)}) collective-permute-start(bf16[48,1664]{1,0:T(8,128)(2,1)S(1)} %collective-permute-done.11.refs_11_), channel_id=1, source_target_pairs={{0,2},{2,0},{4,6},{6,4},{1,3},{3,1},{5,7},{7,5},{8,10},{10,8},{12,... | collective-permute-start | bytes 479240 | tf_op jit(solution)/shard_map/ppermute | solution.py:458
  66.5 7.3 %collective-permute-start.17 = (bf16[256,384]{1,0:T(8,128)(2,1)S(1)}, bf16[256,384]{1,0:T(8,128)(2,1)S(1)}, u32[]{:S(2)}, u32[]{:S(2)}) collective-permute-start(bf16[256,384]{1,0:T(8,128)(2,1)S(1)} %copy-done.2), channel_id=1, source_target_pairs={{0,1},{1,0},{2,3},{3,2},{4,5},{5,4},{6,7},{7,6},{8,9},{9,8},{10,11... | collective-permute-start | bytes 589832 | tf_op jit(solution)/shard_map/ppermute | solution.py:41
  67.0 6.8 %collective-permute-start.18 = (bf16[384,256]{1,0:T(8,128)(2,1)S(1)}, bf16[384,256]{1,0:T(8,128)(2,1)S(1)}, u32[]{:S(2)}, u32[]{:S(2)}) collective-permute-start(bf16[384,256]{1,0:T(8,128)(2,1)S(1)} %get-tuple-element.125), channel_id=1, source_target_pairs={{0,2},{2,0},{4,6},{6,4},{1,3},{3,1},{5,7},{7,5},{8,10},{10,8},{12,... | collective-permute-start | bytes 589832 | tf_op jit(solution)/shard_map/ppermute | solution.py:458
  67.6 6.5 %collective-permute-start.19 = (bf16[384,256]{1,0:T(8,128)(2,1)S(1)}, bf16[384,256]{1,0:T(8,128)(2,1)S(1)}, u32[]{:S(2)}, u32[]{:S(2)}) collective-permute-start(bf16[384,256]{1,0:T(8,128)(2,1)S(1)} %get-tuple-element.125), channel_id=1, source_target_pairs={{0,4},{2,6},{4,0},{6,2},{1,5},{3,7},{5,1},{7,3},{8,12},{10,14},{12... | collective-permute-start | bytes 589832 | tf_op jit(solution)/shard_map/ppermute | solution.py:458
  99.1 7.1 %collective-permute-start.23 = (bf16[192,256]{1,0:T(8,128)(2,1)S(1)}, bf16[192,256]{1,0:T(8,128)(2,1)S(1)}, u32[]{:S(2)}, u32[]{:S(2)}) collective-permute-start(bf16[192,256]{1,0:T(8,128)(2,1)S(1)} %slice.6), channel_id=1, source_target_pairs={{0,4},{2,6},{4,0},{6,2},{1,5},{3,7},{5,1},{7,3},{8,12},{10,14},{12... | collective-permute-start | bytes 294920 | tf_op jit(solution)/shard_map/ppermute | solution.py:458
  100.0 6.1 %collective-permute-start.24 = (bf16[192,256]{1,0:T(8,128)(2,1)S(1)}, bf16[192,256]{1,0:T(8,128)(2,1)S(1)}, u32[]{:S(2)}, u32[]{:S(2)}) collective-permute-start(bf16[192,256]{1,0:T(8,128)(2,1)S(1)} %slice.7), channel_id=1, source_target_pairs={{0,2},{2,0},{4,6},{6,4},{1,3},{3,1},{5,7},{7,5},{8,10},{10,8},{12,... | collective-permute-start | bytes 294920 | tf_op jit(solution)/shard_map/ppermute | solution.py:458
  106.3 10.7 %collective-permute-start.25 = (bf16[1152,256]{1,0:T(8,128)(2,1)S(1)}, bf16[1152,256]{1,0:T(8,128)(2,1)S(1)}, u32[]{:S(2)}, u32[]{:S(2)}) collective-permute-start(bf16[1152,256]{1,0:T(8,128)(2,1)S(1)} %constant_dynamic-update-slice_fusion.refs_0_), channel_id=1, source_target_pairs={{0,1},{1,0},{2,3},{3,2},{4,5},{5,4},{6,7},{7,6},{8,9},{9,8},{10,11... | collective-permute-start | bytes 1769480 | tf_op jit(solution)/shard_map/ppermute | solution.py:41
  106.8 6.6 %collective-permute-start.26 = (bf16[288,256]{1,0:T(8,128)(2,1)S(1)}, bf16[288,256]{1,0:T(8,128)(2,1)S(1)}, u32[]{:S(2)}, u32[]{:S(2)}) collective-permute-start(bf16[288,256]{1,0:T(8,128)(2,1)S(1)} %get-tuple-element.158), channel_id=1, source_target_pairs={{0,2},{2,0},{4,6},{6,4},{1,3},{3,1},{5,7},{7,5},{8,10},{10,8},{12,... | collective-permute-start | bytes 442376 | tf_op jit(solution)/shard_map/ppermute | solution.py:458
  108.3 8.7 %collective-permute-start.27 = (bf16[288,256]{1,0:T(8,128)(2,1)S(1)}, bf16[288,256]{1,0:T(8,128)(2,1)S(1)}, u32[]{:S(2)}, u32[]{:S(2)}) collective-permute-start(bf16[288,256]{1,0:T(8,128)(2,1)S(1)} %get-tuple-element.159), channel_id=1, source_target_pairs={{0,4},{2,6},{4,0},{6,2},{1,5},{3,7},{5,1},{7,3},{8,12},{10,14},{12... | collective-permute-start | bytes 442376 | tf_op jit(solution)/shard_map/ppermute | solution.py:458
  109.4 7.6 %collective-permute-start.28 = (bf16[288,256]{1,0:T(8,128)(2,1)S(1)}, bf16[288,256]{1,0:T(8,128)(2,1)S(1)}, u32[]{:S(2)}, u32[]{:S(2)}) collective-permute-start(bf16[288,256]{1,0:T(8,128)(2,1)S(1)} %get-tuple-element.160), channel_id=1, source_target_pairs={{0,6},{2,4},{4,2},{6,0},{1,7},{3,5},{5,3},{7,1},{8,14},{10,12},{12... | collective-permute-start | bytes 442376 | tf_op jit(solution)/shard_map/ppermute | solution.py:458
  118.7 6.0 %collective-permute-start.29 = (bf16[56,1152]{1,0:T(8,128)(2,1)S(1)}, bf16[56,1152]{1,0:T(8,128)(2,1)S(1)}, u32[]{:S(2)}, u32[]{:S(2)}) collective-permute-start(bf16[56,1152]{1,0:T(8,128)(2,1)S(1)} %get-tuple-element.162), channel_id=1, source_target_pairs={{0,8},{8,0},{16,24},{24,16},{1,9},{9,1},{17,25},{25,17},{2,10},{10... | collective-permute-start | bytes 387080 | tf_op jit(solution)/shard_map/ppermute | solution.py:458
  120.0 13.2 %collective-permute-start.30 = (bf16[56,1152]{1,0:T(8,128)(2,1)S(1)}, bf16[56,1152]{1,0:T(8,128)(2,1)S(1)}, u32[]{:S(2)}, u32[]{:S(2)}) collective-permute-start(bf16[56,1152]{1,0:T(8,128)(2,1)S(1)} %get-tuple-element.163), channel_id=1, source_target_pairs={{0,16},{8,24},{16,0},{24,8},{1,17},{9,25},{17,1},{25,9},{2,18},{10... | collective-permute-start | bytes 387080 | tf_op jit(solution)/shard_map/ppermute | solution.py:458
  121.5 11.8 %collective-permute-start.31 = (bf16[56,1152]{1,0:T(8,128)(2,1)S(1)}, bf16[56,1152]{1,0:T(8,128)(2,1)S(1)}, u32[]{:S(2)}, u32[]{:S(2)}) collective-permute-start(bf16[56,1152]{1,0:T(8,128)(2,1)S(1)} %get-tuple-element.164), channel_id=1, source_target_pairs={{0,24},{8,16},{16,8},{24,0},{1,25},{9,17},{17,9},{25,1},{2,26},{10... | collective-permute-start | bytes 387080 | tf_op jit(solution)/shard_map/ppermute | solution.py:458
  124.7 11.2 %collective-permute-start.35 = (bf16[192,384]{1,0:T(8,128)(2,1)S(1)}, bf16[192,384]{1,0:T(8,128)(2,1)S(1)}, u32[]{:S(2)}, u32[]{:S(2)}) collective-permute-start(bf16[192,384]{1,0:T(8,128)(2,1)S(1)} %get-tuple-element.189), channel_id=1, source_target_pairs={{0,2},{2,0},{4,6},{6,4},{1,3},{3,1},{5,7},{7,5},{8,10},{10,8},{12,... | collective-permute-start | bytes 442376 | tf_op jit(solution)/shard_map/ppermute | solution.py:458
  126.1 11.6 %collective-permute-start.36 = (bf16[192,384]{1,0:T(8,128)(2,1)S(1)}, bf16[192,384]{1,0:T(8,128)(2,1)S(1)}, u32[]{:S(2)}, u32[]{:S(2)}) collective-permute-start(bf16[192,384]{1,0:T(8,128)(2,1)S(1)} %get-tuple-element.190), channel_id=1, source_target_pairs={{0,4},{2,6},{4,0},{6,2},{1,5},{3,7},{5,1},{7,3},{8,12},{10,14},{12... | collective-permute-start | bytes 442376 | tf_op jit(solution)/shard_map/ppermute | solution.py:458
  126.5 11.2 %collective-permute-start.37 = (bf16[192,384]{1,0:T(8,128)(2,1)S(1)}, bf16[192,384]{1,0:T(8,128)(2,1)S(1)}, u32[]{:S(2)}, u32[]{:S(2)}) collective-permute-start(bf16[192,384]{1,0:T(8,128)(2,1)S(1)} %get-tuple-element.191), channel_id=1, source_target_pairs={{0,6},{2,4},{4,2},{6,0},{1,7},{3,5},{5,3},{7,1},{8,14},{10,12},{12... | collective-permute-start | bytes 442376 | tf_op jit(solution)/shard_map/ppermute | solution.py:458
  135.5 7.2 %collective-permute-start.33 = (bf16[48,512]{1,0:T(8,128)(2,1)S(1)}, bf16[48,512]{1,0:T(8,128)(2,1)S(1)}, u32[]{:S(2)}, u32[]{:S(2)}) collective-permute-start(bf16[48,512]{1,0:T(8,128)(2,1)S(1)} %get-tuple-element.179), channel_id=1, source_target_pairs={{0,4},{2,6},{4,0},{6,2},{1,5},{3,7},{5,1},{7,3},{8,12},{10,14},{12... | collective-permute-start | bytes 147464 | tf_op jit(solution)/shard_map/ppermute | solution.py:458
  136.0 6.7 %collective-permute-start.34 = (bf16[48,512]{1,0:T(8,128)(2,1)S(1)}, bf16[48,512]{1,0:T(8,128)(2,1)S(1)}, u32[]{:S(2)}, u32[]{:S(2)}) collective-permute-start(bf16[48,512]{1,0:T(8,128)(2,1)S(1)} %get-tuple-element.180), channel_id=1, source_target_pairs={{0,6},{2,4},{4,2},{6,0},{1,7},{3,5},{5,3},{7,1},{8,14},{10,12},{12... | collective-permute-start | bytes 147464 | tf_op jit(solution)/shard_map/ppermute | solution.py:458
  138.2 5.8 %collective-permute-start.38 = (bf16[48,384]{1,0:T(8,128)(2,1)S(1)}, bf16[48,384]{1,0:T(8,128)(2,1)S(1)}, u32[]{:S(2)}, u32[]{:S(2)}) collective-permute-start(bf16[48,384]{1,0:T(8,128)(2,1)S(1)} %get-tuple-element.197), channel_id=1, source_target_pairs={{0,8},{8,0},{16,24},{24,16},{1,9},{9,1},{17,25},{25,17},{2,10},{10... | collective-permute-start | bytes 110600 | tf_op jit(solution)/shard_map/ppermute | solution.py:458
  140.6 5.8 %collective-permute-start.40 = (bf16[48,384]{1,0:T(8,128)(2,1)S(1)}, bf16[48,384]{1,0:T(8,128)(2,1)S(1)}, u32[]{:S(2)}, u32[]{:S(2)}) collective-permute-start(bf16[48,384]{1,0:T(8,128)(2,1)S(1)} %get-tuple-element.199), channel_id=1, source_target_pairs={{0,24},{8,16},{16,8},{24,0},{1,25},{9,17},{17,9},{25,1},{2,26},{10... | collective-permute-start | bytes 110600 | tf_op jit(solution)/shard_map/ppermute | solution.py:458
  (22 other events, 260.2 us)

commit v5 on v4

--- a/solution.py
+++ b/solution.py
@@ -246,15 +246,24 @@
     grad_router_ref[...] = dot(d_logits, rows_ref[...], 0, 0)
 
 
-def arrive(at_ref, home_ref, slot_ref, x_ref, part_ref, peer_ref, layer_ref, d_h_ref, rows_ref, spare_ref):
+def from_slots(home_ref, slot_ref, low, rows_ref, spare_ref):
+    if len(home_ref.shape) == 3:
+        unpack_slots(home_ref, low, rows_ref, spare_ref)
+    else:
+        rows_ref[...] = home_ref[:, low * 128 : low * 128 + rows_ref.shape[1]]
+    dims = (rows_ref.shape[0], slot_ref.shape[1])
+    place = (lax.broadcasted_iota(jnp.int32, dims, 0) == slot_ref[...]).astype(bf16)
+    return dot(place, rows_ref[...], 0, 0)
+
+
+def arrive(home_ref, slot_ref, d_h_ref, rows_ref, spare_ref):
+    low = d_h_ref.shape[1] // 128
+    d_h_ref[...] = from_slots(home_ref, slot_ref, low, rows_ref, spare_ref).astype(bf16)
+
+
+def land(at_ref, home_ref, slot_ref, x_ref, part_ref, peer_ref, layer_ref, rows_ref, spare_ref):
     half = layer_ref.shape[1]
-    if len(home_ref.shape) == 3:
-        unpack_slots(home_ref, 0, rows_ref, spare_ref)
-        home_ref = rows_ref
-    dims = (home_ref.shape[0], x_ref.shape[0])
-    place = (lax.broadcasted_iota(jnp.int32, dims, 0) == slot_ref[...]).astype(bf16)
-    d_h_ref[...] = dot(place, home_ref[:, half:], 0, 0).astype(bf16)
-    y_home = dot(place, home_ref[:, :half], 0, 0)
+    y_home = from_slots(home_ref, slot_ref, 0, rows_ref, spare_ref)
     mine = lambda ref: jnp.where(at_ref[2] == 0, ref[:, :half], ref[:, half:]).astype(f32)
     layer_ref[...] = (mine(x_ref) + (mine(part_ref) + mine(peer_ref)) + y_home).astype(bf16)
 
@@ -426,23 +435,15 @@
     small_ref[heads + 1 : heads + 2, :] = gain_grad_ref[...]
 
 
-def expert_grads(rows_ref, d_y_ref, act_ref, d_pre_ref, down_ref, up_ref, held_ref, sems):
-    (hidden, width), steps = down_ref.shape, 3
+def expert_grads(left_ref, right_ref, out_ref, held_ref, sems):
+    count = held_ref.shape[1]
     copies = []
-    chunk = 0
-    for left_ref, right_ref, out_ref in ((act_ref, d_y_ref, down_ref), (rows_ref, d_pre_ref, up_ref)):
-        count = out_ref.shape[0] // steps
-        for at in range(steps):
-            rows = pl.ds(at * count, count)
-            slot = chunk % 3
-            if chunk >= 3:
-                copies[chunk - 3].wait()
-            held = held_ref.at[slot, pl.ds(0, count), pl.ds(0, out_ref.shape[1])]
-            held[...] = dot(left_ref[:, rows], right_ref[...], 0, 0)
-            copies.append(pltpu.make_async_copy(held, out_ref.at[rows, :], sems.at[chunk]))
-            copies[-1].start()
-            chunk += 1
-    for copy in copies[-3:]:
+    for at in range(out_ref.shape[0] // count):
+        rows = pl.ds(at * count, count)
+        held_ref[at] = dot(left_ref[:, rows], right_ref[...], 0, 0)
+        copies.append(pltpu.make_async_copy(held_ref.at[at], out_ref.at[rows, :], sems.at[at]))
+        copies[-1].start()
+    for copy in copies:
         copy.wait()
 
 
@@ -643,33 +644,48 @@
             scalars=(device_at,),
         )
         home = lax.all_to_all(back.reshape(exchange), ("ex", "row"), 0, 0, tiled=True).reshape(packed_slots)
-        layer_out, d_h_mine = vmem_call(
+        half_scratch = (pltpu.VMEM((slot_total, half), bf16), slot_scratch[2])
+        (d_h_mine,) = vmem_call(
             arrive,
-            (shape((seq_len, half), bf16), shape((seq_len, half), bf16)),
-            2 * seq_len * slot_total * width,
+            (shape((seq_len, half), bf16),),
+            seq_len * slot_total * width,
             home,
             slot_of,
-            x_in,
-            attn_part,
-            attn_peer,
-            scalars=(device_at,),
-            scratch=slot_scratch[1:],
-        )
-        def grads_of_expert(rows, d_y, act_b, d_pre):
+            scratch=half_scratch,
+        )
+
+        def land_at_home(home):
+            (layer_out,) = vmem_call(
+                land,
+                (shape((seq_len, half), bf16),),
+                seq_len * slot_total * width,
+                home,
+                slot_of,
+                x_in,
+                attn_part,
+                attn_peer,
+                scalars=(device_at,),
+                scratch=half_scratch,
+            )
+            return layer_out
+
+        def grads_of_expert(left, right):
+            dims = (left.shape[1], right.shape[1])
+            chunks = dims[0] // 256
             return pl.pallas_call(
                 expert_grads,
-                out_shape=(shape((hidden, width), f32), shape((width, hidden), f32)),
-                in_specs=[pl.BlockSpec(memory_space=pltpu.VMEM)] * 4,
-                out_specs=[pl.BlockSpec(memory_space=pltpu.HBM)] * 2,
+                out_shape=shape(dims, f32),
+                in_specs=[pl.BlockSpec(memory_space=pltpu.VMEM)] * 2,
+                out_specs=pl.BlockSpec(memory_space=pltpu.HBM),
                 scratch_shapes=[
-                    pltpu.VMEM((3, max(hidden, width) // 3, max(hidden, width)), f32),
-                    pltpu.SemaphoreType.DMA((6,)),
+                    pltpu.VMEM((chunks, dims[0] // chunks, dims[1]), f32),
+                    pltpu.SemaphoreType.DMA((chunks,)),
                 ],
-                compiler_params=pltpu.CompilerParams(vmem_limit_bytes=24 * 2**20),
+                compiler_params=pltpu.CompilerParams(vmem_limit_bytes=16 * 2**20),
                 cost_estimate=pl.CostEstimate(
-                    flops=4 * slot_total * width * hidden, bytes_accessed=12 * width * hidden, transcendentals=0
+                    flops=2 * slot_total * width * hidden, bytes_accessed=6 * width * hidden, transcendentals=0
                 ),
-            )(rows, d_y, act_b, d_pre)
+            )(left, right)
 
         quarter = (width // 4, 3 * inner // 4) if cube else (width, 3 * inner)
         pieces = 4 if cube else 1
@@ -730,6 +746,11 @@
             *normed_hops, _ = lax.optimization_barrier((*normed_hops, d_h_part))
             normed_near = jnp.concatenate(normed_hops, axis=0)
             normed_peer = swap_cores(normed_near)
+            late_home, act_b, d_y, _ = lax.optimization_barrier((home, act_b, d_y, small))
+            d_qkv_hops = plane_hops(d_qkv_turned[1:])
+            *d_qkv_hops, layer_out, grad_down = lax.optimization_barrier(
+                (*d_qkv_hops, land_at_home(late_home), grads_of_expert(act_b, d_y))
+            )
             terms = vmem_call(
                 qkv_terms,
                 [shape((own_rows + 8, 3 * inner), bf16)] * 4,
@@ -740,15 +761,15 @@
                 normed_near,
                 normed_peer,
                 d_qkv_turned[0],
-                *plane_hops(d_qkv_turned[1:]),
+                *d_qkv_hops,
                 scalars=(device_at,),
                 scratch=(pltpu.VMEM((width, quarter[1]), bf16),),
             )
             line = line_hops(terms[1:])
-            first_line = line[0]
-            rows, d_y, act_b, d_pre, _ = lax.optimization_barrier((rows, d_y, act_b, d_pre, terms[0]))
-            grad_down, grad_up = grads_of_expert(rows, d_y, act_b, d_pre)
-            *line, grad_down, grad_up = lax.optimization_barrier((*line, grad_down, grad_up))
+            rows, d_pre, _ = lax.optimization_barrier((rows, d_pre, terms[0]))
+            grad_up = grads_of_expert(rows, d_pre)
+            *out_pieces, _ = lax.optimization_barrier((*out_pieces, grad_up))
+            *line, grad_up = lax.optimization_barrier((*line, grad_up))
             split = vmem_call(
                 join_line,
                 [shape((own_rows, 512), bf16)] * 4,
@@ -773,7 +794,6 @@
                 scalars=(device_at,),
                 scratch=(pltpu.VMEM((own_rows, 3 * inner), f32),),
             )
-            *out_pieces, _ = lax.optimization_barrier((*out_pieces, first_line))
             out_hops = plane_hops(out_pieces[1:])
             out_blocks = vmem_call(
                 join_blocks,
@@ -786,7 +806,8 @@
             out_blocks = (out_blocks[0], *line_hops(out_blocks[1:]))
             grad_out = sum(part.astype(f32) for part in out_blocks)
         else:
-            grad_down, grad_up = grads_of_expert(rows, d_y, act_b, d_pre)
+            layer_out = land_at_home(home)
+            grad_down, grad_up = grads_of_expert(act_b, d_y), grads_of_expert(rows, d_pre)
             grad_qkv = scatter_groups(dot(normed_turned, d_qkv_turned[0], 1, 1), own_rows)
             grad_qkv = grad_qkv.reshape(own_rows, 3, inner).transpose(1, 0, 2)
             grad_out = scatter_groups(out_pieces[0], own_rows)

time: 147 us -> 144 us (0.980)
  waiting for transfers between devices: 26 us -> 21.6 us
    ppermute x34, waiting for transfers between devices: 22.3 us -> 18 us  [hop(): lax.ppermute(values, axis, [(i, i ^ step) for i in range(mesh.shape[axis])])]
    pallas_call x1 -> x2, Pallas kernels: 5 us -> 5.48 us  [grads_of_expert(): pl.pallas_call(expert_grads, out_shape=shape(dims, f32), in_specs=[pl.Blo...]
    pallas_call x13 -> x14, Pallas kernels: 25.9 us -> 26.1 us  [vmem_call(): pl.pallas_call(kernel, out_shape=out_shape, in_specs=[pl.BlockSpec(memory...]
  transfers between devices with their start and end apart: 41 -> 41, of which waited for: 16 -> 15; matrix products, arithmetic and copies ran while one was open for 2% -> 2% of each run, Pallas kernels for 13% -> 15%
where the time goes in v5:
time: 144 us
  starting transfers between devices  42.6 us (30%)
  blocking collectives  40.5 us (28%)
  Pallas kernels  31.6 us (22%)
  waiting for transfers between devices  21.6 us (15%)
  other arithmetic  3.73 us (3%)
  local copies, waits for them, and re-layouts  2.64 us (2%)
    ppermute x34, starting transfers between devices, hop(): lax.ppermute(values, axis, [(i, i ^ step) for i in range(mesh.shape[axis])])  41.4 us
    pallas_call x14, Pallas kernels, vmem_call(): pl.pallas_call(kernel, out_shape=out_shape, in_specs=[pl.BlockSpec(memory...  26.1 us
    all_to_all x1, blocking collectives, per_device(): lax.all_to_all(send.reshape(exchange), ('ex', 'row'), 0, 0, tiled=True)  21.2 us
    all_to_all x1, blocking collectives, per_device(): lax.all_to_all(back.reshape(exchange), ('ex', 'row'), 0, 0, tiled=True)  19.3 us
    ppermute x34, waiting for transfers between devices, hop(): lax.ppermute(values, axis, [(i, i ^ step) for i in range(mesh.shape[axis])])  18 us
    pallas_call x2, Pallas kernels, grads_of_expert(): pl.pallas_call(expert_grads, out_shape=shape(dims, f32), in_specs=[pl.Blo...  5.48 us
    ppermute x7, waiting for transfers between devices, swap_cores(): return lax.ppermute(values, 'col', [(0, 1), (1, 0)])  3.66 us
  transfers between devices with their start and end apart: 41, of which 15 were waited for; matrix products, arithmetic and copies ran while one was open for 2% of the time, Pallas kernels for 15%

profile of v5, /device:TPU:0, one launch (start us, length us, event | category | flops | bytes accessed | tf_op | source)
XLA Modules:
  0.0 144.0 jit_solution(14712234139495502874)
XLA Ops:
  3.4 3.0 %collective-permute-start = (bf16[48,1664]{1,0:T(8,128)(2,1)S(1)}, bf16[48,1664]{1,0:T(8,128)(2,1)S(1)}, u32[]{:S(2)}, u32[]{:S(2)}) collective-permute-start(bf16[48,1664]{1,0:T(8,128)(2,1)S(1)} %shard_map.213.refs_0_), channel_id=1, source_target_pairs={{0,8},{8,0},{16,24},{24,16},{1,9},{9,1},{17,25},{25,17},{2,10},{10... | collective-permute-start | bytes 479240 | tf_op jit(solution)/shard_map/ppermute | solution.py:459
  6.5 1.5 %collective-permute-start.1 = (bf16[48,1664]{1,0:T(8,128)(2,1)S(1)}, bf16[48,1664]{1,0:T(8,128)(2,1)S(1)}, u32[]{:S(2)}, u32[]{:S(2)}) collective-permute-start(bf16[48,1664]{1,0:T(8,128)(2,1)S(1)} %shard_map.213.refs_0_), channel_id=1, source_target_pairs={{0,2},{2,0},{4,6},{6,4},{1,3},{3,1},{5,7},{7,5},{8,10},{10,8},{12,... | collective-permute-start | bytes 479240 | tf_op jit(solution)/shard_map/ppermute | solution.py:459
  8.0 1.5 %collective-permute-start.2 = (bf16[48,1664]{1,0:T(8,128)(2,1)S(1)}, bf16[48,1664]{1,0:T(8,128)(2,1)S(1)}, u32[]{:S(2)}, u32[]{:S(2)}) collective-permute-start(bf16[48,1664]{1,0:T(8,128)(2,1)S(1)} %shard_map.213.refs_0_), channel_id=1, source_target_pairs={{0,4},{2,6},{4,0},{6,2},{1,5},{3,7},{5,1},{7,3},{8,12},{10,14},{12... | collective-permute-start | bytes 479240 | tf_op jit(solution)/shard_map/ppermute | solution.py:459
  9.5 2.6 %collective-permute-start.3 = (bf16[48,1664]{1,0:T(8,128)(2,1)S(1)}, bf16[48,1664]{1,0:T(8,128)(2,1)S(1)}, u32[]{:S(2)}, u32[]{:S(2)}) collective-permute-start(bf16[48,1664]{1,0:T(8,128)(2,1)S(1)} %shard_map.213.refs_0_), channel_id=1, source_target_pairs={{0,16},{8,24},{16,0},{24,8},{1,17},{9,25},{17,1},{25,9},{2,18},{10... | collective-permute-start | bytes 479240 | tf_op jit(solution)/shard_map/ppermute | solution.py:459
  13.2 1.5 %collective-permute-start.5 = (bf16[48,1664]{1,0:T(8,128)(2,1)S(1)}, bf16[48,1664]{1,0:T(8,128)(2,1)S(1)}, u32[]{:S(2)}, u32[]{:S(2)}) collective-permute-start(bf16[48,1664]{1,0:T(8,128)(2,1)S(1)} %collective-permute-done.1.refs_4_), channel_id=1, source_target_pairs={{0,4},{2,6},{4,0},{6,2},{1,5},{3,7},{5,1},{7,3},{8,12},{10,14},{12... | collective-permute-start | bytes 479240 | tf_op jit(solution)/shard_map/ppermute | solution.py:459
  15.8 2.6 %convert_element_type.91.up_ref = bf16[768,1536]{1,0:T(8,128)(2,1)S(1)} convert(f32[768,1536]{1,0:T(8,128)} %bitcast.22) | non-fusion elementwise | flops 1179648 | bytes 7077888 | tf_op jit(solution)/shard_map/convert_element_type | solution.py:556
  18.8 4.4 %collective-permute-done.3.refs_2_ = bf16[48,1664]{1,0:T(8,128)(2,1)S(1)} collective-permute-done((bf16[48,1664]{1,0:T(8,128)(2,1)S(1)}, bf16[48,1664]{1,0:T(8,128)(2,1)S(1)}, u32[]{:S(2)}, u32[]{:S(2)}) %collective-permute-start.3) | collective-permute-done | bytes 159776 | tf_op jit(solution)/shard_map/ppermute | solution.py:459
  28.3 2.0 %collective-permute-done.7.refs_6_ = bf16[48,1664]{1,0:T(8,128)(2,1)S(1)} collective-permute-done((bf16[48,1664]{1,0:T(8,128)(2,1)S(1)}, bf16[48,1664]{1,0:T(8,128)(2,1)S(1)}, u32[]{:S(2)}, u32[]{:S(2)}) %collective-permute-start.7) | collective-permute-done | bytes 159776 | tf_op jit(solution)/shard_map/ppermute | solution.py:459
  33.7 2.2 %collective-permute-done.12.refs_13_ = bf16[48,1664]{1,0:T(8,128)(2,1)S(1)} collective-permute-done((bf16[48,1664]{1,0:T(8,128)(2,1)S(1)}, bf16[48,1664]{1,0:T(8,128)(2,1)S(1)}, u32[]{:S(2)}, u32[]{:S(2)}) %collective-permute-start.12) | collective-permute-done | bytes 159776 | tf_op jit(solution)/shard_map/ppermute | solution.py:459
  35.9 1.7 %collective-permute-done.14.refs_15_ = bf16[48,1664]{1,0:T(8,128)(2,1)S(1)} collective-permute-done((bf16[48,1664]{1,0:T(8,128)(2,1)S(1)}, bf16[48,1664]{1,0:T(8,128)(2,1)S(1)}, u32[]{:S(2)}, u32[]{:S(2)}) %collective-permute-start.14) | collective-permute-done | bytes 159776 | tf_op jit(solution)/shard_map/ppermute | solution.py:459
  37.6 4.5 %shard_map.214 = (bf16[256,768]{1,0:T(8,128)(2,1)S(1)}, bf16[256,1152]{1,0:T(8,128)(2,1)S(1)}, f32[6,256,256]{2,1,0:T(8,128)S(1)}, bf16[256,384]{1,0:T(8,128)(2,...) custom-call(s32[3]{0:T(128)S(1)} %pad_add_fusion.at_ref, ...), custom_call_target="tpu_custom_call" | custom-call | flops 704643072 | bytes 8863744 | tf_op jit(solution)/shard_map/pallas_call | solution.py:52
  42.2 1.7 %collective-permute-done.15.peer_ref.part_peer_ref = bf16[256,768]{1,0:T(8,128)(2,1)S(1)} collective-permute-done((bf16[256,768]{1,0:T(8,128)(2,1)S(1)}, bf16[256,768]{1,0:T(8,128)(2,1)S(1)}, u32[]{:S(2)}, u32[]{:S(2)}) %collective-permute-start.15) | collective-permute-done | bytes 393248 | tf_op jit(solution)/shard_map/ppermute | solution.py:41
  43.9 1.4 %shard_map.215 = bf16[16,120,128]{2,1,0:T(8,128)(2,1)S(1)} custom-call(s32[3]{0:T(128)S(1)} %pad_add_fusion.at_ref, bf16[256,768]{1,0:T(8,128)(2,1)S(1)} %copy-done.1, bf16[256,768]{1,0:T(8,128)(2,1)S(1)} %get-tuple-element.119.part_ref, bf16[256,768]{1,0:T(8,128)(2,1)S(1)} %collective-permute-done.15.peer_ref.part_peer_ref, f32[768]{0:T(1024)S(1)} %copy-done.5, ...), custom_call_target="tpu_custom_call" | custom-call | flops 125829120 | bytes 1871872 | tf_op jit(solution)/shard_map/pallas_call | solution.py:52
  45.3 21.2 %all_to_all.10.got_ref = bf16[16,120,128]{2,1,0:T(8,128)(2,1)S(1)} all-to-all(bf16[16,120,128]{2,1,0:T(8,128)(2,1)S(1)} %shard_map.215), channel_id=1, replica_groups=mesh['ex'=4,'row'=4,'col'=2] {'ex','row'}, dimensions={0} | all-to-all | bytes 983040 | tf_op jit(solution)/shard_map/all_to_all | solution.py:607
  68.5 5.3 %shard_map.216 = (bf16[320,896]{1,0:T(8,128)(2,1)S(1)}, f32[320,768]{1,0:T(8,128)S(1)}, f32[320,16]{1,0:T(8,128)S(1)}, f32[320,1]{1,0:T(8,128)S(1)}, bf16[320,76...) custom-call(s32[3]{0:T(128)S(1)} %pad_add_fusion.at_ref, ...), custom_call_target="tpu_custom_call" | custom-call | flops 3019898880 | bytes 10425600 | tf_op jit(solution)/shard_map/pallas_call | solution.py:52
  74.1 2.0 %collective-permute-done.20.crossed_ref = bf16[320,896]{1,0:T(8,128)(2,1)S(1)} collective-permute-done((bf16[320,896]{1,0:T(8,128)(2,1)S(1)}, bf16[320,896]{1,0:T(8,128)(2,1)S(1)}, u32[]{:S(2)}, u32[]{:S(2)}) %collective-permute-start.20) | collective-permute-done | bytes 573472 | tf_op jit(solution)/shard_map/ppermute | solution.py:41
  76.1 1.5 %shard_map.217 = (bf16[16,120,128]{2,1,0:T(8,128)(2,1)S(1)}, f32[16,768]{1,0:T(8,128)S(1)}) custom-call(s32[3]{0:T(128)S(1)} %pad_add_fusion.at_ref, f32[320,768]{1,0:T(8,128)S(1)} %get-tuple-element.124.mine_ref, bf16[320,896]{1,0:T(8,128)(2,1)S(1)} %collective-permute-done.20.crossed_ref, f32[320,16]{1,0:T(8,128)S(1)} %get-tuple-element.128.probs_ref, ...), custom_call_target="tpu_custom_call" | custom-call | flops 3932160 | bytes 2807040 | tf_op jit(solution)/shard_map/pallas_call | solution.py:52
  77.6 19.3 %all_to_all.11.home_ref = bf16[16,120,128]{2,1,0:T(8,128)(2,1)S(1)} all-to-all(bf16[16,120,128]{2,1,0:T(8,128)(2,1)S(1)} %get-tuple-element.131), channel_id=1, replica_groups=mesh['ex'=4,'row'=4,'col'=2] {'ex','row'}, dimensions={0} | all-to-all | bytes 983040 | tf_op jit(solution)/shard_map/all_to_all | solution.py:646
  99.2 1.7 %shard_map.219 = (f32[256,768]{1,0:T(8,128)S(1)}, f32[1,768]{1,0:T(1,128)S(1)}, bf16[256,384]{1,0:T(8,128)(2,1)S(1)}, bf16[192,384]{1,0:T(8,128)(2,1)S(1)}, bf16...) custom-call(s32[3]{0:T(128)S(1)} %pad_add_fusion.at_ref, ...), custom_call_target="tpu_custom_call" | custom-call | flops 301989888 | bytes 4331520 | tf_op jit(solution)/shard_map/pallas_call | solution.py:52
  100.9 3.8 %shard_map.220 = (bf16[256,768]{1,0:T(8,128)(2,1)S(1)}, f32[8,512]{1,0:T(8,128)S(1)}, bf16[288,256]{1,0:T(8,128)(2,1)S(1)}, bf16[288,256]{1,0:T(8,128)(2,1)S(1)}...) custom-call(s32[3]{0:T(128)S(1)} %pad_add_fusion.at_ref, bf16[256,384]{1,0:T(8,128)(2,1)S(1)} %get-tuple-element.138.d_ctx_ref, ...), custom_call_target="tpu_custom_call" | custom-call | flops 704643072 | bytes 5128192 | tf_op jit(solution)/shard_map/pallas_call | solution.py:52
  105.4 1.5 %collective-permute-start.22 = (bf16[288,256]{1,0:T(8,128)(2,1)S(1)}, bf16[288,256]{1,0:T(8,128)(2,1)S(1)}, u32[]{:S(2)}, u32[]{:S(2)}) collective-permute-start(bf16[288,256]{1,0:T(8,128)(2,1)S(1)} %get-tuple-element.142), channel_id=1, source_target_pairs={{0,2},{2,0},{4,6},{6,4},{1,3},{3,1},{5,7},{7,5},{8,10},{10,8},{12,... | collective-permute-start | bytes 442376 | tf_op jit(solution)/shard_map/ppermute | solution.py:459
  110.3 1.8 %shard_map.222 = bf16[256,384]{1,0:T(8,128)(2,1)} custom-call(s32[3]{0:T(128)S(1)} %pad_add_fusion.at_ref, bf16[16,120,128]{2,1,0:T(8,128)(2,1)S(1)} %all_to_all.11.home_ref, s32[1,256]{1,0:T(1,128)S(1)} %bitcast.20, bf16[256,768]{1,0:T(8,128)(2,1)S(1)} %copy-done.1, bf16[256,768]{1,0:T(8,128)(2,1)S(1)} %get-tuple-element.119.part_ref, ...), custom_call_target="tpu_custom_call" | custom-call | flops 62914560 | bytes 1868800 | tf_op jit(solution)/shard_map/pallas_call | solution.py:52
  112.2 2.7 %shard_map.223 = f32[1536,768]{1,0:T(8,128)} custom-call(bf16[320,1536]{1,0:T(8,128)(2,1)S(1)} %get-tuple-element.153.left_ref, bf16[320,768]{1,0:T(8,128)(2,1)S(1)} %get-tuple-element.154.right_ref), custom_call_target="tpu_custom_call" | custom-call | flops 754974720 | bytes 7077888 | tf_op jit(solution)/shard_map/pallas_call | solution.py:675
  115.6 1.7 %shard_map.224 = (bf16[56,1152]{1,0:T(8,128)(2,1)S(1)}, bf16[56,1152]{1,0:T(8,128)(2,1)S(1)}, bf16[56,1152]{1,0:T(8,128)(2,1)S(1)}, bf16[56,1152]{1,0:T(8,128)(2,1)S(1)}) custom-call(s32[3]{0:T(128)S(1)} %pad_add_fusion.at_ref, bf16[768,256]{1,0:T(8,128)(2,1)S(1)} %get-tuple-element.157.turned_ref, f32[8,768]{1,0:T(8,128)S(1)} %get-tuple-element.151.small_ref, ...), custom_call_target="tpu_custom_call" | custom-call | flops 452984832 | bytes 2752512 | tf_op jit(solution)/shard_map/pallas_call | solution.py:52
  118.6 1.5 %collective-permute-start.30 = (bf16[56,1152]{1,0:T(8,128)(2,1)S(1)}, bf16[56,1152]{1,0:T(8,128)(2,1)S(1)}, u32[]{:S(2)}, u32[]{:S(2)}) collective-permute-start(bf16[56,1152]{1,0:T(8,128)(2,1)S(1)} %get-tuple-element.171), channel_id=1, source_target_pairs={{0,16},{8,24},{16,0},{24,8},{1,17},{9,25},{17,1},{25,9},{2,18},{10... | collective-permute-start | bytes 387080 | tf_op jit(solution)/shard_map/ppermute | solution.py:459
  120.1 1.7 %collective-permute-start.31 = (bf16[56,1152]{1,0:T(8,128)(2,1)S(1)}, bf16[56,1152]{1,0:T(8,128)(2,1)S(1)}, u32[]{:S(2)}, u32[]{:S(2)}) collective-permute-start(bf16[56,1152]{1,0:T(8,128)(2,1)S(1)} %get-tuple-element.172), channel_id=1, source_target_pairs={{0,24},{8,16},{16,8},{24,0},{1,25},{9,17},{17,9},{25,1},{2,26},{10... | collective-permute-start | bytes 387080 | tf_op jit(solution)/shard_map/ppermute | solution.py:459
  121.8 2.8 %shard_map.225 = f32[768,1536]{1,0:T(8,128)} custom-call(bf16[320,768]{1,0:T(8,128)(2,1)S(1)} %get-tuple-element.174.rows_ref.left_ref, bf16[320,1536]{1,0:T(8,128)(2,1)S(1)} %get-tuple-element.175.right_ref), custom_call_target="tpu_custom_call" | custom-call | flops 754974720 | bytes 7077888 | tf_op jit(solution)/shard_map/pallas_call | solution.py:675
  126.6 1.5 %collective-permute-start.37 = (bf16[192,384]{1,0:T(8,128)(2,1)S(1)}, bf16[192,384]{1,0:T(8,128)(2,1)S(1)}, u32[]{:S(2)}, u32[]{:S(2)}) collective-permute-start(bf16[192,384]{1,0:T(8,128)(2,1)S(1)} %get-tuple-element.193), channel_id=1, source_target_pairs={{0,6},{2,4},{4,2},{6,0},{1,7},{3,5},{5,3},{7,1},{8,14},{10,12},{12... | collective-permute-start | bytes 442376 | tf_op jit(solution)/shard_map/ppermute | solution.py:459
  128.1 2.0 %collective-permute-done.30.refs_2_ = bf16[56,1152]{1,0:T(8,128)(2,1)S(1)} collective-permute-done((bf16[56,1152]{1,0:T(8,128)(2,1)S(1)}, bf16[56,1152]{1,0:T(8,128)(2,1)S(1)}, u32[]{:S(2)}, u32[]{:S(2)}) %collective-permute-start.30) | collective-permute-done | bytes 129056 | tf_op jit(solution)/shard_map/ppermute | solution.py:459
  135.1 2.5 %collective-permute-start.38 = (bf16[48,384]{1,0:T(8,128)(2,1)S(1)}, bf16[48,384]{1,0:T(8,128)(2,1)S(1)}, u32[]{:S(2)}, u32[]{:S(2)}) collective-permute-start(bf16[48,384]{1,0:T(8,128)(2,1)S(1)} %get-tuple-element.199), channel_id=1, source_target_pairs={{0,8},{8,0},{16,24},{24,16},{1,9},{9,1},{17,25},{25,17},{2,10},{10... | collective-permute-start | bytes 110600 | tf_op jit(solution)/shard_map/ppermute | solution.py:459
  137.6 2.4 %collective-permute-start.40 = (bf16[48,384]{1,0:T(8,128)(2,1)S(1)}, bf16[48,384]{1,0:T(8,128)(2,1)S(1)}, u32[]{:S(2)}, u32[]{:S(2)}) collective-permute-start(bf16[48,384]{1,0:T(8,128)(2,1)S(1)} %get-tuple-element.201), channel_id=1, source_target_pairs={{0,24},{8,16},{16,8},{24,0},{1,25},{9,17},{17,9},{25,1},{2,26},{10... | collective-permute-start | bytes 110600 | tf_op jit(solution)/shard_map/ppermute | solution.py:459
  140.0 1.4 shard_map.227
  (108 shorter events, 34.2 us)
Async XLA Ops:
  3.4 8.9 %collective-permute-start = (bf16[48,1664]{1,0:T(8,128)(2,1)S(1)}, bf16[48,1664]{1,0:T(8,128)(2,1)S(1)}, u32[]{:S(2)}, u32[]{:S(2)}) collective-permute-start(bf16[48,1664]{1,0:T(8,128)(2,1)S(1)} %shard_map.213.refs_0_), channel_id=1, source_target_pairs={{0,8},{8,0},{16,24},{24,16},{1,9},{9,1},{17,25},{25,17},{2,10},{10... | collective-permute-start | bytes 479240 | tf_op jit(solution)/shard_map/ppermute | solution.py:459
  6.5 5.8 %collective-permute-start.1 = (bf16[48,1664]{1,0:T(8,128)(2,1)S(1)}, bf16[48,1664]{1,0:T(8,128)(2,1)S(1)}, u32[]{:S(2)}, u32[]{:S(2)}) collective-permute-start(bf16[48,1664]{1,0:T(8,128)(2,1)S(1)} %shard_map.213.refs_0_), channel_id=1, source_target_pairs={{0,2},{2,0},{4,6},{6,4},{1,3},{3,1},{5,7},{7,5},{8,10},{10,8},{12,... | collective-permute-start | bytes 479240 | tf_op jit(solution)/shard_map/ppermute | solution.py:459
  9.5 13.7 %collective-permute-start.3 = (bf16[48,1664]{1,0:T(8,128)(2,1)S(1)}, bf16[48,1664]{1,0:T(8,128)(2,1)S(1)}, u32[]{:S(2)}, u32[]{:S(2)}) collective-permute-start(bf16[48,1664]{1,0:T(8,128)(2,1)S(1)} %shard_map.213.refs_0_), channel_id=1, source_target_pairs={{0,16},{8,24},{16,0},{24,8},{1,17},{9,25},{17,1},{25,9},{2,18},{10... | collective-permute-start | bytes 479240 | tf_op jit(solution)/shard_map/ppermute | solution.py:459
  12.1 11.1 %collective-permute-start.4 = (bf16[48,1664]{1,0:T(8,128)(2,1)S(1)}, bf16[48,1664]{1,0:T(8,128)(2,1)S(1)}, u32[]{:S(2)}, u32[]{:S(2)}) collective-permute-start(bf16[48,1664]{1,0:T(8,128)(2,1)S(1)} %shard_map.213.refs_0_), channel_id=1, source_target_pairs={{0,24},{8,16},{16,8},{24,0},{1,25},{9,17},{17,9},{25,1},{2,26},{10... | collective-permute-start | bytes 479240 | tf_op jit(solution)/shard_map/ppermute | solution.py:459
  13.2 10.0 %collective-permute-start.5 = (bf16[48,1664]{1,0:T(8,128)(2,1)S(1)}, bf16[48,1664]{1,0:T(8,128)(2,1)S(1)}, u32[]{:S(2)}, u32[]{:S(2)}) collective-permute-start(bf16[48,1664]{1,0:T(8,128)(2,1)S(1)} %collective-permute-done.1.refs_4_), channel_id=1, source_target_pairs={{0,4},{2,6},{4,0},{6,2},{1,5},{3,7},{5,1},{7,3},{8,12},{10,14},{12... | collective-permute-start | bytes 479240 | tf_op jit(solution)/shard_map/ppermute | solution.py:459
  14.8 11.5 %collective-permute-start.9 = (bf16[48,1664]{1,0:T(8,128)(2,1)S(1)}, bf16[48,1664]{1,0:T(8,128)(2,1)S(1)}, u32[]{:S(2)}, u32[]{:S(2)}) collective-permute-start(bf16[48,1664]{1,0:T(8,128)(2,1)S(1)} %collective-permute-done.refs_1_), channel_id=1, source_target_pairs={{0,4},{2,6},{4,0},{6,2},{1,5},{3,7},{5,1},{7,3},{8,12},{10,14},{12... | collective-permute-start | bytes 479240 | tf_op jit(solution)/shard_map/ppermute | solution.py:459
  15.3 12.1 %collective-permute-start.6 = (bf16[48,1664]{1,0:T(8,128)(2,1)S(1)}, bf16[48,1664]{1,0:T(8,128)(2,1)S(1)}, u32[]{:S(2)}, u32[]{:S(2)}) collective-permute-start(bf16[48,1664]{1,0:T(8,128)(2,1)S(1)} %collective-permute-done.refs_1_), channel_id=1, source_target_pairs={{0,2},{2,0},{4,6},{6,4},{1,3},{3,1},{5,7},{7,5},{8,10},{10,8},{12,... | collective-permute-start | bytes 479240 | tf_op jit(solution)/shard_map/ppermute | solution.py:459
  23.2 7.0 %collective-permute-start.7 = (bf16[48,1664]{1,0:T(8,128)(2,1)S(1)}, bf16[48,1664]{1,0:T(8,128)(2,1)S(1)}, u32[]{:S(2)}, u32[]{:S(2)}) collective-permute-start(bf16[48,1664]{1,0:T(8,128)(2,1)S(1)} %collective-permute-done.3.refs_2_), channel_id=1, source_target_pairs={{0,2},{2,0},{4,6},{6,4},{1,3},{3,1},{5,7},{7,5},{8,10},{10,8},{12,... | collective-permute-start | bytes 479240 | tf_op jit(solution)/shard_map/ppermute | solution.py:459
  24.1 7.0 %collective-permute-start.11 = (bf16[48,1664]{1,0:T(8,128)(2,1)S(1)}, bf16[48,1664]{1,0:T(8,128)(2,1)S(1)}, u32[]{:S(2)}, u32[]{:S(2)}) collective-permute-start(bf16[48,1664]{1,0:T(8,128)(2,1)S(1)} %collective-permute-done.4.refs_3_), channel_id=1, source_target_pairs={{0,4},{2,6},{4,0},{6,2},{1,5},{3,7},{5,1},{7,3},{8,12},{10,14},{12... | collective-permute-start | bytes 479240 | tf_op jit(solution)/shard_map/ppermute | solution.py:459
  25.1 7.8 %collective-permute-start.10 = (bf16[48,1664]{1,0:T(8,128)(2,1)S(1)}, bf16[48,1664]{1,0:T(8,128)(2,1)S(1)}, u32[]{:S(2)}, u32[]{:S(2)}) collective-permute-start(bf16[48,1664]{1,0:T(8,128)(2,1)S(1)} %collective-permute-done.3.refs_2_), channel_id=1, source_target_pairs={{0,4},{2,6},{4,0},{6,2},{1,5},{3,7},{5,1},{7,3},{8,12},{10,14},{12... | collective-permute-start | bytes 479240 | tf_op jit(solution)/shard_map/ppermute | solution.py:459
  26.2 7.4 %collective-permute-start.8 = (bf16[48,1664]{1,0:T(8,128)(2,1)S(1)}, bf16[48,1664]{1,0:T(8,128)(2,1)S(1)}, u32[]{:S(2)}, u32[]{:S(2)}) collective-permute-start(bf16[48,1664]{1,0:T(8,128)(2,1)S(1)} %collective-permute-done.4.refs_3_), channel_id=1, source_target_pairs={{0,2},{2,0},{4,6},{6,4},{1,3},{3,1},{5,7},{7,5},{8,10},{10,8},{12,... | collective-permute-start | bytes 479240 | tf_op jit(solution)/shard_map/ppermute | solution.py:459
  27.3 8.6 %collective-permute-start.12 = (bf16[48,1664]{1,0:T(8,128)(2,1)S(1)}, bf16[48,1664]{1,0:T(8,128)(2,1)S(1)}, u32[]{:S(2)}, u32[]{:S(2)}) collective-permute-start(bf16[48,1664]{1,0:T(8,128)(2,1)S(1)} %collective-permute-done.9.refs_9_), channel_id=1, source_target_pairs={{0,2},{2,0},{4,6},{6,4},{1,3},{3,1},{5,7},{7,5},{8,10},{10,8},{12,... | collective-permute-start | bytes 479240 | tf_op jit(solution)/shard_map/ppermute | solution.py:459
  31.2 6.4 %collective-permute-start.14 = (bf16[48,1664]{1,0:T(8,128)(2,1)S(1)}, bf16[48,1664]{1,0:T(8,128)(2,1)S(1)}, u32[]{:S(2)}, u32[]{:S(2)}) collective-permute-start(bf16[48,1664]{1,0:T(8,128)(2,1)S(1)} %collective-permute-done.11.refs_11_), channel_id=1, source_target_pairs={{0,2},{2,0},{4,6},{6,4},{1,3},{3,1},{5,7},{7,5},{8,10},{10,8},{12,... | collective-permute-start | bytes 479240 | tf_op jit(solution)/shard_map/ppermute | solution.py:459
  66.5 7.3 %collective-permute-start.17 = (bf16[256,384]{1,0:T(8,128)(2,1)S(1)}, bf16[256,384]{1,0:T(8,128)(2,1)S(1)}, u32[]{:S(2)}, u32[]{:S(2)}) collective-permute-start(bf16[256,384]{1,0:T(8,128)(2,1)S(1)} %copy-done.2), channel_id=1, source_target_pairs={{0,1},{1,0},{2,3},{3,2},{4,5},{5,4},{6,7},{7,6},{8,9},{9,8},{10,11... | collective-permute-start | bytes 589832 | tf_op jit(solution)/shard_map/ppermute | solution.py:41
  67.0 6.8 %collective-permute-start.18 = (bf16[384,256]{1,0:T(8,128)(2,1)S(1)}, bf16[384,256]{1,0:T(8,128)(2,1)S(1)}, u32[]{:S(2)}, u32[]{:S(2)}) collective-permute-start(bf16[384,256]{1,0:T(8,128)(2,1)S(1)} %get-tuple-element.126), channel_id=1, source_target_pairs={{0,2},{2,0},{4,6},{6,4},{1,3},{3,1},{5,7},{7,5},{8,10},{10,8},{12,... | collective-permute-start | bytes 589832 | tf_op jit(solution)/shard_map/ppermute | solution.py:459
  67.6 6.5 %collective-permute-start.19 = (bf16[384,256]{1,0:T(8,128)(2,1)S(1)}, bf16[384,256]{1,0:T(8,128)(2,1)S(1)}, u32[]{:S(2)}, u32[]{:S(2)}) collective-permute-start(bf16[384,256]{1,0:T(8,128)(2,1)S(1)} %get-tuple-element.126), channel_id=1, source_target_pairs={{0,4},{2,6},{4,0},{6,2},{1,5},{3,7},{5,1},{7,3},{8,12},{10,14},{12... | collective-permute-start | bytes 589832 | tf_op jit(solution)/shard_map/ppermute | solution.py:459
  97.6 7.1 %collective-permute-start.26 = (bf16[192,256]{1,0:T(8,128)(2,1)S(1)}, bf16[192,256]{1,0:T(8,128)(2,1)S(1)}, u32[]{:S(2)}, u32[]{:S(2)}) collective-permute-start(bf16[192,256]{1,0:T(8,128)(2,1)S(1)} %slice.6), channel_id=1, source_target_pairs={{0,4},{2,6},{4,0},{6,2},{1,5},{3,7},{5,1},{7,3},{8,12},{10,14},{12... | collective-permute-start | bytes 294920 | tf_op jit(solution)/shard_map/ppermute | solution.py:459
  98.6 6.1 %collective-permute-start.27 = (bf16[192,256]{1,0:T(8,128)(2,1)S(1)}, bf16[192,256]{1,0:T(8,128)(2,1)S(1)}, u32[]{:S(2)}, u32[]{:S(2)}) collective-permute-start(bf16[192,256]{1,0:T(8,128)(2,1)S(1)} %slice.7), channel_id=1, source_target_pairs={{0,2},{2,0},{4,6},{6,4},{1,3},{3,1},{5,7},{7,5},{8,10},{10,8},{12,... | collective-permute-start | bytes 294920 | tf_op jit(solution)/shard_map/ppermute | solution.py:459
  104.8 10.8 %collective-permute-start.28 = (bf16[1152,256]{1,0:T(8,128)(2,1)S(1)}, bf16[1152,256]{1,0:T(8,128)(2,1)S(1)}, u32[]{:S(2)}, u32[]{:S(2)}) collective-permute-start(bf16[1152,256]{1,0:T(8,128)(2,1)S(1)} %constant_dynamic-update-slice_fusion.refs_0_), channel_id=1, source_target_pairs={{0,1},{1,0},{2,3},{3,2},{4,5},{5,4},{6,7},{7,6},{8,9},{9,8},{10,11... | collective-permute-start | bytes 1769480 | tf_op jit(solution)/shard_map/ppermute | solution.py:41
  105.4 9.5 %collective-permute-start.22 = (bf16[288,256]{1,0:T(8,128)(2,1)S(1)}, bf16[288,256]{1,0:T(8,128)(2,1)S(1)}, u32[]{:S(2)}, u32[]{:S(2)}) collective-permute-start(bf16[288,256]{1,0:T(8,128)(2,1)S(1)} %get-tuple-element.142), channel_id=1, source_target_pairs={{0,2},{2,0},{4,6},{6,4},{1,3},{3,1},{5,7},{7,5},{8,10},{10,8},{12,... | collective-permute-start | bytes 442376 | tf_op jit(solution)/shard_map/ppermute | solution.py:459
  106.8 8.7 %collective-permute-start.23 = (bf16[288,256]{1,0:T(8,128)(2,1)S(1)}, bf16[288,256]{1,0:T(8,128)(2,1)S(1)}, u32[]{:S(2)}, u32[]{:S(2)}) collective-permute-start(bf16[288,256]{1,0:T(8,128)(2,1)S(1)} %get-tuple-element.143), channel_id=1, source_target_pairs={{0,4},{2,6},{4,0},{6,2},{1,5},{3,7},{5,1},{7,3},{8,12},{10,14},{12... | collective-permute-start | bytes 442376 | tf_op jit(solution)/shard_map/ppermute | solution.py:459
  108.0 7.6 %collective-permute-start.24 = (bf16[288,256]{1,0:T(8,128)(2,1)S(1)}, bf16[288,256]{1,0:T(8,128)(2,1)S(1)}, u32[]{:S(2)}, u32[]{:S(2)}) collective-permute-start(bf16[288,256]{1,0:T(8,128)(2,1)S(1)} %get-tuple-element.144), channel_id=1, source_target_pairs={{0,6},{2,4},{4,2},{6,0},{1,7},{3,5},{5,3},{7,1},{8,14},{10,12},{12... | collective-permute-start | bytes 442376 | tf_op jit(solution)/shard_map/ppermute | solution.py:459
  117.3 9.3 %collective-permute-start.29 = (bf16[56,1152]{1,0:T(8,128)(2,1)S(1)}, bf16[56,1152]{1,0:T(8,128)(2,1)S(1)}, u32[]{:S(2)}, u32[]{:S(2)}) collective-permute-start(bf16[56,1152]{1,0:T(8,128)(2,1)S(1)} %get-tuple-element.170), channel_id=1, source_target_pairs={{0,8},{8,0},{16,24},{24,16},{1,9},{9,1},{17,25},{25,17},{2,10},{10... | collective-permute-start | bytes 387080 | tf_op jit(solution)/shard_map/ppermute | solution.py:459
  118.6 11.6 %collective-permute-start.30 = (bf16[56,1152]{1,0:T(8,128)(2,1)S(1)}, bf16[56,1152]{1,0:T(8,128)(2,1)S(1)}, u32[]{:S(2)}, u32[]{:S(2)}) collective-permute-start(bf16[56,1152]{1,0:T(8,128)(2,1)S(1)} %get-tuple-element.171), channel_id=1, source_target_pairs={{0,16},{8,24},{16,0},{24,8},{1,17},{9,25},{17,1},{25,9},{2,18},{10... | collective-permute-start | bytes 387080 | tf_op jit(solution)/shard_map/ppermute | solution.py:459
  120.1 10.1 %collective-permute-start.31 = (bf16[56,1152]{1,0:T(8,128)(2,1)S(1)}, bf16[56,1152]{1,0:T(8,128)(2,1)S(1)}, u32[]{:S(2)}, u32[]{:S(2)}) collective-permute-start(bf16[56,1152]{1,0:T(8,128)(2,1)S(1)} %get-tuple-element.172), channel_id=1, source_target_pairs={{0,24},{8,16},{16,8},{24,0},{1,25},{9,17},{17,9},{25,1},{2,26},{10... | collective-permute-start | bytes 387080 | tf_op jit(solution)/shard_map/ppermute | solution.py:459
  124.6 8.7 %collective-permute-start.35 = (bf16[192,384]{1,0:T(8,128)(2,1)S(1)}, bf16[192,384]{1,0:T(8,128)(2,1)S(1)}, u32[]{:S(2)}, u32[]{:S(2)}) collective-permute-start(bf16[192,384]{1,0:T(8,128)(2,1)S(1)} %get-tuple-element.191), channel_id=1, source_target_pairs={{0,2},{2,0},{4,6},{6,4},{1,3},{3,1},{5,7},{7,5},{8,10},{10,8},{12,... | collective-permute-start | bytes 442376 | tf_op jit(solution)/shard_map/ppermute | solution.py:459
  125.5 9.1 %collective-permute-start.36 = (bf16[192,384]{1,0:T(8,128)(2,1)S(1)}, bf16[192,384]{1,0:T(8,128)(2,1)S(1)}, u32[]{:S(2)}, u32[]{:S(2)}) collective-permute-start(bf16[192,384]{1,0:T(8,128)(2,1)S(1)} %get-tuple-element.192), channel_id=1, source_target_pairs={{0,4},{2,6},{4,0},{6,2},{1,5},{3,7},{5,1},{7,3},{8,12},{10,14},{12... | collective-permute-start | bytes 442376 | tf_op jit(solution)/shard_map/ppermute | solution.py:459
  126.6 8.0 %collective-permute-start.37 = (bf16[192,384]{1,0:T(8,128)(2,1)S(1)}, bf16[192,384]{1,0:T(8,128)(2,1)S(1)}, u32[]{:S(2)}, u32[]{:S(2)}) collective-permute-start(bf16[192,384]{1,0:T(8,128)(2,1)S(1)} %get-tuple-element.193), channel_id=1, source_target_pairs={{0,6},{2,4},{4,2},{6,0},{1,7},{3,5},{5,3},{7,1},{8,14},{10,12},{12... | collective-permute-start | bytes 442376 | tf_op jit(solution)/shard_map/ppermute | solution.py:459
  132.3 7.7 %collective-permute-start.33 = (bf16[48,512]{1,0:T(8,128)(2,1)S(1)}, bf16[48,512]{1,0:T(8,128)(2,1)S(1)}, u32[]{:S(2)}, u32[]{:S(2)}) collective-permute-start(bf16[48,512]{1,0:T(8,128)(2,1)S(1)} %get-tuple-element.181), channel_id=1, source_target_pairs={{0,4},{2,6},{4,0},{6,2},{1,5},{3,7},{5,1},{7,3},{8,12},{10,14},{12... | collective-permute-start | bytes 147464 | tf_op jit(solution)/shard_map/ppermute | solution.py:459
  133.2 6.8 %collective-permute-start.34 = (bf16[48,512]{1,0:T(8,128)(2,1)S(1)}, bf16[48,512]{1,0:T(8,128)(2,1)S(1)}, u32[]{:S(2)}, u32[]{:S(2)}) collective-permute-start(bf16[48,512]{1,0:T(8,128)(2,1)S(1)} %get-tuple-element.182), channel_id=1, source_target_pairs={{0,6},{2,4},{4,2},{6,0},{1,7},{3,5},{5,3},{7,1},{8,14},{10,12},{12... | collective-permute-start | bytes 147464 | tf_op jit(solution)/shard_map/ppermute | solution.py:459
  135.1 6.2 %collective-permute-start.38 = (bf16[48,384]{1,0:T(8,128)(2,1)S(1)}, bf16[48,384]{1,0:T(8,128)(2,1)S(1)}, u32[]{:S(2)}, u32[]{:S(2)}) collective-permute-start(bf16[48,384]{1,0:T(8,128)(2,1)S(1)} %get-tuple-element.199), channel_id=1, source_target_pairs={{0,8},{8,0},{16,24},{24,16},{1,9},{9,1},{17,25},{25,17},{2,10},{10... | collective-permute-start | bytes 110600 | tf_op jit(solution)/shard_map/ppermute | solution.py:459
  137.6 5.8 %collective-permute-start.40 = (bf16[48,384]{1,0:T(8,128)(2,1)S(1)}, bf16[48,384]{1,0:T(8,128)(2,1)S(1)}, u32[]{:S(2)}, u32[]{:S(2)}) collective-permute-start(bf16[48,384]{1,0:T(8,128)(2,1)S(1)} %get-tuple-element.201), channel_id=1, source_target_pairs={{0,24},{8,16},{16,8},{24,0},{1,25},{9,17},{17,9},{25,1},{2,26},{10... | collective-permute-start | bytes 110600 | tf_op jit(solution)/shard_map/ppermute | solution.py:459
  (22 other events, 260.1 us)

commit v6 on v5

--- a/solution.py
+++ b/solution.py
@@ -77,17 +77,34 @@
     return same.astype(bf16)
 
 
-def pack_weights(qkv_ref, out_turned_ref, router_turned_ref, packed_ref):
+def pack_weights(qkv_in, out_in, router_in, packed_out, qkv_ref, out_turned_ref, router_turned_ref, packed_ref, sems):
+    pairs = ((qkv_in, qkv_ref), (out_in, out_turned_ref), (router_in, router_turned_ref))
+    copies = [pltpu.make_async_copy(source, target, sems.at[i]) for i, (source, target) in enumerate(pairs)]
+    for copy in copies:
+        copy.start()
     inner, experts = qkv_ref.shape[2], router_turned_ref.shape[0]
+    packed_ref[:, 4 * inner :] = jnp.zeros((packed_ref.shape[0], packed_ref.shape[1] - 4 * inner), bf16)
+    for copy in copies:
+        copy.wait()
     for part in range(3):
         packed_ref[:, part * inner : (part + 1) * inner] = qkv_ref[part].astype(bf16)
     packed_ref[:, 3 * inner : 4 * inner] = out_turned_ref[...].astype(bf16)
-    packed_ref[:, 4 * inner :] = jnp.zeros((packed_ref.shape[0], packed_ref.shape[1] - 4 * inner), bf16)
     router = dot(router_turned_ref[...].astype(bf16), eye(experts), 0, 0)
     packed_ref[:, 4 * inner : 4 * inner + experts] = router.astype(bf16)
-
-
-def attend_forward(order, at_ref, x_ref, gain_ref, offset_ref, seg_ref, *refs):
+    copy = pltpu.make_async_copy(packed_ref, packed_out, sems.at[3])
+    copy.start()
+    copy.wait()
+
+
+def spread_bias(offset_ref, bias_ref):
+    heads, seq_len, _ = bias_ref.shape
+    span = offset_ref.shape[1]
+    for at in range(heads):
+        spread = jnp.broadcast_to(offset_ref[at : at + 1, :], (seq_len, span))
+        bias_ref[at] = pltpu.roll(spread, span - seq_len + 1, 1, stride=1, stride_axis=0)[:, :seq_len]
+
+
+def attend_forward(order, at_ref, x_ref, gain_ref, bias_ref, seg_ref, *refs):
     *block_refs, part_ref, qkv_ref, probs_ref, ctx_ref, w_ref, out_w_ref, router_ref, turned_ref, half_ref = refs
     seq_len = x_ref.shape[0]
     heads, inner = probs_ref.shape[0], ctx_ref.shape[1]
@@ -103,14 +120,11 @@
     documents = lax.broadcasted_iota(jnp.int32, (8, seq_len), 0) == seg_ref[...]
     same_doc = dot(documents.astype(bf16), documents.astype(bf16), 0, 0) > 0.5
     qkv_ref[...] = dot(h_one, w_ref[...], 1, 0).astype(bf16)
-    span = offset_ref.shape[1]
     for at in range(heads):
         take = lambda part: qkv_ref[:, part * inner + at * HEAD : part * inner + (at + 1) * HEAD]
-        spread = jnp.broadcast_to(offset_ref[at : at + 1, :], (seq_len, span))
-        bias = pltpu.roll(spread, span - seq_len + 1, 1, stride=1, stride_axis=0)[:, :seq_len]
-        scores = jnp.where(same_doc, dot(take(0), take(1), 1, 1) * 0.125 + bias, -1e30)
+        scores = jnp.where(same_doc, dot(take(0), take(1), 1, 1) * 0.125 + bias_ref[at], -1e30)
         expo = jnp.exp(scores - jnp.max(scores, axis=1, keepdims=True))
-        probs = expo / jnp.sum(expo, axis=1, keepdims=True)
+        probs = expo * (1.0 / jnp.sum(expo, axis=1, keepdims=True))
         probs_ref[at] = probs
         ctx = dot(probs.astype(bf16), take(2), 1, 0)
         ctx_ref[:, at * HEAD : (at + 1) * HEAD] = ctx.astype(bf16)
@@ -193,7 +207,7 @@
     chosen = lax.broadcasted_iota(jnp.int32, probs.shape, 1) == expert_at
     gate = jnp.sum(jnp.where(chosen, probs, 0.0), axis=1, keepdims=True)
     d_y_ref[...] = (g_rows * gate).astype(bf16)
-    step = 512 if hidden % 512 == 0 else hidden
+    step = 768 if hidden % 768 == 0 else hidden
     y_part = None
     for lo in range(0, hidden, step):
         cols = pl.ds(lo, step)
@@ -542,21 +556,20 @@
         )
         gather_order = GATHER_ORDER if cube else None
 
-        (packed,) = vmem_call(
+        turned = (w_qkv, w_out.T, w_router.T)
+        packed_shape = shape((own_rows, 3 * inner + wide), bf16)
+        packed = pl.pallas_call(
             pack_weights,
-            (shape((own_rows, 3 * inner + wide), bf16),),
-            0,
-            w_qkv,
-            w_out.T,
-            w_router.T,
-        )
-
-        def round_weights(after):
-            late_up, late_down, _ = lax.optimization_barrier((w_up[0], w_down[0], after))
-            return [late_up.astype(bf16), late_down.astype(bf16)]
-
-        blocks, (up_w, down_w) = gather_blocks(packed, round_weights)
-        g_peer = swap_cores(d_out)
+            out_shape=packed_shape,
+            in_specs=[pl.BlockSpec(memory_space=pltpu.HBM)] * 3,
+            out_specs=pl.BlockSpec(memory_space=pltpu.HBM),
+            scratch_shapes=[
+                *(pltpu.VMEM(v.shape, v.dtype) for v in turned),
+                pltpu.VMEM(packed_shape.shape, bf16),
+                pltpu.SemaphoreType.DMA((4,)),
+            ],
+            compiler_params=pltpu.CompilerParams(vmem_limit_bytes=60 * 2**20),
+        )(*turned)
 
         span = 2 * seq_len
         offsets = jnp.arange(span, dtype=jnp.int32) - (seq_len - 1)
@@ -564,6 +577,18 @@
             bucket_of(offsets)[:, None] == jnp.arange(BUCKETS, dtype=jnp.int32)[None, :]
         ).astype(f32)
         per_offset = jnp.einsum("bh,ob->ho", rel_bias, offset_hot, precision=highest)
+
+        def prepare(after):
+            late_up, late_down, _ = lax.optimization_barrier((w_up[0], w_down[0], after))
+            late_offset, _ = lax.optimization_barrier((per_offset, after))
+            (bias,) = vmem_call(
+                spread_bias, (shape((heads_here, seq_len, seq_len), f32),), 0, late_offset
+            )
+            return [late_up.astype(bf16), late_down.astype(bf16), bias]
+
+        blocks, (up_w, down_w, bias) = gather_blocks(packed, prepare)
+        g_peer = swap_cores(d_out)
+
         square = seq_len * seq_len * heads_here * HEAD
         attn_part, qkv, probs, context, qkv_w, out_w, router_w, normed_turned, normed_mine = vmem_call(
             functools.partial(attend_forward, gather_order),
@@ -581,7 +606,7 @@
             8 * seq_len * width * inner + 4 * square,
             x_in,
             gain_attn,
-            per_offset,
+            bias,
             seg_ids,
             *blocks,
             scalars=(device_at,),

time: 144 us -> 143 us (level)
  local copies, waits for them, and re-layouts: 2.64 us -> 1.1 us
    pallas_call x0 -> x1, Pallas kernels: none -> 1.87 us  [per_device(): pl.pallas_call(pack_weights, out_shape=packed_shape, in_specs=[pl.BlockSp...]
    unnamed x29 -> x25, local copies, waits for them, and re-layouts: 2.62 us -> 1.07 us
  transfers between devices with their start and end apart: 41 -> 41, of which waited for: 15 -> 16; matrix products, arithmetic and copies ran while one was open for 2% -> 2% of each run, Pallas kernels for 15% -> 15%
where the time goes in v6:
time: 143 us
  starting transfers between devices  42.6 us (30%)
  blocking collectives  40.5 us (28%)
  Pallas kernels  32.7 us (23%)
  waiting for transfers between devices  20.4 us (14%)
  other arithmetic  3.88 us (3%)
    ppermute x34, starting transfers between devices, hop(): lax.ppermute(values, axis, [(i, i ^ step) for i in range(mesh.shape[axis])])  41.4 us
    pallas_call x14, Pallas kernels, vmem_call(): pl.pallas_call(kernel, out_shape=out_shape, in_specs=[pl.BlockSpec(memory...  25.3 us
    all_to_all x1, blocking collectives, per_device(): lax.all_to_all(send.reshape(exchange), ('ex', 'row'), 0, 0, tiled=True)  21.1 us
    all_to_all x1, blocking collectives, per_device(): lax.all_to_all(back.reshape(exchange), ('ex', 'row'), 0, 0, tiled=True)  19.3 us
    ppermute x34, waiting for transfers between devices, hop(): lax.ppermute(values, axis, [(i, i ^ step) for i in range(mesh.shape[axis])])  16.8 us
    pallas_call x2, Pallas kernels, grads_of_expert(): pl.pallas_call(expert_grads, out_shape=shape(dims, f32), in_specs=[pl.Blo...  5.48 us
    ppermute x7, waiting for transfers between devices, swap_cores(): return lax.ppermute(values, 'col', [(0, 1), (1, 0)])  3.66 us
    convert_element_type x2, other arithmetic, prepare(): return [late_up.astype(bf16), late_down.astype(bf16), bias]  3 us
  transfers between devices with their start and end apart: 41, of which 16 were waited for; matrix products, arithmetic and copies ran while one was open for 2% of the time, Pallas kernels for 15%

profile of v6, /device:TPU:0, one launch (start us, length us, event | category | flops | bytes accessed | tf_op | source)
XLA Modules:
  0.0 142.5 jit_solution(13975780910664898718)
XLA Ops:
  0.7 1.9 %shard_map.213.refs_0_ = bf16[48,1664]{1,0:T(8,128)(2,1)} custom-call(f32[3,48,384]{2,1,0:T(8,128)} %qkv_in, f32[48,384]{1,0:T(8,128)} %bitcast.24, f32[16,48]{1,0:T(8,128)} %bitcast.25), custom_call_target="tpu_custom_call" | custom-call | tf_op jit(solution)/shard_map/pallas_call | solution.py:561
  2.6 3.1 %collective-permute-start.2 = (bf16[48,1664]{1,0:T(8,128)(2,1)}, bf16[48,1664]{1,0:T(8,128)(2,1)S(1)}, u32[]{:S(2)}, u32[]{:S(2)}) collective-permute-start(bf16[48,1664]{1,0:T(8,128)(2,1)} %shard_map.213.refs_0_), channel_id=1, source_target_pairs={{0,8},{8,0},{16,24},{24,16},{1,9},{9,1},{17,25},{25,17},{2,10},{10... | collective-permute-start | bytes 479240 | tf_op jit(solution)/shard_map/ppermute | solution.py:473
  5.7 1.5 %collective-permute-start.3 = (bf16[48,1664]{1,0:T(8,128)(2,1)}, bf16[48,1664]{1,0:T(8,128)(2,1)S(1)}, u32[]{:S(2)}, u32[]{:S(2)}) collective-permute-start(bf16[48,1664]{1,0:T(8,128)(2,1)} %shard_map.213.refs_0_), channel_id=1, source_target_pairs={{0,2},{2,0},{4,6},{6,4},{1,3},{3,1},{5,7},{7,5},{8,10},{10,8},{12,... | collective-permute-start | bytes 479240 | tf_op jit(solution)/shard_map/ppermute | solution.py:473
  7.2 1.5 %collective-permute-start.4 = (bf16[48,1664]{1,0:T(8,128)(2,1)}, bf16[48,1664]{1,0:T(8,128)(2,1)S(1)}, u32[]{:S(2)}, u32[]{:S(2)}) collective-permute-start(bf16[48,1664]{1,0:T(8,128)(2,1)} %shard_map.213.refs_0_), channel_id=1, source_target_pairs={{0,4},{2,6},{4,0},{6,2},{1,5},{3,7},{5,1},{7,3},{8,12},{10,14},{12... | collective-permute-start | bytes 479240 | tf_op jit(solution)/shard_map/ppermute | solution.py:473
  8.7 2.6 %collective-permute-start = (bf16[48,1664]{1,0:T(8,128)(2,1)}, bf16[48,1664]{1,0:T(8,128)(2,1)S(1)}, u32[]{:S(2)}, u32[]{:S(2)}) collective-permute-start(bf16[48,1664]{1,0:T(8,128)(2,1)} %shard_map.213.refs_0_), channel_id=1, source_target_pairs={{0,16},{8,24},{16,0},{24,8},{1,17},{9,25},{17,1},{25,9},{2,18},{10... | collective-permute-start | bytes 479240 | tf_op jit(solution)/shard_map/ppermute | solution.py:473
  12.7 1.5 %collective-permute-start.5 = (bf16[48,1664]{1,0:T(8,128)(2,1)S(1)}, bf16[48,1664]{1,0:T(8,128)(2,1)S(1)}, u32[]{:S(2)}, u32[]{:S(2)}) collective-permute-start(bf16[48,1664]{1,0:T(8,128)(2,1)S(1)} %collective-permute-done.3.refs_4_), channel_id=1, source_target_pairs={{0,4},{2,6},{4,0},{6,2},{1,5},{3,7},{5,1},{7,3},{8,12},{10,14},{12... | collective-permute-start | bytes 479240 | tf_op jit(solution)/shard_map/ppermute | solution.py:473
  15.6 2.8 %convert_element_type.84.up_ref = bf16[768,1536]{1,0:T(8,128)(2,1)S(1)} convert(f32[768,1536]{1,0:T(8,128)} %bitcast.20) | non-fusion elementwise | flops 1179648 | bytes 7077888 | tf_op jit(solution)/shard_map/convert_element_type | solution.py:587
  20.1 2.5 %collective-permute-done.refs_2_ = bf16[48,1664]{1,0:T(8,128)(2,1)S(1)} collective-permute-done((bf16[48,1664]{1,0:T(8,128)(2,1)}, bf16[48,1664]{1,0:T(8,128)(2,1)S(1)}, u32[]{:S(2)}, u32[]{:S(2)}) %collective-permute-start) | collective-permute-done | bytes 159776 | tf_op jit(solution)/shard_map/ppermute | solution.py:473
  27.7 2.1 %collective-permute-done.7.refs_6_ = bf16[48,1664]{1,0:T(8,128)(2,1)S(1)} collective-permute-done((bf16[48,1664]{1,0:T(8,128)(2,1)S(1)}, bf16[48,1664]{1,0:T(8,128)(2,1)S(1)}, u32[]{:S(2)}, u32[]{:S(2)}) %collective-permute-start.7) | collective-permute-done | bytes 159776 | tf_op jit(solution)/shard_map/ppermute | solution.py:473
  33.1 2.3 %collective-permute-done.12.refs_13_ = bf16[48,1664]{1,0:T(8,128)(2,1)S(1)} collective-permute-done((bf16[48,1664]{1,0:T(8,128)(2,1)S(1)}, bf16[48,1664]{1,0:T(8,128)(2,1)S(1)}, u32[]{:S(2)}, u32[]{:S(2)}) %collective-permute-start.12) | collective-permute-done | bytes 159776 | tf_op jit(solution)/shard_map/ppermute | solution.py:473
  35.4 1.7 %collective-permute-done.14.refs_15_ = bf16[48,1664]{1,0:T(8,128)(2,1)S(1)} collective-permute-done((bf16[48,1664]{1,0:T(8,128)(2,1)S(1)}, bf16[48,1664]{1,0:T(8,128)(2,1)S(1)}, u32[]{:S(2)}, u32[]{:S(2)}) %collective-permute-start.14) | collective-permute-done | bytes 159776 | tf_op jit(solution)/shard_map/ppermute | solution.py:473
  37.1 3.5 %shard_map.215 = (bf16[256,768]{1,0:T(8,128)(2,1)S(1)}, bf16[256,1152]{1,0:T(8,128)(2,1)S(1)}, f32[6,256,256]{2,1,0:T(8,128)S(1)}, bf16[256,384]{1,0:T(8,128)(2,...) custom-call(s32[3]{0:T(128)S(1)} %pad_add_fusion.at_ref, ...), custom_call_target="tpu_custom_call" | custom-call | flops 704643072 | bytes 10424320 | tf_op jit(solution)/shard_map/pallas_call | solution.py:52
  40.8 1.7 %collective-permute-done.15.peer_ref.part_peer_ref = bf16[256,768]{1,0:T(8,128)(2,1)S(1)} collective-permute-done((bf16[256,768]{1,0:T(8,128)(2,1)S(1)}, bf16[256,768]{1,0:T(8,128)(2,1)S(1)}, u32[]{:S(2)}, u32[]{:S(2)}) %collective-permute-start.15) | collective-permute-done | bytes 393248 | tf_op jit(solution)/shard_map/ppermute | solution.py:41
  42.4 1.4 %shard_map.216 = bf16[16,120,128]{2,1,0:T(8,128)(2,1)S(1)} custom-call(s32[3]{0:T(128)S(1)} %pad_add_fusion.at_ref, bf16[256,768]{1,0:T(8,128)(2,1)S(1)} %copy-done.1, bf16[256,768]{1,0:T(8,128)(2,1)S(1)} %get-tuple-element.123.part_ref, bf16[256,768]{1,0:T(8,128)(2,1)S(1)} %collective-permute-done.15.peer_ref.part_peer_ref, f32[768]{0:T(1024)S(1)} %copy-done.4, ...), custom_call_target="tpu_custom_call" | custom-call | flops 125829120 | bytes 1871872 | tf_op jit(solution)/shard_map/pallas_call | solution.py:52
  43.9 21.1 %all_to_all.10.got_ref = bf16[16,120,128]{2,1,0:T(8,128)(2,1)S(1)} all-to-all(bf16[16,120,128]{2,1,0:T(8,128)(2,1)S(1)} %shard_map.216), channel_id=1, replica_groups=mesh['ex'=4,'row'=4,'col'=2] {'ex','row'}, dimensions={0} | all-to-all | bytes 983040 | tf_op jit(solution)/shard_map/all_to_all | solution.py:632
  67.0 5.2 %shard_map.217 = (bf16[320,896]{1,0:T(8,128)(2,1)S(1)}, f32[320,768]{1,0:T(8,128)S(1)}, f32[320,16]{1,0:T(8,128)S(1)}, f32[320,1]{1,0:T(8,128)S(1)}, bf16[320,76...) custom-call(s32[3]{0:T(128)S(1)} %pad_add_fusion.at_ref, ...), custom_call_target="tpu_custom_call" | custom-call | flops 3019898880 | bytes 10425600 | tf_op jit(solution)/shard_map/pallas_call | solution.py:52
  72.6 2.0 %collective-permute-done.20.crossed_ref = bf16[320,896]{1,0:T(8,128)(2,1)S(1)} collective-permute-done((bf16[320,896]{1,0:T(8,128)(2,1)S(1)}, bf16[320,896]{1,0:T(8,128)(2,1)S(1)}, u32[]{:S(2)}, u32[]{:S(2)}) %collective-permute-start.20) | collective-permute-done | bytes 573472 | tf_op jit(solution)/shard_map/ppermute | solution.py:41
  74.6 1.5 %shard_map.218 = (bf16[16,120,128]{2,1,0:T(8,128)(2,1)S(1)}, f32[16,768]{1,0:T(8,128)S(1)}) custom-call(s32[3]{0:T(128)S(1)} %pad_add_fusion.at_ref, f32[320,768]{1,0:T(8,128)S(1)} %get-tuple-element.128.mine_ref, bf16[320,896]{1,0:T(8,128)(2,1)S(1)} %collective-permute-done.20.crossed_ref, f32[320,16]{1,0:T(8,128)S(1)} %get-tuple-element.132.probs_ref, ...), custom_call_target="tpu_custom_call" | custom-call | flops 3932160 | bytes 2807040 | tf_op jit(solution)/shard_map/pallas_call | solution.py:52
  76.1 19.3 %all_to_all.11.home_ref = bf16[16,120,128]{2,1,0:T(8,128)(2,1)S(1)} all-to-all(bf16[16,120,128]{2,1,0:T(8,128)(2,1)S(1)} %get-tuple-element.135), channel_id=1, replica_groups=mesh['ex'=4,'row'=4,'col'=2] {'ex','row'}, dimensions={0} | all-to-all | bytes 983040 | tf_op jit(solution)/shard_map/all_to_all | solution.py:671
  97.7 1.7 %shard_map.220 = (f32[256,768]{1,0:T(8,128)S(1)}, f32[1,768]{1,0:T(1,128)S(1)}, bf16[256,384]{1,0:T(8,128)(2,1)S(1)}, bf16[192,384]{1,0:T(8,128)(2,1)S(1)}, bf16...) custom-call(s32[3]{0:T(128)S(1)} %pad_add_fusion.at_ref, ...), custom_call_target="tpu_custom_call" | custom-call | flops 301989888 | bytes 4331520 | tf_op jit(solution)/shard_map/pallas_call | solution.py:52
  99.5 3.7 %shard_map.221 = (bf16[256,768]{1,0:T(8,128)(2,1)S(1)}, f32[8,512]{1,0:T(8,128)S(1)}, bf16[288,256]{1,0:T(8,128)(2,1)S(1)}, bf16[288,256]{1,0:T(8,128)(2,1)S(1)}...) custom-call(s32[3]{0:T(128)S(1)} %pad_add_fusion.at_ref, bf16[256,384]{1,0:T(8,128)(2,1)S(1)} %get-tuple-element.142.d_ctx_ref, ...), custom_call_target="tpu_custom_call" | custom-call | flops 704643072 | bytes 5128192 | tf_op jit(solution)/shard_map/pallas_call | solution.py:52
  103.9 1.5 %collective-permute-start.22 = (bf16[288,256]{1,0:T(8,128)(2,1)S(1)}, bf16[288,256]{1,0:T(8,128)(2,1)S(1)}, u32[]{:S(2)}, u32[]{:S(2)}) collective-permute-start(bf16[288,256]{1,0:T(8,128)(2,1)S(1)} %get-tuple-element.146), channel_id=1, source_target_pairs={{0,2},{2,0},{4,6},{6,4},{1,3},{3,1},{5,7},{7,5},{8,10},{10,8},{12,... | collective-permute-start | bytes 442376 | tf_op jit(solution)/shard_map/ppermute | solution.py:473
  108.8 1.8 %shard_map.223 = bf16[256,384]{1,0:T(8,128)(2,1)} custom-call(s32[3]{0:T(128)S(1)} %pad_add_fusion.at_ref, bf16[16,120,128]{2,1,0:T(8,128)(2,1)S(1)} %all_to_all.11.home_ref, s32[1,256]{1,0:T(1,128)S(1)} %bitcast.19, bf16[256,768]{1,0:T(8,128)(2,1)S(1)} %copy-done.1, bf16[256,768]{1,0:T(8,128)(2,1)S(1)} %get-tuple-element.123.part_ref, ...), custom_call_target="tpu_custom_call" | custom-call | flops 62914560 | bytes 1868800 | tf_op jit(solution)/shard_map/pallas_call | solution.py:52
  110.7 2.7 %shard_map.224 = f32[1536,768]{1,0:T(8,128)} custom-call(bf16[320,1536]{1,0:T(8,128)(2,1)S(1)} %get-tuple-element.157.left_ref, bf16[320,768]{1,0:T(8,128)(2,1)S(1)} %get-tuple-element.158.right_ref), custom_call_target="tpu_custom_call" | custom-call | flops 754974720 | bytes 7077888 | tf_op jit(solution)/shard_map/pallas_call | solution.py:700
  114.1 1.7 %shard_map.225 = (bf16[56,1152]{1,0:T(8,128)(2,1)S(1)}, bf16[56,1152]{1,0:T(8,128)(2,1)S(1)}, bf16[56,1152]{1,0:T(8,128)(2,1)S(1)}, bf16[56,1152]{1,0:T(8,128)(2,1)S(1)}) custom-call(s32[3]{0:T(128)S(1)} %pad_add_fusion.at_ref, bf16[768,256]{1,0:T(8,128)(2,1)S(1)} %get-tuple-element.161.turned_ref, f32[8,768]{1,0:T(8,128)S(1)} %get-tuple-element.155.small_ref, ...), custom_call_target="tpu_custom_call" | custom-call | flops 452984832 | bytes 2752512 | tf_op jit(solution)/shard_map/pallas_call | solution.py:52
  117.1 1.5 %collective-permute-start.30 = (bf16[56,1152]{1,0:T(8,128)(2,1)S(1)}, bf16[56,1152]{1,0:T(8,128)(2,1)S(1)}, u32[]{:S(2)}, u32[]{:S(2)}) collective-permute-start(bf16[56,1152]{1,0:T(8,128)(2,1)S(1)} %get-tuple-element.175), channel_id=1, source_target_pairs={{0,16},{8,24},{16,0},{24,8},{1,17},{9,25},{17,1},{25,9},{2,18},{10... | collective-permute-start | bytes 387080 | tf_op jit(solution)/shard_map/ppermute | solution.py:473
  118.5 1.7 %collective-permute-start.31 = (bf16[56,1152]{1,0:T(8,128)(2,1)S(1)}, bf16[56,1152]{1,0:T(8,128)(2,1)S(1)}, u32[]{:S(2)}, u32[]{:S(2)}) collective-permute-start(bf16[56,1152]{1,0:T(8,128)(2,1)S(1)} %get-tuple-element.176), channel_id=1, source_target_pairs={{0,24},{8,16},{16,8},{24,0},{1,25},{9,17},{17,9},{25,1},{2,26},{10... | collective-permute-start | bytes 387080 | tf_op jit(solution)/shard_map/ppermute | solution.py:473
  120.3 2.8 %shard_map.226 = f32[768,1536]{1,0:T(8,128)} custom-call(bf16[320,768]{1,0:T(8,128)(2,1)S(1)} %get-tuple-element.178.rows_ref.left_ref, bf16[320,1536]{1,0:T(8,128)(2,1)S(1)} %get-tuple-element.179.right_ref), custom_call_target="tpu_custom_call" | custom-call | flops 754974720 | bytes 7077888 | tf_op jit(solution)/shard_map/pallas_call | solution.py:700
  125.1 1.6 %collective-permute-start.37 = (bf16[192,384]{1,0:T(8,128)(2,1)S(1)}, bf16[192,384]{1,0:T(8,128)(2,1)S(1)}, u32[]{:S(2)}, u32[]{:S(2)}) collective-permute-start(bf16[192,384]{1,0:T(8,128)(2,1)S(1)} %get-tuple-element.197), channel_id=1, source_target_pairs={{0,6},{2,4},{4,2},{6,0},{1,7},{3,5},{5,3},{7,1},{8,14},{10,12},{12... | collective-permute-start | bytes 442376 | tf_op jit(solution)/shard_map/ppermute | solution.py:473
  126.6 2.0 %collective-permute-done.30.refs_2_ = bf16[56,1152]{1,0:T(8,128)(2,1)S(1)} collective-permute-done((bf16[56,1152]{1,0:T(8,128)(2,1)S(1)}, bf16[56,1152]{1,0:T(8,128)(2,1)S(1)}, u32[]{:S(2)}, u32[]{:S(2)}) %collective-permute-start.30) | collective-permute-done | bytes 129056 | tf_op jit(solution)/shard_map/ppermute | solution.py:473
  133.6 2.5 %collective-permute-start.38 = (bf16[48,384]{1,0:T(8,128)(2,1)S(1)}, bf16[48,384]{1,0:T(8,128)(2,1)S(1)}, u32[]{:S(2)}, u32[]{:S(2)}) collective-permute-start(bf16[48,384]{1,0:T(8,128)(2,1)S(1)} %get-tuple-element.203), channel_id=1, source_target_pairs={{0,8},{8,0},{16,24},{24,16},{1,9},{9,1},{17,25},{25,17},{2,10},{10... | collective-permute-start | bytes 110600 | tf_op jit(solution)/shard_map/ppermute | solution.py:473
  136.1 2.4 %collective-permute-start.40 = (bf16[48,384]{1,0:T(8,128)(2,1)S(1)}, bf16[48,384]{1,0:T(8,128)(2,1)S(1)}, u32[]{:S(2)}, u32[]{:S(2)}) collective-permute-start(bf16[48,384]{1,0:T(8,128)(2,1)S(1)} %get-tuple-element.205), channel_id=1, source_target_pairs={{0,24},{8,16},{16,8},{24,0},{1,25},{9,17},{17,9},{25,1},{2,26},{10... | collective-permute-start | bytes 110600 | tf_op jit(solution)/shard_map/ppermute | solution.py:473
  (105 shorter events, 34.8 us)
Async XLA Ops:
  2.6 8.9 %collective-permute-start.2 = (bf16[48,1664]{1,0:T(8,128)(2,1)}, bf16[48,1664]{1,0:T(8,128)(2,1)S(1)}, u32[]{:S(2)}, u32[]{:S(2)}) collective-permute-start(bf16[48,1664]{1,0:T(8,128)(2,1)} %shard_map.213.refs_0_), channel_id=1, source_target_pairs={{0,8},{8,0},{16,24},{24,16},{1,9},{9,1},{17,25},{25,17},{2,10},{10... | collective-permute-start | bytes 479240 | tf_op jit(solution)/shard_map/ppermute | solution.py:473
  5.7 5.8 %collective-permute-start.3 = (bf16[48,1664]{1,0:T(8,128)(2,1)}, bf16[48,1664]{1,0:T(8,128)(2,1)S(1)}, u32[]{:S(2)}, u32[]{:S(2)}) collective-permute-start(bf16[48,1664]{1,0:T(8,128)(2,1)} %shard_map.213.refs_0_), channel_id=1, source_target_pairs={{0,2},{2,0},{4,6},{6,4},{1,3},{3,1},{5,7},{7,5},{8,10},{10,8},{12,... | collective-permute-start | bytes 479240 | tf_op jit(solution)/shard_map/ppermute | solution.py:473
  8.7 13.9 %collective-permute-start = (bf16[48,1664]{1,0:T(8,128)(2,1)}, bf16[48,1664]{1,0:T(8,128)(2,1)S(1)}, u32[]{:S(2)}, u32[]{:S(2)}) collective-permute-start(bf16[48,1664]{1,0:T(8,128)(2,1)} %shard_map.213.refs_0_), channel_id=1, source_target_pairs={{0,16},{8,24},{16,0},{24,8},{1,17},{9,25},{17,1},{25,9},{2,18},{10... | collective-permute-start | bytes 479240 | tf_op jit(solution)/shard_map/ppermute | solution.py:473
  11.3 11.3 %collective-permute-start.1 = (bf16[48,1664]{1,0:T(8,128)(2,1)}, bf16[48,1664]{1,0:T(8,128)(2,1)S(1)}, u32[]{:S(2)}, u32[]{:S(2)}) collective-permute-start(bf16[48,1664]{1,0:T(8,128)(2,1)} %shard_map.213.refs_0_), channel_id=1, source_target_pairs={{0,24},{8,16},{16,8},{24,0},{1,25},{9,17},{17,9},{25,1},{2,26},{10... | collective-permute-start | bytes 479240 | tf_op jit(solution)/shard_map/ppermute | solution.py:473
  12.7 10.0 %collective-permute-start.5 = (bf16[48,1664]{1,0:T(8,128)(2,1)S(1)}, bf16[48,1664]{1,0:T(8,128)(2,1)S(1)}, u32[]{:S(2)}, u32[]{:S(2)}) collective-permute-start(bf16[48,1664]{1,0:T(8,128)(2,1)S(1)} %collective-permute-done.3.refs_4_), channel_id=1, source_target_pairs={{0,4},{2,6},{4,0},{6,2},{1,5},{3,7},{5,1},{7,3},{8,12},{10,14},{12... | collective-permute-start | bytes 479240 | tf_op jit(solution)/shard_map/ppermute | solution.py:473
  14.5 11.1 %collective-permute-start.9 = (bf16[48,1664]{1,0:T(8,128)(2,1)S(1)}, bf16[48,1664]{1,0:T(8,128)(2,1)S(1)}, u32[]{:S(2)}, u32[]{:S(2)}) collective-permute-start(bf16[48,1664]{1,0:T(8,128)(2,1)S(1)} %collective-permute-done.2.refs_1_), channel_id=1, source_target_pairs={{0,4},{2,6},{4,0},{6,2},{1,5},{3,7},{5,1},{7,3},{8,12},{10,14},{12... | collective-permute-start | bytes 479240 | tf_op jit(solution)/shard_map/ppermute | solution.py:473
  15.1 11.6 %collective-permute-start.6 = (bf16[48,1664]{1,0:T(8,128)(2,1)S(1)}, bf16[48,1664]{1,0:T(8,128)(2,1)S(1)}, u32[]{:S(2)}, u32[]{:S(2)}) collective-permute-start(bf16[48,1664]{1,0:T(8,128)(2,1)S(1)} %collective-permute-done.2.refs_1_), channel_id=1, source_target_pairs={{0,2},{2,0},{4,6},{6,4},{1,3},{3,1},{5,7},{7,5},{8,10},{10,8},{12,... | collective-permute-start | bytes 479240 | tf_op jit(solution)/shard_map/ppermute | solution.py:473
  22.7 7.0 %collective-permute-start.7 = (bf16[48,1664]{1,0:T(8,128)(2,1)S(1)}, bf16[48,1664]{1,0:T(8,128)(2,1)S(1)}, u32[]{:S(2)}, u32[]{:S(2)}) collective-permute-start(bf16[48,1664]{1,0:T(8,128)(2,1)S(1)} %collective-permute-done.refs_2_), channel_id=1, source_target_pairs={{0,2},{2,0},{4,6},{6,4},{1,3},{3,1},{5,7},{7,5},{8,10},{10,8},{12,... | collective-permute-start | bytes 479240 | tf_op jit(solution)/shard_map/ppermute | solution.py:473
  23.6 7.1 %collective-permute-start.11 = (bf16[48,1664]{1,0:T(8,128)(2,1)S(1)}, bf16[48,1664]{1,0:T(8,128)(2,1)S(1)}, u32[]{:S(2)}, u32[]{:S(2)}) collective-permute-start(bf16[48,1664]{1,0:T(8,128)(2,1)S(1)} %collective-permute-done.1.refs_3_), channel_id=1, source_target_pairs={{0,4},{2,6},{4,0},{6,2},{1,5},{3,7},{5,1},{7,3},{8,12},{10,14},{12... | collective-permute-start | bytes 479240 | tf_op jit(solution)/shard_map/ppermute | solution.py:473
  24.5 7.8 %collective-permute-start.10 = (bf16[48,1664]{1,0:T(8,128)(2,1)S(1)}, bf16[48,1664]{1,0:T(8,128)(2,1)S(1)}, u32[]{:S(2)}, u32[]{:S(2)}) collective-permute-start(bf16[48,1664]{1,0:T(8,128)(2,1)S(1)} %collective-permute-done.refs_2_), channel_id=1, source_target_pairs={{0,4},{2,6},{4,0},{6,2},{1,5},{3,7},{5,1},{7,3},{8,12},{10,14},{12... | collective-permute-start | bytes 479240 | tf_op jit(solution)/shard_map/ppermute | solution.py:473
  25.6 7.5 %collective-permute-start.8 = (bf16[48,1664]{1,0:T(8,128)(2,1)S(1)}, bf16[48,1664]{1,0:T(8,128)(2,1)S(1)}, u32[]{:S(2)}, u32[]{:S(2)}) collective-permute-start(bf16[48,1664]{1,0:T(8,128)(2,1)S(1)} %collective-permute-done.1.refs_3_), channel_id=1, source_target_pairs={{0,2},{2,0},{4,6},{6,4},{1,3},{3,1},{5,7},{7,5},{8,10},{10,8},{12,... | collective-permute-start | bytes 479240 | tf_op jit(solution)/shard_map/ppermute | solution.py:473
  26.7 8.7 %collective-permute-start.12 = (bf16[48,1664]{1,0:T(8,128)(2,1)S(1)}, bf16[48,1664]{1,0:T(8,128)(2,1)S(1)}, u32[]{:S(2)}, u32[]{:S(2)}) collective-permute-start(bf16[48,1664]{1,0:T(8,128)(2,1)S(1)} %collective-permute-done.9.refs_9_), channel_id=1, source_target_pairs={{0,2},{2,0},{4,6},{6,4},{1,3},{3,1},{5,7},{7,5},{8,10},{10,8},{12,... | collective-permute-start | bytes 479240 | tf_op jit(solution)/shard_map/ppermute | solution.py:473
  30.6 6.5 %collective-permute-start.14 = (bf16[48,1664]{1,0:T(8,128)(2,1)S(1)}, bf16[48,1664]{1,0:T(8,128)(2,1)S(1)}, u32[]{:S(2)}, u32[]{:S(2)}) collective-permute-start(bf16[48,1664]{1,0:T(8,128)(2,1)S(1)} %collective-permute-done.11.refs_11_), channel_id=1, source_target_pairs={{0,2},{2,0},{4,6},{6,4},{1,3},{3,1},{5,7},{7,5},{8,10},{10,8},{12,... | collective-permute-start | bytes 479240 | tf_op jit(solution)/shard_map/ppermute | solution.py:473
  65.0 7.2 %collective-permute-start.17 = (bf16[256,384]{1,0:T(8,128)(2,1)S(1)}, bf16[256,384]{1,0:T(8,128)(2,1)S(1)}, u32[]{:S(2)}, u32[]{:S(2)}) collective-permute-start(bf16[256,384]{1,0:T(8,128)(2,1)S(1)} %copy-done.2), channel_id=1, source_target_pairs={{0,1},{1,0},{2,3},{3,2},{4,5},{5,4},{6,7},{7,6},{8,9},{9,8},{10,11... | collective-permute-start | bytes 589832 | tf_op jit(solution)/shard_map/ppermute | solution.py:41
  65.5 6.8 %collective-permute-start.18 = (bf16[384,256]{1,0:T(8,128)(2,1)S(1)}, bf16[384,256]{1,0:T(8,128)(2,1)S(1)}, u32[]{:S(2)}, u32[]{:S(2)}) collective-permute-start(bf16[384,256]{1,0:T(8,128)(2,1)S(1)} %get-tuple-element.130), channel_id=1, source_target_pairs={{0,2},{2,0},{4,6},{6,4},{1,3},{3,1},{5,7},{7,5},{8,10},{10,8},{12,... | collective-permute-start | bytes 589832 | tf_op jit(solution)/shard_map/ppermute | solution.py:473
  66.1 6.5 %collective-permute-start.19 = (bf16[384,256]{1,0:T(8,128)(2,1)S(1)}, bf16[384,256]{1,0:T(8,128)(2,1)S(1)}, u32[]{:S(2)}, u32[]{:S(2)}) collective-permute-start(bf16[384,256]{1,0:T(8,128)(2,1)S(1)} %get-tuple-element.130), channel_id=1, source_target_pairs={{0,4},{2,6},{4,0},{6,2},{1,5},{3,7},{5,1},{7,3},{8,12},{10,14},{12... | collective-permute-start | bytes 589832 | tf_op jit(solution)/shard_map/ppermute | solution.py:473
  96.2 7.1 %collective-permute-start.26 = (bf16[192,256]{1,0:T(8,128)(2,1)S(1)}, bf16[192,256]{1,0:T(8,128)(2,1)S(1)}, u32[]{:S(2)}, u32[]{:S(2)}) collective-permute-start(bf16[192,256]{1,0:T(8,128)(2,1)S(1)} %slice.6), channel_id=1, source_target_pairs={{0,4},{2,6},{4,0},{6,2},{1,5},{3,7},{5,1},{7,3},{8,12},{10,14},{12... | collective-permute-start | bytes 294920 | tf_op jit(solution)/shard_map/ppermute | solution.py:473
  97.1 6.1 %collective-permute-start.27 = (bf16[192,256]{1,0:T(8,128)(2,1)S(1)}, bf16[192,256]{1,0:T(8,128)(2,1)S(1)}, u32[]{:S(2)}, u32[]{:S(2)}) collective-permute-start(bf16[192,256]{1,0:T(8,128)(2,1)S(1)} %slice.7), channel_id=1, source_target_pairs={{0,2},{2,0},{4,6},{6,4},{1,3},{3,1},{5,7},{7,5},{8,10},{10,8},{12,... | collective-permute-start | bytes 294920 | tf_op jit(solution)/shard_map/ppermute | solution.py:473
  103.3 10.8 %collective-permute-start.28 = (bf16[1152,256]{1,0:T(8,128)(2,1)S(1)}, bf16[1152,256]{1,0:T(8,128)(2,1)S(1)}, u32[]{:S(2)}, u32[]{:S(2)}) collective-permute-start(bf16[1152,256]{1,0:T(8,128)(2,1)S(1)} %constant_dynamic-update-slice_fusion.refs_0_), channel_id=1, source_target_pairs={{0,1},{1,0},{2,3},{3,2},{4,5},{5,4},{6,7},{7,6},{8,9},{9,8},{10,11... | collective-permute-start | bytes 1769480 | tf_op jit(solution)/shard_map/ppermute | solution.py:41
  103.9 9.5 %collective-permute-start.22 = (bf16[288,256]{1,0:T(8,128)(2,1)S(1)}, bf16[288,256]{1,0:T(8,128)(2,1)S(1)}, u32[]{:S(2)}, u32[]{:S(2)}) collective-permute-start(bf16[288,256]{1,0:T(8,128)(2,1)S(1)} %get-tuple-element.146), channel_id=1, source_target_pairs={{0,2},{2,0},{4,6},{6,4},{1,3},{3,1},{5,7},{7,5},{8,10},{10,8},{12,... | collective-permute-start | bytes 442376 | tf_op jit(solution)/shard_map/ppermute | solution.py:473
  105.3 8.7 %collective-permute-start.23 = (bf16[288,256]{1,0:T(8,128)(2,1)S(1)}, bf16[288,256]{1,0:T(8,128)(2,1)S(1)}, u32[]{:S(2)}, u32[]{:S(2)}) collective-permute-start(bf16[288,256]{1,0:T(8,128)(2,1)S(1)} %get-tuple-element.147), channel_id=1, source_target_pairs={{0,4},{2,6},{4,0},{6,2},{1,5},{3,7},{5,1},{7,3},{8,12},{10,14},{12... | collective-permute-start | bytes 442376 | tf_op jit(solution)/shard_map/ppermute | solution.py:473
  106.5 7.6 %collective-permute-start.24 = (bf16[288,256]{1,0:T(8,128)(2,1)S(1)}, bf16[288,256]{1,0:T(8,128)(2,1)S(1)}, u32[]{:S(2)}, u32[]{:S(2)}) collective-permute-start(bf16[288,256]{1,0:T(8,128)(2,1)S(1)} %get-tuple-element.148), channel_id=1, source_target_pairs={{0,6},{2,4},{4,2},{6,0},{1,7},{3,5},{5,3},{7,1},{8,14},{10,12},{12... | collective-permute-start | bytes 442376 | tf_op jit(solution)/shard_map/ppermute | solution.py:473
  115.8 9.3 %collective-permute-start.29 = (bf16[56,1152]{1,0:T(8,128)(2,1)S(1)}, bf16[56,1152]{1,0:T(8,128)(2,1)S(1)}, u32[]{:S(2)}, u32[]{:S(2)}) collective-permute-start(bf16[56,1152]{1,0:T(8,128)(2,1)S(1)} %get-tuple-element.174), channel_id=1, source_target_pairs={{0,8},{8,0},{16,24},{24,16},{1,9},{9,1},{17,25},{25,17},{2,10},{10... | collective-permute-start | bytes 387080 | tf_op jit(solution)/shard_map/ppermute | solution.py:473
  117.1 11.6 %collective-permute-start.30 = (bf16[56,1152]{1,0:T(8,128)(2,1)S(1)}, bf16[56,1152]{1,0:T(8,128)(2,1)S(1)}, u32[]{:S(2)}, u32[]{:S(2)}) collective-permute-start(bf16[56,1152]{1,0:T(8,128)(2,1)S(1)} %get-tuple-element.175), channel_id=1, source_target_pairs={{0,16},{8,24},{16,0},{24,8},{1,17},{9,25},{17,1},{25,9},{2,18},{10... | collective-permute-start | bytes 387080 | tf_op jit(solution)/shard_map/ppermute | solution.py:473
  118.5 10.1 %collective-permute-start.31 = (bf16[56,1152]{1,0:T(8,128)(2,1)S(1)}, bf16[56,1152]{1,0:T(8,128)(2,1)S(1)}, u32[]{:S(2)}, u32[]{:S(2)}) collective-permute-start(bf16[56,1152]{1,0:T(8,128)(2,1)S(1)} %get-tuple-element.176), channel_id=1, source_target_pairs={{0,24},{8,16},{16,8},{24,0},{1,25},{9,17},{17,9},{25,1},{2,26},{10... | collective-permute-start | bytes 387080 | tf_op jit(solution)/shard_map/ppermute | solution.py:473
  123.1 8.6 %collective-permute-start.35 = (bf16[192,384]{1,0:T(8,128)(2,1)S(1)}, bf16[192,384]{1,0:T(8,128)(2,1)S(1)}, u32[]{:S(2)}, u32[]{:S(2)}) collective-permute-start(bf16[192,384]{1,0:T(8,128)(2,1)S(1)} %get-tuple-element.195), channel_id=1, source_target_pairs={{0,2},{2,0},{4,6},{6,4},{1,3},{3,1},{5,7},{7,5},{8,10},{10,8},{12,... | collective-permute-start | bytes 442376 | tf_op jit(solution)/shard_map/ppermute | solution.py:473
  124.0 9.1 %collective-permute-start.36 = (bf16[192,384]{1,0:T(8,128)(2,1)S(1)}, bf16[192,384]{1,0:T(8,128)(2,1)S(1)}, u32[]{:S(2)}, u32[]{:S(2)}) collective-permute-start(bf16[192,384]{1,0:T(8,128)(2,1)S(1)} %get-tuple-element.196), channel_id=1, source_target_pairs={{0,4},{2,6},{4,0},{6,2},{1,5},{3,7},{5,1},{7,3},{8,12},{10,14},{12... | collective-permute-start | bytes 442376 | tf_op jit(solution)/shard_map/ppermute | solution.py:473
  125.1 8.0 %collective-permute-start.37 = (bf16[192,384]{1,0:T(8,128)(2,1)S(1)}, bf16[192,384]{1,0:T(8,128)(2,1)S(1)}, u32[]{:S(2)}, u32[]{:S(2)}) collective-permute-start(bf16[192,384]{1,0:T(8,128)(2,1)S(1)} %get-tuple-element.197), channel_id=1, source_target_pairs={{0,6},{2,4},{4,2},{6,0},{1,7},{3,5},{5,3},{7,1},{8,14},{10,12},{12... | collective-permute-start | bytes 442376 | tf_op jit(solution)/shard_map/ppermute | solution.py:473
  130.8 7.7 %collective-permute-start.33 = (bf16[48,512]{1,0:T(8,128)(2,1)S(1)}, bf16[48,512]{1,0:T(8,128)(2,1)S(1)}, u32[]{:S(2)}, u32[]{:S(2)}) collective-permute-start(bf16[48,512]{1,0:T(8,128)(2,1)S(1)} %get-tuple-element.185), channel_id=1, source_target_pairs={{0,4},{2,6},{4,0},{6,2},{1,5},{3,7},{5,1},{7,3},{8,12},{10,14},{12... | collective-permute-start | bytes 147464 | tf_op jit(solution)/shard_map/ppermute | solution.py:473
  131.7 6.8 %collective-permute-start.34 = (bf16[48,512]{1,0:T(8,128)(2,1)S(1)}, bf16[48,512]{1,0:T(8,128)(2,1)S(1)}, u32[]{:S(2)}, u32[]{:S(2)}) collective-permute-start(bf16[48,512]{1,0:T(8,128)(2,1)S(1)} %get-tuple-element.186), channel_id=1, source_target_pairs={{0,6},{2,4},{4,2},{6,0},{1,7},{3,5},{5,3},{7,1},{8,14},{10,12},{12... | collective-permute-start | bytes 147464 | tf_op jit(solution)/shard_map/ppermute | solution.py:473
  133.6 6.2 %collective-permute-start.38 = (bf16[48,384]{1,0:T(8,128)(2,1)S(1)}, bf16[48,384]{1,0:T(8,128)(2,1)S(1)}, u32[]{:S(2)}, u32[]{:S(2)}) collective-permute-start(bf16[48,384]{1,0:T(8,128)(2,1)S(1)} %get-tuple-element.203), channel_id=1, source_target_pairs={{0,8},{8,0},{16,24},{24,16},{1,9},{9,1},{17,25},{25,17},{2,10},{10... | collective-permute-start | bytes 110600 | tf_op jit(solution)/shard_map/ppermute | solution.py:473
  136.1 5.8 %collective-permute-start.40 = (bf16[48,384]{1,0:T(8,128)(2,1)S(1)}, bf16[48,384]{1,0:T(8,128)(2,1)S(1)}, u32[]{:S(2)}, u32[]{:S(2)}) collective-permute-start(bf16[48,384]{1,0:T(8,128)(2,1)S(1)} %get-tuple-element.205), channel_id=1, source_target_pairs={{0,24},{8,16},{16,8},{24,0},{1,25},{9,17},{17,9},{25,1},{2,26},{10... | collective-permute-start | bytes 110600 | tf_op jit(solution)/shard_map/ppermute | solution.py:473
  (20 other events, 226.6 us)

commit v7 on v6

--- a/solution.py
+++ b/solution.py
@@ -96,33 +96,37 @@
     copy.wait()
 
 
-def spread_bias(offset_ref, bias_ref):
+def spread_bias(offset_ref, seg_ref, bias_ref):
     heads, seq_len, _ = bias_ref.shape
     span = offset_ref.shape[1]
+    documents = lax.broadcasted_iota(jnp.int32, (8, seq_len), 0) == seg_ref[...]
+    same_doc = dot(documents.astype(bf16), documents.astype(bf16), 0, 0) > 0.5
     for at in range(heads):
         spread = jnp.broadcast_to(offset_ref[at : at + 1, :], (seq_len, span))
-        bias_ref[at] = pltpu.roll(spread, span - seq_len + 1, 1, stride=1, stride_axis=0)[:, :seq_len]
-
-
-def attend_forward(order, at_ref, x_ref, gain_ref, bias_ref, seg_ref, *refs):
-    *block_refs, part_ref, qkv_ref, probs_ref, ctx_ref, w_ref, out_w_ref, router_ref, turned_ref, half_ref = refs
-    seq_len = x_ref.shape[0]
+        bias = pltpu.roll(spread, span - seq_len + 1, 1, stride=1, stride_axis=0)[:, :seq_len]
+        bias_ref[at] = jnp.where(same_doc, bias, -1e30)
+
+
+def first_norm(at_ref, x_ref, gain_ref, h_ref, turned_ref, half_ref):
+    x_float = x_ref[...].astype(f32)
+    h_one = (x_float * rms_scale(x_float) * gain_ref[...].reshape(1, -1)).astype(bf16)
+    h_ref[...] = h_one
+    turned_ref[...] = dot(h_one, eye(h_one.shape[0]), 0, 0).astype(bf16)
+    half = half_ref.shape[0]
+    half_ref[...] = jnp.where(at_ref[2] == 0, turned_ref[:half, :], turned_ref[half:, :])
+
+
+def attend_forward(order, at_ref, h_ref, bias_ref, *refs):
+    *block_refs, part_ref, qkv_ref, probs_ref, ctx_ref, w_ref, out_w_ref, router_ref = refs
     heads, inner = probs_ref.shape[0], ctx_ref.shape[1]
     for rows, block_ref in zip(block_rows(at_ref, order, block_refs[0].shape[0]), block_refs):
         w_ref[rows, :] = block_ref[:, : 3 * inner]
         out_w_ref[rows, :] = block_ref[:, 3 * inner : 4 * inner]
         router_ref[rows, :] = block_ref[:, 4 * inner :]
-    x_float = x_ref[...].astype(f32)
-    h_one = (x_float * rms_scale(x_float) * gain_ref[...].reshape(1, -1)).astype(bf16)
-    turned_ref[...] = dot(h_one, eye(seq_len), 0, 0).astype(bf16)
-    half = half_ref.shape[0]
-    half_ref[...] = jnp.where(at_ref[2] == 0, turned_ref[:half, :], turned_ref[half:, :])
-    documents = lax.broadcasted_iota(jnp.int32, (8, seq_len), 0) == seg_ref[...]
-    same_doc = dot(documents.astype(bf16), documents.astype(bf16), 0, 0) > 0.5
-    qkv_ref[...] = dot(h_one, w_ref[...], 1, 0).astype(bf16)
+    qkv_ref[...] = dot(h_ref[...], w_ref[...], 1, 0).astype(bf16)
     for at in range(heads):
         take = lambda part: qkv_ref[:, part * inner + at * HEAD : part * inner + (at + 1) * HEAD]
-        scores = jnp.where(same_doc, dot(take(0), take(1), 1, 1) * 0.125 + bias_ref[at], -1e30)
+        scores = dot(take(0), take(1), 1, 1) * 0.125 + bias_ref[at]
         expo = jnp.exp(scores - jnp.max(scores, axis=1, keepdims=True))
         probs = expo * (1.0 / jnp.sum(expo, axis=1, keepdims=True))
         probs_ref[at] = probs
@@ -140,20 +144,24 @@
     return ((column == wanted) & (inside >= chunk * 4) & (inside < chunk * 4 + 4)).astype(bf16)
 
 
-def pack_slots(values, packed_ref):
+def pack_slots(values, packed_ref, low=0, before=None):
     if len(packed_ref.shape) == 2:
-        packed_ref[...] = values.astype(bf16)
+        packed_ref[:, low * 128 : low * 128 + values.shape[1]] = values.astype(bf16)
         return
     experts, chunks = packed_ref.shape[0], values.shape[1] // 128
+    first = (packed_ref.shape[1] - 24) // 16 * 16
     values = values.astype(bf16)
     spare = 0.0
     for c in range(chunks):
         chunk = values[:, c * 128 : (c + 1) * 128]
         for e in range(experts):
-            packed_ref[e, c * 16 : (c + 1) * 16, :] = chunk[e * 16 : (e + 1) * 16]
-        spare = spare + dot(spare_rows(experts, c), chunk[experts * 16 :], 1, 0)
+            packed_ref[e, (low + c) * 16 : (low + c + 1) * 16, :] = chunk[e * 16 : (e + 1) * 16]
+        spare = spare + dot(spare_rows(experts, low + c), chunk[experts * 16 :], 1, 0)
     for e in range(experts):
-        packed_ref[e, chunks * 16 :, :] = spare[e * 24 : (e + 1) * 24].astype(bf16)
+        rows = spare[e * 24 : (e + 1) * 24]
+        if before is not None:
+            rows = rows + before[e, first:, :].astype(f32)
+        packed_ref[e, first:, :] = rows.astype(bf16)
 
 
 def unpack_slots(packed_ref, low, target_ref, spare_ref):
@@ -170,16 +178,28 @@
         target_ref[experts * 16 :, lanes] = dot(spare_rows(experts, low + c), spare, 0, 0).astype(bf16)
 
 
-def dispatch(at_ref, x_ref, part_ref, peer_ref, gain_ref, slot_ref, g_ref, send_ref):
-    half = g_ref.shape[1]
+def slot_places(slot_ref, packed_ref):
+    slots = packed_ref.shape[0] * (1 if len(packed_ref.shape) == 2 else 20)
+    dims = (slots, slot_ref.shape[1])
+    return (lax.broadcasted_iota(jnp.int32, dims, 0) == slot_ref[...]).astype(bf16)
+
+
+def pack_cotangent(g_ref, slot_ref, packed_ref):
+    packed_ref[...] = jnp.zeros(packed_ref.shape, bf16)
+    pack_slots(dot(slot_places(slot_ref, packed_ref), g_ref[...], 1, 0), packed_ref, g_ref.shape[1] // 128)
+
+
+def dispatch(at_ref, x_ref, part_ref, peer_ref, gain_ref, slot_ref, before_ref, send_ref):
+    half = x_ref.shape[1] // 2
     x_one = x_ref[...].astype(f32) + (part_ref[...].astype(f32) + peer_ref[...].astype(f32))
     h_two = (x_one * rms_scale(x_one) * gain_ref[...].reshape(1, -1)).astype(bf16)
     mine = jnp.where(at_ref[2] == 0, h_two[:, :half], h_two[:, half:])
-    slots = send_ref.shape[0] * (1 if len(send_ref.shape) == 2 else 20)
-    dims = (slots, x_ref.shape[0])
-    place = (lax.broadcasted_iota(jnp.int32, dims, 0) == slot_ref[...]).astype(bf16)
-    sent = jnp.concatenate([dot(place, mine, 1, 0), dot(place, g_ref[...], 1, 0)], axis=1)
-    pack_slots(sent, send_ref)
+    if len(send_ref.shape) == 2:
+        send_ref[:, half:] = before_ref[:, half:]
+    else:
+        low, high = half // 128 * 16, half // 64 * 16
+        send_ref[:, low:high, :] = before_ref[:, low:high, :]
+    pack_slots(dot(slot_places(slot_ref, send_ref), mine, 1, 0), send_ref, 0, before_ref)
 
 
 def run_expert(
@@ -578,19 +598,34 @@
         ).astype(f32)
         per_offset = jnp.einsum("bh,ob->ho", rel_bias, offset_hot, precision=highest)
 
+        slot_of = expert_ids * slots + slot_ids
+        if tight:
+            spare_of = experts * 16 + expert_ids * 4 + slot_ids - 16
+            slot_of = jnp.where(slot_ids < 16, expert_ids * 16 + slot_ids, spare_of)
+        slot_of = jnp.where(drop_flags == 1, slot_total, slot_of)[None]
+
         def prepare(after):
             late_up, late_down, _ = lax.optimization_barrier((w_up[0], w_down[0], after))
-            late_offset, _ = lax.optimization_barrier((per_offset, after))
+            late_offset, late_x, _ = lax.optimization_barrier((per_offset, x_in, after))
             (bias,) = vmem_call(
-                spread_bias, (shape((heads_here, seq_len, seq_len), f32),), 0, late_offset
+                spread_bias, (shape((heads_here, seq_len, seq_len), f32),), 0, late_offset, seg_ids
             )
-            return [late_up.astype(bf16), late_down.astype(bf16), bias]
-
-        blocks, (up_w, down_w, bias) = gather_blocks(packed, prepare)
+            normed = vmem_call(
+                first_norm,
+                (shape((seq_len, width), bf16), shape((width, seq_len), bf16), shape((half, seq_len), bf16)),
+                0,
+                late_x,
+                gain_attn,
+                scalars=(device_at,),
+            )
+            return [late_up.astype(bf16), late_down.astype(bf16), bias, *normed]
+
+        blocks, beside = gather_blocks(packed, prepare)
+        up_w, down_w, bias, h_one, normed_turned, normed_mine = beside
         g_peer = swap_cores(d_out)
 
         square = seq_len * seq_len * heads_here * HEAD
-        attn_part, qkv, probs, context, qkv_w, out_w, router_w, normed_turned, normed_mine = vmem_call(
+        attn_part, qkv, probs, context, qkv_w, out_w, router_w = vmem_call(
             functools.partial(attend_forward, gather_order),
             (
                 shape((seq_len, width), bf16),
@@ -600,23 +635,16 @@
                 shape((width, 3 * inner), bf16),
                 shape((width, inner), bf16),
                 shape((width, wide - inner), bf16),
-                shape((width, seq_len), bf16),
-                shape((half, seq_len), bf16),
             ),
             8 * seq_len * width * inner + 4 * square,
-            x_in,
-            gain_attn,
+            h_one,
             bias,
-            seg_ids,
             *blocks,
             scalars=(device_at,),
         )
         attn_peer = swap_cores(attn_part)
-        slot_of = expert_ids * slots + slot_ids
-        if tight:
-            spare_of = experts * 16 + expert_ids * 4 + slot_ids - 16
-            slot_of = jnp.where(slot_ids < 16, expert_ids * 16 + slot_ids, spare_of)
-        slot_of = jnp.where(drop_flags == 1, slot_total, slot_of)[None]
+        late_g, _ = lax.optimization_barrier((d_out, attn_part))
+        (g_packed,) = vmem_call(pack_cotangent, (shape(packed_slots, bf16),), 0, late_g, slot_of)
         (send,) = vmem_call(
             dispatch,
             (shape(packed_slots, bf16),),
@@ -626,7 +654,7 @@
             attn_peer,
             gain_ffn,
             slot_of,
-            d_out,
+            g_packed,
             scalars=(device_at,),
         )
         got = lax.all_to_all(send.reshape(exchange), ("ex", "row"), 0, 0, tiled=True).reshape(packed_slots)

time: 143 us -> 142 us (level)
  waiting for transfers between devices: 20.4 us -> 18.4 us
    ppermute x34, waiting for transfers between devices: 16.8 us -> 15.3 us  [hop(): lax.ppermute(values, axis, [(i, i ^ step) for i in range(mesh.shape[axis])])]
    pallas_call x14 -> x16, Pallas kernels: 25.3 us -> 26.4 us  [vmem_call(): pl.pallas_call(kernel, out_shape=out_shape, in_specs=[pl.BlockSpec(memory...]
  transfers between devices with their start and end apart: 41 -> 41, of which waited for: 16 -> 16; matrix products, arithmetic and copies ran while one was open for 2% -> 2% of each run, Pallas kernels for 15% -> 17%
where the time goes in v7:
time: 142 us
  starting transfers between devices  42.7 us (30%)
  blocking collectives  40.4 us (28%)
  Pallas kernels  33.8 us (24%)
  waiting for transfers between devices  18.4 us (13%)
  other arithmetic  3.88 us (3%)
  local copies, waits for them, and re-layouts  1.52 us (1%)
    ppermute x34, starting transfers between devices, hop(): lax.ppermute(values, axis, [(i, i ^ step) for i in range(mesh.shape[axis])])  41.5 us
    pallas_call x16, Pallas kernels, vmem_call(): pl.pallas_call(kernel, out_shape=out_shape, in_specs=[pl.BlockSpec(memory...  26.4 us
    all_to_all x1, blocking collectives, per_device(): lax.all_to_all(send.reshape(exchange), ('ex', 'row'), 0, 0, tiled=True)  21.1 us
    all_to_all x1, blocking collectives, per_device(): lax.all_to_all(back.reshape(exchange), ('ex', 'row'), 0, 0, tiled=True)  19.3 us
    ppermute x34, waiting for transfers between devices, hop(): lax.ppermute(values, axis, [(i, i ^ step) for i in range(mesh.shape[axis])])  15.3 us
    pallas_call x2, Pallas kernels, grads_of_expert(): pl.pallas_call(expert_grads, out_shape=shape(dims, f32), in_specs=[pl.Blo...  5.48 us
    ppermute x7, waiting for transfers between devices, swap_cores(): return lax.ppermute(values, 'col', [(0, 1), (1, 0)])  3.13 us
    convert_element_type x2, other arithmetic, prepare(): return [late_up.astype(bf16), late_down.astype(bf16), bias, *normed]  3 us
  transfers between devices with their start and end apart: 41, of which 16 were waited for; matrix products, arithmetic and copies ran while one was open for 2% of the time, Pallas kernels for 17%

profile of v7, /device:TPU:0, one launch (start us, length us, event | category | flops | bytes accessed | tf_op | source)
XLA Modules:
  0.0 142.0 jit_solution(4036546128210885767)
XLA Ops:
  0.7 1.9 %shard_map.213.refs_0_ = bf16[48,1664]{1,0:T(8,128)(2,1)} custom-call(f32[3,48,384]{2,1,0:T(8,128)} %qkv_in, f32[48,384]{1,0:T(8,128)} %bitcast.25, f32[16,48]{1,0:T(8,128)} %bitcast.26), custom_call_target="tpu_custom_call" | custom-call | tf_op jit(solution)/shard_map/pallas_call | solution.py:581
  2.6 3.1 %collective-permute-start.2 = (bf16[48,1664]{1,0:T(8,128)(2,1)}, bf16[48,1664]{1,0:T(8,128)(2,1)S(1)}, u32[]{:S(2)}, u32[]{:S(2)}) collective-permute-start(bf16[48,1664]{1,0:T(8,128)(2,1)} %shard_map.213.refs_0_), channel_id=1, source_target_pairs={{0,8},{8,0},{16,24},{24,16},{1,9},{9,1},{17,25},{25,17},{2,10},{10... | collective-permute-start | bytes 479240 | tf_op jit(solution)/shard_map/ppermute | solution.py:493
  5.7 1.5 %collective-permute-start.3 = (bf16[48,1664]{1,0:T(8,128)(2,1)}, bf16[48,1664]{1,0:T(8,128)(2,1)S(1)}, u32[]{:S(2)}, u32[]{:S(2)}) collective-permute-start(bf16[48,1664]{1,0:T(8,128)(2,1)} %shard_map.213.refs_0_), channel_id=1, source_target_pairs={{0,2},{2,0},{4,6},{6,4},{1,3},{3,1},{5,7},{7,5},{8,10},{10,8},{12,... | collective-permute-start | bytes 479240 | tf_op jit(solution)/shard_map/ppermute | solution.py:493
  7.2 1.5 %collective-permute-start.4 = (bf16[48,1664]{1,0:T(8,128)(2,1)}, bf16[48,1664]{1,0:T(8,128)(2,1)S(1)}, u32[]{:S(2)}, u32[]{:S(2)}) collective-permute-start(bf16[48,1664]{1,0:T(8,128)(2,1)} %shard_map.213.refs_0_), channel_id=1, source_target_pairs={{0,4},{2,6},{4,0},{6,2},{1,5},{3,7},{5,1},{7,3},{8,12},{10,14},{12... | collective-permute-start | bytes 479240 | tf_op jit(solution)/shard_map/ppermute | solution.py:493
  8.7 2.6 %collective-permute-start = (bf16[48,1664]{1,0:T(8,128)(2,1)}, bf16[48,1664]{1,0:T(8,128)(2,1)S(1)}, u32[]{:S(2)}, u32[]{:S(2)}) collective-permute-start(bf16[48,1664]{1,0:T(8,128)(2,1)} %shard_map.213.refs_0_), channel_id=1, source_target_pairs={{0,16},{8,24},{16,0},{24,8},{1,17},{9,25},{17,1},{25,9},{2,18},{10... | collective-permute-start | bytes 479240 | tf_op jit(solution)/shard_map/ppermute | solution.py:493
  12.7 1.5 %collective-permute-start.5 = (bf16[48,1664]{1,0:T(8,128)(2,1)S(1)}, bf16[48,1664]{1,0:T(8,128)(2,1)S(1)}, u32[]{:S(2)}, u32[]{:S(2)}) collective-permute-start(bf16[48,1664]{1,0:T(8,128)(2,1)S(1)} %collective-permute-done.3.refs_4_), channel_id=1, source_target_pairs={{0,4},{2,6},{4,0},{6,2},{1,5},{3,7},{5,1},{7,3},{8,12},{10,14},{12... | collective-permute-start | bytes 479240 | tf_op jit(solution)/shard_map/ppermute | solution.py:493
  15.6 2.8 %convert_element_type.84.up_ref = bf16[768,1536]{1,0:T(8,128)(2,1)S(1)} convert(f32[768,1536]{1,0:T(8,128)} %bitcast.21) | non-fusion elementwise | flops 1179648 | bytes 7077888 | tf_op jit(solution)/shard_map/convert_element_type | solution.py:621
  27.7 2.1 %collective-permute-done.7.refs_6_ = bf16[48,1664]{1,0:T(8,128)(2,1)S(1)} collective-permute-done((bf16[48,1664]{1,0:T(8,128)(2,1)S(1)}, bf16[48,1664]{1,0:T(8,128)(2,1)S(1)}, u32[]{:S(2)}, u32[]{:S(2)}) %collective-permute-start.7) | collective-permute-done | bytes 159776 | tf_op jit(solution)/shard_map/ppermute | solution.py:493
  33.2 2.3 %collective-permute-done.12.refs_13_ = bf16[48,1664]{1,0:T(8,128)(2,1)S(1)} collective-permute-done((bf16[48,1664]{1,0:T(8,128)(2,1)S(1)}, bf16[48,1664]{1,0:T(8,128)(2,1)S(1)}, u32[]{:S(2)}, u32[]{:S(2)}) %collective-permute-start.12) | collective-permute-done | bytes 159776 | tf_op jit(solution)/shard_map/ppermute | solution.py:493
  35.5 1.7 %collective-permute-done.14.refs_15_ = bf16[48,1664]{1,0:T(8,128)(2,1)S(1)} collective-permute-done((bf16[48,1664]{1,0:T(8,128)(2,1)S(1)}, bf16[48,1664]{1,0:T(8,128)(2,1)S(1)}, u32[]{:S(2)}, u32[]{:S(2)}) %collective-permute-start.14) | collective-permute-done | bytes 159776 | tf_op jit(solution)/shard_map/ppermute | solution.py:493
  37.2 3.2 %shard_map.216 = (bf16[256,768]{1,0:T(8,128)(2,1)S(1)}, bf16[256,1152]{1,0:T(8,128)(2,1)S(1)}, f32[6,256,256]{2,1,0:T(8,128)S(1)}, bf16[256,384]{1,0:T(8,128)(2,...) custom-call(s32[3]{0:T(128)S(1)} %pad_add_fusion.at_ref, ...), custom_call_target="tpu_custom_call" | custom-call | flops 704643072 | bytes 9830400 | tf_op jit(solution)/shard_map/pallas_call | solution.py:52
  43.5 21.1 %all_to_all.10.got_ref = bf16[16,120,128]{2,1,0:T(8,128)(2,1)S(1)} all-to-all(bf16[16,120,128]{2,1,0:T(8,128)(2,1)S(1)} %shard_map.218), channel_id=1, replica_groups=mesh['ex'=4,'row'=4,'col'=2] {'ex','row'}, dimensions={0} | all-to-all | bytes 983040 | tf_op jit(solution)/shard_map/all_to_all | solution.py:660
  66.5 5.2 %shard_map.219 = (bf16[320,896]{1,0:T(8,128)(2,1)S(1)}, f32[320,768]{1,0:T(8,128)S(1)}, f32[320,16]{1,0:T(8,128)S(1)}, f32[320,1]{1,0:T(8,128)S(1)}, bf16[320,76...) custom-call(s32[3]{0:T(128)S(1)} %pad_add_fusion.at_ref, ...), custom_call_target="tpu_custom_call" | custom-call | flops 3019898880 | bytes 10425600 | tf_op jit(solution)/shard_map/pallas_call | solution.py:52
  72.1 2.0 %collective-permute-done.20.crossed_ref = bf16[320,896]{1,0:T(8,128)(2,1)S(1)} collective-permute-done((bf16[320,896]{1,0:T(8,128)(2,1)S(1)}, bf16[320,896]{1,0:T(8,128)(2,1)S(1)}, u32[]{:S(2)}, u32[]{:S(2)}) %collective-permute-start.20) | collective-permute-done | bytes 573472 | tf_op jit(solution)/shard_map/ppermute | solution.py:41
  74.1 1.5 %shard_map.220 = (bf16[16,120,128]{2,1,0:T(8,128)(2,1)S(1)}, f32[16,768]{1,0:T(8,128)S(1)}) custom-call(s32[3]{0:T(128)S(1)} %pad_add_fusion.at_ref, f32[320,768]{1,0:T(8,128)S(1)} %get-tuple-element.140.mine_ref, bf16[320,896]{1,0:T(8,128)(2,1)S(1)} %collective-permute-done.20.crossed_ref, f32[320,16]{1,0:T(8,128)S(1)} %get-tuple-element.144.probs_ref, ...), custom_call_target="tpu_custom_call" | custom-call | flops 3932160 | bytes 2807040 | tf_op jit(solution)/shard_map/pallas_call | solution.py:52
  75.6 19.3 %all_to_all.11.home_ref = bf16[16,120,128]{2,1,0:T(8,128)(2,1)S(1)} all-to-all(bf16[16,120,128]{2,1,0:T(8,128)(2,1)S(1)} %get-tuple-element.147), channel_id=1, replica_groups=mesh['ex'=4,'row'=4,'col'=2] {'ex','row'}, dimensions={0} | all-to-all | bytes 983040 | tf_op jit(solution)/shard_map/all_to_all | solution.py:699
  97.3 1.7 %shard_map.222 = (f32[256,768]{1,0:T(8,128)S(1)}, f32[1,768]{1,0:T(1,128)S(1)}, bf16[256,384]{1,0:T(8,128)(2,1)S(1)}, bf16[192,384]{1,0:T(8,128)(2,1)S(1)}, bf16...) custom-call(s32[3]{0:T(128)S(1)} %pad_add_fusion.at_ref, ...), custom_call_target="tpu_custom_call" | custom-call | flops 301989888 | bytes 4331520 | tf_op jit(solution)/shard_map/pallas_call | solution.py:52
  99.0 3.7 %shard_map.223 = (bf16[256,768]{1,0:T(8,128)(2,1)S(1)}, f32[8,512]{1,0:T(8,128)S(1)}, bf16[288,256]{1,0:T(8,128)(2,1)S(1)}, bf16[288,256]{1,0:T(8,128)(2,1)S(1)}...) custom-call(s32[3]{0:T(128)S(1)} %pad_add_fusion.at_ref, bf16[256,384]{1,0:T(8,128)(2,1)S(1)} %get-tuple-element.154.d_ctx_ref, ...), custom_call_target="tpu_custom_call" | custom-call | flops 704643072 | bytes 5128192 | tf_op jit(solution)/shard_map/pallas_call | solution.py:52
  103.4 1.5 %collective-permute-start.22 = (bf16[288,256]{1,0:T(8,128)(2,1)S(1)}, bf16[288,256]{1,0:T(8,128)(2,1)S(1)}, u32[]{:S(2)}, u32[]{:S(2)}) collective-permute-start(bf16[288,256]{1,0:T(8,128)(2,1)S(1)} %get-tuple-element.158), channel_id=1, source_target_pairs={{0,2},{2,0},{4,6},{6,4},{1,3},{3,1},{5,7},{7,5},{8,10},{10,8},{12,... | collective-permute-start | bytes 442376 | tf_op jit(solution)/shard_map/ppermute | solution.py:493
  107.0 1.3 shard_map.224
  108.4 1.8 %shard_map.225 = bf16[256,384]{1,0:T(8,128)(2,1)} custom-call(s32[3]{0:T(128)S(1)} %pad_add_fusion.at_ref, bf16[16,120,128]{2,1,0:T(8,128)(2,1)S(1)} %all_to_all.11.home_ref, s32[1,256]{1,0:T(1,128)S(1)} %bitcast.20, bf16[256,768]{1,0:T(8,128)(2,1)S(1)} %copy-done.1, bf16[256,768]{1,0:T(8,128)(2,1)S(1)} %get-tuple-element.134.part_ref, ...), custom_call_target="tpu_custom_call" | custom-call | flops 62914560 | bytes 1868800 | tf_op jit(solution)/shard_map/pallas_call | solution.py:52
  110.2 2.7 %shard_map.226 = f32[1536,768]{1,0:T(8,128)} custom-call(bf16[320,1536]{1,0:T(8,128)(2,1)S(1)} %get-tuple-element.169.left_ref, bf16[320,768]{1,0:T(8,128)(2,1)S(1)} %get-tuple-element.170.right_ref), custom_call_target="tpu_custom_call" | custom-call | flops 754974720 | bytes 7077888 | tf_op jit(solution)/shard_map/pallas_call | solution.py:728
  113.6 1.7 %shard_map.227 = (bf16[56,1152]{1,0:T(8,128)(2,1)S(1)}, bf16[56,1152]{1,0:T(8,128)(2,1)S(1)}, bf16[56,1152]{1,0:T(8,128)(2,1)S(1)}, bf16[56,1152]{1,0:T(8,128)(2,1)S(1)}) custom-call(s32[3]{0:T(128)S(1)} %pad_add_fusion.at_ref, bf16[768,256]{1,0:T(8,128)(2,1)S(1)} %get-tuple-element.173.turned_ref, f32[8,768]{1,0:T(8,128)S(1)} %get-tuple-element.167.small_ref, ...), custom_call_target="tpu_custom_call" | custom-call | flops 452984832 | bytes 2752512 | tf_op jit(solution)/shard_map/pallas_call | solution.py:52
  116.6 1.5 %collective-permute-start.30 = (bf16[56,1152]{1,0:T(8,128)(2,1)S(1)}, bf16[56,1152]{1,0:T(8,128)(2,1)S(1)}, u32[]{:S(2)}, u32[]{:S(2)}) collective-permute-start(bf16[56,1152]{1,0:T(8,128)(2,1)S(1)} %get-tuple-element.187), channel_id=1, source_target_pairs={{0,16},{8,24},{16,0},{24,8},{1,17},{9,25},{17,1},{25,9},{2,18},{10... | collective-permute-start | bytes 387080 | tf_op jit(solution)/shard_map/ppermute | solution.py:493
  118.1 1.7 %collective-permute-start.31 = (bf16[56,1152]{1,0:T(8,128)(2,1)S(1)}, bf16[56,1152]{1,0:T(8,128)(2,1)S(1)}, u32[]{:S(2)}, u32[]{:S(2)}) collective-permute-start(bf16[56,1152]{1,0:T(8,128)(2,1)S(1)} %get-tuple-element.188), channel_id=1, source_target_pairs={{0,24},{8,16},{16,8},{24,0},{1,25},{9,17},{17,9},{25,1},{2,26},{10... | collective-permute-start | bytes 387080 | tf_op jit(solution)/shard_map/ppermute | solution.py:493
  119.8 2.8 %shard_map.228 = f32[768,1536]{1,0:T(8,128)} custom-call(bf16[320,768]{1,0:T(8,128)(2,1)S(1)} %get-tuple-element.190.rows_ref.left_ref, bf16[320,1536]{1,0:T(8,128)(2,1)S(1)} %get-tuple-element.191.right_ref), custom_call_target="tpu_custom_call" | custom-call | flops 754974720 | bytes 7077888 | tf_op jit(solution)/shard_map/pallas_call | solution.py:728
  124.6 1.6 %collective-permute-start.37 = (bf16[192,384]{1,0:T(8,128)(2,1)S(1)}, bf16[192,384]{1,0:T(8,128)(2,1)S(1)}, u32[]{:S(2)}, u32[]{:S(2)}) collective-permute-start(bf16[192,384]{1,0:T(8,128)(2,1)S(1)} %get-tuple-element.209), channel_id=1, source_target_pairs={{0,6},{2,4},{4,2},{6,0},{1,7},{3,5},{5,3},{7,1},{8,14},{10,12},{12... | collective-permute-start | bytes 442376 | tf_op jit(solution)/shard_map/ppermute | solution.py:493
  126.1 2.0 %collective-permute-done.30.refs_2_ = bf16[56,1152]{1,0:T(8,128)(2,1)S(1)} collective-permute-done((bf16[56,1152]{1,0:T(8,128)(2,1)S(1)}, bf16[56,1152]{1,0:T(8,128)(2,1)S(1)}, u32[]{:S(2)}, u32[]{:S(2)}) %collective-permute-start.30) | collective-permute-done | bytes 129056 | tf_op jit(solution)/shard_map/ppermute | solution.py:493
  131.2 1.3 collective-permute-start.34
  133.2 2.5 %collective-permute-start.38 = (bf16[48,384]{1,0:T(8,128)(2,1)S(1)}, bf16[48,384]{1,0:T(8,128)(2,1)S(1)}, u32[]{:S(2)}, u32[]{:S(2)}) collective-permute-start(bf16[48,384]{1,0:T(8,128)(2,1)S(1)} %get-tuple-element.215), channel_id=1, source_target_pairs={{0,8},{8,0},{16,24},{24,16},{1,9},{9,1},{17,25},{25,17},{2,10},{10... | collective-permute-start | bytes 110600 | tf_op jit(solution)/shard_map/ppermute | solution.py:493
  135.6 2.4 %collective-permute-start.40 = (bf16[48,384]{1,0:T(8,128)(2,1)S(1)}, bf16[48,384]{1,0:T(8,128)(2,1)S(1)}, u32[]{:S(2)}, u32[]{:S(2)}) collective-permute-start(bf16[48,384]{1,0:T(8,128)(2,1)S(1)} %get-tuple-element.217), channel_id=1, source_target_pairs={{0,24},{8,16},{16,8},{24,0},{1,25},{9,17},{17,9},{25,1},{2,26},{10... | collective-permute-start | bytes 110600 | tf_op jit(solution)/shard_map/ppermute | solution.py:493
  138.0 1.4 shard_map.230
  (107 shorter events, 36.3 us)
Async XLA Ops:
  2.6 8.9 %collective-permute-start.2 = (bf16[48,1664]{1,0:T(8,128)(2,1)}, bf16[48,1664]{1,0:T(8,128)(2,1)S(1)}, u32[]{:S(2)}, u32[]{:S(2)}) collective-permute-start(bf16[48,1664]{1,0:T(8,128)(2,1)} %shard_map.213.refs_0_), channel_id=1, source_target_pairs={{0,8},{8,0},{16,24},{24,16},{1,9},{9,1},{17,25},{25,17},{2,10},{10... | collective-permute-start | bytes 479240 | tf_op jit(solution)/shard_map/ppermute | solution.py:493
  5.7 5.8 %collective-permute-start.3 = (bf16[48,1664]{1,0:T(8,128)(2,1)}, bf16[48,1664]{1,0:T(8,128)(2,1)S(1)}, u32[]{:S(2)}, u32[]{:S(2)}) collective-permute-start(bf16[48,1664]{1,0:T(8,128)(2,1)} %shard_map.213.refs_0_), channel_id=1, source_target_pairs={{0,2},{2,0},{4,6},{6,4},{1,3},{3,1},{5,7},{7,5},{8,10},{10,8},{12,... | collective-permute-start | bytes 479240 | tf_op jit(solution)/shard_map/ppermute | solution.py:493
  8.7 13.9 %collective-permute-start = (bf16[48,1664]{1,0:T(8,128)(2,1)}, bf16[48,1664]{1,0:T(8,128)(2,1)S(1)}, u32[]{:S(2)}, u32[]{:S(2)}) collective-permute-start(bf16[48,1664]{1,0:T(8,128)(2,1)} %shard_map.213.refs_0_), channel_id=1, source_target_pairs={{0,16},{8,24},{16,0},{24,8},{1,17},{9,25},{17,1},{25,9},{2,18},{10... | collective-permute-start | bytes 479240 | tf_op jit(solution)/shard_map/ppermute | solution.py:493
  11.3 11.3 %collective-permute-start.1 = (bf16[48,1664]{1,0:T(8,128)(2,1)}, bf16[48,1664]{1,0:T(8,128)(2,1)S(1)}, u32[]{:S(2)}, u32[]{:S(2)}) collective-permute-start(bf16[48,1664]{1,0:T(8,128)(2,1)} %shard_map.213.refs_0_), channel_id=1, source_target_pairs={{0,24},{8,16},{16,8},{24,0},{1,25},{9,17},{17,9},{25,1},{2,26},{10... | collective-permute-start | bytes 479240 | tf_op jit(solution)/shard_map/ppermute | solution.py:493
  12.7 10.0 %collective-permute-start.5 = (bf16[48,1664]{1,0:T(8,128)(2,1)S(1)}, bf16[48,1664]{1,0:T(8,128)(2,1)S(1)}, u32[]{:S(2)}, u32[]{:S(2)}) collective-permute-start(bf16[48,1664]{1,0:T(8,128)(2,1)S(1)} %collective-permute-done.3.refs_4_), channel_id=1, source_target_pairs={{0,4},{2,6},{4,0},{6,2},{1,5},{3,7},{5,1},{7,3},{8,12},{10,14},{12... | collective-permute-start | bytes 479240 | tf_op jit(solution)/shard_map/ppermute | solution.py:493
  14.5 11.2 %collective-permute-start.9 = (bf16[48,1664]{1,0:T(8,128)(2,1)S(1)}, bf16[48,1664]{1,0:T(8,128)(2,1)S(1)}, u32[]{:S(2)}, u32[]{:S(2)}) collective-permute-start(bf16[48,1664]{1,0:T(8,128)(2,1)S(1)} %collective-permute-done.2.refs_1_), channel_id=1, source_target_pairs={{0,4},{2,6},{4,0},{6,2},{1,5},{3,7},{5,1},{7,3},{8,12},{10,14},{12... | collective-permute-start | bytes 479240 | tf_op jit(solution)/shard_map/ppermute | solution.py:493
  15.1 11.7 %collective-permute-start.6 = (bf16[48,1664]{1,0:T(8,128)(2,1)S(1)}, bf16[48,1664]{1,0:T(8,128)(2,1)S(1)}, u32[]{:S(2)}, u32[]{:S(2)}) collective-permute-start(bf16[48,1664]{1,0:T(8,128)(2,1)S(1)} %collective-permute-done.2.refs_1_), channel_id=1, source_target_pairs={{0,2},{2,0},{4,6},{6,4},{1,3},{3,1},{5,7},{7,5},{8,10},{10,8},{12,... | collective-permute-start | bytes 479240 | tf_op jit(solution)/shard_map/ppermute | solution.py:493
  22.7 7.1 %collective-permute-start.7 = (bf16[48,1664]{1,0:T(8,128)(2,1)S(1)}, bf16[48,1664]{1,0:T(8,128)(2,1)S(1)}, u32[]{:S(2)}, u32[]{:S(2)}) collective-permute-start(bf16[48,1664]{1,0:T(8,128)(2,1)S(1)} %collective-permute-done.refs_2_), channel_id=1, source_target_pairs={{0,2},{2,0},{4,6},{6,4},{1,3},{3,1},{5,7},{7,5},{8,10},{10,8},{12,... | collective-permute-start | bytes 479240 | tf_op jit(solution)/shard_map/ppermute | solution.py:493
  23.7 7.0 %collective-permute-start.11 = (bf16[48,1664]{1,0:T(8,128)(2,1)S(1)}, bf16[48,1664]{1,0:T(8,128)(2,1)S(1)}, u32[]{:S(2)}, u32[]{:S(2)}) collective-permute-start(bf16[48,1664]{1,0:T(8,128)(2,1)S(1)} %collective-permute-done.1.refs_3_), channel_id=1, source_target_pairs={{0,4},{2,6},{4,0},{6,2},{1,5},{3,7},{5,1},{7,3},{8,12},{10,14},{12... | collective-permute-start | bytes 479240 | tf_op jit(solution)/shard_map/ppermute | solution.py:493
  24.8 7.6 %collective-permute-start.10 = (bf16[48,1664]{1,0:T(8,128)(2,1)S(1)}, bf16[48,1664]{1,0:T(8,128)(2,1)S(1)}, u32[]{:S(2)}, u32[]{:S(2)}) collective-permute-start(bf16[48,1664]{1,0:T(8,128)(2,1)S(1)} %collective-permute-done.refs_2_), channel_id=1, source_target_pairs={{0,4},{2,6},{4,0},{6,2},{1,5},{3,7},{5,1},{7,3},{8,12},{10,14},{12... | collective-permute-start | bytes 479240 | tf_op jit(solution)/shard_map/ppermute | solution.py:493
  25.7 7.5 %collective-permute-start.8 = (bf16[48,1664]{1,0:T(8,128)(2,1)S(1)}, bf16[48,1664]{1,0:T(8,128)(2,1)S(1)}, u32[]{:S(2)}, u32[]{:S(2)}) collective-permute-start(bf16[48,1664]{1,0:T(8,128)(2,1)S(1)} %collective-permute-done.1.refs_3_), channel_id=1, source_target_pairs={{0,2},{2,0},{4,6},{6,4},{1,3},{3,1},{5,7},{7,5},{8,10},{10,8},{12,... | collective-permute-start | bytes 479240 | tf_op jit(solution)/shard_map/ppermute | solution.py:493
  26.8 8.7 %collective-permute-start.12 = (bf16[48,1664]{1,0:T(8,128)(2,1)S(1)}, bf16[48,1664]{1,0:T(8,128)(2,1)S(1)}, u32[]{:S(2)}, u32[]{:S(2)}) collective-permute-start(bf16[48,1664]{1,0:T(8,128)(2,1)S(1)} %collective-permute-done.9.refs_9_), channel_id=1, source_target_pairs={{0,2},{2,0},{4,6},{6,4},{1,3},{3,1},{5,7},{7,5},{8,10},{10,8},{12,... | collective-permute-start | bytes 479240 | tf_op jit(solution)/shard_map/ppermute | solution.py:493
  30.7 6.5 %collective-permute-start.14 = (bf16[48,1664]{1,0:T(8,128)(2,1)S(1)}, bf16[48,1664]{1,0:T(8,128)(2,1)S(1)}, u32[]{:S(2)}, u32[]{:S(2)}) collective-permute-start(bf16[48,1664]{1,0:T(8,128)(2,1)S(1)} %collective-permute-done.11.refs_11_), channel_id=1, source_target_pairs={{0,2},{2,0},{4,6},{6,4},{1,3},{3,1},{5,7},{7,5},{8,10},{10,8},{12,... | collective-permute-start | bytes 479240 | tf_op jit(solution)/shard_map/ppermute | solution.py:493
  64.5 7.2 %collective-permute-start.17 = (bf16[256,384]{1,0:T(8,128)(2,1)S(1)}, bf16[256,384]{1,0:T(8,128)(2,1)S(1)}, u32[]{:S(2)}, u32[]{:S(2)}) collective-permute-start(bf16[256,384]{1,0:T(8,128)(2,1)S(1)} %copy-done.2), channel_id=1, source_target_pairs={{0,1},{1,0},{2,3},{3,2},{4,5},{5,4},{6,7},{7,6},{8,9},{9,8},{10,11... | collective-permute-start | bytes 589832 | tf_op jit(solution)/shard_map/ppermute | solution.py:41
  65.1 6.8 %collective-permute-start.18 = (bf16[384,256]{1,0:T(8,128)(2,1)S(1)}, bf16[384,256]{1,0:T(8,128)(2,1)S(1)}, u32[]{:S(2)}, u32[]{:S(2)}) collective-permute-start(bf16[384,256]{1,0:T(8,128)(2,1)S(1)} %get-tuple-element.142), channel_id=1, source_target_pairs={{0,2},{2,0},{4,6},{6,4},{1,3},{3,1},{5,7},{7,5},{8,10},{10,8},{12,... | collective-permute-start | bytes 589832 | tf_op jit(solution)/shard_map/ppermute | solution.py:493
  65.6 6.5 %collective-permute-start.19 = (bf16[384,256]{1,0:T(8,128)(2,1)S(1)}, bf16[384,256]{1,0:T(8,128)(2,1)S(1)}, u32[]{:S(2)}, u32[]{:S(2)}) collective-permute-start(bf16[384,256]{1,0:T(8,128)(2,1)S(1)} %get-tuple-element.142), channel_id=1, source_target_pairs={{0,4},{2,6},{4,0},{6,2},{1,5},{3,7},{5,1},{7,3},{8,12},{10,14},{12... | collective-permute-start | bytes 589832 | tf_op jit(solution)/shard_map/ppermute | solution.py:493
  95.7 7.0 %collective-permute-start.26 = (bf16[192,256]{1,0:T(8,128)(2,1)S(1)}, bf16[192,256]{1,0:T(8,128)(2,1)S(1)}, u32[]{:S(2)}, u32[]{:S(2)}) collective-permute-start(bf16[192,256]{1,0:T(8,128)(2,1)S(1)} %slice.6), channel_id=1, source_target_pairs={{0,4},{2,6},{4,0},{6,2},{1,5},{3,7},{5,1},{7,3},{8,12},{10,14},{12... | collective-permute-start | bytes 294920 | tf_op jit(solution)/shard_map/ppermute | solution.py:493
  96.6 6.1 %collective-permute-start.27 = (bf16[192,256]{1,0:T(8,128)(2,1)S(1)}, bf16[192,256]{1,0:T(8,128)(2,1)S(1)}, u32[]{:S(2)}, u32[]{:S(2)}) collective-permute-start(bf16[192,256]{1,0:T(8,128)(2,1)S(1)} %slice.7), channel_id=1, source_target_pairs={{0,2},{2,0},{4,6},{6,4},{1,3},{3,1},{5,7},{7,5},{8,10},{10,8},{12,... | collective-permute-start | bytes 294920 | tf_op jit(solution)/shard_map/ppermute | solution.py:493
  102.8 10.8 %collective-permute-start.28 = (bf16[1152,256]{1,0:T(8,128)(2,1)S(1)}, bf16[1152,256]{1,0:T(8,128)(2,1)S(1)}, u32[]{:S(2)}, u32[]{:S(2)}) collective-permute-start(bf16[1152,256]{1,0:T(8,128)(2,1)S(1)} %constant_dynamic-update-slice_fusion.refs_0_), channel_id=1, source_target_pairs={{0,1},{1,0},{2,3},{3,2},{4,5},{5,4},{6,7},{7,6},{8,9},{9,8},{10,11... | collective-permute-start | bytes 1769480 | tf_op jit(solution)/shard_map/ppermute | solution.py:41
  103.4 9.5 %collective-permute-start.22 = (bf16[288,256]{1,0:T(8,128)(2,1)S(1)}, bf16[288,256]{1,0:T(8,128)(2,1)S(1)}, u32[]{:S(2)}, u32[]{:S(2)}) collective-permute-start(bf16[288,256]{1,0:T(8,128)(2,1)S(1)} %get-tuple-element.158), channel_id=1, source_target_pairs={{0,2},{2,0},{4,6},{6,4},{1,3},{3,1},{5,7},{7,5},{8,10},{10,8},{12,... | collective-permute-start | bytes 442376 | tf_op jit(solution)/shard_map/ppermute | solution.py:493
  104.9 8.7 %collective-permute-start.23 = (bf16[288,256]{1,0:T(8,128)(2,1)S(1)}, bf16[288,256]{1,0:T(8,128)(2,1)S(1)}, u32[]{:S(2)}, u32[]{:S(2)}) collective-permute-start(bf16[288,256]{1,0:T(8,128)(2,1)S(1)} %get-tuple-element.159), channel_id=1, source_target_pairs={{0,4},{2,6},{4,0},{6,2},{1,5},{3,7},{5,1},{7,3},{8,12},{10,14},{12... | collective-permute-start | bytes 442376 | tf_op jit(solution)/shard_map/ppermute | solution.py:493
  106.0 7.6 %collective-permute-start.24 = (bf16[288,256]{1,0:T(8,128)(2,1)S(1)}, bf16[288,256]{1,0:T(8,128)(2,1)S(1)}, u32[]{:S(2)}, u32[]{:S(2)}) collective-permute-start(bf16[288,256]{1,0:T(8,128)(2,1)S(1)} %get-tuple-element.160), channel_id=1, source_target_pairs={{0,6},{2,4},{4,2},{6,0},{1,7},{3,5},{5,3},{7,1},{8,14},{10,12},{12... | collective-permute-start | bytes 442376 | tf_op jit(solution)/shard_map/ppermute | solution.py:493
  115.3 9.3 %collective-permute-start.29 = (bf16[56,1152]{1,0:T(8,128)(2,1)S(1)}, bf16[56,1152]{1,0:T(8,128)(2,1)S(1)}, u32[]{:S(2)}, u32[]{:S(2)}) collective-permute-start(bf16[56,1152]{1,0:T(8,128)(2,1)S(1)} %get-tuple-element.186), channel_id=1, source_target_pairs={{0,8},{8,0},{16,24},{24,16},{1,9},{9,1},{17,25},{25,17},{2,10},{10... | collective-permute-start | bytes 387080 | tf_op jit(solution)/shard_map/ppermute | solution.py:493
  116.6 11.6 %collective-permute-start.30 = (bf16[56,1152]{1,0:T(8,128)(2,1)S(1)}, bf16[56,1152]{1,0:T(8,128)(2,1)S(1)}, u32[]{:S(2)}, u32[]{:S(2)}) collective-permute-start(bf16[56,1152]{1,0:T(8,128)(2,1)S(1)} %get-tuple-element.187), channel_id=1, source_target_pairs={{0,16},{8,24},{16,0},{24,8},{1,17},{9,25},{17,1},{25,9},{2,18},{10... | collective-permute-start | bytes 387080 | tf_op jit(solution)/shard_map/ppermute | solution.py:493
  118.1 10.1 %collective-permute-start.31 = (bf16[56,1152]{1,0:T(8,128)(2,1)S(1)}, bf16[56,1152]{1,0:T(8,128)(2,1)S(1)}, u32[]{:S(2)}, u32[]{:S(2)}) collective-permute-start(bf16[56,1152]{1,0:T(8,128)(2,1)S(1)} %get-tuple-element.188), channel_id=1, source_target_pairs={{0,24},{8,16},{16,8},{24,0},{1,25},{9,17},{17,9},{25,1},{2,26},{10... | collective-permute-start | bytes 387080 | tf_op jit(solution)/shard_map/ppermute | solution.py:493
  122.6 8.6 %collective-permute-start.35 = (bf16[192,384]{1,0:T(8,128)(2,1)S(1)}, bf16[192,384]{1,0:T(8,128)(2,1)S(1)}, u32[]{:S(2)}, u32[]{:S(2)}) collective-permute-start(bf16[192,384]{1,0:T(8,128)(2,1)S(1)} %get-tuple-element.207), channel_id=1, source_target_pairs={{0,2},{2,0},{4,6},{6,4},{1,3},{3,1},{5,7},{7,5},{8,10},{10,8},{12,... | collective-permute-start | bytes 442376 | tf_op jit(solution)/shard_map/ppermute | solution.py:493
  123.5 9.1 %collective-permute-start.36 = (bf16[192,384]{1,0:T(8,128)(2,1)S(1)}, bf16[192,384]{1,0:T(8,128)(2,1)S(1)}, u32[]{:S(2)}, u32[]{:S(2)}) collective-permute-start(bf16[192,384]{1,0:T(8,128)(2,1)S(1)} %get-tuple-element.208), channel_id=1, source_target_pairs={{0,4},{2,6},{4,0},{6,2},{1,5},{3,7},{5,1},{7,3},{8,12},{10,14},{12... | collective-permute-start | bytes 442376 | tf_op jit(solution)/shard_map/ppermute | solution.py:493
  124.6 8.0 %collective-permute-start.37 = (bf16[192,384]{1,0:T(8,128)(2,1)S(1)}, bf16[192,384]{1,0:T(8,128)(2,1)S(1)}, u32[]{:S(2)}, u32[]{:S(2)}) collective-permute-start(bf16[192,384]{1,0:T(8,128)(2,1)S(1)} %get-tuple-element.209), channel_id=1, source_target_pairs={{0,6},{2,4},{4,2},{6,0},{1,7},{3,5},{5,3},{7,1},{8,14},{10,12},{12... | collective-permute-start | bytes 442376 | tf_op jit(solution)/shard_map/ppermute | solution.py:493
  130.3 7.7 %collective-permute-start.33 = (bf16[48,512]{1,0:T(8,128)(2,1)S(1)}, bf16[48,512]{1,0:T(8,128)(2,1)S(1)}, u32[]{:S(2)}, u32[]{:S(2)}) collective-permute-start(bf16[48,512]{1,0:T(8,128)(2,1)S(1)} %get-tuple-element.197), channel_id=1, source_target_pairs={{0,4},{2,6},{4,0},{6,2},{1,5},{3,7},{5,1},{7,3},{8,12},{10,14},{12... | collective-permute-start | bytes 147464 | tf_op jit(solution)/shard_map/ppermute | solution.py:493
  131.2 6.8 %collective-permute-start.34 = (bf16[48,512]{1,0:T(8,128)(2,1)S(1)}, bf16[48,512]{1,0:T(8,128)(2,1)S(1)}, u32[]{:S(2)}, u32[]{:S(2)}) collective-permute-start(bf16[48,512]{1,0:T(8,128)(2,1)S(1)} %get-tuple-element.198), channel_id=1, source_target_pairs={{0,6},{2,4},{4,2},{6,0},{1,7},{3,5},{5,3},{7,1},{8,14},{10,12},{12... | collective-permute-start | bytes 147464 | tf_op jit(solution)/shard_map/ppermute | solution.py:493
  133.2 6.2 %collective-permute-start.38 = (bf16[48,384]{1,0:T(8,128)(2,1)S(1)}, bf16[48,384]{1,0:T(8,128)(2,1)S(1)}, u32[]{:S(2)}, u32[]{:S(2)}) collective-permute-start(bf16[48,384]{1,0:T(8,128)(2,1)S(1)} %get-tuple-element.215), channel_id=1, source_target_pairs={{0,8},{8,0},{16,24},{24,16},{1,9},{9,1},{17,25},{25,17},{2,10},{10... | collective-permute-start | bytes 110600 | tf_op jit(solution)/shard_map/ppermute | solution.py:493
  135.6 5.8 %collective-permute-start.40 = (bf16[48,384]{1,0:T(8,128)(2,1)S(1)}, bf16[48,384]{1,0:T(8,128)(2,1)S(1)}, u32[]{:S(2)}, u32[]{:S(2)}) collective-permute-start(bf16[48,384]{1,0:T(8,128)(2,1)S(1)} %get-tuple-element.217), channel_id=1, source_target_pairs={{0,24},{8,16},{16,8},{24,0},{1,25},{9,17},{17,9},{25,1},{2,26},{10... | collective-permute-start | bytes 110600 | tf_op jit(solution)/shard_map/ppermute | solution.py:493
  (20 other events, 165.1 us)

commit v8 on v7

--- a/solution.py
+++ b/solution.py
@@ -799,11 +799,9 @@
             *normed_hops, _ = lax.optimization_barrier((*normed_hops, d_h_part))
             normed_near = jnp.concatenate(normed_hops, axis=0)
             normed_peer = swap_cores(normed_near)
-            late_home, act_b, d_y, _ = lax.optimization_barrier((home, act_b, d_y, small))
+            act_b, d_y, _ = lax.optimization_barrier((act_b, d_y, small))
             d_qkv_hops = plane_hops(d_qkv_turned[1:])
-            *d_qkv_hops, layer_out, grad_down = lax.optimization_barrier(
-                (*d_qkv_hops, land_at_home(late_home), grads_of_expert(act_b, d_y))
-            )
+            *d_qkv_hops, grad_down = lax.optimization_barrier((*d_qkv_hops, grads_of_expert(act_b, d_y)))
             terms = vmem_call(
                 qkv_terms,
                 [shape((own_rows + 8, 3 * inner), bf16)] * 4,
@@ -821,8 +819,8 @@
             line = line_hops(terms[1:])
             rows, d_pre, _ = lax.optimization_barrier((rows, d_pre, terms[0]))
             grad_up = grads_of_expert(rows, d_pre)
-            *out_pieces, _ = lax.optimization_barrier((*out_pieces, grad_up))
-            *line, grad_up = lax.optimization_barrier((*line, grad_up))
+            *out_pieces, late_home, _ = lax.optimization_barrier((*out_pieces, home, grad_up))
+            *line, grad_up, layer_out = lax.optimization_barrier((*line, grad_up, land_at_home(late_home)))
             split = vmem_call(
                 join_line,
                 [shape((own_rows, 512), bf16)] * 4,

time: 142 us -> 142 us (level)
  transfers between devices with their start and end apart: 41 -> 41, of which waited for: 16 -> 15; matrix products, arithmetic and copies ran while one was open for 2% -> 2% of each run, Pallas kernels for 17% -> 17%
where the time goes in v8:
time: 142 us
  starting transfers between devices  42.3 us (30%)
  blocking collectives  40.3 us (28%)
  Pallas kernels  33.8 us (24%)
  waiting for transfers between devices  18.5 us (13%)
  other arithmetic  3.88 us (3%)
  local copies, waits for them, and re-layouts  1.52 us (1%)
    ppermute x34, starting transfers between devices, hop(): lax.ppermute(values, axis, [(i, i ^ step) for i in range(mesh.shape[axis])])  41 us
    pallas_call x16, Pallas kernels, vmem_call(): pl.pallas_call(kernel, out_shape=out_shape, in_specs=[pl.BlockSpec(memory...  26.4 us
    all_to_all x1, blocking collectives, per_device(): lax.all_to_all(send.reshape(exchange), ('ex', 'row'), 0, 0, tiled=True)  21 us
    all_to_all x1, blocking collectives, per_device(): lax.all_to_all(back.reshape(exchange), ('ex', 'row'), 0, 0, tiled=True)  19.3 us
    ppermute x34, waiting for transfers between devices, hop(): lax.ppermute(values, axis, [(i, i ^ step) for i in range(mesh.shape[axis])])  15.4 us
    pallas_call x2, Pallas kernels, grads_of_expert(): pl.pallas_call(expert_grads, out_shape=shape(dims, f32), in_specs=[pl.Blo...  5.48 us
    ppermute x7, waiting for transfers between devices, swap_cores(): return lax.ppermute(values, 'col', [(0, 1), (1, 0)])  3.13 us
    convert_element_type x2, other arithmetic, prepare(): return [late_up.astype(bf16), late_down.astype(bf16), bias, *normed]  3 us
  transfers between devices with their start and end apart: 41, of which 15 were waited for; matrix products, arithmetic and copies ran while one was open for 2% of the time, Pallas kernels for 17%

profile of v8, /device:TPU:0, one launch (start us, length us, event | category | flops | bytes accessed | tf_op | source)
XLA Modules:
  0.0 141.6 jit_solution(5469438599453324268)
XLA Ops:
  0.7 1.9 %shard_map.213.refs_0_ = bf16[48,1664]{1,0:T(8,128)(2,1)} custom-call(f32[3,48,384]{2,1,0:T(8,128)} %qkv_in, f32[48,384]{1,0:T(8,128)} %bitcast.25, f32[16,48]{1,0:T(8,128)} %bitcast.26), custom_call_target="tpu_custom_call" | custom-call | tf_op jit(solution)/shard_map/pallas_call | solution.py:581
  2.6 3.1 %collective-permute-start.2 = (bf16[48,1664]{1,0:T(8,128)(2,1)}, bf16[48,1664]{1,0:T(8,128)(2,1)S(1)}, u32[]{:S(2)}, u32[]{:S(2)}) collective-permute-start(bf16[48,1664]{1,0:T(8,128)(2,1)} %shard_map.213.refs_0_), channel_id=1, source_target_pairs={{0,8},{8,0},{16,24},{24,16},{1,9},{9,1},{17,25},{25,17},{2,10},{10... | collective-permute-start | bytes 479240 | tf_op jit(solution)/shard_map/ppermute | solution.py:493
  5.7 1.5 %collective-permute-start.3 = (bf16[48,1664]{1,0:T(8,128)(2,1)}, bf16[48,1664]{1,0:T(8,128)(2,1)S(1)}, u32[]{:S(2)}, u32[]{:S(2)}) collective-permute-start(bf16[48,1664]{1,0:T(8,128)(2,1)} %shard_map.213.refs_0_), channel_id=1, source_target_pairs={{0,2},{2,0},{4,6},{6,4},{1,3},{3,1},{5,7},{7,5},{8,10},{10,8},{12,... | collective-permute-start | bytes 479240 | tf_op jit(solution)/shard_map/ppermute | solution.py:493
  7.2 1.5 %collective-permute-start.4 = (bf16[48,1664]{1,0:T(8,128)(2,1)}, bf16[48,1664]{1,0:T(8,128)(2,1)S(1)}, u32[]{:S(2)}, u32[]{:S(2)}) collective-permute-start(bf16[48,1664]{1,0:T(8,128)(2,1)} %shard_map.213.refs_0_), channel_id=1, source_target_pairs={{0,4},{2,6},{4,0},{6,2},{1,5},{3,7},{5,1},{7,3},{8,12},{10,14},{12... | collective-permute-start | bytes 479240 | tf_op jit(solution)/shard_map/ppermute | solution.py:493
  8.7 2.6 %collective-permute-start = (bf16[48,1664]{1,0:T(8,128)(2,1)}, bf16[48,1664]{1,0:T(8,128)(2,1)S(1)}, u32[]{:S(2)}, u32[]{:S(2)}) collective-permute-start(bf16[48,1664]{1,0:T(8,128)(2,1)} %shard_map.213.refs_0_), channel_id=1, source_target_pairs={{0,16},{8,24},{16,0},{24,8},{1,17},{9,25},{17,1},{25,9},{2,18},{10... | collective-permute-start | bytes 479240 | tf_op jit(solution)/shard_map/ppermute | solution.py:493
  12.7 1.5 %collective-permute-start.5 = (bf16[48,1664]{1,0:T(8,128)(2,1)S(1)}, bf16[48,1664]{1,0:T(8,128)(2,1)S(1)}, u32[]{:S(2)}, u32[]{:S(2)}) collective-permute-start(bf16[48,1664]{1,0:T(8,128)(2,1)S(1)} %collective-permute-done.3.refs_4_), channel_id=1, source_target_pairs={{0,4},{2,6},{4,0},{6,2},{1,5},{3,7},{5,1},{7,3},{8,12},{10,14},{12... | collective-permute-start | bytes 479240 | tf_op jit(solution)/shard_map/ppermute | solution.py:493
  15.6 2.8 %convert_element_type.84.up_ref = bf16[768,1536]{1,0:T(8,128)(2,1)S(1)} convert(f32[768,1536]{1,0:T(8,128)} %bitcast.21) | non-fusion elementwise | flops 1179648 | bytes 7077888 | tf_op jit(solution)/shard_map/convert_element_type | solution.py:621
  27.7 2.1 %collective-permute-done.7.refs_6_ = bf16[48,1664]{1,0:T(8,128)(2,1)S(1)} collective-permute-done((bf16[48,1664]{1,0:T(8,128)(2,1)S(1)}, bf16[48,1664]{1,0:T(8,128)(2,1)S(1)}, u32[]{:S(2)}, u32[]{:S(2)}) %collective-permute-start.7) | collective-permute-done | bytes 159776 | tf_op jit(solution)/shard_map/ppermute | solution.py:493
  31.8 1.4 collective-permute-done.8.refs_7_
  33.2 2.3 %collective-permute-done.12.refs_13_ = bf16[48,1664]{1,0:T(8,128)(2,1)S(1)} collective-permute-done((bf16[48,1664]{1,0:T(8,128)(2,1)S(1)}, bf16[48,1664]{1,0:T(8,128)(2,1)S(1)}, u32[]{:S(2)}, u32[]{:S(2)}) %collective-permute-start.12) | collective-permute-done | bytes 159776 | tf_op jit(solution)/shard_map/ppermute | solution.py:493
  35.5 1.7 %collective-permute-done.14.refs_15_ = bf16[48,1664]{1,0:T(8,128)(2,1)S(1)} collective-permute-done((bf16[48,1664]{1,0:T(8,128)(2,1)S(1)}, bf16[48,1664]{1,0:T(8,128)(2,1)S(1)}, u32[]{:S(2)}, u32[]{:S(2)}) %collective-permute-start.14) | collective-permute-done | bytes 159776 | tf_op jit(solution)/shard_map/ppermute | solution.py:493
  37.2 3.2 %shard_map.216 = (bf16[256,768]{1,0:T(8,128)(2,1)S(1)}, bf16[256,1152]{1,0:T(8,128)(2,1)S(1)}, f32[6,256,256]{2,1,0:T(8,128)S(1)}, bf16[256,384]{1,0:T(8,128)(2,...) custom-call(s32[3]{0:T(128)S(1)} %pad_add_fusion.at_ref, ...), custom_call_target="tpu_custom_call" | custom-call | flops 704643072 | bytes 9830400 | tf_op jit(solution)/shard_map/pallas_call | solution.py:52
  43.5 21.0 %all_to_all.10.got_ref = bf16[16,120,128]{2,1,0:T(8,128)(2,1)S(1)} all-to-all(bf16[16,120,128]{2,1,0:T(8,128)(2,1)S(1)} %shard_map.218), channel_id=1, replica_groups=mesh['ex'=4,'row'=4,'col'=2] {'ex','row'}, dimensions={0} | all-to-all | bytes 983040 | tf_op jit(solution)/shard_map/all_to_all | solution.py:660
  66.5 5.2 %shard_map.219 = (bf16[320,896]{1,0:T(8,128)(2,1)S(1)}, f32[320,768]{1,0:T(8,128)S(1)}, f32[320,16]{1,0:T(8,128)S(1)}, f32[320,1]{1,0:T(8,128)S(1)}, bf16[320,76...) custom-call(s32[3]{0:T(128)S(1)} %pad_add_fusion.at_ref, ...), custom_call_target="tpu_custom_call" | custom-call | flops 3019898880 | bytes 10425600 | tf_op jit(solution)/shard_map/pallas_call | solution.py:52
  72.1 2.0 %collective-permute-done.20.crossed_ref = bf16[320,896]{1,0:T(8,128)(2,1)S(1)} collective-permute-done((bf16[320,896]{1,0:T(8,128)(2,1)S(1)}, bf16[320,896]{1,0:T(8,128)(2,1)S(1)}, u32[]{:S(2)}, u32[]{:S(2)}) %collective-permute-start.20) | collective-permute-done | bytes 573472 | tf_op jit(solution)/shard_map/ppermute | solution.py:41
  74.1 1.5 %shard_map.220 = (bf16[16,120,128]{2,1,0:T(8,128)(2,1)S(1)}, f32[16,768]{1,0:T(8,128)S(1)}) custom-call(s32[3]{0:T(128)S(1)} %pad_add_fusion.at_ref, f32[320,768]{1,0:T(8,128)S(1)} %get-tuple-element.141.mine_ref, bf16[320,896]{1,0:T(8,128)(2,1)S(1)} %collective-permute-done.20.crossed_ref, f32[320,16]{1,0:T(8,128)S(1)} %get-tuple-element.145.probs_ref, ...), custom_call_target="tpu_custom_call" | custom-call | flops 3932160 | bytes 2807040 | tf_op jit(solution)/shard_map/pallas_call | solution.py:52
  75.6 19.3 %all_to_all.11.home_ref = bf16[16,120,128]{2,1,0:T(8,128)(2,1)S(1)} all-to-all(bf16[16,120,128]{2,1,0:T(8,128)(2,1)S(1)} %get-tuple-element.148), channel_id=1, replica_groups=mesh['ex'=4,'row'=4,'col'=2] {'ex','row'}, dimensions={0} | all-to-all | bytes 983040 | tf_op jit(solution)/shard_map/all_to_all | solution.py:699
  97.2 1.7 %shard_map.222 = (f32[256,768]{1,0:T(8,128)S(1)}, f32[1,768]{1,0:T(1,128)S(1)}, bf16[256,384]{1,0:T(8,128)(2,1)S(1)}, bf16[192,384]{1,0:T(8,128)(2,1)S(1)}, bf16...) custom-call(s32[3]{0:T(128)S(1)} %pad_add_fusion.at_ref, ...), custom_call_target="tpu_custom_call" | custom-call | flops 301989888 | bytes 4331520 | tf_op jit(solution)/shard_map/pallas_call | solution.py:52
  98.9 3.7 %shard_map.223 = (bf16[256,768]{1,0:T(8,128)(2,1)S(1)}, f32[8,512]{1,0:T(8,128)S(1)}, bf16[288,256]{1,0:T(8,128)(2,1)S(1)}, bf16[288,256]{1,0:T(8,128)(2,1)S(1)}...) custom-call(s32[3]{0:T(128)S(1)} %pad_add_fusion.at_ref, bf16[256,384]{1,0:T(8,128)(2,1)S(1)} %get-tuple-element.155.d_ctx_ref, ...), custom_call_target="tpu_custom_call" | custom-call | flops 704643072 | bytes 5128192 | tf_op jit(solution)/shard_map/pallas_call | solution.py:52
  103.3 1.5 %collective-permute-start.26 = (bf16[288,256]{1,0:T(8,128)(2,1)S(1)}, bf16[288,256]{1,0:T(8,128)(2,1)S(1)}, u32[]{:S(2)}, u32[]{:S(2)}) collective-permute-start(bf16[288,256]{1,0:T(8,128)(2,1)S(1)} %get-tuple-element.172), channel_id=1, source_target_pairs={{0,2},{2,0},{4,6},{6,4},{1,3},{3,1},{5,7},{7,5},{8,10},{10,8},{12,... | collective-permute-start | bytes 442376 | tf_op jit(solution)/shard_map/ppermute | solution.py:493
  108.3 2.7 %shard_map.225 = f32[1536,768]{1,0:T(8,128)} custom-call(bf16[320,1536]{1,0:T(8,128)(2,1)S(1)} %get-tuple-element.177.left_ref, bf16[320,768]{1,0:T(8,128)(2,1)S(1)} %get-tuple-element.178.right_ref), custom_call_target="tpu_custom_call" | custom-call | flops 754974720 | bytes 7077888 | tf_op jit(solution)/shard_map/pallas_call | solution.py:728
  111.0 2.5 %collective-permute-done.27.refs_4_ = bf16[288,256]{1,0:T(8,128)(2,1)S(1)} collective-permute-done((bf16[288,256]{1,0:T(8,128)(2,1)S(1)}, bf16[288,256]{1,0:T(8,128)(2,1)S(1)}, u32[]{:S(2)}, u32[]{:S(2)}) %collective-permute-start.27) | collective-permute-done | bytes 147488 | tf_op jit(solution)/shard_map/ppermute | solution.py:493
  113.5 1.7 %shard_map.226 = (bf16[56,1152]{1,0:T(8,128)(2,1)S(1)}, bf16[56,1152]{1,0:T(8,128)(2,1)S(1)}, bf16[56,1152]{1,0:T(8,128)(2,1)S(1)}, bf16[56,1152]{1,0:T(8,128)(2,1)S(1)}) custom-call(s32[3]{0:T(128)S(1)} %pad_add_fusion.at_ref, bf16[768,256]{1,0:T(8,128)(2,1)S(1)} %get-tuple-element.127.turned_ref, f32[8,768]{1,0:T(8,128)S(1)} %get-tuple-element.163.small_ref, ...), custom_call_target="tpu_custom_call" | custom-call | flops 452984832 | bytes 2752512 | tf_op jit(solution)/shard_map/pallas_call | solution.py:52
  116.6 1.5 %collective-permute-start.30 = (bf16[56,1152]{1,0:T(8,128)(2,1)S(1)}, bf16[56,1152]{1,0:T(8,128)(2,1)S(1)}, u32[]{:S(2)}, u32[]{:S(2)}) collective-permute-start(bf16[56,1152]{1,0:T(8,128)(2,1)S(1)} %get-tuple-element.183), channel_id=1, source_target_pairs={{0,16},{8,24},{16,0},{24,8},{1,17},{9,25},{17,1},{25,9},{2,18},{10... | collective-permute-start | bytes 387080 | tf_op jit(solution)/shard_map/ppermute | solution.py:493
  118.0 1.7 %collective-permute-start.31 = (bf16[56,1152]{1,0:T(8,128)(2,1)S(1)}, bf16[56,1152]{1,0:T(8,128)(2,1)S(1)}, u32[]{:S(2)}, u32[]{:S(2)}) collective-permute-start(bf16[56,1152]{1,0:T(8,128)(2,1)S(1)} %get-tuple-element.184), channel_id=1, source_target_pairs={{0,24},{8,16},{16,8},{24,0},{1,25},{9,17},{17,9},{25,1},{2,26},{10... | collective-permute-start | bytes 387080 | tf_op jit(solution)/shard_map/ppermute | solution.py:493
  119.7 2.8 %shard_map.227 = f32[768,1536]{1,0:T(8,128)} custom-call(bf16[320,768]{1,0:T(8,128)(2,1)S(1)} %get-tuple-element.187.rows_ref.left_ref, bf16[320,1536]{1,0:T(8,128)(2,1)S(1)} %get-tuple-element.188.right_ref), custom_call_target="tpu_custom_call" | custom-call | flops 754974720 | bytes 7077888 | tf_op jit(solution)/shard_map/pallas_call | solution.py:728
  124.3 1.8 %collective-permute-start.37 = (bf16[192,384]{1,0:T(8,128)(2,1)S(1)}, bf16[192,384]{1,0:T(8,128)(2,1)S(1)}, u32[]{:S(2)}, u32[]{:S(2)}) collective-permute-start(bf16[192,384]{1,0:T(8,128)(2,1)S(1)} %get-tuple-element.209), channel_id=1, source_target_pairs={{0,6},{2,4},{4,2},{6,0},{1,7},{3,5},{5,3},{7,1},{8,14},{10,12},{12... | collective-permute-start | bytes 442376 | tf_op jit(solution)/shard_map/ppermute | solution.py:493
  126.1 1.8 %shard_map.228 = bf16[256,384]{1,0:T(8,128)(2,1)} custom-call(s32[3]{0:T(128)S(1)} %pad_add_fusion.at_ref, bf16[16,120,128]{2,1,0:T(8,128)(2,1)S(1)} %all_to_all.11.home_ref, s32[1,256]{1,0:T(1,128)S(1)} %bitcast.20, bf16[256,768]{1,0:T(8,128)(2,1)S(1)} %copy-done.1, bf16[256,768]{1,0:T(8,128)(2,1)S(1)} %get-tuple-element.135.part_ref, ...), custom_call_target="tpu_custom_call" | custom-call | flops 62914560 | bytes 1868800 | tf_op jit(solution)/shard_map/pallas_call | solution.py:52
  130.9 1.6 %collective-permute-start.34 = (bf16[48,512]{1,0:T(8,128)(2,1)S(1)}, bf16[48,512]{1,0:T(8,128)(2,1)S(1)}, u32[]{:S(2)}, u32[]{:S(2)}) collective-permute-start(bf16[48,512]{1,0:T(8,128)(2,1)S(1)} %get-tuple-element.202), channel_id=1, source_target_pairs={{0,6},{2,4},{4,2},{6,0},{1,7},{3,5},{5,3},{7,1},{8,14},{10,12},{12... | collective-permute-start | bytes 147464 | tf_op jit(solution)/shard_map/ppermute | solution.py:493
  133.1 1.9 %collective-permute-start.40 = (bf16[48,384]{1,0:T(8,128)(2,1)S(1)}, bf16[48,384]{1,0:T(8,128)(2,1)S(1)}, u32[]{:S(2)}, u32[]{:S(2)}) collective-permute-start(bf16[48,384]{1,0:T(8,128)(2,1)S(1)} %get-tuple-element.217), channel_id=1, source_target_pairs={{0,24},{8,16},{16,8},{24,0},{1,25},{9,17},{17,9},{25,1},{2,26},{10... | collective-permute-start | bytes 110600 | tf_op jit(solution)/shard_map/ppermute | solution.py:493
  135.0 2.0 %collective-permute-start.39 = (bf16[48,384]{1,0:T(8,128)(2,1)S(1)}, bf16[48,384]{1,0:T(8,128)(2,1)S(1)}, u32[]{:S(2)}, u32[]{:S(2)}) collective-permute-start(bf16[48,384]{1,0:T(8,128)(2,1)S(1)} %get-tuple-element.216), channel_id=1, source_target_pairs={{0,16},{8,24},{16,0},{24,8},{1,17},{9,25},{17,1},{25,9},{2,18},{10... | collective-permute-start | bytes 110600 | tf_op jit(solution)/shard_map/ppermute | solution.py:493
  137.5 1.4 shard_map.230
  (107 shorter events, 35.8 us)
Async XLA Ops:
  2.6 8.9 %collective-permute-start.2 = (bf16[48,1664]{1,0:T(8,128)(2,1)}, bf16[48,1664]{1,0:T(8,128)(2,1)S(1)}, u32[]{:S(2)}, u32[]{:S(2)}) collective-permute-start(bf16[48,1664]{1,0:T(8,128)(2,1)} %shard_map.213.refs_0_), channel_id=1, source_target_pairs={{0,8},{8,0},{16,24},{24,16},{1,9},{9,1},{17,25},{25,17},{2,10},{10... | collective-permute-start | bytes 479240 | tf_op jit(solution)/shard_map/ppermute | solution.py:493
  5.7 5.8 %collective-permute-start.3 = (bf16[48,1664]{1,0:T(8,128)(2,1)}, bf16[48,1664]{1,0:T(8,128)(2,1)S(1)}, u32[]{:S(2)}, u32[]{:S(2)}) collective-permute-start(bf16[48,1664]{1,0:T(8,128)(2,1)} %shard_map.213.refs_0_), channel_id=1, source_target_pairs={{0,2},{2,0},{4,6},{6,4},{1,3},{3,1},{5,7},{7,5},{8,10},{10,8},{12,... | collective-permute-start | bytes 479240 | tf_op jit(solution)/shard_map/ppermute | solution.py:493
  8.7 13.9 %collective-permute-start = (bf16[48,1664]{1,0:T(8,128)(2,1)}, bf16[48,1664]{1,0:T(8,128)(2,1)S(1)}, u32[]{:S(2)}, u32[]{:S(2)}) collective-permute-start(bf16[48,1664]{1,0:T(8,128)(2,1)} %shard_map.213.refs_0_), channel_id=1, source_target_pairs={{0,16},{8,24},{16,0},{24,8},{1,17},{9,25},{17,1},{25,9},{2,18},{10... | collective-permute-start | bytes 479240 | tf_op jit(solution)/shard_map/ppermute | solution.py:493
  11.3 11.3 %collective-permute-start.1 = (bf16[48,1664]{1,0:T(8,128)(2,1)}, bf16[48,1664]{1,0:T(8,128)(2,1)S(1)}, u32[]{:S(2)}, u32[]{:S(2)}) collective-permute-start(bf16[48,1664]{1,0:T(8,128)(2,1)} %shard_map.213.refs_0_), channel_id=1, source_target_pairs={{0,24},{8,16},{16,8},{24,0},{1,25},{9,17},{17,9},{25,1},{2,26},{10... | collective-permute-start | bytes 479240 | tf_op jit(solution)/shard_map/ppermute | solution.py:493
  12.7 10.0 %collective-permute-start.5 = (bf16[48,1664]{1,0:T(8,128)(2,1)S(1)}, bf16[48,1664]{1,0:T(8,128)(2,1)S(1)}, u32[]{:S(2)}, u32[]{:S(2)}) collective-permute-start(bf16[48,1664]{1,0:T(8,128)(2,1)S(1)} %collective-permute-done.3.refs_4_), channel_id=1, source_target_pairs={{0,4},{2,6},{4,0},{6,2},{1,5},{3,7},{5,1},{7,3},{8,12},{10,14},{12... | collective-permute-start | bytes 479240 | tf_op jit(solution)/shard_map/ppermute | solution.py:493
  14.5 11.2 %collective-permute-start.6 = (bf16[48,1664]{1,0:T(8,128)(2,1)S(1)}, bf16[48,1664]{1,0:T(8,128)(2,1)S(1)}, u32[]{:S(2)}, u32[]{:S(2)}) collective-permute-start(bf16[48,1664]{1,0:T(8,128)(2,1)S(1)} %collective-permute-done.2.refs_1_), channel_id=1, source_target_pairs={{0,2},{2,0},{4,6},{6,4},{1,3},{3,1},{5,7},{7,5},{8,10},{10,8},{12,... | collective-permute-start | bytes 479240 | tf_op jit(solution)/shard_map/ppermute | solution.py:493
  15.4 11.4 %collective-permute-start.9 = (bf16[48,1664]{1,0:T(8,128)(2,1)S(1)}, bf16[48,1664]{1,0:T(8,128)(2,1)S(1)}, u32[]{:S(2)}, u32[]{:S(2)}) collective-permute-start(bf16[48,1664]{1,0:T(8,128)(2,1)S(1)} %collective-permute-done.2.refs_1_), channel_id=1, source_target_pairs={{0,4},{2,6},{4,0},{6,2},{1,5},{3,7},{5,1},{7,3},{8,12},{10,14},{12... | collective-permute-start | bytes 479240 | tf_op jit(solution)/shard_map/ppermute | solution.py:493
  22.7 7.1 %collective-permute-start.7 = (bf16[48,1664]{1,0:T(8,128)(2,1)S(1)}, bf16[48,1664]{1,0:T(8,128)(2,1)S(1)}, u32[]{:S(2)}, u32[]{:S(2)}) collective-permute-start(bf16[48,1664]{1,0:T(8,128)(2,1)S(1)} %collective-permute-done.refs_2_), channel_id=1, source_target_pairs={{0,2},{2,0},{4,6},{6,4},{1,3},{3,1},{5,7},{7,5},{8,10},{10,8},{12,... | collective-permute-start | bytes 479240 | tf_op jit(solution)/shard_map/ppermute | solution.py:493
  23.7 7.0 %collective-permute-start.11 = (bf16[48,1664]{1,0:T(8,128)(2,1)S(1)}, bf16[48,1664]{1,0:T(8,128)(2,1)S(1)}, u32[]{:S(2)}, u32[]{:S(2)}) collective-permute-start(bf16[48,1664]{1,0:T(8,128)(2,1)S(1)} %collective-permute-done.1.refs_3_), channel_id=1, source_target_pairs={{0,4},{2,6},{4,0},{6,2},{1,5},{3,7},{5,1},{7,3},{8,12},{10,14},{12... | collective-permute-start | bytes 479240 | tf_op jit(solution)/shard_map/ppermute | solution.py:493
  24.8 8.4 %collective-permute-start.8 = (bf16[48,1664]{1,0:T(8,128)(2,1)S(1)}, bf16[48,1664]{1,0:T(8,128)(2,1)S(1)}, u32[]{:S(2)}, u32[]{:S(2)}) collective-permute-start(bf16[48,1664]{1,0:T(8,128)(2,1)S(1)} %collective-permute-done.1.refs_3_), channel_id=1, source_target_pairs={{0,2},{2,0},{4,6},{6,4},{1,3},{3,1},{5,7},{7,5},{8,10},{10,8},{12,... | collective-permute-start | bytes 479240 | tf_op jit(solution)/shard_map/ppermute | solution.py:493
  25.7 7.5 %collective-permute-start.10 = (bf16[48,1664]{1,0:T(8,128)(2,1)S(1)}, bf16[48,1664]{1,0:T(8,128)(2,1)S(1)}, u32[]{:S(2)}, u32[]{:S(2)}) collective-permute-start(bf16[48,1664]{1,0:T(8,128)(2,1)S(1)} %collective-permute-done.refs_2_), channel_id=1, source_target_pairs={{0,4},{2,6},{4,0},{6,2},{1,5},{3,7},{5,1},{7,3},{8,12},{10,14},{12... | collective-permute-start | bytes 479240 | tf_op jit(solution)/shard_map/ppermute | solution.py:493
  26.8 8.7 %collective-permute-start.12 = (bf16[48,1664]{1,0:T(8,128)(2,1)S(1)}, bf16[48,1664]{1,0:T(8,128)(2,1)S(1)}, u32[]{:S(2)}, u32[]{:S(2)}) collective-permute-start(bf16[48,1664]{1,0:T(8,128)(2,1)S(1)} %collective-permute-done.9.refs_9_), channel_id=1, source_target_pairs={{0,2},{2,0},{4,6},{6,4},{1,3},{3,1},{5,7},{7,5},{8,10},{10,8},{12,... | collective-permute-start | bytes 479240 | tf_op jit(solution)/shard_map/ppermute | solution.py:493
  29.8 5.7 %collective-permute-start.13 = (bf16[48,1664]{1,0:T(8,128)(2,1)S(1)}, bf16[48,1664]{1,0:T(8,128)(2,1)S(1)}, u32[]{:S(2)}, u32[]{:S(2)}) collective-permute-start(bf16[48,1664]{1,0:T(8,128)(2,1)S(1)} %collective-permute-done.7.refs_6_), channel_id=1, source_target_pairs={{0,4},{2,6},{4,0},{6,2},{1,5},{3,7},{5,1},{7,3},{8,12},{10,14},{12... | collective-permute-start | bytes 479240 | tf_op jit(solution)/shard_map/ppermute | solution.py:493
  30.7 6.5 %collective-permute-start.14 = (bf16[48,1664]{1,0:T(8,128)(2,1)S(1)}, bf16[48,1664]{1,0:T(8,128)(2,1)S(1)}, u32[]{:S(2)}, u32[]{:S(2)}) collective-permute-start(bf16[48,1664]{1,0:T(8,128)(2,1)S(1)} %collective-permute-done.11.refs_11_), channel_id=1, source_target_pairs={{0,2},{2,0},{4,6},{6,4},{1,3},{3,1},{5,7},{7,5},{8,10},{10,8},{12,... | collective-permute-start | bytes 479240 | tf_op jit(solution)/shard_map/ppermute | solution.py:493
  64.5 7.2 %collective-permute-start.17 = (bf16[256,384]{1,0:T(8,128)(2,1)S(1)}, bf16[256,384]{1,0:T(8,128)(2,1)S(1)}, u32[]{:S(2)}, u32[]{:S(2)}) collective-permute-start(bf16[256,384]{1,0:T(8,128)(2,1)S(1)} %copy-done.2), channel_id=1, source_target_pairs={{0,1},{1,0},{2,3},{3,2},{4,5},{5,4},{6,7},{7,6},{8,9},{9,8},{10,11... | collective-permute-start | bytes 589832 | tf_op jit(solution)/shard_map/ppermute | solution.py:41
  65.0 6.8 %collective-permute-start.18 = (bf16[384,256]{1,0:T(8,128)(2,1)S(1)}, bf16[384,256]{1,0:T(8,128)(2,1)S(1)}, u32[]{:S(2)}, u32[]{:S(2)}) collective-permute-start(bf16[384,256]{1,0:T(8,128)(2,1)S(1)} %get-tuple-element.143), channel_id=1, source_target_pairs={{0,2},{2,0},{4,6},{6,4},{1,3},{3,1},{5,7},{7,5},{8,10},{10,8},{12,... | collective-permute-start | bytes 589832 | tf_op jit(solution)/shard_map/ppermute | solution.py:493
  65.6 6.5 %collective-permute-start.19 = (bf16[384,256]{1,0:T(8,128)(2,1)S(1)}, bf16[384,256]{1,0:T(8,128)(2,1)S(1)}, u32[]{:S(2)}, u32[]{:S(2)}) collective-permute-start(bf16[384,256]{1,0:T(8,128)(2,1)S(1)} %get-tuple-element.143), channel_id=1, source_target_pairs={{0,4},{2,6},{4,0},{6,2},{1,5},{3,7},{5,1},{7,3},{8,12},{10,14},{12... | collective-permute-start | bytes 589832 | tf_op jit(solution)/shard_map/ppermute | solution.py:493
  95.6 7.0 %collective-permute-start.23 = (bf16[192,256]{1,0:T(8,128)(2,1)S(1)}, bf16[192,256]{1,0:T(8,128)(2,1)S(1)}, u32[]{:S(2)}, u32[]{:S(2)}) collective-permute-start(bf16[192,256]{1,0:T(8,128)(2,1)S(1)} %slice.6), channel_id=1, source_target_pairs={{0,4},{2,6},{4,0},{6,2},{1,5},{3,7},{5,1},{7,3},{8,12},{10,14},{12... | collective-permute-start | bytes 294920 | tf_op jit(solution)/shard_map/ppermute | solution.py:493
  96.6 6.1 %collective-permute-start.24 = (bf16[192,256]{1,0:T(8,128)(2,1)S(1)}, bf16[192,256]{1,0:T(8,128)(2,1)S(1)}, u32[]{:S(2)}, u32[]{:S(2)}) collective-permute-start(bf16[192,256]{1,0:T(8,128)(2,1)S(1)} %slice.7), channel_id=1, source_target_pairs={{0,2},{2,0},{4,6},{6,4},{1,3},{3,1},{5,7},{7,5},{8,10},{10,8},{12,... | collective-permute-start | bytes 294920 | tf_op jit(solution)/shard_map/ppermute | solution.py:493
  102.8 10.8 %collective-permute-start.25 = (bf16[1152,256]{1,0:T(8,128)(2,1)S(1)}, bf16[1152,256]{1,0:T(8,128)(2,1)S(1)}, u32[]{:S(2)}, u32[]{:S(2)}) collective-permute-start(bf16[1152,256]{1,0:T(8,128)(2,1)S(1)} %constant_dynamic-update-slice_fusion.refs_0_), channel_id=1, source_target_pairs={{0,1},{1,0},{2,3},{3,2},{4,5},{5,4},{6,7},{7,6},{8,9},{9,8},{10,11... | collective-permute-start | bytes 1769480 | tf_op jit(solution)/shard_map/ppermute | solution.py:41
  103.3 7.7 %collective-permute-start.26 = (bf16[288,256]{1,0:T(8,128)(2,1)S(1)}, bf16[288,256]{1,0:T(8,128)(2,1)S(1)}, u32[]{:S(2)}, u32[]{:S(2)}) collective-permute-start(bf16[288,256]{1,0:T(8,128)(2,1)S(1)} %get-tuple-element.172), channel_id=1, source_target_pairs={{0,2},{2,0},{4,6},{6,4},{1,3},{3,1},{5,7},{7,5},{8,10},{10,8},{12,... | collective-permute-start | bytes 442376 | tf_op jit(solution)/shard_map/ppermute | solution.py:493
  104.8 8.7 %collective-permute-start.27 = (bf16[288,256]{1,0:T(8,128)(2,1)S(1)}, bf16[288,256]{1,0:T(8,128)(2,1)S(1)}, u32[]{:S(2)}, u32[]{:S(2)}) collective-permute-start(bf16[288,256]{1,0:T(8,128)(2,1)S(1)} %get-tuple-element.173), channel_id=1, source_target_pairs={{0,4},{2,6},{4,0},{6,2},{1,5},{3,7},{5,1},{7,3},{8,12},{10,14},{12... | collective-permute-start | bytes 442376 | tf_op jit(solution)/shard_map/ppermute | solution.py:493
  105.9 7.6 %collective-permute-start.28 = (bf16[288,256]{1,0:T(8,128)(2,1)S(1)}, bf16[288,256]{1,0:T(8,128)(2,1)S(1)}, u32[]{:S(2)}, u32[]{:S(2)}) collective-permute-start(bf16[288,256]{1,0:T(8,128)(2,1)S(1)} %get-tuple-element.174), channel_id=1, source_target_pairs={{0,6},{2,4},{4,2},{6,0},{1,7},{3,5},{5,3},{7,1},{8,14},{10,12},{12... | collective-permute-start | bytes 442376 | tf_op jit(solution)/shard_map/ppermute | solution.py:493
  115.3 9.1 %collective-permute-start.29 = (bf16[56,1152]{1,0:T(8,128)(2,1)S(1)}, bf16[56,1152]{1,0:T(8,128)(2,1)S(1)}, u32[]{:S(2)}, u32[]{:S(2)}) collective-permute-start(bf16[56,1152]{1,0:T(8,128)(2,1)S(1)} %get-tuple-element.182), channel_id=1, source_target_pairs={{0,8},{8,0},{16,24},{24,16},{1,9},{9,1},{17,25},{25,17},{2,10},{10... | collective-permute-start | bytes 387080 | tf_op jit(solution)/shard_map/ppermute | solution.py:493
  116.6 11.6 %collective-permute-start.30 = (bf16[56,1152]{1,0:T(8,128)(2,1)S(1)}, bf16[56,1152]{1,0:T(8,128)(2,1)S(1)}, u32[]{:S(2)}, u32[]{:S(2)}) collective-permute-start(bf16[56,1152]{1,0:T(8,128)(2,1)S(1)} %get-tuple-element.183), channel_id=1, source_target_pairs={{0,16},{8,24},{16,0},{24,8},{1,17},{9,25},{17,1},{25,9},{2,18},{10... | collective-permute-start | bytes 387080 | tf_op jit(solution)/shard_map/ppermute | solution.py:493
  118.0 10.1 %collective-permute-start.31 = (bf16[56,1152]{1,0:T(8,128)(2,1)S(1)}, bf16[56,1152]{1,0:T(8,128)(2,1)S(1)}, u32[]{:S(2)}, u32[]{:S(2)}) collective-permute-start(bf16[56,1152]{1,0:T(8,128)(2,1)S(1)} %get-tuple-element.184), channel_id=1, source_target_pairs={{0,24},{8,16},{16,8},{24,0},{1,25},{9,17},{17,9},{25,1},{2,26},{10... | collective-permute-start | bytes 387080 | tf_op jit(solution)/shard_map/ppermute | solution.py:493
  122.5 8.3 %collective-permute-start.35 = (bf16[192,384]{1,0:T(8,128)(2,1)S(1)}, bf16[192,384]{1,0:T(8,128)(2,1)S(1)}, u32[]{:S(2)}, u32[]{:S(2)}) collective-permute-start(bf16[192,384]{1,0:T(8,128)(2,1)S(1)} %get-tuple-element.207), channel_id=1, source_target_pairs={{0,2},{2,0},{4,6},{6,4},{1,3},{3,1},{5,7},{7,5},{8,10},{10,8},{12,... | collective-permute-start | bytes 442376 | tf_op jit(solution)/shard_map/ppermute | solution.py:493
  123.4 9.1 %collective-permute-start.36 = (bf16[192,384]{1,0:T(8,128)(2,1)S(1)}, bf16[192,384]{1,0:T(8,128)(2,1)S(1)}, u32[]{:S(2)}, u32[]{:S(2)}) collective-permute-start(bf16[192,384]{1,0:T(8,128)(2,1)S(1)} %get-tuple-element.208), channel_id=1, source_target_pairs={{0,4},{2,6},{4,0},{6,2},{1,5},{3,7},{5,1},{7,3},{8,12},{10,14},{12... | collective-permute-start | bytes 442376 | tf_op jit(solution)/shard_map/ppermute | solution.py:493
  124.3 8.2 %collective-permute-start.37 = (bf16[192,384]{1,0:T(8,128)(2,1)S(1)}, bf16[192,384]{1,0:T(8,128)(2,1)S(1)}, u32[]{:S(2)}, u32[]{:S(2)}) collective-permute-start(bf16[192,384]{1,0:T(8,128)(2,1)S(1)} %get-tuple-element.209), channel_id=1, source_target_pairs={{0,6},{2,4},{4,2},{6,0},{1,7},{3,5},{5,3},{7,1},{8,14},{10,12},{12... | collective-permute-start | bytes 442376 | tf_op jit(solution)/shard_map/ppermute | solution.py:493
  130.2 7.3 %collective-permute-start.33 = (bf16[48,512]{1,0:T(8,128)(2,1)S(1)}, bf16[48,512]{1,0:T(8,128)(2,1)S(1)}, u32[]{:S(2)}, u32[]{:S(2)}) collective-permute-start(bf16[48,512]{1,0:T(8,128)(2,1)S(1)} %get-tuple-element.201), channel_id=1, source_target_pairs={{0,4},{2,6},{4,0},{6,2},{1,5},{3,7},{5,1},{7,3},{8,12},{10,14},{12... | collective-permute-start | bytes 147464 | tf_op jit(solution)/shard_map/ppermute | solution.py:493
  130.9 6.6 %collective-permute-start.34 = (bf16[48,512]{1,0:T(8,128)(2,1)S(1)}, bf16[48,512]{1,0:T(8,128)(2,1)S(1)}, u32[]{:S(2)}, u32[]{:S(2)}) collective-permute-start(bf16[48,512]{1,0:T(8,128)(2,1)S(1)} %get-tuple-element.202), channel_id=1, source_target_pairs={{0,6},{2,4},{4,2},{6,0},{1,7},{3,5},{5,3},{7,1},{8,14},{10,12},{12... | collective-permute-start | bytes 147464 | tf_op jit(solution)/shard_map/ppermute | solution.py:493
  133.1 5.8 %collective-permute-start.40 = (bf16[48,384]{1,0:T(8,128)(2,1)S(1)}, bf16[48,384]{1,0:T(8,128)(2,1)S(1)}, u32[]{:S(2)}, u32[]{:S(2)}) collective-permute-start(bf16[48,384]{1,0:T(8,128)(2,1)S(1)} %get-tuple-element.217), channel_id=1, source_target_pairs={{0,24},{8,16},{16,8},{24,0},{1,25},{9,17},{17,9},{25,1},{2,26},{10... | collective-permute-start | bytes 110600 | tf_op jit(solution)/shard_map/ppermute | solution.py:493
  (20 other events, 163.4 us)
